TPU v7x, 512 devices: a whole 4x8x8 slice. The times are simulated.
512 devices in a mesh: gx: 8 (over x, y_lo), gy: 8 (over z), gz: 8 (over y_hi, core).
Axes of the slice: x: 4, y: 8 (y_hi: 4, y_lo: 2; y = y_hi * 2 + y_lo), z: 8, core: 2. Of those that a mesh axis runs over, the one named last changes fastest.
Arguments:
- tokens: bfloat16 [2048, 7168], P(('gy', 'gx'), 'gz'), may hold values from -6 to 6
- w_up: bfloat16 [7168, 28672], P('gz', ('gx', 'gy')), may hold values from -0.1875 to 0.1875
- act_grad: bfloat16 [2048, 28672], P('gy', ('gx', 'gz')), may hold values from -6 to 6
Outputs:
- activated: bfloat16 [2048, 28672], P('gy', ('gx', 'gz'))
- input_grad: bfloat16 [2048, 7168], P(('gy', 'gx'), 'gz')
- weight_grad: bfloat16 [7168, 28672], P('gz', ('gx', 'gy'))
All inputs are finite; a program needn't handle non-finite values.
Results may differ from a plain program's by a relative error of at most 0.022.
Values may be sent and summed in bfloat16 or wider, within the bound.
No kernel may reach another device: no remote copies, remote signals or barrier semaphores. Data moves between devices by JAX's collectives and lax.ppermute only.
A program may use at most 64 MiB of HBM per device.

v0:
```python
import jax
import jax.numpy as jnp
from jax import lax
from jax.sharding import PartitionSpec as P


def gelu_tanh(values):
    return jax.nn.gelu(values, approximate=True)


def body(tokens, w_up, act_grad):
    near = lax.all_gather(tokens, "gx", axis=0, tiled=True)
    weight_cols = lax.all_gather(w_up, "gy", axis=1, tiled=True)
    partial_value = jnp.dot(near, weight_cols, preferred_element_type=jnp.float32)
    hidden = lax.psum_scatter(
        partial_value.astype(jnp.bfloat16), "gz", scatter_dimension=1, tiled=True
    ).astype(jnp.float32)
    activated, pullback = jax.vjp(gelu_tanh, hidden)
    hidden_grad = pullback(act_grad.astype(jnp.float32))[0].astype(jnp.bfloat16)
    activated = activated.astype(jnp.bfloat16)
    cot_cols = lax.all_gather(hidden_grad, "gz", axis=1, tiled=True)
    cot_rows = lax.all_to_all(cot_cols, "gy", split_axis=1, concat_axis=0, tiled=True)
    all_rows = lax.all_gather(near, "gy", axis=0, tiled=True)
    weight_grad = lax.dot_general(
        all_rows, cot_rows, (((0,), (0,)), ((), ())), preferred_element_type=jnp.float32
    ).astype(jnp.bfloat16)
    input_grad = lax.psum_scatter(
        lax.dot_general(
            cot_cols, weight_cols, (((1,), (1,)), ((), ())), preferred_element_type=jnp.float32
        ).astype(jnp.bfloat16),
        "gx",
        scatter_dimension=0,
        tiled=True,
    )
    return (activated, input_grad, weight_grad)


def solution(mesh):
    in_specs = (P(("gy", "gx"), "gz"), P("gz", ("gx", "gy")), P("gy", ("gx", "gz")))
    out_specs = (P("gy", ("gx", "gz")), P(("gy", "gx"), "gz"), P("gz", ("gx", "gy")))
    return jax.shard_map(body, mesh=mesh, in_specs=in_specs, out_specs=out_specs, check_vma=False)
```

profile of v0, /device:TPU:1, one launch (start us, length us, event | category | flops | bytes accessed | tf_op | source)
XLA Modules:
  0.0 312.1 jit_solution(11031358648810543055)
XLA Ops:
  7.2 0.0 all-gather.4.cloned.1.call-start
  7.2 0.7 all-gather.4.cloned.1.call-update
  7.9 0.0 reduce-scatter.3.cloned.1.call-start
  7.9 24.4 %all_gather.12 = bf16[256,896]{1,0:T(8,128)(2,1)S(1)} all-gather(bf16[32,896]{1,0:T(8,128)(2,1)} %param.3), channel_id=1, replica_groups=mesh['gx'=8,'gy'=8,'gz'=8] {'gx'}, dimensions={0}, use_global_device_ids=true | all-gather | bytes 516096 | tf_op jit(solution)/shard_map/all_gather | solution.py:12
  32.3 0.0 copy-start.1
  32.3 0.0 copy-start.2
  32.3 62.4 %all-gather.4.cloned.1.call-done = bf16[896,3584]{0,1:T(8,128)(2,1)} async-done(((bf16[896,448]{0,1:T(8,128)(2,1)}), bf16[896,3584]{0,1:T(8,128)(2,1)}) %all-gather.4.cloned.1.call-update) | async-done | bytes 6422544 | tf_op jit(solution)/shard_map/all_gather | solution.py:13
  94.7 6.2 %convolution_convert_fusion = bf16[256,3584]{0,1:T(8,128)(2,1)} fusion(bf16[256,896]{1,0:T(8,128)(2,1)S(1)} %all_gather.12, bf16[896,3584]{0,1:T(8,128)(2,1)} %all-gather.4.cloned.1.call-done), kind=kOutput, calls=%fused_computation | convolution fusion | flops 1645084672 | bytes 8716288 | tf_op jit(solution)/shard_map/dot_general | solution.py:14
  100.9 0.0 copy-done.1
  100.9 0.0 reduce-scatter.3.cloned.1.call-update
  100.9 0.0 all-gather.6.cloned.1.call-start
  101.0 41.4 %reduce-scatter.3.cloned.1.call-done = bf16[256,448]{0,1:T(8,128)(2,1)} async-done(((bf16[256,3584]{0,1:T(8,128)(2,1)}), bf16[256,448]{0,1:T(8,128)(2,1)}) %reduce-scatter.3.cloned.1.call-update) | async-done | bytes 229392 | tf_op jit(solution)/shard_map/reduce_scatter | solution.py:15
  142.4 0.0 copy-done.2
  142.4 2.1 fusion.4
  144.5 0.0 all-gather.6.cloned.1.call-update
  144.5 0.0 all-gather.8.cloned.1.call-start
  144.6 0.5 all-gather.8.cloned.1.call-update
  145.1 37.1 %all-gather.6.cloned.1.call-done = bf16[256,3584]{0,1:T(8,128)(2,1)} async-done(((bf16[256,448]{0,1:T(8,128)(2,1)}), bf16[256,3584]{0,1:T(8,128)(2,1)}) %all-gather.6.cloned.1.call-update) | async-done | bytes 1835024 | tf_op jit(solution)/shard_map/all_gather | solution.py:21
  182.2 0.0 copy-start
  182.2 8.1 %all-to-all-start = ((bf16[256,8,448]{0,2,1:T(8,128)(2,1)}), bf16[256,8,448]{0,2,1:T(8,128)(2,1)}, u32[]{:S(2)}, u32[]{:S(2)}) async-start(bf16[256,8,448]{0,2,1:T(8,128)(2,1)} %bitcast.12), calls=%async_computation.2 | async-start | bytes 3670016 | tf_op jit(solution)/shard_map/all_to_all | solution.py:22
  190.3 0.0 reduce-scatter.5.cloned.1.call-start
  190.3 0.0 copy-done
  190.3 5.7 %convolution_convert_fusion.2 = bf16[256,896]{1,0:T(8,128)(2,1)} fusion(bf16[256,3584]{0,1:T(8,128)(2,1)S(1)} %copy-done, bf16[896,3584]{0,1:T(8,128)(2,1)} %all-gather.4.cloned.1.call-done), kind=kOutput, calls=%fused_computation.3 | convolution fusion | flops 1644396544 | bytes 8716288 | tf_op jit(solution)/shard_map/dot_general | solution.py:28
  196.0 0.0 reduce-scatter.5.cloned.1.call-update
  196.1 55.8 %all-to-all-done = bf16[256,8,448]{0,2,1:T(8,128)(2,1)} async-done(((bf16[256,8,448]{0,2,1:T(8,128)(2,1)}), bf16[256,8,448]{0,2,1:T(8,128)(2,1)}, u32[]{:S(2)}, u32[]{:S(2)}) %all-to-all-start) | async-done | bytes 1835040 | tf_op jit(solution)/shard_map/all_to_all | solution.py:22
  251.9 1.7 copy.8
  253.6 15.1 %all-gather.8.cloned.1.call-done = bf16[2048,896]{1,0:T(8,128)(2,1)} async-done(((bf16[256,896]{1,0:T(8,128)(2,1)}), bf16[2048,896]{1,0:T(8,128)(2,1)}) %all-gather.8.cloned.1.call-update) | async-done | bytes 3670032 | tf_op jit(solution)/shard_map/all_gather | solution.py:23
  268.7 5.0 %fusion = bf16[896,448]{0,1:T(8,128)(2,1)} fusion(bf16[2048,448]{0,1:T(8,128)(2,1)S(1)} %bitcast.13, bf16[2048,896]{1,0:T(8,128)(2,1)} %all-gather.8.cloned.1.call-done), kind=kOutput, calls=%fused_computation.2 | convolution fusion | flops 1644568576 | bytes 6307840 | tf_op jit(solution)/shard_map/dot_general | solution.py:24
  273.7 31.9 %reduce-scatter.5.cloned.1.call-done = bf16[32,896]{1,0:T(8,128)(2,1)} async-done(((bf16[256,896]{1,0:T(8,128)(2,1)}), bf16[32,896]{1,0:T(8,128)(2,1)}) %reduce-scatter.5.cloned.1.call-update) | async-done | bytes 57360 | tf_op jit(solution)/shard_map/reduce_scatter | solution.py:27
Async XLA Ops:
  7.2 87.6 %all-gather.4.cloned.1.call-start = ((), (), s32[]{:S(2)}) async-start(), calls=%async_computation.3 | async-start | bytes 7225344 | tf_op jit(solution)/shard_map/all_gather | solution.py:13
  7.9 134.5 %reduce-scatter.3.cloned.1.call-start = ((), (), s32[]{:S(2)}) async-start(), calls=%async_computation.4 | async-start | bytes 2064384 | tf_op jit(solution)/shard_map/reduce_scatter | solution.py:15
  32.3 68.6 %copy-start.1 = (bf16[256,896]{1,0:T(8,128)(2,1)}, bf16[256,896]{1,0:T(8,128)(2,1)S(1)}, u32[]{:S(2)}) copy-start(bf16[256,896]{1,0:T(8,128)(2,1)S(1)} %all_gather.12) | copy-start | bytes 1376260
  32.3 110.1 %copy-start.2 = (bf16[256,448]{0,1:T(8,128)(2,1)S(1)}, bf16[256,448]{0,1:T(8,128)(2,1)}, u32[]{:S(2)}) copy-start(bf16[256,448]{0,1:T(8,128)(2,1)} %param.5) | copy-start | bytes 688132
  100.9 81.2 %all-gather.6.cloned.1.call-start = ((), (), s32[]{:S(2)}) async-start(), calls=%async_computation.5 | async-start | bytes 2064384 | tf_op jit(solution)/shard_map/all_gather | solution.py:21
  144.5 124.2 %all-gather.8.cloned.1.call-start = ((), (), s32[]{:S(2)}) async-start(), calls=%async_computation.7 | async-start | bytes 4128768 | tf_op jit(solution)/shard_map/all_gather | solution.py:23
  182.2 8.1 %copy-start = (bf16[256,3584]{0,1:T(8,128)(2,1)S(1)}, bf16[256,3584]{0,1:T(8,128)(2,1)}, u32[]{:S(2)}) copy-start(bf16[256,3584]{0,1:T(8,128)(2,1)} %all-gather.6.cloned.1.call-done) | copy-start | bytes 5505028
  182.2 69.7 %all-to-all-start = ((bf16[256,8,448]{0,2,1:T(8,128)(2,1)}), bf16[256,8,448]{0,2,1:T(8,128)(2,1)}, u32[]{:S(2)}, u32[]{:S(2)}) async-start(bf16[256,8,448]{0,2,1:T(8,128)(2,1)} %bitcast.12), calls=%async_computation.2 | async-start | bytes 3670016 | tf_op jit(solution)/shard_map/all_to_all | solution.py:22
  190.3 115.3 %reduce-scatter.5.cloned.1.call-start = ((), (), s32[]{:S(2)}) async-start(), calls=%async_computation.6 | async-start | bytes 516096 | tf_op jit(solution)/shard_map/reduce_scatter | solution.py:27
Sparse Core Ops, SparseCore 0:
  10.1 84.6 all-gather.3
  101.1 41.3 reduce-scatter.2
  144.7 37.4 all-gather.5
  184.7 83.9 all-gather.7
  271.9 33.5 reduce-scatter.4
where the time goes:
time: 316 us; the launch traced here: 312 us
  waiting for transfers between devices  245 us (78%)
  blocking collectives  24.4 us (8%)
  matrix products  16.9 us (5%)
  between operations  13.8 us (4%)
  starting transfers between devices  8.27 us (3%)
    all_gather x1, waiting for transfers between devices, body(): weight_cols = lax.all_gather(w_up, 'gy', axis=1, tiled=True)  62.4 us
    all_to_all x1, waiting for transfers between devices, body(): lax.all_to_all(cot_cols, 'gy', split_axis=1, concat_axis=0, tiled=True)  55.8 us
    reduce_scatter x1, waiting for transfers between devices, body(): lax.psum_scatter(partial_value.astype(jnp.bfloat16), 'gz', scatter_dimens...  41.4 us
    all_gather x1, waiting for transfers between devices, body(): cot_cols = lax.all_gather(hidden_grad, 'gz', axis=1, tiled=True)  37.1 us
    reduce_scatter x1, waiting for transfers between devices, body(): lax.psum_scatter(lax.dot_general(cot_cols, weight_cols, (((1,), (1,)), ((...  31.9 us
    all_gather x1, blocking collectives, body(): near = lax.all_gather(tokens, 'gx', axis=0, tiled=True)  24.4 us
    all_gather x1, waiting for transfers between devices, body(): all_rows = lax.all_gather(near, 'gy', axis=0, tiled=True)  15.1 us
    all_to_all x1, starting transfers between devices, body(): lax.all_to_all(cot_cols, 'gy', split_axis=1, concat_axis=0, tiled=True)  8.08 us
  transfers between devices with their start and end apart: 6, of which 6 were waited for; matrix products, arithmetic and copies ran while one was open for 4% of the time, Pallas kernels for 0%

commit v1 on v0

v1 whole, which is shorter than its diff:
```python
import jax
import jax.numpy as jnp
from jax import lax
from jax.sharding import Mesh
from jax.sharding import PartitionSpec as P

AXES = ("x", "yl", "z", "yh", "c")
NX = 4
BF = jnp.bfloat16


def gelu_tanh(values):
    return jax.nn.gelu(values, approximate=True)


def along_x(value, shift):
    return lax.ppermute(value, "x", [(i, (i + shift) % NX) for i in range(NX)])


def swap_cores(value):
    return lax.ppermute(value, "c", [(0, 1), (1, 0)])


def swap_z_g(value):
    pairs = [(a * 8 + b, b * 8 + a) for a in range(8) for b in range(8)]
    return lax.ppermute(value, ("z", "yh", "c"), pairs)


def dot_nt(a, b):
    return lax.dot_general(a, b, (((1,), (1,)), ((), ())), preferred_element_type=jnp.float32)


def dot_nn(a, b):
    return lax.dot_general(a, b, (((1,), (0,)), ((), ())), preferred_element_type=jnp.float32)


def dot_tn(a, b):
    return lax.dot_general(a, b, (((0,), (0,)), ((), ())), preferred_element_type=jnp.float32)


def body(tokens, w_up, act_grad):
    rows, feats = tokens.shape
    cols = w_up.shape[1]
    pair = 2 * rows
    core = lax.axis_index("c")
    here = lax.axis_index("x")

    w_own = w_up.T
    w_low = along_x(w_own, 1)
    w_high = along_x(w_own, -1)
    half = cols // 2
    w_far = jnp.concatenate([along_x(w_high[:half], -1), along_x(w_low[half:], 1)], axis=0)
    w_all = jnp.concatenate([w_own, w_high, w_far, w_low], axis=0)

    near = lax.all_gather(tokens, "yl", axis=0, tiled=True)
    near = lax.all_gather(near, "z", axis=0, tiled=False).reshape(4, 2, pair, feats)
    mine = lax.dynamic_index_in_dim(near, core, 1, keepdims=False).reshape(4 * pair, feats)
    theirs = lax.dynamic_index_in_dim(near, 1 - core, 1, keepdims=False).reshape(4 * pair, feats)

    cot = swap_z_g(act_grad)
    cot = lax.all_to_all(cot.reshape(NX, pair, cols), "x", split_axis=0, concat_axis=0)
    order = (here + jnp.arange(NX)) % NX
    cot = jnp.take(cot, order, axis=0)

    sent = swap_cores(dot_nt(theirs, w_all).astype(BF))
    partial_value = (dot_nt(mine, w_all) + sent.astype(jnp.float32)).astype(BF)
    partial_value = partial_value.reshape(4, pair, NX * cols)
    parts = lax.all_to_all(partial_value, "yh", split_axis=0, concat_axis=0)
    hidden = jnp.sum(parts.astype(jnp.float32), axis=0)
    hidden = hidden.reshape(pair, NX, cols).transpose(1, 0, 2)

    activated, pullback = jax.vjp(gelu_tanh, hidden)
    hidden_grad = pullback(cot.astype(jnp.float32))[0].astype(BF)
    activated = activated.astype(BF)

    grad_half = lax.all_gather(
        hidden_grad.transpose(1, 0, 2).reshape(pair, NX * cols), "yh", axis=0, tiled=True
    )
    grad_other = swap_cores(grad_half)
    blocks = [grad_half[:, r * cols : (r + 1) * cols] for r in range(NX)]
    blocks = [blocks[0]] + [along_x(blocks[r], r) for r in range(1, NX)]
    order = (here - jnp.arange(NX)) % NX
    cols_mine = jnp.concatenate(blocks, axis=0)
    cols_theirs = swap_cores(cols_mine)

    ig_mine = dot_nn(grad_half, w_all).astype(BF).reshape(4, pair, feats)
    ig_theirs = dot_nn(grad_other, w_all).astype(BF).reshape(4, pair, feats)
    first = jnp.where(core == 0, ig_mine, ig_theirs)
    second = jnp.where(core == 0, ig_theirs, ig_mine)
    ig = jnp.stack([first, second], axis=1).reshape(16, rows, feats)
    ig = lax.all_to_all(ig, ("z", "yl"), split_axis=0, concat_axis=0)
    input_grad = jnp.sum(ig.astype(jnp.float32), axis=0).astype(BF)

    far = lax.all_gather(jnp.stack([mine, theirs]), "x", axis=0, tiled=False)
    far = jnp.take(far, order, axis=0)
    weight_grad = dot_tn(far[:, 0].reshape(-1, feats), cols_mine)
    weight_grad = weight_grad + dot_tn(far[:, 1].reshape(-1, feats), cols_theirs)
    weight_grad = weight_grad.astype(BF)

    order = (jnp.arange(NX) - here) % NX
    out = jnp.take(activated, order, axis=0)
    out = lax.all_to_all(out, "x", split_axis=0, concat_axis=0).reshape(NX * pair, cols)
    out = swap_z_g(out)
    return out, input_grad, weight_grad


def solution(mesh):
    fine = Mesh(mesh.devices.reshape(NX, 2, 8, 4, 2), AXES)
    in_specs = (P(("z", "x", "yl"), ("yh", "c")), P(("yh", "c"), ("x", "yl", "z")), P("z", ("x", "yl", "yh", "c")))
    out_specs = (in_specs[2], in_specs[0], in_specs[1])
    return jax.shard_map(body, mesh=fine, in_specs=in_specs, out_specs=out_specs, check_vma=False)
```

time: 316 us -> 248 us (0.78)
  the two profiles are of different devices: /device:TPU:1 before, /device:TPU:49 now
where the time goes in v1:
time: 248 us; the launch traced here: 247 us
  waiting for transfers between devices  79.7 us (32%)
  starting transfers between devices  67.5 us (27%)
  blocking collectives  49.3 us (20%)
  matrix products  15.1 us (6%)
  between operations  14.5 us (6%)
  local copies, waits for them, and re-layouts  13.8 us (6%)
  other arithmetic  6.99 us (3%)
    ppermute x2, waiting for transfers between devices, swap_z_g(): return lax.ppermute(value, ('z', 'yh', 'c'), pairs)  37.7 us
    all_gather x1, blocking collectives, body(): lax.all_gather(near, 'z', axis=0, tiled=False).reshape(4, 2, pair, feats)  27.9 us
    ppermute x3, starting transfers between devices, swap_cores(): return lax.ppermute(value, 'c', [(0, 1), (1, 0)])  21.2 us
    ppermute x7, starting transfers between devices, along_x(): return lax.ppermute(value, 'x', [(i, (i + shift) % NX) for i in range(NX)])  20.8 us
    all_to_all x1, waiting for transfers between devices, body(): parts = lax.all_to_all(partial_value, 'yh', split_axis=0, concat_axis=0)  19.3 us
    all_gather x1, blocking collectives, body(): lax.all_gather(hidden_grad.transpose(1, 0, 2).reshape(pair, NX * cols), '...  17.1 us
    all_to_all x1, waiting for transfers between devices, body(): lax.all_to_all(out, 'x', split_axis=0, concat_axis=0)  8.82 us
    all_to_all x1, starting transfers between devices, body(): ig = lax.all_to_all(ig, ('z', 'yl'), split_axis=0, concat_axis=0)  7.14 us
  transfers between devices with their start and end apart: 17, of which 8 were waited for; matrix products, arithmetic and copies ran while one was open for 14% of the time, Pallas kernels for 0%

profile of v1, /device:TPU:49, one launch (start us, length us, event | category | flops | bytes accessed | tf_op | source)
XLA Modules:
  0.0 246.8 jit_solution(4639518767614973893)
XLA Ops:
  7.2 4.4 %collective-permute-start = (bf16[448,896]{1,0:T(8,128)(2,1)}, bf16[448,896]{1,0:T(8,128)(2,1)S(1)}, u32[]{:S(2)}, u32[]{:S(2)}) collective-permute-start(bf16[448,896]{1,0:T(8,128)(2,1)} %bitcast.64), channel_id=1, source_target_pairs={{0,384},{128,0},{256,128},{384,256},{1,385},{129,1},{257,129},{385... | collective-permute-start | bytes 2408456 | tf_op jit(solution)/shard_map/ppermute | solution.py:17
  11.6 1.9 collective-permute-start.2
  13.5 4.2 %all_gather.18 = bf16[64,896]{1,0:T(8,128)(2,1)S(1)} all-gather(bf16[32,896]{1,0:T(8,128)(2,1)} %param.5), channel_id=1, replica_groups=mesh['x'=4,'yl'=2,'z'=8,'yh'=4,'c'=2] {'yl'}, dimensions={0}, use_global_device_ids=true | all-gather | bytes 172032 | tf_op jit(solution)/shard_map/all_gather | solution.py:55
  17.8 27.9 %all-gather = bf16[512,896]{1,0:T(8,128)(2,1)S(1)} all-gather(bf16[64,896]{1,0:T(8,128)(2,1)S(1)} %all_gather.18), channel_id=2, replica_groups=mesh['x'=4,'yl'=2,'z'=8,'yh'=4,'c'=2] {'z'}, dimensions={0}, use_global_device_ids=true | all-gather | bytes 1032192 | tf_op jit(solution)/shard_map/all_gather | solution.py:56
  46.6 4.8 %collective-permute-start.1 = (bf16[224,896]{1,0:T(8,128)(2,1)}, bf16[224,896]{1,0:T(8,128)(2,1)}, u32[]{:S(2)}, u32[]{:S(2)}) collective-permute-start(bf16[224,896]{1,0:T(8,128)(2,1)} %slice.38), channel_id=1, source_target_pairs={{0,384},{128,0},{256,128},{384,256},{1,385},{129,1},{257,129},{385... | collective-permute-start | bytes 1204232 | tf_op jit(solution)/shard_map/ppermute | solution.py:17
  52.5 1.9 collective-permute-start.3
  57.5 4.8 %collective-permute-done.3 = bf16[224,896]{1,0:T(8,128)(2,1)S(1)} collective-permute-done((bf16[224,896]{1,0:T(8,128)(2,1)S(1)}, bf16[224,896]{1,0:T(8,128)(2,1)S(1)}, u32[]{:S(2)}, u32[]{:S(2)}) %collective-permute-start.3) | collective-permute-done | bytes 401440 | tf_op jit(solution)/shard_map/ppermute | solution.py:17
  62.5 2.2 convolution_convert_fusion
  64.7 10.3 %collective-permute-start.4 = (bf16[256,1792]{1,0:T(8,128)(2,1)}, bf16[256,1792]{1,0:T(8,128)(2,1)S(1)}, u32[]{:S(2)}, u32[]{:S(2)}) collective-permute-start(bf16[256,1792]{1,0:T(8,128)(2,1)} %convolution_convert_fusion), channel_id=1, source_target_pairs={{0,1},{1,0},{2,3},{3,2},{4,5},{5,4},{6,7},{7,6},{8,9},{9,8},{10,11... | collective-permute-start | bytes 2752520 | tf_op jit(solution)/shard_map/ppermute | solution.py:21
  75.2 3.0 %collective-permute-start.6 = (bf16[256,448]{1,0:T(8,128)(2,1)S(1)}, bf16[256,448]{1,0:T(8,128)(2,1)}, u32[]{:S(2)}, u32[]{:S(2)}) collective-permute-start(bf16[256,448]{1,0:T(8,128)(2,1)S(1)} %copy.15), channel_id=1, source_target_pairs={{0,0},{1,8},{2,16},{3,24},{4,32},{5,40},{6,48},{7,56},{8,1},{9,9},... | collective-permute-start | bytes 688136 | tf_op jit(solution)/shard_map/ppermute | solution.py:26
  78.1 26.5 %collective-permute-done.6 = bf16[256,448]{1,0:T(8,128)(2,1)} collective-permute-done((bf16[256,448]{1,0:T(8,128)(2,1)S(1)}, bf16[256,448]{1,0:T(8,128)(2,1)}, u32[]{:S(2)}, u32[]{:S(2)}) %collective-permute-start.6) | collective-permute-done | bytes 229408 | tf_op jit(solution)/shard_map/ppermute | solution.py:26
  104.6 3.4 %all-to-all-start.2 = ((bf16[4,64,448]{2,1,0:T(8,128)(2,1)}), bf16[4,64,448]{2,1,0:T(8,128)(2,1)S(1)}, u32[]{:S(2)}, u32[]{:S(2)}) async-start(bf16[4,64,448]{2,1,0:T(8,128)(2,1)} %bitcast.7), calls=%async_computation.2 | async-start | bytes 524288 | tf_op jit(solution)/shard_map/all_to_all | solution.py:61
  108.0 4.1 %fusion = bf16[256,1792]{1,0:T(8,128)(2,1)} fusion(bf16[256,896]{1,0:T(8,128)(2,1)S(1)} %bitcast.61, bf16[1792,896]{1,0:T(8,128)(2,1)} %copy-done.8, bf16[256,1792]{1,0:T(8,128)(2,1)S(1)} %collective-permute-done.4), kind=kOutput, calls=%fused_computation.5 | convolution fusion | flops 823459840 | bytes 5505024 | tf_op jit(solution)/shard_map/dot_general | solution.py:30
  113.5 4.8 %all-to-all-start = ((bf16[4,64,1792]{2,1,0:T(8,128)(2,1)}), bf16[4,64,1792]{2,1,0:T(8,128)(2,1)S(1)}, u32[]{:S(2)}, u32[]{:S(2)}) async-start(bf16[4,64,1792]{2,1,0:T(8,128)(2,1)} %bitcast.4), calls=%async_computation | async-start | bytes 1835008 | tf_op jit(solution)/shard_map/all_to_all | solution.py:68
  119.0 19.3 %all-to-all-done = bf16[4,64,1792]{2,1,0:T(8,128)(2,1)S(1)} async-done(((bf16[4,64,1792]{2,1,0:T(8,128)(2,1)}), bf16[4,64,1792]{2,1,0:T(8,128)(2,1)S(1)}, u32[]{:S(2)}, u32[]{:S(2)}) %all-to-all-start) | async-done | bytes 917536 | tf_op jit(solution)/shard_map/all_to_all | solution.py:68
  139.9 17.1 %all_gather.21 = bf16[256,1792]{1,0:T(8,128)(2,1)S(1)} all-gather(bf16[64,1792]{1,0:T(8,128)(2,1)S(1)} %reshape.143), channel_id=1, replica_groups=mesh['x'=4,'yl'=2,'z'=8,'yh'=4,'c'=2] {'yh'}, dimensions={0}, use_global_device_ids=true | all-gather | bytes 1146880 | tf_op jit(solution)/shard_map/all_gather | solution.py:76
  157.0 6.8 %collective-permute-start.7 = (bf16[256,1792]{1,0:T(8,128)(2,1)S(1)}, bf16[256,1792]{1,0:T(8,128)(2,1)}, u32[]{:S(2)}, u32[]{:S(2)}) collective-permute-start(bf16[256,1792]{1,0:T(8,128)(2,1)S(1)} %all_gather.21), channel_id=1, source_target_pairs={{0,1},{1,0},{2,3},{3,2},{4,5},{5,4},{6,7},{7,6},{8,9},{9,8},{10,11... | collective-permute-start | bytes 2752520 | tf_op jit(solution)/shard_map/ppermute | solution.py:21
  164.8 3.0 %collective-permute-start.10 = (bf16[256,448]{1,0:T(8,128)(2,1)}, bf16[256,448]{1,0:T(8,128)(2,1)S(1)}, u32[]{:S(2)}, u32[]{:S(2)}) collective-permute-start(bf16[256,448]{1,0:T(8,128)(2,1)} %get-tuple-element.13), channel_id=1, source_target_pairs={{0,384},{128,0},{256,128},{384,256},{1,385},{129,1},{257,129},{385... | collective-permute-start | bytes 688136 | tf_op jit(solution)/shard_map/ppermute | solution.py:17
  167.8 2.8 %collective-permute-start.9 = (bf16[256,448]{1,0:T(8,128)(2,1)S(1)}, bf16[256,448]{1,0:T(8,128)(2,1)S(1)}, u32[]{:S(2)}, u32[]{:S(2)}) collective-permute-start(bf16[256,448]{1,0:T(8,128)(2,1)S(1)} %get-tuple-element.14), channel_id=1, source_target_pairs={{0,256},{128,384},{256,0},{384,128},{1,257},{129,385},{257,1},{385... | collective-permute-start | bytes 688136 | tf_op jit(solution)/shard_map/ppermute | solution.py:17
  170.7 1.9 collective-permute-start.8
  174.0 4.3 %all-to-all-start.1 = ((bf16[4,64,448]{2,1,0:T(8,128)(2,1)}), bf16[4,64,448]{2,1,0:T(8,128)(2,1)S(1)}, u32[]{:S(2)}, u32[]{:S(2)}) async-start(bf16[4,64,448]{2,1,0:T(8,128)(2,1)} %broadcast_select_fusion.3), calls=%async_computation.1 | async-start | bytes 524288 | tf_op jit(solution)/shard_map/all_to_all | solution.py:102
  178.2 8.8 %all-to-all-done.1 = bf16[4,64,448]{2,1,0:T(8,128)(2,1)S(1)} async-done(((bf16[4,64,448]{2,1,0:T(8,128)(2,1)}), bf16[4,64,448]{2,1,0:T(8,128)(2,1)S(1)}, u32[]{:S(2)}, u32[]{:S(2)}) %all-to-all-start.1) | async-done | bytes 229408 | tf_op jit(solution)/shard_map/all_to_all | solution.py:102
  187.1 2.8 %collective-permute-start.5 = (bf16[256,448]{1,0:T(8,128)(2,1)S(1)}, bf16[256,448]{1,0:T(8,128)(2,1)}, u32[]{:S(2)}, u32[]{:S(2)}) collective-permute-start(bf16[256,448]{1,0:T(8,128)(2,1)S(1)} %bitcast.68), channel_id=1, source_target_pairs={{0,0},{1,8},{2,16},{3,24},{4,32},{5,40},{6,48},{7,56},{8,1},{9,9},... | collective-permute-start | bytes 688136 | tf_op jit(solution)/shard_map/ppermute | solution.py:26
  191.5 4.1 %collective-permute-start.11 = (bf16[1024,448]{0,1:T(8,128)(2,1)S(1)}, bf16[1024,448]{0,1:T(8,128)(2,1)}, u32[]{:S(2)}, u32[]{:S(2)}) collective-permute-start(bf16[1024,448]{0,1:T(8,128)(2,1)S(1)} %copy.19), channel_id=1, source_target_pairs={{0,1},{1,0},{2,3},{3,2},{4,5},{5,4},{6,7},{7,6},{8,9},{9,8},{10,11... | collective-permute-start | bytes 2752520 | tf_op jit(solution)/shard_map/ppermute | solution.py:21
  195.6 3.3 %convolution_convert_fusion.1 = bf16[256,896]{1,0:T(8,128)(2,1)S(1)} fusion(bf16[256,1792]{1,0:T(8,128)(2,1)} %collective-permute-done.7, bf16[1792,896]{1,0:T(8,128)(2,1)} %copy-done.8), kind=kOutput, calls=%fused_computation.9 | convolution fusion | flops 822312960 | bytes 4587520 | tf_op jit(solution)/shard_map/dot_general | solution.py:34
  201.2 7.1 %all-to-all-start.3 = ((bf16[16,32,896]{2,1,0:T(8,128)(2,1)}), bf16[16,32,896]{2,1,0:T(8,128)(2,1)S(1)}, u32[]{:S(2)}, u32[]{:S(2)}) async-start(bf16[16,32,896]{2,1,0:T(8,128)(2,1)} %bitcast.13), calls=%async_computation.3 | async-start | bytes 1835008 | tf_op jit(solution)/shard_map/all_to_all | solution.py:91
  208.3 11.2 %collective-permute-done.5 = bf16[256,448]{1,0:T(8,128)(2,1)} collective-permute-done((bf16[256,448]{1,0:T(8,128)(2,1)S(1)}, bf16[256,448]{1,0:T(8,128)(2,1)}, u32[]{:S(2)}, u32[]{:S(2)}) %collective-permute-start.5) | collective-permute-done | bytes 229408 | tf_op jit(solution)/shard_map/ppermute | solution.py:26
  221.3 4.8 %gather_fusion = bf16[4,2,256,896]{3,2,1,0:T(8,128)(2,1)} fusion(bf16[4,2,256,896]{3,2,1,0:T(8,128)(2,1)} %bitcast.57, s32[1024]{0:T(1024)S(1)} %pad_clamp_fusion), kind=kCustom, calls=%fused_computation.2 | custom fusion | bytes 7340048 | tf_op jit(solution)/shard_map/jit(_take)/gather | solution.py:95
  226.1 2.5 %broadcast_select_fusion = bf16[4,2,256,896]{3,2,1,0:T(8,128)(2,1)S(1)} fusion(bf16[4,2,256,896]{3,2,1,0:T(8,128)(2,1)} %gather_fusion, pred[4]{0:T(512)(128)(4,1)S(1)} %compare_and_fusion.2), kind=kLoop, calls=%fused_computation.3 | loop fusion | flops 1835008 | bytes 7340036 | tf_op jit(solution)/shard_map/jit(_take)/select_n | solution.py:95
  229.0 2.4 fusion.20
  231.4 2.1 add_convert_fusion
  233.4 5.8 %all-to-all-done.3 = bf16[16,32,896]{2,1,0:T(8,128)(2,1)S(1)} async-done(((bf16[16,32,896]{2,1,0:T(8,128)(2,1)}), bf16[16,32,896]{2,1,0:T(8,128)(2,1)S(1)}, u32[]{:S(2)}, u32[]{:S(2)}) %all-to-all-start.3) | async-done | bytes 917536 | tf_op jit(solution)/shard_map/all_to_all | solution.py:91
  (68 shorter events, 18.0 us)
Async XLA Ops:
  7.2 214.1 %all-gather.4.cloned.1.call-start = ((), (), s32[]{:S(2)}) async-start(), calls=%async_computation.4 | async-start | bytes 4587520 | tf_op jit(solution)/shard_map/all_gather | solution.py:94
  7.2 38.6 %collective-permute-start = (bf16[448,896]{1,0:T(8,128)(2,1)}, bf16[448,896]{1,0:T(8,128)(2,1)S(1)}, u32[]{:S(2)}, u32[]{:S(2)}) collective-permute-start(bf16[448,896]{1,0:T(8,128)(2,1)} %bitcast.64), channel_id=1, source_target_pairs={{0,384},{128,0},{256,128},{384,256},{1,385},{129,1},{257,129},{385... | collective-permute-start | bytes 2408456 | tf_op jit(solution)/shard_map/ppermute | solution.py:17
  11.6 40.8 %collective-permute-start.2 = (bf16[448,896]{1,0:T(8,128)(2,1)}, bf16[448,896]{1,0:T(8,128)(2,1)S(1)}, u32[]{:S(2)}, u32[]{:S(2)}) collective-permute-start(bf16[448,896]{1,0:T(8,128)(2,1)} %bitcast.65), channel_id=1, source_target_pairs={{0,128},{128,256},{256,384},{384,0},{1,129},{129,257},{257,385},{3... | collective-permute-start | bytes 2408456 | tf_op jit(solution)/shard_map/ppermute | solution.py:17
  45.7 8.7 %copy-start = (bf16[896,448]{0,1:T(8,128)(2,1)S(1)}, bf16[896,448]{0,1:T(8,128)(2,1)}, u32[]{:S(2)}) copy-start(bf16[896,448]{0,1:T(8,128)(2,1)} %param.6) | copy-start | bytes 2408452
  46.6 9.9 %collective-permute-start.1 = (bf16[224,896]{1,0:T(8,128)(2,1)}, bf16[224,896]{1,0:T(8,128)(2,1)}, u32[]{:S(2)}, u32[]{:S(2)}) collective-permute-start(bf16[224,896]{1,0:T(8,128)(2,1)} %slice.38), channel_id=1, source_target_pairs={{0,384},{128,0},{256,128},{384,256},{1,385},{129,1},{257,129},{385... | collective-permute-start | bytes 1204232 | tf_op jit(solution)/shard_map/ppermute | solution.py:17
  52.5 9.8 %collective-permute-start.3 = (bf16[224,896]{1,0:T(8,128)(2,1)S(1)}, bf16[224,896]{1,0:T(8,128)(2,1)S(1)}, u32[]{:S(2)}, u32[]{:S(2)}) collective-permute-start(bf16[224,896]{1,0:T(8,128)(2,1)S(1)} %slice.39), channel_id=1, source_target_pairs={{0,128},{128,256},{256,384},{384,0},{1,129},{129,257},{257,385},{3... | collective-permute-start | bytes 1204232 | tf_op jit(solution)/shard_map/ppermute | solution.py:17
  62.4 12.7 %copy-start.7 = (bf16[256,448]{0,1:T(8,128)(2,1)S(1)}, bf16[256,448]{0,1:T(8,128)(2,1)}, u32[]{:S(2)}) copy-start(bf16[256,448]{0,1:T(8,128)(2,1)} %param.7) | copy-start | bytes 688132
  62.5 2.2 copy-start.8
  64.7 43.4 %collective-permute-start.4 = (bf16[256,1792]{1,0:T(8,128)(2,1)}, bf16[256,1792]{1,0:T(8,128)(2,1)S(1)}, u32[]{:S(2)}, u32[]{:S(2)}) collective-permute-start(bf16[256,1792]{1,0:T(8,128)(2,1)} %convolution_convert_fusion), channel_id=1, source_target_pairs={{0,1},{1,0},{2,3},{3,2},{4,5},{5,4},{6,7},{7,6},{8,9},{9,8},{10,11... | collective-permute-start | bytes 2752520 | tf_op jit(solution)/shard_map/ppermute | solution.py:21
  75.2 29.4 %collective-permute-start.6 = (bf16[256,448]{1,0:T(8,128)(2,1)S(1)}, bf16[256,448]{1,0:T(8,128)(2,1)}, u32[]{:S(2)}, u32[]{:S(2)}) collective-permute-start(bf16[256,448]{1,0:T(8,128)(2,1)S(1)} %copy.15), channel_id=1, source_target_pairs={{0,0},{1,8},{2,16},{3,24},{4,32},{5,40},{6,48},{7,56},{8,1},{9,9},... | collective-permute-start | bytes 688136 | tf_op jit(solution)/shard_map/ppermute | solution.py:26
  104.6 8.9 %all-to-all-start.2 = ((bf16[4,64,448]{2,1,0:T(8,128)(2,1)}), bf16[4,64,448]{2,1,0:T(8,128)(2,1)S(1)}, u32[]{:S(2)}, u32[]{:S(2)}) async-start(bf16[4,64,448]{2,1,0:T(8,128)(2,1)} %bitcast.7), calls=%async_computation.2 | async-start | bytes 524288 | tf_op jit(solution)/shard_map/all_to_all | solution.py:61
  113.5 24.8 %all-to-all-start = ((bf16[4,64,1792]{2,1,0:T(8,128)(2,1)}), bf16[4,64,1792]{2,1,0:T(8,128)(2,1)S(1)}, u32[]{:S(2)}, u32[]{:S(2)}) async-start(bf16[4,64,1792]{2,1,0:T(8,128)(2,1)} %bitcast.4), calls=%async_computation | async-start | bytes 1835008 | tf_op jit(solution)/shard_map/all_to_all | solution.py:68
  157.0 38.5 %collective-permute-start.7 = (bf16[256,1792]{1,0:T(8,128)(2,1)S(1)}, bf16[256,1792]{1,0:T(8,128)(2,1)}, u32[]{:S(2)}, u32[]{:S(2)}) collective-permute-start(bf16[256,1792]{1,0:T(8,128)(2,1)S(1)} %all_gather.21), channel_id=1, source_target_pairs={{0,1},{1,0},{2,3},{3,2},{4,5},{5,4},{6,7},{7,6},{8,9},{9,8},{10,11... | collective-permute-start | bytes 2752520 | tf_op jit(solution)/shard_map/ppermute | solution.py:21
  164.8 25.1 %collective-permute-start.10 = (bf16[256,448]{1,0:T(8,128)(2,1)}, bf16[256,448]{1,0:T(8,128)(2,1)S(1)}, u32[]{:S(2)}, u32[]{:S(2)}) collective-permute-start(bf16[256,448]{1,0:T(8,128)(2,1)} %get-tuple-element.13), channel_id=1, source_target_pairs={{0,384},{128,0},{256,128},{384,256},{1,385},{129,1},{257,129},{385... | collective-permute-start | bytes 688136 | tf_op jit(solution)/shard_map/ppermute | solution.py:17
  167.8 22.1 %collective-permute-start.9 = (bf16[256,448]{1,0:T(8,128)(2,1)S(1)}, bf16[256,448]{1,0:T(8,128)(2,1)S(1)}, u32[]{:S(2)}, u32[]{:S(2)}) collective-permute-start(bf16[256,448]{1,0:T(8,128)(2,1)S(1)} %get-tuple-element.14), channel_id=1, source_target_pairs={{0,256},{128,384},{256,0},{384,128},{1,257},{129,385},{257,1},{385... | collective-permute-start | bytes 688136 | tf_op jit(solution)/shard_map/ppermute | solution.py:17
  170.7 19.3 %collective-permute-start.8 = (bf16[256,448]{1,0:T(8,128)(2,1)S(1)}, bf16[256,448]{1,0:T(8,128)(2,1)S(1)}, u32[]{:S(2)}, u32[]{:S(2)}) collective-permute-start(bf16[256,448]{1,0:T(8,128)(2,1)S(1)} %get-tuple-element.15), channel_id=1, source_target_pairs={{0,128},{128,256},{256,384},{384,0},{1,129},{129,257},{257,385},{3... | collective-permute-start | bytes 688136 | tf_op jit(solution)/shard_map/ppermute | solution.py:17
  174.0 13.1 %all-to-all-start.1 = ((bf16[4,64,448]{2,1,0:T(8,128)(2,1)}), bf16[4,64,448]{2,1,0:T(8,128)(2,1)S(1)}, u32[]{:S(2)}, u32[]{:S(2)}) async-start(bf16[4,64,448]{2,1,0:T(8,128)(2,1)} %broadcast_select_fusion.3), calls=%async_computation.1 | async-start | bytes 524288 | tf_op jit(solution)/shard_map/all_to_all | solution.py:102
  187.1 32.5 %collective-permute-start.5 = (bf16[256,448]{1,0:T(8,128)(2,1)S(1)}, bf16[256,448]{1,0:T(8,128)(2,1)}, u32[]{:S(2)}, u32[]{:S(2)}) collective-permute-start(bf16[256,448]{1,0:T(8,128)(2,1)S(1)} %bitcast.68), channel_id=1, source_target_pairs={{0,0},{1,8},{2,16},{3,24},{4,32},{5,40},{6,48},{7,56},{8,1},{9,9},... | collective-permute-start | bytes 688136 | tf_op jit(solution)/shard_map/ppermute | solution.py:26
  189.9 0.7 copy-start.1
  189.9 0.8 copy-start.3
  189.9 0.9 copy-start.5
  191.4 7.4 %copy-start.9 = (bf16[1792,896]{1,0:T(8,128)(2,1)S(1)}, bf16[1792,896]{1,0:T(8,128)(2,1)}, u32[]{:S(2)}) copy-start(bf16[1792,896]{1,0:T(8,128)(2,1)} %copy-done.8) | copy-start | bytes 9633796
  191.5 37.5 %collective-permute-start.11 = (bf16[1024,448]{0,1:T(8,128)(2,1)S(1)}, bf16[1024,448]{0,1:T(8,128)(2,1)}, u32[]{:S(2)}, u32[]{:S(2)}) collective-permute-start(bf16[1024,448]{0,1:T(8,128)(2,1)S(1)} %copy.19), channel_id=1, source_target_pairs={{0,1},{1,0},{2,3},{3,2},{4,5},{5,4},{6,7},{7,6},{8,9},{9,8},{10,11... | collective-permute-start | bytes 2752520 | tf_op jit(solution)/shard_map/ppermute | solution.py:21
  201.2 38.0 %all-to-all-start.3 = ((bf16[16,32,896]{2,1,0:T(8,128)(2,1)}), bf16[16,32,896]{2,1,0:T(8,128)(2,1)S(1)}, u32[]{:S(2)}, u32[]{:S(2)}) async-start(bf16[16,32,896]{2,1,0:T(8,128)(2,1)} %bitcast.13), calls=%async_computation.3 | async-start | bytes 1835008 | tf_op jit(solution)/shard_map/all_to_all | solution.py:91
  228.9 2.4 copy-start.2
  228.9 2.4 copy-start.4
  228.9 2.4 copy-start.6
Sparse Core Ops, SparseCore 0:
  52.6 50.9 all-gather.3

commit v2 on v1

v2 whole, which is shorter than its diff:
```python
import jax
import jax.numpy as jnp
from jax import lax
from jax.sharding import Mesh
from jax.sharding import PartitionSpec as P

AXES = ("x", "yl", "z", "yh", "c")
NX = 4
BF = jnp.bfloat16


def gelu_tanh(values):
    return jax.nn.gelu(values, approximate=True)


def along_x(value, shift):
    return lax.ppermute(value, "x", [(i, (i + shift) % NX) for i in range(NX)])


def swap_cores(value):
    return lax.ppermute(value, "c", [(0, 1), (1, 0)])


def swap_z_g(value, shift):
    pairs = []
    for x in range(NX):
        for a in range(8):
            for b in range(8):
                pairs.append((x * 64 + a * 8 + b, (x + shift) % NX * 64 + b * 8 + a))
    return lax.ppermute(value, ("x", "z", "yh", "c"), pairs)


def pick(blocks, index):
    return lax.dynamic_index_in_dim(blocks, index & (NX - 1), 0, keepdims=False)


def dot_nt(a, b):
    return lax.dot_general(a, b, (((1,), (1,)), ((), ())), preferred_element_type=jnp.float32)


def dot_nn(a, b):
    return lax.dot_general(a, b, (((1,), (0,)), ((), ())), preferred_element_type=jnp.float32)


def dot_tn(a, b):
    return lax.dot_general(a, b, (((0,), (0,)), ((), ())), preferred_element_type=jnp.float32)


def body(tokens, w_up, act_grad):
    rows, feats = tokens.shape
    cols = w_up.shape[1]
    pair = 2 * rows
    core = lax.axis_index("c").astype(jnp.uint32)
    here = lax.axis_index("x").astype(jnp.uint32)

    w_own = w_up.T
    w_low = along_x(w_own, 1)
    w_high = along_x(w_own, -1)
    half = cols // 2
    far_top = along_x(w_high[:half], -1)
    far_bottom = along_x(w_low[half:], 1)

    cot = act_grad.reshape(NX, pair, cols)
    cot = [swap_z_g(pick(cot, here + (NX - r)), -r) for r in range(NX)]

    near = jnp.broadcast_to(tokens[None], (16, rows, feats))
    near = lax.all_to_all(near, ("z", "yl"), split_axis=0, concat_axis=0)
    near, *cot = lax.optimization_barrier((near, *cot))
    near = near.reshape(4, 2, pair, feats)
    mine = lax.dynamic_index_in_dim(near, core, 1, keepdims=False).reshape(4 * pair, feats)
    theirs = lax.dynamic_index_in_dim(near, core ^ 1, 1, keepdims=False).reshape(4 * pair, feats)

    w_all = jnp.concatenate([w_own, w_high, far_top, far_bottom, w_low], axis=0)
    sent = swap_cores(dot_nt(theirs, w_all).astype(BF))
    partial_value = (dot_nt(mine, w_all) + sent.astype(jnp.float32)).astype(BF)
    partial_value = partial_value.reshape(4, pair, NX * cols)
    parts = lax.all_to_all(partial_value, "yh", split_axis=0, concat_axis=0)
    hidden = jnp.sum(parts.astype(jnp.float32), axis=0)

    activated, pullback = jax.vjp(gelu_tanh, hidden)
    hidden_grad = pullback(jnp.concatenate(cot, axis=1).astype(jnp.float32))[0].astype(BF)
    activated = activated.astype(BF)

    grad_half = lax.all_gather(hidden_grad, "yh", axis=0, tiled=True)
    grad_other = swap_cores(grad_half)
    ig_mine = dot_nn(grad_half, w_all).astype(BF).reshape(4, pair, feats)
    ig_theirs = dot_nn(grad_other, w_all).astype(BF).reshape(4, pair, feats)
    first = jnp.where(core == 0, ig_mine, ig_theirs)
    second = jnp.where(core == 0, ig_theirs, ig_mine)
    ig = jnp.stack([first, second], axis=1).reshape(16, rows, feats)
    ig, grad_half, activated = lax.optimization_barrier((ig, grad_half, activated))
    ig = lax.all_to_all(ig, ("z", "yl"), split_axis=0, concat_axis=0)
    input_grad = jnp.sum(ig.astype(jnp.float32), axis=0).astype(BF)

    cols_mine = jnp.zeros((NX, 4 * pair, cols), BF)
    for r in range(NX):
        block = grad_half[:, r * cols : (r + 1) * cols]
        block = along_x(block, r) if r else block
        cols_mine = lax.dynamic_update_index_in_dim(cols_mine, block, (here + (NX - r)) & (NX - 1), 0)
    cols_theirs = swap_cores(cols_mine)
    far_cols = jnp.stack([cols_mine, cols_theirs], axis=1).reshape(-1, cols)
    far = lax.all_gather(jnp.stack([mine, theirs]), "x", axis=0, tiled=False)
    weight_grad = dot_tn(far.reshape(-1, feats), far_cols).astype(BF)

    out = jnp.zeros((NX, pair, cols), BF)
    for r in range(NX):
        block = swap_z_g(activated[:, r * cols : (r + 1) * cols], r)
        out = lax.dynamic_update_index_in_dim(out, block, (here + (NX - r)) & (NX - 1), 0)
    return out.reshape(NX * pair, cols), input_grad, weight_grad


def solution(mesh):
    fine = Mesh(mesh.devices.reshape(NX, 2, 8, 4, 2), AXES)
    in_specs = (P(("z", "x", "yl"), ("yh", "c")), P(("yh", "c"), ("x", "yl", "z")), P("z", ("x", "yl", "yh", "c")))
    out_specs = (in_specs[2], in_specs[0], in_specs[1])
    return jax.shard_map(body, mesh=fine, in_specs=in_specs, out_specs=out_specs, check_vma=False)
```

time: 248 us -> 238 us (0.960)
  the two profiles are of different devices: /device:TPU:49 before, /device:TPU:42 now
where the time goes in v2:
time: 238 us; the launch traced here: 237 us
  starting transfers between devices  118 us (50%)
  waiting for transfers between devices  55.9 us (23%)
  blocking collectives  20.4 us (9%)
  matrix products  14.5 us (6%)
  between operations  14.5 us (6%)
  local copies, waits for them, and re-layouts  10.6 us (4%)
  other arithmetic  3.28 us (1%)
    ppermute x8, starting transfers between devices, swap_z_g(): return lax.ppermute(value, ('x', 'z', 'yh', 'c'), pairs)  63.7 us
    ppermute x7, starting transfers between devices, along_x(): return lax.ppermute(value, 'x', [(i, (i + shift) % NX) for i in range(NX)])  22.9 us
    all_gather x1, blocking collectives, body(): grad_half = lax.all_gather(hidden_grad, 'yh', axis=0, tiled=True)  20.4 us
    all_to_all x1, waiting for transfers between devices, body(): parts = lax.all_to_all(partial_value, 'yh', split_axis=0, concat_axis=0)  19.7 us
    ppermute x8, waiting for transfers between devices, swap_z_g(): return lax.ppermute(value, ('x', 'z', 'yh', 'c'), pairs)  17.1 us
    ppermute x7, waiting for transfers between devices, along_x(): return lax.ppermute(value, 'x', [(i, (i + shift) % NX) for i in range(NX)])  14.2 us
    all_to_all x1, starting transfers between devices, body(): near = lax.all_to_all(near, ('z', 'yl'), split_axis=0, concat_axis=0)  11.8 us
    all_to_all x1, starting transfers between devices, body(): parts = lax.all_to_all(partial_value, 'yh', split_axis=0, concat_axis=0)  7.2 us
  transfers between devices with their start and end apart: 22, of which 7 were waited for; matrix products, arithmetic and copies ran while one was open for 6% of the time, Pallas kernels for 0%

profile of v2, /device:TPU:42, one launch (start us, length us, event | category | flops | bytes accessed | tf_op | source)
XLA Modules:
  0.0 237.0 jit_solution(1684990755075247182)
XLA Ops:
  9.0 11.8 %all-to-all-start = ((bf16[16,32,896]{2,1,0:T(8,128)(2,1)}), bf16[16,32,896]{2,1,0:T(8,128)(2,1)S(1)}, u32[]{:S(2)}, u32[]{:S(2)}) async-start(bf16[16,32,896]{2,1,0:T(8,128)(2,1)} %broadcast_in_dim.39), calls=%async_computation | async-start | bytes 1835008 | tf_op jit(solution)/shard_map/all_to_all | solution.py:67
  20.8 2.4 %collective-permute-start.4 = (bf16[448,896]{1,0:T(8,128)(2,1)}, bf16[448,896]{1,0:T(8,128)(2,1)S(1)}, u32[]{:S(2)}, u32[]{:S(2)}) collective-permute-start(bf16[448,896]{1,0:T(8,128)(2,1)} %bitcast.69), channel_id=1, source_target_pairs={{0,384},{128,0},{256,128},{384,256},{1,385},{129,1},{257,129},{385... | collective-permute-start | bytes 2408456 | tf_op jit(solution)/shard_map/ppermute | solution.py:17
  23.2 3.4 %collective-permute-start.6 = (bf16[448,896]{1,0:T(8,128)(2,1)}, bf16[448,896]{1,0:T(8,128)(2,1)S(1)}, u32[]{:S(2)}, u32[]{:S(2)}) collective-permute-start(bf16[448,896]{1,0:T(8,128)(2,1)} %bitcast.70), channel_id=1, source_target_pairs={{0,128},{128,256},{256,384},{384,0},{1,129},{129,257},{257,385},{3... | collective-permute-start | bytes 2408456 | tf_op jit(solution)/shard_map/ppermute | solution.py:17
  27.7 14.2 %collective-permute-done.4 = bf16[448,896]{1,0:T(8,128)(2,1)S(1)} collective-permute-done((bf16[448,896]{1,0:T(8,128)(2,1)}, bf16[448,896]{1,0:T(8,128)(2,1)S(1)}, u32[]{:S(2)}, u32[]{:S(2)}) %collective-permute-start.4) | collective-permute-done | bytes 802848 | tf_op jit(solution)/shard_map/ppermute | solution.py:17
  42.7 2.8 %collective-permute-start.5 = (bf16[224,896]{1,0:T(8,128)(2,1)}, bf16[224,896]{1,0:T(8,128)(2,1)S(1)}, u32[]{:S(2)}, u32[]{:S(2)}) collective-permute-start(bf16[224,896]{1,0:T(8,128)(2,1)} %slice.40), channel_id=1, source_target_pairs={{0,384},{128,0},{256,128},{384,256},{1,385},{129,1},{257,129},{385... | collective-permute-start | bytes 1204232 | tf_op jit(solution)/shard_map/ppermute | solution.py:17
  45.6 7.7 %collective-permute-start = (bf16[64,448]{1,0:T(8,128)(2,1)S(1)}, bf16[64,448]{1,0:T(8,128)(2,1)S(1)}, u32[]{:S(2)}, u32[]{:S(2)}) collective-permute-start(bf16[64,448]{1,0:T(8,128)(2,1)S(1)} %get-tuple-element.37), channel_id=1, source_target_pairs={{0,0},{1,8},{2,16},{3,24},{4,32},{5,40},{6,48},{7,56},{8,1},{9,9},... | collective-permute-start | bytes 172040 | tf_op jit(solution)/shard_map/ppermute | solution.py:30
  53.3 9.9 %collective-permute-start.1 = (bf16[64,448]{1,0:T(8,128)(2,1)S(1)}, bf16[64,448]{1,0:T(8,128)(2,1)S(1)}, u32[]{:S(2)}, u32[]{:S(2)}) collective-permute-start(bf16[64,448]{1,0:T(8,128)(2,1)S(1)} %get-tuple-element.36), channel_id=1, source_target_pairs={{0,384},{1,392},{2,400},{3,408},{4,416},{5,424},{6,432},{7,440},{8... | collective-permute-start | bytes 172040 | tf_op jit(solution)/shard_map/ppermute | solution.py:30
  63.2 6.1 %collective-permute-start.2 = (bf16[64,448]{1,0:T(8,128)(2,1)S(1)}, bf16[64,448]{1,0:T(8,128)(2,1)S(1)}, u32[]{:S(2)}, u32[]{:S(2)}) collective-permute-start(bf16[64,448]{1,0:T(8,128)(2,1)S(1)} %get-tuple-element.35), channel_id=1, source_target_pairs={{0,256},{1,264},{2,272},{3,280},{4,288},{5,296},{6,304},{7,312},{8... | collective-permute-start | bytes 172040 | tf_op jit(solution)/shard_map/ppermute | solution.py:30
  69.4 4.4 %collective-permute-start.7 = (bf16[224,896]{1,0:T(8,128)(2,1)S(1)}, bf16[224,896]{1,0:T(8,128)(2,1)S(1)}, u32[]{:S(2)}, u32[]{:S(2)}) collective-permute-start(bf16[224,896]{1,0:T(8,128)(2,1)S(1)} %slice.41), channel_id=1, source_target_pairs={{0,128},{128,256},{256,384},{384,0},{1,129},{129,257},{257,385},{3... | collective-permute-start | bytes 1204232 | tf_op jit(solution)/shard_map/ppermute | solution.py:17
  75.2 8.9 %collective-permute-start.3 = (bf16[64,448]{1,0:T(8,128)(2,1)S(1)}, bf16[64,448]{1,0:T(8,128)(2,1)S(1)}, u32[]{:S(2)}, u32[]{:S(2)}) collective-permute-start(bf16[64,448]{1,0:T(8,128)(2,1)S(1)} %get-tuple-element.34), channel_id=1, source_target_pairs={{0,128},{1,136},{2,144},{3,152},{4,160},{5,168},{6,176},{7,184},{8... | collective-permute-start | bytes 172040 | tf_op jit(solution)/shard_map/ppermute | solution.py:30
  86.0 4.9 %collective-permute-done.3 = bf16[64,448]{1,0:T(8,128)(2,1)S(1)} collective-permute-done((bf16[64,448]{1,0:T(8,128)(2,1)S(1)}, bf16[64,448]{1,0:T(8,128)(2,1)S(1)}, u32[]{:S(2)}, u32[]{:S(2)}) %collective-permute-start.3) | collective-permute-done | bytes 57376 | tf_op jit(solution)/shard_map/ppermute | solution.py:30
  91.0 3.2 %convolution_convert_fusion = bf16[256,1792]{1,0:T(8,128)(2,1)S(1)} fusion(bf16[256,896]{1,0:T(8,128)(2,1)S(1)} %bitcast.62, bf16[1792,896]{1,0:T(8,128)(2,1)} %copy-done), kind=kOutput, calls=%fused_computation.2 | convolution fusion | flops 822542336 | bytes 4587520 | tf_op jit(solution)/shard_map/dot_general | solution.py:38
  94.2 1.9 collective-permute-start.8
  96.2 2.4 %collective-permute-done.8 = bf16[256,1792]{1,0:T(8,128)(2,1)S(1)} collective-permute-done((bf16[256,1792]{1,0:T(8,128)(2,1)S(1)}, bf16[256,1792]{1,0:T(8,128)(2,1)S(1)}, u32[]{:S(2)}, u32[]{:S(2)}) %collective-permute-start.8) | collective-permute-done | bytes 917536 | tf_op jit(solution)/shard_map/ppermute | solution.py:21
  98.6 2.2 fusion
  100.8 7.2 %all-to-all-start.1 = ((bf16[4,64,1792]{2,1,0:T(8,128)(2,1)}), bf16[4,64,1792]{2,1,0:T(8,128)(2,1)S(1)}, u32[]{:S(2)}, u32[]{:S(2)}) async-start(bf16[4,64,1792]{2,1,0:T(8,128)(2,1)} %bitcast.9), calls=%async_computation.1 | async-start | bytes 1835008 | tf_op jit(solution)/shard_map/all_to_all | solution.py:77
  109.1 19.7 %all-to-all-done.1 = bf16[4,64,1792]{2,1,0:T(8,128)(2,1)S(1)} async-done(((bf16[4,64,1792]{2,1,0:T(8,128)(2,1)}), bf16[4,64,1792]{2,1,0:T(8,128)(2,1)S(1)}, u32[]{:S(2)}, u32[]{:S(2)}) %all-to-all-start.1) | async-done | bytes 917536 | tf_op jit(solution)/shard_map/all_to_all | solution.py:77
  129.3 20.4 %all_gather.9 = bf16[256,1792]{1,0:T(8,128)(2,1)S(1)} all-gather(bf16[64,1792]{1,0:T(8,128)(2,1)S(1)} %get-tuple-element.33), channel_id=1, replica_groups=mesh['x'=4,'yl'=2,'z'=8,'yh'=4,'c'=2] {'yh'}, dimensions={0}, use_global_device_ids=true | all-gather | bytes 1146880 | tf_op jit(solution)/shard_map/all_gather | solution.py:84
  149.7 1.9 collective-permute-start.9
  151.7 2.4 %collective-permute-done.9 = bf16[256,1792]{1,0:T(8,128)(2,1)S(1)} collective-permute-done((bf16[256,1792]{1,0:T(8,128)(2,1)S(1)}, bf16[256,1792]{1,0:T(8,128)(2,1)S(1)}, u32[]{:S(2)}, u32[]{:S(2)}) %collective-permute-start.9) | collective-permute-done | bytes 917536 | tf_op jit(solution)/shard_map/ppermute | solution.py:21
  154.1 3.0 %convolution_convert_fusion.1 = bf16[256,896]{1,0:T(8,128)(2,1)S(1)} fusion(bf16[256,1792]{1,0:T(8,128)(2,1)S(1)} %collective-permute-done.9, bf16[1792,896]{1,0:T(8,128)(2,1)} %copy-done), kind=kOutput, calls=%fused_computation.9 | convolution fusion | flops 822312960 | bytes 4587520 | tf_op jit(solution)/shard_map/dot_general | solution.py:42
  160.7 3.9 %collective-permute-start.14 = (bf16[256,448]{0,1:T(8,128)(2,1)}, bf16[256,448]{0,1:T(8,128)(2,1)}, u32[]{:S(2)}, u32[]{:S(2)}) collective-permute-start(bf16[256,448]{0,1:T(8,128)(2,1)} %get-tuple-element.27), channel_id=1, source_target_pairs={{0,128},{128,256},{256,384},{384,0},{1,129},{129,257},{257,385},{3... | collective-permute-start | bytes 688136 | tf_op jit(solution)/shard_map/ppermute | solution.py:17
  164.7 2.2 collective-permute-start.15
  166.9 3.7 %collective-permute-start.16 = (bf16[256,448]{0,1:T(8,128)(2,1)}, bf16[256,448]{0,1:T(8,128)(2,1)S(1)}, u32[]{:S(2)}, u32[]{:S(2)}) collective-permute-start(bf16[256,448]{0,1:T(8,128)(2,1)} %get-tuple-element.25), channel_id=1, source_target_pairs={{0,384},{128,0},{256,128},{384,256},{1,385},{129,1},{257,129},{385... | collective-permute-start | bytes 688136 | tf_op jit(solution)/shard_map/ppermute | solution.py:17
  170.6 6.4 %all-to-all-start.2 = ((bf16[16,32,896]{2,1,0:T(8,128)(2,1)}), bf16[16,32,896]{2,1,0:T(8,128)(2,1)S(1)}, u32[]{:S(2)}, u32[]{:S(2)}) async-start(bf16[16,32,896]{2,1,0:T(8,128)(2,1)} %bitcast.14), calls=%async_computation.2 | async-start | bytes 1835008 | tf_op jit(solution)/shard_map/all_to_all | solution.py:92
  177.2 9.4 %collective-permute-start.10 = (bf16[64,448]{1,0:T(8,128)(2,1)S(1)}, bf16[64,448]{1,0:T(8,128)(2,1)S(1)}, u32[]{:S(2)}, u32[]{:S(2)}) collective-permute-start(bf16[64,448]{1,0:T(8,128)(2,1)S(1)} %get-tuple-element.41), channel_id=1, source_target_pairs={{0,0},{1,8},{2,16},{3,24},{4,32},{5,40},{6,48},{7,56},{8,1},{9,9},... | collective-permute-start | bytes 172040 | tf_op jit(solution)/shard_map/ppermute | solution.py:30
  187.7 1.9 collective-permute-start.17
  189.7 5.2 %collective-permute-start.11 = (bf16[64,448]{1,0:T(8,128)(2,1)S(1)}, bf16[64,448]{1,0:T(8,128)(2,1)S(1)}, u32[]{:S(2)}, u32[]{:S(2)}) collective-permute-start(bf16[64,448]{1,0:T(8,128)(2,1)S(1)} %get-tuple-element.40), channel_id=1, source_target_pairs={{0,128},{1,136},{2,144},{3,152},{4,160},{5,168},{6,176},{7,184},{8... | collective-permute-start | bytes 172040 | tf_op jit(solution)/shard_map/ppermute | solution.py:30
  194.9 12.9 %collective-permute-start.12 = (bf16[64,448]{1,0:T(8,128)(2,1)S(1)}, bf16[64,448]{1,0:T(8,128)(2,1)S(1)}, u32[]{:S(2)}, u32[]{:S(2)}) collective-permute-start(bf16[64,448]{1,0:T(8,128)(2,1)S(1)} %get-tuple-element.39), channel_id=1, source_target_pairs={{0,256},{1,264},{2,272},{3,280},{4,288},{5,296},{6,304},{7,312},{8... | collective-permute-start | bytes 172040 | tf_op jit(solution)/shard_map/ppermute | solution.py:30
  207.8 3.5 %collective-permute-start.13 = (bf16[64,448]{1,0:T(8,128)(2,1)S(1)}, bf16[64,448]{1,0:T(8,128)(2,1)S(1)}, u32[]{:S(2)}, u32[]{:S(2)}) collective-permute-start(bf16[64,448]{1,0:T(8,128)(2,1)S(1)} %get-tuple-element.38), channel_id=1, source_target_pairs={{0,384},{1,392},{2,400},{3,408},{4,416},{5,424},{6,432},{7,440},{8... | collective-permute-start | bytes 172040 | tf_op jit(solution)/shard_map/ppermute | solution.py:30
  213.2 10.4 %collective-permute-done.13 = bf16[64,448]{1,0:T(8,128)(2,1)S(1)} collective-permute-done((bf16[64,448]{1,0:T(8,128)(2,1)S(1)}, bf16[64,448]{1,0:T(8,128)(2,1)S(1)}, u32[]{:S(2)}, u32[]{:S(2)}) %collective-permute-start.13) | collective-permute-done | bytes 57376 | tf_op jit(solution)/shard_map/ppermute | solution.py:30
  225.2 5.0 %bitcast_convert_fusion = bf16[896,448]{0,1:T(8,128)(2,1)} fusion(bf16[4,2,256,896]{3,2,1,0:T(8,128)(2,1)} %bitcast.73, bf16[4,1,256,448]{2,3,1,0:T(8,128)(2,1)S(1)} %bitcast.74, bf16[4,1,256,448]{2,3,1,0:T(8,128)(2,1)S(1)} %bitcast.68), kind=kOutput, calls=%fused_computation.8 | convolution fusion | flops 1645486080 | bytes 6307840 | tf_op jit(solution)/shard_map/dot_general | solution.py:46
  (56 shorter events, 16.9 us)
Async XLA Ops:
  9.0 81.9 %all-to-all-start = ((bf16[16,32,896]{2,1,0:T(8,128)(2,1)}), bf16[16,32,896]{2,1,0:T(8,128)(2,1)S(1)}, u32[]{:S(2)}, u32[]{:S(2)}) async-start(bf16[16,32,896]{2,1,0:T(8,128)(2,1)} %broadcast_in_dim.39), calls=%async_computation | async-start | bytes 1835008 | tf_op jit(solution)/shard_map/all_to_all | solution.py:67
  20.8 21.2 %collective-permute-start.4 = (bf16[448,896]{1,0:T(8,128)(2,1)}, bf16[448,896]{1,0:T(8,128)(2,1)S(1)}, u32[]{:S(2)}, u32[]{:S(2)}) collective-permute-start(bf16[448,896]{1,0:T(8,128)(2,1)} %bitcast.69), channel_id=1, source_target_pairs={{0,384},{128,0},{256,128},{384,256},{1,385},{129,1},{257,129},{385... | collective-permute-start | bytes 2408456 | tf_op jit(solution)/shard_map/ppermute | solution.py:17
  23.2 46.1 %collective-permute-start.6 = (bf16[448,896]{1,0:T(8,128)(2,1)}, bf16[448,896]{1,0:T(8,128)(2,1)S(1)}, u32[]{:S(2)}, u32[]{:S(2)}) collective-permute-start(bf16[448,896]{1,0:T(8,128)(2,1)} %bitcast.70), channel_id=1, source_target_pairs={{0,128},{128,256},{256,384},{384,0},{1,129},{129,257},{257,385},{3... | collective-permute-start | bytes 2408456 | tf_op jit(solution)/shard_map/ppermute | solution.py:17
  42.7 32.4 %collective-permute-start.5 = (bf16[224,896]{1,0:T(8,128)(2,1)}, bf16[224,896]{1,0:T(8,128)(2,1)S(1)}, u32[]{:S(2)}, u32[]{:S(2)}) collective-permute-start(bf16[224,896]{1,0:T(8,128)(2,1)} %slice.40), channel_id=1, source_target_pairs={{0,384},{128,0},{256,128},{384,256},{1,385},{129,1},{257,129},{385... | collective-permute-start | bytes 1204232 | tf_op jit(solution)/shard_map/ppermute | solution.py:17
  45.6 38.7 %collective-permute-start = (bf16[64,448]{1,0:T(8,128)(2,1)S(1)}, bf16[64,448]{1,0:T(8,128)(2,1)S(1)}, u32[]{:S(2)}, u32[]{:S(2)}) collective-permute-start(bf16[64,448]{1,0:T(8,128)(2,1)S(1)} %get-tuple-element.37), channel_id=1, source_target_pairs={{0,0},{1,8},{2,16},{3,24},{4,32},{5,40},{6,48},{7,56},{8,1},{9,9},... | collective-permute-start | bytes 172040 | tf_op jit(solution)/shard_map/ppermute | solution.py:30
  53.3 31.0 %collective-permute-start.1 = (bf16[64,448]{1,0:T(8,128)(2,1)S(1)}, bf16[64,448]{1,0:T(8,128)(2,1)S(1)}, u32[]{:S(2)}, u32[]{:S(2)}) collective-permute-start(bf16[64,448]{1,0:T(8,128)(2,1)S(1)} %get-tuple-element.36), channel_id=1, source_target_pairs={{0,384},{1,392},{2,400},{3,408},{4,416},{5,424},{6,432},{7,440},{8... | collective-permute-start | bytes 172040 | tf_op jit(solution)/shard_map/ppermute | solution.py:30
  63.2 21.1 %collective-permute-start.2 = (bf16[64,448]{1,0:T(8,128)(2,1)S(1)}, bf16[64,448]{1,0:T(8,128)(2,1)S(1)}, u32[]{:S(2)}, u32[]{:S(2)}) collective-permute-start(bf16[64,448]{1,0:T(8,128)(2,1)S(1)} %get-tuple-element.35), channel_id=1, source_target_pairs={{0,256},{1,264},{2,272},{3,280},{4,288},{5,296},{6,304},{7,312},{8... | collective-permute-start | bytes 172040 | tf_op jit(solution)/shard_map/ppermute | solution.py:30
  69.4 14.7 %collective-permute-start.7 = (bf16[224,896]{1,0:T(8,128)(2,1)S(1)}, bf16[224,896]{1,0:T(8,128)(2,1)S(1)}, u32[]{:S(2)}, u32[]{:S(2)}) collective-permute-start(bf16[224,896]{1,0:T(8,128)(2,1)S(1)} %slice.41), channel_id=1, source_target_pairs={{0,128},{128,256},{256,384},{384,0},{1,129},{129,257},{257,385},{3... | collective-permute-start | bytes 1204232 | tf_op jit(solution)/shard_map/ppermute | solution.py:17
  75.2 15.8 %collective-permute-start.3 = (bf16[64,448]{1,0:T(8,128)(2,1)S(1)}, bf16[64,448]{1,0:T(8,128)(2,1)S(1)}, u32[]{:S(2)}, u32[]{:S(2)}) collective-permute-start(bf16[64,448]{1,0:T(8,128)(2,1)S(1)} %get-tuple-element.34), channel_id=1, source_target_pairs={{0,128},{1,136},{2,144},{3,152},{4,160},{5,168},{6,176},{7,184},{8... | collective-permute-start | bytes 172040 | tf_op jit(solution)/shard_map/ppermute | solution.py:30
  84.3 1.7 copy-start
  90.9 7.7 %copy-start.1 = (bf16[1792,896]{1,0:T(8,128)(2,1)S(1)}, bf16[1792,896]{1,0:T(8,128)(2,1)}, u32[]{:S(2)}) copy-start(bf16[1792,896]{1,0:T(8,128)(2,1)} %copy-done) | copy-start | bytes 9633796
  94.2 4.4 %collective-permute-start.8 = (bf16[256,1792]{1,0:T(8,128)(2,1)S(1)}, bf16[256,1792]{1,0:T(8,128)(2,1)S(1)}, u32[]{:S(2)}, u32[]{:S(2)}) collective-permute-start(bf16[256,1792]{1,0:T(8,128)(2,1)S(1)} %convolution_convert_fusion), channel_id=1, source_target_pairs={{0,1},{1,0},{2,3},{3,2},{4,5},{5,4},{6,7},{7,6},{8,9},{9,8},{10,11... | collective-permute-start | bytes 2752520 | tf_op jit(solution)/shard_map/ppermute | solution.py:21
  100.8 28.1 %all-to-all-start.1 = ((bf16[4,64,1792]{2,1,0:T(8,128)(2,1)}), bf16[4,64,1792]{2,1,0:T(8,128)(2,1)S(1)}, u32[]{:S(2)}, u32[]{:S(2)}) async-start(bf16[4,64,1792]{2,1,0:T(8,128)(2,1)} %bitcast.9), calls=%async_computation.1 | async-start | bytes 1835008 | tf_op jit(solution)/shard_map/all_to_all | solution.py:77
  108.0 117.2 %all-gather.3.cloned.1.call-start = ((), (), s32[]{:S(2)}) async-start(), calls=%async_computation.3 | async-start | bytes 4587520 | tf_op jit(solution)/shard_map/all_gather | solution.py:102
  149.7 4.4 %collective-permute-start.9 = (bf16[256,1792]{1,0:T(8,128)(2,1)S(1)}, bf16[256,1792]{1,0:T(8,128)(2,1)S(1)}, u32[]{:S(2)}, u32[]{:S(2)}) collective-permute-start(bf16[256,1792]{1,0:T(8,128)(2,1)S(1)} %all_gather.9), channel_id=1, source_target_pairs={{0,1},{1,0},{2,3},{3,2},{4,5},{5,4},{6,7},{7,6},{8,9},{9,8},{10,11... | collective-permute-start | bytes 2752520 | tf_op jit(solution)/shard_map/ppermute | solution.py:21
  151.7 5.5 %copy-start.2 = (bf16[1792,896]{1,0:T(8,128)(2,1)S(1)}, bf16[1792,896]{1,0:T(8,128)(2,1)}, u32[]{:S(2)}) copy-start(bf16[1792,896]{1,0:T(8,128)(2,1)} %copy-done) | copy-start | bytes 9633796
  160.7 26.0 %collective-permute-start.14 = (bf16[256,448]{0,1:T(8,128)(2,1)}, bf16[256,448]{0,1:T(8,128)(2,1)}, u32[]{:S(2)}, u32[]{:S(2)}) collective-permute-start(bf16[256,448]{0,1:T(8,128)(2,1)} %get-tuple-element.27), channel_id=1, source_target_pairs={{0,128},{128,256},{256,384},{384,0},{1,129},{129,257},{257,385},{3... | collective-permute-start | bytes 688136 | tf_op jit(solution)/shard_map/ppermute | solution.py:17
  164.7 23.0 %collective-permute-start.15 = (bf16[256,448]{0,1:T(8,128)(2,1)}, bf16[256,448]{0,1:T(8,128)(2,1)S(1)}, u32[]{:S(2)}, u32[]{:S(2)}) collective-permute-start(bf16[256,448]{0,1:T(8,128)(2,1)} %get-tuple-element.26), channel_id=1, source_target_pairs={{0,256},{128,384},{256,0},{384,128},{1,257},{129,385},{257,1},{385... | collective-permute-start | bytes 688136 | tf_op jit(solution)/shard_map/ppermute | solution.py:17
  166.9 20.8 %collective-permute-start.16 = (bf16[256,448]{0,1:T(8,128)(2,1)}, bf16[256,448]{0,1:T(8,128)(2,1)S(1)}, u32[]{:S(2)}, u32[]{:S(2)}) collective-permute-start(bf16[256,448]{0,1:T(8,128)(2,1)} %get-tuple-element.25), channel_id=1, source_target_pairs={{0,384},{128,0},{256,128},{384,256},{1,385},{129,1},{257,129},{385... | collective-permute-start | bytes 688136 | tf_op jit(solution)/shard_map/ppermute | solution.py:17
  170.6 53.8 %all-to-all-start.2 = ((bf16[16,32,896]{2,1,0:T(8,128)(2,1)}), bf16[16,32,896]{2,1,0:T(8,128)(2,1)S(1)}, u32[]{:S(2)}, u32[]{:S(2)}) async-start(bf16[16,32,896]{2,1,0:T(8,128)(2,1)} %bitcast.14), calls=%async_computation.2 | async-start | bytes 1835008 | tf_op jit(solution)/shard_map/all_to_all | solution.py:92
  177.2 34.1 %collective-permute-start.10 = (bf16[64,448]{1,0:T(8,128)(2,1)S(1)}, bf16[64,448]{1,0:T(8,128)(2,1)S(1)}, u32[]{:S(2)}, u32[]{:S(2)}) collective-permute-start(bf16[64,448]{1,0:T(8,128)(2,1)S(1)} %get-tuple-element.41), channel_id=1, source_target_pairs={{0,0},{1,8},{2,16},{3,24},{4,32},{5,40},{6,48},{7,56},{8,1},{9,9},... | collective-permute-start | bytes 172040 | tf_op jit(solution)/shard_map/ppermute | solution.py:30
  187.7 37.4 %collective-permute-start.17 = (bf16[4,256,448]{1,2,0:T(8,128)(2,1)S(1)}, bf16[4,256,448]{1,2,0:T(8,128)(2,1)S(1)}, u32[]{:S(2)}, u32[]{:S(2)}) collective-permute-start(bf16[4,256,448]{1,2,0:T(8,128)(2,1)S(1)} %bitcast_dynamic-update-slice_fusion), channel_id=1, source_target_pairs={{0,1},{1,0},{2,3},{3,2},{4,5},{5,4},{6,7},{7,6},{8,9},{9,8},{10,11... | collective-permute-start | bytes 2752520 | tf_op jit(solution)/shard_map/ppermute | solution.py:21
  189.7 21.7 %collective-permute-start.11 = (bf16[64,448]{1,0:T(8,128)(2,1)S(1)}, bf16[64,448]{1,0:T(8,128)(2,1)S(1)}, u32[]{:S(2)}, u32[]{:S(2)}) collective-permute-start(bf16[64,448]{1,0:T(8,128)(2,1)S(1)} %get-tuple-element.40), channel_id=1, source_target_pairs={{0,128},{1,136},{2,144},{3,152},{4,160},{5,168},{6,176},{7,184},{8... | collective-permute-start | bytes 172040 | tf_op jit(solution)/shard_map/ppermute | solution.py:30
  194.9 18.2 %collective-permute-start.12 = (bf16[64,448]{1,0:T(8,128)(2,1)S(1)}, bf16[64,448]{1,0:T(8,128)(2,1)S(1)}, u32[]{:S(2)}, u32[]{:S(2)}) collective-permute-start(bf16[64,448]{1,0:T(8,128)(2,1)S(1)} %get-tuple-element.39), channel_id=1, source_target_pairs={{0,256},{1,264},{2,272},{3,280},{4,288},{5,296},{6,304},{7,312},{8... | collective-permute-start | bytes 172040 | tf_op jit(solution)/shard_map/ppermute | solution.py:30
  207.8 15.8 %collective-permute-start.13 = (bf16[64,448]{1,0:T(8,128)(2,1)S(1)}, bf16[64,448]{1,0:T(8,128)(2,1)S(1)}, u32[]{:S(2)}, u32[]{:S(2)}) collective-permute-start(bf16[64,448]{1,0:T(8,128)(2,1)S(1)} %get-tuple-element.38), channel_id=1, source_target_pairs={{0,384},{1,392},{2,400},{3,408},{4,416},{5,424},{6,432},{7,440},{8... | collective-permute-start | bytes 172040 | tf_op jit(solution)/shard_map/ppermute | solution.py:30
Sparse Core Ops, SparseCore 0:
  110.9 45.7 all-gather.2

commit v3 on v2

--- a/solution.py
+++ b/solution.py
@@ -21,13 +21,9 @@
     return lax.ppermute(value, "c", [(0, 1), (1, 0)])
 
 
-def swap_z_g(value, shift):
-    pairs = []
-    for x in range(NX):
-        for a in range(8):
-            for b in range(8):
-                pairs.append((x * 64 + a * 8 + b, (x + shift) % NX * 64 + b * 8 + a))
-    return lax.ppermute(value, ("x", "z", "yh", "c"), pairs)
+def swap_z_g(value):
+    pairs = [(a * 8 + b, b * 8 + a) for a in range(8) for b in range(8)]
+    return lax.ppermute(value, ("z", "yh", "c"), pairs)
 
 
 def pick(blocks, index):
@@ -57,15 +53,14 @@
     w_low = along_x(w_own, 1)
     w_high = along_x(w_own, -1)
     half = cols // 2
+    cot = swap_z_g(act_grad)
     far_top = along_x(w_high[:half], -1)
     far_bottom = along_x(w_low[half:], 1)
 
-    cot = act_grad.reshape(NX, pair, cols)
-    cot = [swap_z_g(pick(cot, here + (NX - r)), -r) for r in range(NX)]
 
     near = jnp.broadcast_to(tokens[None], (16, rows, feats))
     near = lax.all_to_all(near, ("z", "yl"), split_axis=0, concat_axis=0)
-    near, *cot = lax.optimization_barrier((near, *cot))
+    near, cot = lax.optimization_barrier((near, cot))
     near = near.reshape(4, 2, pair, feats)
     mine = lax.dynamic_index_in_dim(near, core, 1, keepdims=False).reshape(4 * pair, feats)
     theirs = lax.dynamic_index_in_dim(near, core ^ 1, 1, keepdims=False).reshape(4 * pair, feats)
@@ -73,22 +68,29 @@
     w_all = jnp.concatenate([w_own, w_high, far_top, far_bottom, w_low], axis=0)
     sent = swap_cores(dot_nt(theirs, w_all).astype(BF))
     partial_value = (dot_nt(mine, w_all) + sent.astype(jnp.float32)).astype(BF)
+    partial_value, cot = lax.optimization_barrier((partial_value, cot))
+    cot = cot.reshape(NX, pair, cols)
+    cot = [pick(cot, here + (NX - r)) for r in range(NX)]
+    cot = [along_x(cot[r], -r) if r else cot[r] for r in range(NX)]
+    cot = jnp.concatenate(cot, axis=1)
     partial_value = partial_value.reshape(4, pair, NX * cols)
     parts = lax.all_to_all(partial_value, "yh", split_axis=0, concat_axis=0)
     hidden = jnp.sum(parts.astype(jnp.float32), axis=0)
 
     activated, pullback = jax.vjp(gelu_tanh, hidden)
-    hidden_grad = pullback(jnp.concatenate(cot, axis=1).astype(jnp.float32))[0].astype(BF)
+    hidden_grad = pullback(cot.astype(jnp.float32))[0].astype(BF)
     activated = activated.astype(BF)
 
     grad_half = lax.all_gather(hidden_grad, "yh", axis=0, tiled=True)
+    grad_half, activated = lax.optimization_barrier((grad_half, activated))
     grad_other = swap_cores(grad_half)
+    activated = swap_z_g(activated)
     ig_mine = dot_nn(grad_half, w_all).astype(BF).reshape(4, pair, feats)
     ig_theirs = dot_nn(grad_other, w_all).astype(BF).reshape(4, pair, feats)
     first = jnp.where(core == 0, ig_mine, ig_theirs)
     second = jnp.where(core == 0, ig_theirs, ig_mine)
     ig = jnp.stack([first, second], axis=1).reshape(16, rows, feats)
-    ig, grad_half, activated = lax.optimization_barrier((ig, grad_half, activated))
+    ig, grad_half = lax.optimization_barrier((ig, grad_half))
     ig = lax.all_to_all(ig, ("z", "yl"), split_axis=0, concat_axis=0)
     input_grad = jnp.sum(ig.astype(jnp.float32), axis=0).astype(BF)
 
@@ -104,7 +106,8 @@
 
     out = jnp.zeros((NX, pair, cols), BF)
     for r in range(NX):
-        block = swap_z_g(activated[:, r * cols : (r + 1) * cols], r)
+        block = activated[:, r * cols : (r + 1) * cols]
+        block = along_x(block, r) if r else block
         out = lax.dynamic_update_index_in_dim(out, block, (here + (NX - r)) & (NX - 1), 0)
     return out.reshape(NX * pair, cols), input_grad, weight_grad
 

time: 238 us -> 210 us (0.88)
  the two profiles are of different devices: /device:TPU:42 before, /device:TPU:24 now
where the time goes in v3:
time: 210 us; the launch traced here: 209 us
  starting transfers between devices  83.7 us (40%)
  waiting for transfers between devices  53.5 us (25%)
  blocking collectives  21.2 us (10%)
  matrix products  18.4 us (9%)
  between operations  14.4 us (7%)
  local copies, waits for them, and re-layouts  13.7 us (7%)
  other arithmetic  3.96 us (2%)
    ppermute x13, starting transfers between devices, along_x(): return lax.ppermute(value, 'x', [(i, (i + shift) % NX) for i in range(NX)])  42 us
    ppermute x13, waiting for transfers between devices, along_x(): return lax.ppermute(value, 'x', [(i, (i + shift) % NX) for i in range(NX)])  31.2 us
    all_gather x1, blocking collectives, body(): grad_half = lax.all_gather(hidden_grad, 'yh', axis=0, tiled=True)  21.2 us
    all_to_all x1, starting transfers between devices, body(): near = lax.all_to_all(near, ('z', 'yl'), split_axis=0, concat_axis=0)  11.8 us
    ppermute x2, starting transfers between devices, swap_z_g(): return lax.ppermute(value, ('z', 'yh', 'c'), pairs)  10 us
    all_to_all x1, starting transfers between devices, body(): ig = lax.all_to_all(ig, ('z', 'yl'), split_axis=0, concat_axis=0)  10 us
    all_to_all x1, waiting for transfers between devices, body(): parts = lax.all_to_all(partial_value, 'yh', split_axis=0, concat_axis=0)  9.05 us
    dot_general x2, matrix products, dot_nt(): lax.dot_general(a, b, (((1,), (1,)), ((), ())), preferred_element_type=jn...  7.1 us
  transfers between devices with their start and end apart: 22, of which 9 were waited for; matrix products, arithmetic and copies ran while one was open for 10% of the time, Pallas kernels for 0%

profile of v3, /device:TPU:24, one launch (start us, length us, event | category | flops | bytes accessed | tf_op | source)
XLA Modules:
  0.0 208.9 jit_solution(166885531222539686)
XLA Ops:
  9.1 11.8 %all-to-all-start = ((bf16[16,32,896]{2,1,0:T(8,128)(2,1)}), bf16[16,32,896]{2,1,0:T(8,128)(2,1)S(1)}, u32[]{:S(2)}, u32[]{:S(2)}) async-start(bf16[16,32,896]{2,1,0:T(8,128)(2,1)} %broadcast_in_dim.39), calls=%async_computation | async-start | bytes 1835008 | tf_op jit(solution)/shard_map/all_to_all | solution.py:62
  20.9 4.7 %collective-permute-start.1 = (bf16[448,896]{1,0:T(8,128)(2,1)}, bf16[448,896]{1,0:T(8,128)(2,1)S(1)}, u32[]{:S(2)}, u32[]{:S(2)}) collective-permute-start(bf16[448,896]{1,0:T(8,128)(2,1)} %bitcast.70), channel_id=1, source_target_pairs={{0,384},{128,0},{256,128},{384,256},{1,385},{129,1},{257,129},{385... | collective-permute-start | bytes 2408456 | tf_op jit(solution)/shard_map/ppermute | solution.py:17
  25.6 1.9 collective-permute-start.3
  27.5 15.0 %collective-permute-done.1 = bf16[448,896]{1,0:T(8,128)(2,1)S(1)} collective-permute-done((bf16[448,896]{1,0:T(8,128)(2,1)}, bf16[448,896]{1,0:T(8,128)(2,1)S(1)}, u32[]{:S(2)}, u32[]{:S(2)}) %collective-permute-start.1) | collective-permute-done | bytes 802848 | tf_op jit(solution)/shard_map/ppermute | solution.py:17
  43.2 5.5 %collective-permute-start.2 = (bf16[224,896]{1,0:T(8,128)(2,1)}, bf16[224,896]{1,0:T(8,128)(2,1)}, u32[]{:S(2)}, u32[]{:S(2)}) collective-permute-start(bf16[224,896]{1,0:T(8,128)(2,1)} %slice.40), channel_id=1, source_target_pairs={{0,384},{128,0},{256,128},{384,256},{1,385},{129,1},{257,129},{385... | collective-permute-start | bytes 1204232 | tf_op jit(solution)/shard_map/ppermute | solution.py:17
  49.6 4.0 %collective-permute-start = (bf16[256,448]{1,0:T(8,128)(2,1)}, bf16[256,448]{1,0:T(8,128)(2,1)}, u32[]{:S(2)}, u32[]{:S(2)}) collective-permute-start(bf16[256,448]{1,0:T(8,128)(2,1)} %copy.26), channel_id=1, source_target_pairs={{0,0},{1,8},{2,16},{3,24},{4,32},{5,40},{6,48},{7,56},{8,1},{9,9},... | collective-permute-start | bytes 688136 | tf_op jit(solution)/shard_map/ppermute | solution.py:26
  53.7 1.9 collective-permute-start.4
  59.3 9.6 %collective-permute-done.4 = bf16[224,896]{1,0:T(8,128)(2,1)S(1)} collective-permute-done((bf16[224,896]{1,0:T(8,128)(2,1)S(1)}, bf16[224,896]{1,0:T(8,128)(2,1)S(1)}, u32[]{:S(2)}, u32[]{:S(2)}) %collective-permute-start.4) | collective-permute-done | bytes 401440 | tf_op jit(solution)/shard_map/ppermute | solution.py:17
  70.7 5.0 %collective-permute-done = bf16[256,448]{1,0:T(8,128)(2,1)} collective-permute-done((bf16[256,448]{1,0:T(8,128)(2,1)}, bf16[256,448]{1,0:T(8,128)(2,1)}, u32[]{:S(2)}, u32[]{:S(2)}) %collective-permute-start) | collective-permute-done | bytes 229408 | tf_op jit(solution)/shard_map/ppermute | solution.py:26
  75.8 3.0 %convolution_convert_fusion = bf16[256,1792]{1,0:T(8,128)(2,1)S(1)} fusion(bf16[256,896]{1,0:T(8,128)(2,1)S(1)} %bitcast.64, bf16[1792,896]{1,0:T(8,128)(2,1)} %constant_dynamic-update-slice_fusion), kind=kOutput, calls=%fused_computation.2 | convolution fusion | flops 822542336 | bytes 4587520 | tf_op jit(solution)/shard_map/dot_general | solution.py:34
  78.8 1.9 collective-permute-start.5
  80.7 2.4 %collective-permute-done.5 = bf16[256,1792]{1,0:T(8,128)(2,1)S(1)} collective-permute-done((bf16[256,1792]{1,0:T(8,128)(2,1)S(1)}, bf16[256,1792]{1,0:T(8,128)(2,1)S(1)}, u32[]{:S(2)}, u32[]{:S(2)}) %collective-permute-start.5) | collective-permute-done | bytes 917536 | tf_op jit(solution)/shard_map/ppermute | solution.py:21
  83.2 4.1 %fusion = bf16[256,1792]{1,0:T(8,128)(2,1)} fusion(bf16[256,896]{1,0:T(8,128)(2,1)S(1)} %bitcast.66, bf16[1792,896]{1,0:T(8,128)(2,1)} %constant_dynamic-update-slice_fusion, bf16[256,1792]{1,0:T(8,128)(2,1)S(1)} %collective-permute-done.5), kind=kOutput, calls=%fused_computation.1 | convolution fusion | flops 823459840 | bytes 5505024 | tf_op jit(solution)/shard_map/dot_general | solution.py:34
  87.2 4.2 %all-to-all-start.1 = ((bf16[4,64,1792]{2,1,0:T(8,128)(2,1)}), bf16[4,64,1792]{2,1,0:T(8,128)(2,1)S(1)}, u32[]{:S(2)}, u32[]{:S(2)}) async-start(bf16[4,64,1792]{2,1,0:T(8,128)(2,1)} %bitcast.9), calls=%async_computation.1 | async-start | bytes 1835008 | tf_op jit(solution)/shard_map/all_to_all | solution.py:77
  93.5 1.9 collective-permute-start.6
  95.4 2.4 %collective-permute-start.7 = (bf16[64,448]{1,0:T(8,128)(2,1)S(1)}, bf16[64,448]{1,0:T(8,128)(2,1)S(1)}, u32[]{:S(2)}, u32[]{:S(2)}) collective-permute-start(bf16[64,448]{1,0:T(8,128)(2,1)S(1)} %get-tuple-element.35), channel_id=1, source_target_pairs={{0,256},{128,384},{256,0},{384,128},{1,257},{129,385},{257,1},{385... | collective-permute-start | bytes 172040 | tf_op jit(solution)/shard_map/ppermute | solution.py:17
  97.8 3.4 %collective-permute-start.8 = (bf16[64,448]{1,0:T(8,128)(2,1)S(1)}, bf16[64,448]{1,0:T(8,128)(2,1)S(1)}, u32[]{:S(2)}, u32[]{:S(2)}) collective-permute-start(bf16[64,448]{1,0:T(8,128)(2,1)S(1)} %get-tuple-element.34), channel_id=1, source_target_pairs={{0,128},{128,256},{256,384},{384,0},{1,129},{129,257},{257,385},{3... | collective-permute-start | bytes 172040 | tf_op jit(solution)/shard_map/ppermute | solution.py:17
  103.0 3.1 %collective-permute-done.8 = bf16[64,448]{1,0:T(8,128)(2,1)S(1)} collective-permute-done((bf16[64,448]{1,0:T(8,128)(2,1)S(1)}, bf16[64,448]{1,0:T(8,128)(2,1)S(1)}, u32[]{:S(2)}, u32[]{:S(2)}) %collective-permute-start.8) | collective-permute-done | bytes 57376 | tf_op jit(solution)/shard_map/ppermute | solution.py:17
  106.3 9.0 %all-to-all-done.1 = bf16[4,64,1792]{2,1,0:T(8,128)(2,1)S(1)} async-done(((bf16[4,64,1792]{2,1,0:T(8,128)(2,1)}), bf16[4,64,1792]{2,1,0:T(8,128)(2,1)S(1)}, u32[]{:S(2)}, u32[]{:S(2)}) %all-to-all-start.1) | async-done | bytes 917536 | tf_op jit(solution)/shard_map/all_to_all | solution.py:77
  116.5 21.2 %all_gather.9 = bf16[256,1792]{1,0:T(8,128)(2,1)S(1)} all-gather(bf16[64,1792]{1,0:T(8,128)(2,1)S(1)} %get-tuple-element.33), channel_id=1, replica_groups=mesh['x'=4,'yl'=2,'z'=8,'yh'=4,'c'=2] {'yh'}, dimensions={0}, use_global_device_ids=true | all-gather | bytes 1146880 | tf_op jit(solution)/shard_map/all_gather | solution.py:84
  139.6 6.0 %collective-permute-start.9 = (bf16[64,1792]{1,0:T(8,128)(2,1)}, bf16[64,1792]{1,0:T(8,128)(2,1)S(1)}, u32[]{:S(2)}, u32[]{:S(2)}) collective-permute-start(bf16[64,1792]{1,0:T(8,128)(2,1)} %get-tuple-element.15), channel_id=1, source_target_pairs={{0,0},{1,8},{2,16},{3,24},{4,32},{5,40},{6,48},{7,56},{8,1},{9,9},... | collective-permute-start | bytes 688136 | tf_op jit(solution)/shard_map/ppermute | solution.py:26
  145.6 3.0 %convolution_convert_fusion.1 = bf16[256,896]{1,0:T(8,128)(2,1)S(1)} fusion(bf16[256,1792]{1,0:T(8,128)(2,1)S(1)} %collective-permute-done.13, bf16[1792,896]{1,0:T(8,128)(2,1)} %constant_dynamic-update-slice_fusion), kind=kOutput, calls=%fused_computation.9 | convolution fusion | flops 822312960 | bytes 4587520 | tf_op jit(solution)/shard_map/dot_general | solution.py:38
  148.6 3.0 %broadcast_select_fusion.1 = (bf16[256,896]{1,0:T(8,128)(2,1)S(1)}, bf16[256,896]{1,0:T(8,128)(2,1)S(1)}) fusion(bf16[256,896]{1,0:T(8,128)(2,1)S(1)} %convolution_convert_fusion.1, pred[]{:T(512)S(6)} %eq.4, bf16[256,1792]{1,0:T(8,128)(2,1)S(1)} %all_gather.9, bf16[1792,896]{1,0:T(8,128)(2,1)} %constant_dynamic-update-slice_fusion), kind=kOutput, calls=%fused_computation.29 | convolution fusion | flops 822771712 | bytes 5505025 | tf_op jit(solution)/shard_map/dot_general | solution.py:38
  156.0 3.9 %collective-permute-start.15 = (bf16[256,448]{0,1:T(8,128)(2,1)}, bf16[256,448]{0,1:T(8,128)(2,1)S(1)}, u32[]{:S(2)}, u32[]{:S(2)}) collective-permute-start(bf16[256,448]{0,1:T(8,128)(2,1)} %get-tuple-element.26), channel_id=1, source_target_pairs={{0,256},{128,384},{256,0},{384,128},{1,257},{129,385},{257,1},{385... | collective-permute-start | bytes 688136 | tf_op jit(solution)/shard_map/ppermute | solution.py:17
  159.9 3.2 %collective-permute-start.16 = (bf16[256,448]{0,1:T(8,128)(2,1)}, bf16[256,448]{0,1:T(8,128)(2,1)S(1)}, u32[]{:S(2)}, u32[]{:S(2)}) collective-permute-start(bf16[256,448]{0,1:T(8,128)(2,1)} %get-tuple-element.25), channel_id=1, source_target_pairs={{0,384},{128,0},{256,128},{384,256},{1,385},{129,1},{257,129},{385... | collective-permute-start | bytes 688136 | tf_op jit(solution)/shard_map/ppermute | solution.py:17
  163.1 10.0 %all-to-all-start.2 = ((bf16[16,32,896]{2,1,0:T(8,128)(2,1)}), bf16[16,32,896]{2,1,0:T(8,128)(2,1)S(1)}, u32[]{:S(2)}, u32[]{:S(2)}) async-start(bf16[16,32,896]{2,1,0:T(8,128)(2,1)} %bitcast.19), calls=%async_computation.2 | async-start | bytes 1835008 | tf_op jit(solution)/shard_map/all_to_all | solution.py:94
  174.2 1.9 collective-permute-start.17
  176.3 2.8 %collective-permute-start.10 = (bf16[64,448]{1,0:T(8,128)(2,1)S(1)}, bf16[64,448]{1,0:T(8,128)(2,1)S(1)}, u32[]{:S(2)}, u32[]{:S(2)}) collective-permute-start(bf16[64,448]{1,0:T(8,128)(2,1)S(1)} %get-tuple-element.40), channel_id=1, source_target_pairs={{0,128},{128,256},{256,384},{384,0},{1,129},{129,257},{257,385},{3... | collective-permute-start | bytes 172040 | tf_op jit(solution)/shard_map/ppermute | solution.py:17
  179.1 4.2 %collective-permute-start.11 = (bf16[64,448]{1,0:T(8,128)(2,1)S(1)}, bf16[64,448]{1,0:T(8,128)(2,1)S(1)}, u32[]{:S(2)}, u32[]{:S(2)}) collective-permute-start(bf16[64,448]{1,0:T(8,128)(2,1)S(1)} %get-tuple-element.39), channel_id=1, source_target_pairs={{0,256},{128,384},{256,0},{384,128},{1,257},{129,385},{257,1},{385... | collective-permute-start | bytes 172040 | tf_op jit(solution)/shard_map/ppermute | solution.py:17
  183.2 4.3 %collective-permute-start.12 = (bf16[64,448]{1,0:T(8,128)(2,1)S(1)}, bf16[64,448]{1,0:T(8,128)(2,1)S(1)}, u32[]{:S(2)}, u32[]{:S(2)}) collective-permute-start(bf16[64,448]{1,0:T(8,128)(2,1)S(1)} %get-tuple-element.38), channel_id=1, source_target_pairs={{0,384},{128,0},{256,128},{384,256},{1,385},{129,1},{257,129},{385... | collective-permute-start | bytes 172040 | tf_op jit(solution)/shard_map/ppermute | solution.py:17
  190.3 5.8 %all-to-all-done.2 = bf16[16,32,896]{2,1,0:T(8,128)(2,1)S(1)} async-done(((bf16[16,32,896]{2,1,0:T(8,128)(2,1)}), bf16[16,32,896]{2,1,0:T(8,128)(2,1)S(1)}, u32[]{:S(2)}, u32[]{:S(2)}) %all-to-all-start.2) | async-done | bytes 917536 | tf_op jit(solution)/shard_map/all_to_all | solution.py:94
  196.8 5.3 %bitcast_convert_fusion = bf16[896,448]{0,1:T(8,128)(2,1)} fusion(bf16[4,2,256,896]{3,2,1,0:T(8,128)(2,1)} %bitcast.74, bf16[4,1,256,448]{2,3,1,0:T(8,128)(2,1)} %bitcast.29, bf16[4,1,256,448]{2,3,1,0:T(8,128)(2,1)S(1)} %bitcast.69), kind=kOutput, calls=%fused_computation.8 | convolution fusion | flops 1645486080 | bytes 6307840 | tf_op jit(solution)/shard_map/dot_general | solution.py:42
  (54 shorter events, 25.1 us)
Async XLA Ops:
  7.2 48.4 %copy-start = (bf16[896,448]{0,1:T(8,128)(2,1)S(1)}, bf16[896,448]{0,1:T(8,128)(2,1)}, u32[]{:S(2)}) copy-start(bf16[896,448]{0,1:T(8,128)(2,1)} %param.4) | copy-start | bytes 2408452
  7.2 41.5 %copy-start.1 = (bf16[256,448]{0,1:T(8,128)(2,1)S(1)}, bf16[256,448]{0,1:T(8,128)(2,1)}, u32[]{:S(2)}) copy-start(bf16[256,448]{0,1:T(8,128)(2,1)} %param.5) | copy-start | bytes 688132
  9.1 66.6 %all-to-all-start = ((bf16[16,32,896]{2,1,0:T(8,128)(2,1)}), bf16[16,32,896]{2,1,0:T(8,128)(2,1)S(1)}, u32[]{:S(2)}, u32[]{:S(2)}) async-start(bf16[16,32,896]{2,1,0:T(8,128)(2,1)} %broadcast_in_dim.39), calls=%async_computation | async-start | bytes 1835008 | tf_op jit(solution)/shard_map/all_to_all | solution.py:62
  20.9 21.5 %collective-permute-start.1 = (bf16[448,896]{1,0:T(8,128)(2,1)}, bf16[448,896]{1,0:T(8,128)(2,1)S(1)}, u32[]{:S(2)}, u32[]{:S(2)}) collective-permute-start(bf16[448,896]{1,0:T(8,128)(2,1)} %bitcast.70), channel_id=1, source_target_pairs={{0,384},{128,0},{256,128},{384,256},{1,385},{129,1},{257,129},{385... | collective-permute-start | bytes 2408456 | tf_op jit(solution)/shard_map/ppermute | solution.py:17
  25.6 28.1 %collective-permute-start.3 = (bf16[448,896]{1,0:T(8,128)(2,1)}, bf16[448,896]{1,0:T(8,128)(2,1)S(1)}, u32[]{:S(2)}, u32[]{:S(2)}) collective-permute-start(bf16[448,896]{1,0:T(8,128)(2,1)} %bitcast.71), channel_id=1, source_target_pairs={{0,128},{128,256},{256,384},{384,0},{1,129},{129,257},{257,385},{3... | collective-permute-start | bytes 2408456 | tf_op jit(solution)/shard_map/ppermute | solution.py:17
  43.2 14.3 %collective-permute-start.2 = (bf16[224,896]{1,0:T(8,128)(2,1)}, bf16[224,896]{1,0:T(8,128)(2,1)}, u32[]{:S(2)}, u32[]{:S(2)}) collective-permute-start(bf16[224,896]{1,0:T(8,128)(2,1)} %slice.40), channel_id=1, source_target_pairs={{0,384},{128,0},{256,128},{384,256},{1,385},{129,1},{257,129},{385... | collective-permute-start | bytes 1204232 | tf_op jit(solution)/shard_map/ppermute | solution.py:17
  49.6 26.1 %collective-permute-start = (bf16[256,448]{1,0:T(8,128)(2,1)}, bf16[256,448]{1,0:T(8,128)(2,1)}, u32[]{:S(2)}, u32[]{:S(2)}) collective-permute-start(bf16[256,448]{1,0:T(8,128)(2,1)} %copy.26), channel_id=1, source_target_pairs={{0,0},{1,8},{2,16},{3,24},{4,32},{5,40},{6,48},{7,56},{8,1},{9,9},... | collective-permute-start | bytes 688136 | tf_op jit(solution)/shard_map/ppermute | solution.py:26
  53.7 15.2 %collective-permute-start.4 = (bf16[224,896]{1,0:T(8,128)(2,1)S(1)}, bf16[224,896]{1,0:T(8,128)(2,1)S(1)}, u32[]{:S(2)}, u32[]{:S(2)}) collective-permute-start(bf16[224,896]{1,0:T(8,128)(2,1)S(1)} %slice.41), channel_id=1, source_target_pairs={{0,128},{128,256},{256,384},{384,0},{1,129},{129,257},{257,385},{3... | collective-permute-start | bytes 1204232 | tf_op jit(solution)/shard_map/ppermute | solution.py:17
  78.8 4.4 %collective-permute-start.5 = (bf16[256,1792]{1,0:T(8,128)(2,1)S(1)}, bf16[256,1792]{1,0:T(8,128)(2,1)S(1)}, u32[]{:S(2)}, u32[]{:S(2)}) collective-permute-start(bf16[256,1792]{1,0:T(8,128)(2,1)S(1)} %convolution_convert_fusion), channel_id=1, source_target_pairs={{0,1},{1,0},{2,3},{3,2},{4,5},{5,4},{6,7},{7,6},{8,9},{9,8},{10,11... | collective-permute-start | bytes 2752520 | tf_op jit(solution)/shard_map/ppermute | solution.py:21
  87.2 28.1 %all-to-all-start.1 = ((bf16[4,64,1792]{2,1,0:T(8,128)(2,1)}), bf16[4,64,1792]{2,1,0:T(8,128)(2,1)S(1)}, u32[]{:S(2)}, u32[]{:S(2)}) async-start(bf16[4,64,1792]{2,1,0:T(8,128)(2,1)} %bitcast.9), calls=%async_computation.1 | async-start | bytes 1835008 | tf_op jit(solution)/shard_map/all_to_all | solution.py:77
  91.4 105.4 %all-gather.3.cloned.1.call-start = ((), (), s32[]{:S(2)}) async-start(), calls=%async_computation.3 | async-start | bytes 4587520 | tf_op jit(solution)/shard_map/all_gather | solution.py:104
  93.5 7.8 %collective-permute-start.6 = (bf16[64,448]{1,0:T(8,128)(2,1)S(1)}, bf16[64,448]{1,0:T(8,128)(2,1)S(1)}, u32[]{:S(2)}, u32[]{:S(2)}) collective-permute-start(bf16[64,448]{1,0:T(8,128)(2,1)S(1)} %get-tuple-element.36), channel_id=1, source_target_pairs={{0,384},{128,0},{256,128},{384,256},{1,385},{129,1},{257,129},{385... | collective-permute-start | bytes 172040 | tf_op jit(solution)/shard_map/ppermute | solution.py:17
  95.4 7.7 %collective-permute-start.7 = (bf16[64,448]{1,0:T(8,128)(2,1)S(1)}, bf16[64,448]{1,0:T(8,128)(2,1)S(1)}, u32[]{:S(2)}, u32[]{:S(2)}) collective-permute-start(bf16[64,448]{1,0:T(8,128)(2,1)S(1)} %get-tuple-element.35), channel_id=1, source_target_pairs={{0,256},{128,384},{256,0},{384,128},{1,257},{129,385},{257,1},{385... | collective-permute-start | bytes 172040 | tf_op jit(solution)/shard_map/ppermute | solution.py:17
  97.8 8.3 %collective-permute-start.8 = (bf16[64,448]{1,0:T(8,128)(2,1)S(1)}, bf16[64,448]{1,0:T(8,128)(2,1)S(1)}, u32[]{:S(2)}, u32[]{:S(2)}) collective-permute-start(bf16[64,448]{1,0:T(8,128)(2,1)S(1)} %get-tuple-element.34), channel_id=1, source_target_pairs={{0,128},{128,256},{256,384},{384,0},{1,129},{129,257},{257,385},{3... | collective-permute-start | bytes 172040 | tf_op jit(solution)/shard_map/ppermute | solution.py:17
  137.7 7.9 %collective-permute-start.13 = (bf16[256,1792]{1,0:T(8,128)(2,1)S(1)}, bf16[256,1792]{1,0:T(8,128)(2,1)S(1)}, u32[]{:S(2)}, u32[]{:S(2)}) collective-permute-start(bf16[256,1792]{1,0:T(8,128)(2,1)S(1)} %all_gather.9), channel_id=1, source_target_pairs={{0,1},{1,0},{2,3},{3,2},{4,5},{5,4},{6,7},{7,6},{8,9},{9,8},{10,11... | collective-permute-start | bytes 2752520 | tf_op jit(solution)/shard_map/ppermute | solution.py:21
  139.6 36.6 %collective-permute-start.9 = (bf16[64,1792]{1,0:T(8,128)(2,1)}, bf16[64,1792]{1,0:T(8,128)(2,1)S(1)}, u32[]{:S(2)}, u32[]{:S(2)}) collective-permute-start(bf16[64,1792]{1,0:T(8,128)(2,1)} %get-tuple-element.15), channel_id=1, source_target_pairs={{0,0},{1,8},{2,16},{3,24},{4,32},{5,40},{6,48},{7,56},{8,1},{9,9},... | collective-permute-start | bytes 688136 | tf_op jit(solution)/shard_map/ppermute | solution.py:26
  154.1 19.1 %collective-permute-start.14 = (bf16[256,448]{0,1:T(8,128)(2,1)}, bf16[256,448]{0,1:T(8,128)(2,1)}, u32[]{:S(2)}, u32[]{:S(2)}) collective-permute-start(bf16[256,448]{0,1:T(8,128)(2,1)} %get-tuple-element.27), channel_id=1, source_target_pairs={{0,128},{128,256},{256,384},{384,0},{1,129},{129,257},{257,385},{3... | collective-permute-start | bytes 688136 | tf_op jit(solution)/shard_map/ppermute | solution.py:17
  156.0 18.1 %collective-permute-start.15 = (bf16[256,448]{0,1:T(8,128)(2,1)}, bf16[256,448]{0,1:T(8,128)(2,1)S(1)}, u32[]{:S(2)}, u32[]{:S(2)}) collective-permute-start(bf16[256,448]{0,1:T(8,128)(2,1)} %get-tuple-element.26), channel_id=1, source_target_pairs={{0,256},{128,384},{256,0},{384,128},{1,257},{129,385},{257,1},{385... | collective-permute-start | bytes 688136 | tf_op jit(solution)/shard_map/ppermute | solution.py:17
  159.9 14.3 %collective-permute-start.16 = (bf16[256,448]{0,1:T(8,128)(2,1)}, bf16[256,448]{0,1:T(8,128)(2,1)S(1)}, u32[]{:S(2)}, u32[]{:S(2)}) collective-permute-start(bf16[256,448]{0,1:T(8,128)(2,1)} %get-tuple-element.25), channel_id=1, source_target_pairs={{0,384},{128,0},{256,128},{384,256},{1,385},{129,1},{257,129},{385... | collective-permute-start | bytes 688136 | tf_op jit(solution)/shard_map/ppermute | solution.py:17
  163.1 33.0 %all-to-all-start.2 = ((bf16[16,32,896]{2,1,0:T(8,128)(2,1)}), bf16[16,32,896]{2,1,0:T(8,128)(2,1)S(1)}, u32[]{:S(2)}, u32[]{:S(2)}) async-start(bf16[16,32,896]{2,1,0:T(8,128)(2,1)} %bitcast.19), calls=%async_computation.2 | async-start | bytes 1835008 | tf_op jit(solution)/shard_map/all_to_all | solution.py:94
  174.2 22.6 %collective-permute-start.17 = (bf16[4,256,448]{1,2,0:T(8,128)(2,1)S(1)}, bf16[4,256,448]{1,2,0:T(8,128)(2,1)}, u32[]{:S(2)}, u32[]{:S(2)}) collective-permute-start(bf16[4,256,448]{1,2,0:T(8,128)(2,1)S(1)} %bitcast_dynamic-update-slice_fusion), channel_id=1, source_target_pairs={{0,1},{1,0},{2,3},{3,2},{4,5},{5,4},{6,7},{7,6},{8,9},{9,8},{10,11... | collective-permute-start | bytes 2752520 | tf_op jit(solution)/shard_map/ppermute | solution.py:21
  176.3 11.3 %collective-permute-start.10 = (bf16[64,448]{1,0:T(8,128)(2,1)S(1)}, bf16[64,448]{1,0:T(8,128)(2,1)S(1)}, u32[]{:S(2)}, u32[]{:S(2)}) collective-permute-start(bf16[64,448]{1,0:T(8,128)(2,1)S(1)} %get-tuple-element.40), channel_id=1, source_target_pairs={{0,128},{128,256},{256,384},{384,0},{1,129},{129,257},{257,385},{3... | collective-permute-start | bytes 172040 | tf_op jit(solution)/shard_map/ppermute | solution.py:17
  179.1 8.6 %collective-permute-start.11 = (bf16[64,448]{1,0:T(8,128)(2,1)S(1)}, bf16[64,448]{1,0:T(8,128)(2,1)S(1)}, u32[]{:S(2)}, u32[]{:S(2)}) collective-permute-start(bf16[64,448]{1,0:T(8,128)(2,1)S(1)} %get-tuple-element.39), channel_id=1, source_target_pairs={{0,256},{128,384},{256,0},{384,128},{1,257},{129,385},{257,1},{385... | collective-permute-start | bytes 172040 | tf_op jit(solution)/shard_map/ppermute | solution.py:17
  183.2 6.2 %collective-permute-start.12 = (bf16[64,448]{1,0:T(8,128)(2,1)S(1)}, bf16[64,448]{1,0:T(8,128)(2,1)S(1)}, u32[]{:S(2)}, u32[]{:S(2)}) collective-permute-start(bf16[64,448]{1,0:T(8,128)(2,1)S(1)} %get-tuple-element.38), channel_id=1, source_target_pairs={{0,384},{128,0},{256,128},{384,256},{1,385},{129,1},{257,129},{385... | collective-permute-start | bytes 172040 | tf_op jit(solution)/shard_map/ppermute | solution.py:17
Sparse Core Ops, SparseCore 0:
  94.4 50.3 all-gather.2

commit v4 on v0

v4 whole, which is shorter than its diff:
```python
import jax
import jax.numpy as jnp
from jax import lax
from jax.sharding import Mesh
from jax.sharding import PartitionSpec as P

AXES = ("x", "yl", "z", "yh", "c")
NX = 4
BF = jnp.bfloat16
GROUPS = [
    [(2 * h + (c ^ p)) * 4 + l * 2 + c for p in range(2) for h in range(4) for l in range(2)] for c in range(2)
]


def gelu_tanh(values):
    return jax.nn.gelu(values, approximate=True)


def along_x(value, shift):
    return lax.ppermute(value, "x", [(i, (i + shift) % NX) for i in range(NX)])


def swap_cores(value):
    return lax.ppermute(value, "c", [(0, 1), (1, 0)])


def homes():
    for x in range(NX):
        for zh in range(4):
            for zc in range(2):
                for g in range(8):
                    yield x * 64 + (zh * 2 + zc) * 8 + g, zh * 64 + g * 8 + x * 2 + zc


def from_home(value):
    return lax.ppermute(value, ("x", "z", "yh", "c"), [(a, b) for a, b in homes()])


def to_home(value):
    return lax.ppermute(value, ("x", "z", "yh", "c"), [(b, a) for a, b in homes()])


def exchange_rows(value):
    return lax.all_to_all(
        value, ("z", "yl", "c"), split_axis=0, concat_axis=0, axis_index_groups=GROUPS
    )


def dot(a, b, contract):
    return lax.dot_general(a, b, (contract, ((), ())), preferred_element_type=jnp.float32)


def body(tokens, w_up, act_grad):
    rows, feats = tokens.shape
    cols = w_up.shape[1]
    pair = 2 * rows
    here = lax.axis_index("x").astype(jnp.uint32)

    w_all = lax.all_gather(w_up.T, "x", axis=0, tiled=False)

    near = exchange_rows(jnp.broadcast_to(tokens[None], (16, rows, feats)))
    near = near.reshape(2, 4 * pair, feats)

    near, cot = lax.optimization_barrier((near, from_home(act_grad)))
    cot = lax.all_to_all(cot.reshape(NX, pair, cols), "x", split_axis=0, concat_axis=0)
    cot = cot.reshape(NX * pair, cols).T
    w_all, near, cot = lax.optimization_barrier((w_all, near, cot))

    sent = swap_cores(dot(w_all, near[1], ((2,), (1,))).astype(BF))
    partial_value = (dot(w_all, near[0], ((2,), (1,))) + sent.astype(jnp.float32)).astype(BF)
    parts = lax.all_to_all(partial_value, "yh", split_axis=0, concat_axis=0)
    hidden = jnp.sum(parts.astype(jnp.float32), axis=0)

    activated, pullback = jax.vjp(gelu_tanh, hidden)
    hidden_grad = pullback(cot.astype(jnp.float32))[0].astype(BF)
    activated = activated.astype(BF)

    grad_own = lax.all_gather(hidden_grad, "yh", axis=0, tiled=False)
    grad_own, activated = lax.optimization_barrier((grad_own, activated))
    grad_other = swap_cores(grad_own)

    pieces = activated.T.reshape(NX, pair, cols)
    blocks = []
    for r in range(NX):
        block = lax.dynamic_index_in_dim(pieces, (here + r) & (NX - 1), 0, keepdims=False)
        blocks.append(along_x(block, r) if r else block)

    ig_own = dot(grad_own, w_all, ((0, 1), (0, 1))).astype(BF)
    ig_own, grad_other, *blocks = lax.optimization_barrier((ig_own, grad_other, *blocks))
    out = jnp.zeros((NX, pair, cols), BF)
    for r in range(NX):
        out = lax.dynamic_update_index_in_dim(out, blocks[r], (here + (NX - r)) & (NX - 1), 0)
    out = out.reshape(NX * pair, cols)
    ig_other = dot(grad_other, w_all, ((0, 1), (0, 1))).astype(BF)
    ig = jnp.stack([ig_own, ig_other]).reshape(16, rows, feats)
    ig, grad_own, out = lax.optimization_barrier((ig, grad_own, out))
    out = to_home(out)
    ig = exchange_rows(ig)
    input_grad = jnp.sum(ig.astype(jnp.float32), axis=0).astype(BF)

    far_own = jnp.zeros((NX, cols, 4 * pair), BF)
    for r in range(NX):
        block = lax.dynamic_index_in_dim(grad_own, (here + r) & (NX - 1), 0, keepdims=False)
        block = along_x(block, r) if r else block
        far_own = lax.dynamic_update_index_in_dim(far_own, block, (here + (NX - r)) & (NX - 1), 0)
    far_other = swap_cores(far_own)
    far = lax.all_gather(near, "x", axis=0, tiled=False)
    far_grad = jnp.stack([far_own, far_other], axis=1)
    far_grad = far_grad.transpose(2, 0, 1, 3).reshape(cols, -1)
    weight_grad = dot(far_grad, far.reshape(-1, feats), ((1,), (0,))).astype(BF).T
    return out, input_grad, weight_grad


def solution(mesh):
    fine = Mesh(mesh.devices.reshape(NX, 2, 8, 4, 2), AXES)
    in_specs = (P(("z", "x", "yl"), ("yh", "c")), P(("yh", "c"), ("x", "yl", "z")), P("z", ("x", "yl", "yh", "c")))
    out_specs = (in_specs[2], in_specs[0], in_specs[1])
    return jax.shard_map(body, mesh=fine, in_specs=in_specs, out_specs=out_specs, check_vma=False)
```

time: 316 us -> 272 us (0.86)
  the two profiles are of different devices: /device:TPU:1 before, /device:TPU:63 now
where the time goes in v4:
time: 272 us; the launch traced here: 271 us
  waiting for transfers between devices  138 us (51%)
  starting transfers between devices  69.2 us (25%)
  blocking collectives  24.9 us (9%)
  matrix products  15 us (6%)
  between operations  14.3 us (5%)
  local copies, waits for them, and re-layouts  5.55 us (2%)
  other arithmetic  4.2 us (2%)
    ppermute x1, waiting for transfers between devices, from_home(): lax.ppermute(value, ('x', 'z', 'yh', 'c'), [(a, b) for a, b in homes()])  50.8 us
    ppermute x1, waiting for transfers between devices, to_home(): lax.ppermute(value, ('x', 'z', 'yh', 'c'), [(b, a) for a, b in homes()])  47.1 us
    all_to_all x1, waiting for transfers between devices, body(): parts = lax.all_to_all(partial_value, 'yh', split_axis=0, concat_axis=0)  21.8 us
    all_to_all x2, starting transfers between devices, exchange_rows(): lax.all_to_all(value, ('z', 'yl', 'c'), split_axis=0, concat_axis=0, axis...  18.9 us
    all_gather x1, blocking collectives, body(): grad_own = lax.all_gather(hidden_grad, 'yh', axis=0, tiled=False)  17.4 us
    ppermute x6, starting transfers between devices, along_x(): return lax.ppermute(value, 'x', [(i, (i + shift) % NX) for i in range(NX)])  16.1 us
    dot_general x5, matrix products, dot(): lax.dot_general(a, b, (contract, ((), ())), preferred_element_type=jnp.fl...  15 us
    ppermute x3, starting transfers between devices, swap_cores(): return lax.ppermute(value, 'c', [(0, 1), (1, 0)])  12.6 us
  transfers between devices with their start and end apart: 16, of which 8 were waited for; matrix products, arithmetic and copies ran while one was open for 5% of the time, Pallas kernels for 0%

profile of v4, /device:TPU:63, one launch (start us, length us, event | category | flops | bytes accessed | tf_op | source)
XLA Modules:
  0.0 271.1 jit_solution(11818570631440208332)
XLA Ops:
  7.9 1.8 broadcast_in_dim.36
  9.7 12.1 %all-to-all-start = ((bf16[16,32,896]{2,1,0:T(8,128)(2,1)}), bf16[16,32,896]{2,1,0:T(8,128)(2,1)S(1)}, u32[]{:S(2)}, u32[]{:S(2)}) async-start(bf16[16,32,896]{2,1,0:T(8,128)(2,1)} %broadcast_in_dim.36), calls=%async_computation | async-start | bytes 1835008 | tf_op jit(solution)/shard_map/all_to_all | solution.py:44
  22.0 4.4 %collective-permute-start = (bf16[256,448]{1,0:T(8,128)(2,1)S(1)}, bf16[256,448]{1,0:T(8,128)(2,1)S(1)}, u32[]{:S(2)}, u32[]{:S(2)}) collective-permute-start(bf16[256,448]{1,0:T(8,128)(2,1)S(1)} %copy.11), channel_id=1, source_target_pairs={{0,0},{1,8},{2,16},{3,24},{4,32},{5,40},{6,48},{7,56},{8,1},{9,9},... | collective-permute-start | bytes 688136 | tf_op jit(solution)/shard_map/ppermute | solution.py:36
  26.5 50.8 %collective-permute-done = bf16[256,448]{1,0:T(8,128)(2,1)S(1)} collective-permute-done((bf16[256,448]{1,0:T(8,128)(2,1)S(1)}, bf16[256,448]{1,0:T(8,128)(2,1)S(1)}, u32[]{:S(2)}, u32[]{:S(2)}) %collective-permute-start) | collective-permute-done | bytes 229408 | tf_op jit(solution)/shard_map/ppermute | solution.py:36
  77.2 3.3 %all-to-all-done = bf16[16,32,896]{2,1,0:T(8,128)(2,1)S(1)} async-done(((bf16[16,32,896]{2,1,0:T(8,128)(2,1)}), bf16[16,32,896]{2,1,0:T(8,128)(2,1)S(1)}, u32[]{:S(2)}, u32[]{:S(2)}) %all-to-all-start) | async-done | bytes 917536 | tf_op jit(solution)/shard_map/all_to_all | solution.py:44
  80.5 7.5 %all_to_all.20 = bf16[4,64,448]{2,1,0:T(8,128)(2,1)S(1)} all-to-all(bf16[4,64,448]{2,1,0:T(8,128)(2,1)S(1)} %bitcast.97), channel_id=1, replica_groups=mesh['x'=4,'yl'=2,'z'=8,'yh'=4,'c'=2] {'x'}, dimensions={0} | all-to-all | bytes 458752 | tf_op jit(solution)/shard_map/all_to_all | solution.py:65
  88.2 3.3 %convolution_convert_fusion = bf16[4,448,256]{2,1,0:T(8,128)(2,1)S(1)} fusion(bf16[4,448,896]{2,1,0:T(8,128)(2,1)} %bitcast.83, bf16[2,256,896]{2,1,0:T(8,128)(2,1)} %bitcast.87), kind=kOutput, calls=%fused_computation.7 | convolution fusion | flops 822542336 | bytes 4587520 | tf_op jit(solution)/shard_map/dot_general | solution.py:50
  91.5 4.1 %collective-permute-start.1 = (bf16[4,448,256]{2,1,0:T(8,128)(2,1)S(1)}, bf16[4,448,256]{2,1,0:T(8,128)(2,1)S(1)}, u32[]{:S(2)}, u32[]{:S(2)}) collective-permute-start(bf16[4,448,256]{2,1,0:T(8,128)(2,1)S(1)} %convolution_convert_fusion), channel_id=1, source_target_pairs={{0,1},{1,0},{2,3},{3,2},{4,5},{5,4},{6,7},{7,6},{8,9},{9,8},{10,11... | collective-permute-start | bytes 2752520 | tf_op jit(solution)/shard_map/ppermute | solution.py:24
  95.6 2.1 collective-permute-done.1
  97.7 2.1 add_convert_fusion
  99.8 11.3 %all-to-all-start.2 = ((bf16[4,448,256]{2,1,0:T(8,128)(2,1)}), bf16[4,448,256]{2,1,0:T(8,128)(2,1)}, u32[]{:S(2)}, u32[]{:S(2)}) async-start(bf16[4,448,256]{2,1,0:T(8,128)(2,1)} %add_convert_fusion), calls=%async_computation.2 | async-start | bytes 1835008 | tf_op jit(solution)/shard_map/all_to_all | solution.py:71
  111.9 21.8 %all-to-all-done.2 = bf16[4,448,256]{2,1,0:T(8,128)(2,1)} async-done(((bf16[4,448,256]{2,1,0:T(8,128)(2,1)}), bf16[4,448,256]{2,1,0:T(8,128)(2,1)}, u32[]{:S(2)}, u32[]{:S(2)}) %all-to-all-start.2) | async-done | bytes 917536 | tf_op jit(solution)/shard_map/all_to_all | solution.py:71
  133.7 1.4 convert_reduce_fusion
  136.1 17.4 %all-gather.1 = bf16[1792,256]{1,0:T(8,128)(2,1)} all-gather(bf16[448,256]{1,0:T(8,128)(2,1)S(1)} %get-tuple-element.46), channel_id=3, replica_groups=mesh['x'=4,'yl'=2,'z'=8,'yh'=4,'c'=2] {'yh'}, dimensions={0}, use_global_device_ids=true | all-gather | bytes 1146880 | tf_op jit(solution)/shard_map/all_gather | solution.py:78
  153.5 5.5 %collective-permute-start.2 = (bf16[4,448,256]{2,1,0:T(8,128)(2,1)}, bf16[4,448,256]{2,1,0:T(8,128)(2,1)}, u32[]{:S(2)}, u32[]{:S(2)}) collective-permute-start(bf16[4,448,256]{2,1,0:T(8,128)(2,1)} %bitcast.10), channel_id=1, source_target_pairs={{0,1},{1,0},{2,3},{3,2},{4,5},{5,4},{6,7},{7,6},{8,9},{9,8},{10,11... | collective-permute-start | bytes 2752520 | tf_op jit(solution)/shard_map/ppermute | solution.py:24
  160.1 3.5 %collective-permute-start.3 = (bf16[64,448]{1,0:T(8,128)(2,1)S(1)}, bf16[64,448]{1,0:T(8,128)(2,1)S(1)}, u32[]{:S(2)}, u32[]{:S(2)}) collective-permute-start(bf16[64,448]{1,0:T(8,128)(2,1)S(1)} %get-tuple-element.49), channel_id=1, source_target_pairs={{0,128},{128,256},{256,384},{384,0},{1,129},{129,257},{257,385},{3... | collective-permute-start | bytes 172040 | tf_op jit(solution)/shard_map/ppermute | solution.py:20
  163.6 1.9 collective-permute-start.4
  165.6 2.5 collective-permute-start.5
  168.1 2.3 fusion.3
  170.4 1.4 collective-permute-done.5
  171.8 2.3 fusion.5
  175.3 1.3 dynamic-slice_bitcast_fusion
  176.7 2.9 %collective-permute-start.7 = (bf16[448,256]{1,0:T(8,128)(2,1)S(1)}, bf16[448,256]{1,0:T(8,128)(2,1)S(1)}, u32[]{:S(2)}, u32[]{:S(2)}) collective-permute-start(bf16[448,256]{1,0:T(8,128)(2,1)S(1)} %get-tuple-element.43), channel_id=1, source_target_pairs={{0,128},{128,256},{256,384},{384,0},{1,129},{129,257},{257,385},{3... | collective-permute-start | bytes 688136 | tf_op jit(solution)/shard_map/ppermute | solution.py:20
  179.6 6.8 %all-to-all-start.3 = ((bf16[16,32,896]{2,1,0:T(8,128)(2,1)}), bf16[16,32,896]{2,1,0:T(8,128)(2,1)S(1)}, u32[]{:S(2)}, u32[]{:S(2)}) async-start(bf16[16,32,896]{2,1,0:T(8,128)(2,1)} %bitcast.21), calls=%async_computation.3 | async-start | bytes 1835008 | tf_op jit(solution)/shard_map/all_to_all | solution.py:44
  186.4 3.2 %collective-permute-start.8 = (bf16[448,256]{1,0:T(8,128)(2,1)S(1)}, bf16[448,256]{1,0:T(8,128)(2,1)S(1)}, u32[]{:S(2)}, u32[]{:S(2)}) collective-permute-start(bf16[448,256]{1,0:T(8,128)(2,1)S(1)} %get-tuple-element.42), channel_id=1, source_target_pairs={{0,256},{128,384},{256,0},{384,128},{1,257},{129,385},{257,1},{385... | collective-permute-start | bytes 688136 | tf_op jit(solution)/shard_map/ppermute | solution.py:20
  189.6 2.0 collective-permute-start.9
  191.7 3.6 %collective-permute-done.8 = bf16[448,256]{1,0:T(8,128)(2,1)S(1)} collective-permute-done((bf16[448,256]{1,0:T(8,128)(2,1)S(1)}, bf16[448,256]{1,0:T(8,128)(2,1)S(1)}, u32[]{:S(2)}, u32[]{:S(2)}) %collective-permute-start.8) | collective-permute-done | bytes 229408 | tf_op jit(solution)/shard_map/ppermute | solution.py:20
  195.2 6.4 %collective-permute-done.9 = bf16[448,256]{1,0:T(8,128)(2,1)S(1)} collective-permute-done((bf16[448,256]{1,0:T(8,128)(2,1)S(1)}, bf16[448,256]{1,0:T(8,128)(2,1)S(1)}, u32[]{:S(2)}, u32[]{:S(2)}) %collective-permute-start.9) | collective-permute-done | bytes 229408 | tf_op jit(solution)/shard_map/ppermute | solution.py:20
  201.6 3.0 %collective-permute-start.10 = (bf16[4,448,256]{2,1,0:T(8,128)(2,1)S(1)}, bf16[4,448,256]{2,1,0:T(8,128)(2,1)S(1)}, u32[]{:S(2)}, u32[]{:S(2)}) collective-permute-start(bf16[4,448,256]{2,1,0:T(8,128)(2,1)S(1)} %bitcast_dynamic-update-slice_fusion), channel_id=1, source_target_pairs={{0,1},{1,0},{2,3},{3,2},{4,5},{5,4},{6,7},{7,6},{8,9},{9,8},{10,11... | collective-permute-start | bytes 2752520 | tf_op jit(solution)/shard_map/ppermute | solution.py:24
  204.7 5.9 %collective-permute-start.6 = (bf16[256,448]{1,0:T(8,128)(2,1)S(1)}, bf16[256,448]{1,0:T(8,128)(2,1)S(1)}, u32[]{:S(2)}, u32[]{:S(2)}) collective-permute-start(bf16[256,448]{1,0:T(8,128)(2,1)S(1)} %bitcast.98), channel_id=1, source_target_pairs={{0,0},{8,1},{16,2},{24,3},{32,4},{40,5},{48,6},{56,7},{1,8},{9,9},... | collective-permute-start | bytes 688136 | tf_op jit(solution)/shard_map/ppermute | solution.py:40
  210.5 47.1 %collective-permute-done.6 = bf16[256,448]{1,0:T(8,128)(2,1)S(1)} collective-permute-done((bf16[256,448]{1,0:T(8,128)(2,1)S(1)}, bf16[256,448]{1,0:T(8,128)(2,1)S(1)}, u32[]{:S(2)}, u32[]{:S(2)}) %collective-permute-start.6) | collective-permute-done | bytes 229408 | tf_op jit(solution)/shard_map/ppermute | solution.py:40
  259.3 5.0 %bitcast_convert_fusion = bf16[896,448]{0,1:T(8,128)(2,1)} fusion(bf16[4,2,256,896]{3,2,1,0:T(8,128)(2,1)} %bitcast.99, bf16[4,1,448,256]{3,2,1,0:T(8,128)(2,1)S(1)} %bitcast.100, bf16[4,1,448,256]{3,2,1,0:T(8,128)(2,1)S(1)} %bitcast.93), kind=kOutput, calls=%fused_computation.6 | convolution fusion | flops 1645486080 | bytes 6307840 | tf_op jit(solution)/shard_map/dot_general | solution.py:50
  (37 shorter events, 6.7 us)
Async XLA Ops:
  7.2 14.7 %copy-start.3 = (bf16[256,448]{0,1:T(8,128)(2,1)S(1)}, bf16[256,448]{0,1:T(8,128)(2,1)}, u32[]{:S(2)}) copy-start(bf16[256,448]{0,1:T(8,128)(2,1)} %param.5) | copy-start | bytes 688132
  7.2 81.0 %all-gather.6.cloned.1.call-start = ((), (), s32[]{:S(2)}) async-start(), calls=%async_computation.4 | async-start | bytes 4014080 | tf_op jit(solution)/shard_map/all_gather | solution.py:59
  9.7 70.8 %all-to-all-start = ((bf16[16,32,896]{2,1,0:T(8,128)(2,1)}), bf16[16,32,896]{2,1,0:T(8,128)(2,1)S(1)}, u32[]{:S(2)}, u32[]{:S(2)}) async-start(bf16[16,32,896]{2,1,0:T(8,128)(2,1)} %broadcast_in_dim.36), calls=%async_computation | async-start | bytes 1835008 | tf_op jit(solution)/shard_map/all_to_all | solution.py:44
  22.0 55.2 %collective-permute-start = (bf16[256,448]{1,0:T(8,128)(2,1)S(1)}, bf16[256,448]{1,0:T(8,128)(2,1)S(1)}, u32[]{:S(2)}, u32[]{:S(2)}) collective-permute-start(bf16[256,448]{1,0:T(8,128)(2,1)S(1)} %copy.11), channel_id=1, source_target_pairs={{0,0},{1,8},{2,16},{3,24},{4,32},{5,40},{6,48},{7,56},{8,1},{9,9},... | collective-permute-start | bytes 688136 | tf_op jit(solution)/shard_map/ppermute | solution.py:36
  80.5 7.7 %copy-start.1 = (bf16[16,32,896]{2,1,0:T(8,128)(2,1)}, bf16[16,32,896]{2,1,0:T(8,128)(2,1)S(1)}, u32[]{:S(2)}) copy-start(bf16[16,32,896]{2,1,0:T(8,128)(2,1)S(1)} %all-to-all-done) | copy-start | bytes 2752516
  88.2 9.5 %copy-start = (bf16[1792,896]{1,0:T(8,128)(2,1)S(1)}, bf16[1792,896]{1,0:T(8,128)(2,1)}, u32[]{:S(2)}) copy-start(bf16[1792,896]{1,0:T(8,128)(2,1)} %all-gather.6.cloned.1.call-done) | copy-start | bytes 9633796
  88.2 9.5 %copy-start.2 = (bf16[16,32,896]{2,1,0:T(8,128)(2,1)S(1)}, bf16[16,32,896]{2,1,0:T(8,128)(2,1)}, u32[]{:S(2)}) copy-start(bf16[16,32,896]{2,1,0:T(8,128)(2,1)} %copy-done.1) | copy-start | bytes 2752516
  91.5 6.2 %collective-permute-start.1 = (bf16[4,448,256]{2,1,0:T(8,128)(2,1)S(1)}, bf16[4,448,256]{2,1,0:T(8,128)(2,1)S(1)}, u32[]{:S(2)}, u32[]{:S(2)}) collective-permute-start(bf16[4,448,256]{2,1,0:T(8,128)(2,1)S(1)} %convolution_convert_fusion), channel_id=1, source_target_pairs={{0,1},{1,0},{2,3},{3,2},{4,5},{5,4},{6,7},{7,6},{8,9},{9,8},{10,11... | collective-permute-start | bytes 2752520 | tf_op jit(solution)/shard_map/ppermute | solution.py:24
  99.8 33.9 %all-to-all-start.2 = ((bf16[4,448,256]{2,1,0:T(8,128)(2,1)}), bf16[4,448,256]{2,1,0:T(8,128)(2,1)}, u32[]{:S(2)}, u32[]{:S(2)}) async-start(bf16[4,448,256]{2,1,0:T(8,128)(2,1)} %add_convert_fusion), calls=%async_computation.2 | async-start | bytes 1835008 | tf_op jit(solution)/shard_map/all_to_all | solution.py:71
  111.1 148.1 %all-gather.8.cloned.1.call-start = ((), (), s32[]{:S(2)}) async-start(), calls=%async_computation.5 | async-start | bytes 4587520 | tf_op jit(solution)/shard_map/all_gather | solution.py:107
  153.5 18.3 %collective-permute-start.2 = (bf16[4,448,256]{2,1,0:T(8,128)(2,1)}, bf16[4,448,256]{2,1,0:T(8,128)(2,1)}, u32[]{:S(2)}, u32[]{:S(2)}) collective-permute-start(bf16[4,448,256]{2,1,0:T(8,128)(2,1)} %bitcast.10), channel_id=1, source_target_pairs={{0,1},{1,0},{2,3},{3,2},{4,5},{5,4},{6,7},{7,6},{8,9},{9,8},{10,11... | collective-permute-start | bytes 2752520 | tf_op jit(solution)/shard_map/ppermute | solution.py:24
  160.1 10.3 %collective-permute-start.3 = (bf16[64,448]{1,0:T(8,128)(2,1)S(1)}, bf16[64,448]{1,0:T(8,128)(2,1)S(1)}, u32[]{:S(2)}, u32[]{:S(2)}) collective-permute-start(bf16[64,448]{1,0:T(8,128)(2,1)S(1)} %get-tuple-element.49), channel_id=1, source_target_pairs={{0,128},{128,256},{256,384},{384,0},{1,129},{129,257},{257,385},{3... | collective-permute-start | bytes 172040 | tf_op jit(solution)/shard_map/ppermute | solution.py:20
  163.6 6.8 %collective-permute-start.4 = (bf16[64,448]{1,0:T(8,128)(2,1)S(1)}, bf16[64,448]{1,0:T(8,128)(2,1)S(1)}, u32[]{:S(2)}, u32[]{:S(2)}) collective-permute-start(bf16[64,448]{1,0:T(8,128)(2,1)S(1)} %get-tuple-element.48), channel_id=1, source_target_pairs={{0,256},{128,384},{256,0},{384,128},{1,257},{129,385},{257,1},{385... | collective-permute-start | bytes 172040 | tf_op jit(solution)/shard_map/ppermute | solution.py:20
  165.6 6.2 %collective-permute-start.5 = (bf16[64,448]{1,0:T(8,128)(2,1)S(1)}, bf16[64,448]{1,0:T(8,128)(2,1)S(1)}, u32[]{:S(2)}, u32[]{:S(2)}) collective-permute-start(bf16[64,448]{1,0:T(8,128)(2,1)S(1)} %get-tuple-element.47), channel_id=1, source_target_pairs={{0,384},{128,0},{256,128},{384,256},{1,385},{129,1},{257,129},{385... | collective-permute-start | bytes 172040 | tf_op jit(solution)/shard_map/ppermute | solution.py:20
  176.7 14.9 %collective-permute-start.7 = (bf16[448,256]{1,0:T(8,128)(2,1)S(1)}, bf16[448,256]{1,0:T(8,128)(2,1)S(1)}, u32[]{:S(2)}, u32[]{:S(2)}) collective-permute-start(bf16[448,256]{1,0:T(8,128)(2,1)S(1)} %get-tuple-element.43), channel_id=1, source_target_pairs={{0,128},{128,256},{256,384},{384,0},{1,129},{129,257},{257,385},{3... | collective-permute-start | bytes 688136 | tf_op jit(solution)/shard_map/ppermute | solution.py:20
  179.6 78.9 %all-to-all-start.3 = ((bf16[16,32,896]{2,1,0:T(8,128)(2,1)}), bf16[16,32,896]{2,1,0:T(8,128)(2,1)S(1)}, u32[]{:S(2)}, u32[]{:S(2)}) async-start(bf16[16,32,896]{2,1,0:T(8,128)(2,1)} %bitcast.21), calls=%async_computation.3 | async-start | bytes 1835008 | tf_op jit(solution)/shard_map/all_to_all | solution.py:44
  186.4 8.8 %collective-permute-start.8 = (bf16[448,256]{1,0:T(8,128)(2,1)S(1)}, bf16[448,256]{1,0:T(8,128)(2,1)S(1)}, u32[]{:S(2)}, u32[]{:S(2)}) collective-permute-start(bf16[448,256]{1,0:T(8,128)(2,1)S(1)} %get-tuple-element.42), channel_id=1, source_target_pairs={{0,256},{128,384},{256,0},{384,128},{1,257},{129,385},{257,1},{385... | collective-permute-start | bytes 688136 | tf_op jit(solution)/shard_map/ppermute | solution.py:20
  189.6 12.0 %collective-permute-start.9 = (bf16[448,256]{1,0:T(8,128)(2,1)S(1)}, bf16[448,256]{1,0:T(8,128)(2,1)S(1)}, u32[]{:S(2)}, u32[]{:S(2)}) collective-permute-start(bf16[448,256]{1,0:T(8,128)(2,1)S(1)} %get-tuple-element.41), channel_id=1, source_target_pairs={{0,384},{128,0},{256,128},{384,256},{1,385},{129,1},{257,129},{385... | collective-permute-start | bytes 688136 | tf_op jit(solution)/shard_map/ppermute | solution.py:20
  201.6 57.6 %collective-permute-start.10 = (bf16[4,448,256]{2,1,0:T(8,128)(2,1)S(1)}, bf16[4,448,256]{2,1,0:T(8,128)(2,1)S(1)}, u32[]{:S(2)}, u32[]{:S(2)}) collective-permute-start(bf16[4,448,256]{2,1,0:T(8,128)(2,1)S(1)} %bitcast_dynamic-update-slice_fusion), channel_id=1, source_target_pairs={{0,1},{1,0},{2,3},{3,2},{4,5},{5,4},{6,7},{7,6},{8,9},{9,8},{10,11... | collective-permute-start | bytes 2752520 | tf_op jit(solution)/shard_map/ppermute | solution.py:24
  204.7 53.0 %collective-permute-start.6 = (bf16[256,448]{1,0:T(8,128)(2,1)S(1)}, bf16[256,448]{1,0:T(8,128)(2,1)S(1)}, u32[]{:S(2)}, u32[]{:S(2)}) collective-permute-start(bf16[256,448]{1,0:T(8,128)(2,1)S(1)} %bitcast.98), channel_id=1, source_target_pairs={{0,0},{8,1},{16,2},{24,3},{32,4},{40,5},{48,6},{56,7},{1,8},{9,9},... | collective-permute-start | bytes 688136 | tf_op jit(solution)/shard_map/ppermute | solution.py:40
Sparse Core Ops, SparseCore 0:
  10.1 53.0 all-gather.5
  114.1 45.6 all-gather.7

commit v5 on v4

v5 whole, which is shorter than its diff:
```python
import jax
import jax.numpy as jnp
from jax import lax
from jax.sharding import Mesh
from jax.sharding import PartitionSpec as P

AXES = ("x", "yl", "z", "yh", "c")
NX = 4
BF = jnp.bfloat16
GROUPS = [
    [(2 * h + (c ^ p)) * 4 + l * 2 + c for p in range(2) for h in range(4) for l in range(2)] for c in range(2)
]


def gelu_tanh(values):
    return jax.nn.gelu(values, approximate=True)


def along_x(value, shift):
    return lax.ppermute(value, "x", [(i, (i + shift) % NX) for i in range(NX)])


def swap_cores(value):
    return lax.ppermute(value, "c", [(0, 1), (1, 0)])


def swap_z_g(value):
    pairs = [(a * 8 + b, b * 8 + a) for a in range(8) for b in range(8)]
    return lax.ppermute(value, ("z", "yh", "c"), pairs)


def shift_blocks(blocks, here):
    parts = []
    for r in range(NX):
        block = lax.dynamic_index_in_dim(blocks, (here + r) & (NX - 1), 0, keepdims=False)
        parts.append(along_x(block, r) if r else block)
    return parts


def in_order(parts, here):
    out = jnp.zeros((NX,) + parts[0].shape, BF)
    for r in range(NX):
        out = lax.dynamic_update_index_in_dim(out, parts[r], (here + (NX - r)) & (NX - 1), 0)
    return out


def exchange_rows(value):
    return lax.all_to_all(
        value, ("z", "yl", "c"), split_axis=0, concat_axis=0, axis_index_groups=GROUPS
    )


def dot(a, b, contract):
    return lax.dot_general(a, b, (contract, ((), ())), preferred_element_type=jnp.float32)


def body(tokens, w_up, act_grad):
    rows, feats = tokens.shape
    cols = w_up.shape[1]
    pair = 2 * rows
    here = lax.axis_index("x").astype(jnp.uint32)

    w_all = lax.all_gather(w_up.T, "x", axis=0, tiled=False)

    near = exchange_rows(jnp.broadcast_to(tokens[None], (16, rows, feats)))
    near = near.reshape(2, 4 * pair, feats)

    near, cot, w_all = lax.optimization_barrier((near, swap_z_g(act_grad), w_all))
    w_all = w_all.reshape(NX * cols, feats)

    sent = swap_cores(dot(near[1], w_all, ((1,), (1,))).astype(BF))
    partial_value = (dot(near[0], w_all, ((1,), (1,))) + sent.astype(jnp.float32)).astype(BF)
    partial_value = partial_value.reshape(4, pair, NX * cols)
    partial_value, cot = lax.optimization_barrier((partial_value, cot))
    parts = lax.all_to_all(partial_value, "yh", split_axis=0, concat_axis=0)
    hidden = jnp.sum(parts.astype(jnp.float32), axis=0)

    cot = in_order(shift_blocks(cot.reshape(NX, pair, cols), here), here)
    cot = cot.transpose(1, 0, 2).reshape(pair, NX * cols)

    activated, pullback = jax.vjp(gelu_tanh, hidden)
    hidden_grad = pullback(cot.astype(jnp.float32))[0].astype(BF)
    activated = activated.astype(BF)

    grad_own = lax.all_gather(hidden_grad, "yh", axis=0, tiled=True)
    grad_own, activated = lax.optimization_barrier((grad_own, activated))
    grad_other = swap_cores(grad_own)
    activated = swap_z_g(activated)

    ig_own = dot(grad_own, w_all, ((1,), (0,))).astype(BF)
    ig_own, grad_other = lax.optimization_barrier((ig_own, grad_other))
    ig_other = dot(grad_other, w_all, ((1,), (0,))).astype(BF)
    ig = jnp.stack([ig_own, ig_other]).reshape(16, rows, feats)
    ig, grad_own = lax.optimization_barrier((ig, grad_own))
    ig = exchange_rows(ig)
    input_grad = jnp.sum(ig.astype(jnp.float32), axis=0).astype(BF)

    far_own = grad_own.reshape(4 * pair, NX, cols).transpose(1, 0, 2)
    far_own = in_order(shift_blocks(far_own, here), here)
    far_own, activated = lax.optimization_barrier((far_own, activated))
    far_other = swap_cores(far_own)
    far = lax.all_gather(near, "x", axis=0, tiled=False)
    far_grad = jnp.stack([far_own, far_other], axis=1)
    weight_grad = dot(far.reshape(-1, feats), far_grad.reshape(-1, cols), ((0,), (0,))).astype(BF)

    activated = activated.reshape(pair, NX, cols).transpose(1, 0, 2)
    out = in_order(shift_blocks(activated, here), here).reshape(NX * pair, cols)
    return out, input_grad, weight_grad


def solution(mesh):
    fine = Mesh(mesh.devices.reshape(NX, 2, 8, 4, 2), AXES)
    in_specs = (P(("z", "x", "yl"), ("yh", "c")), P(("yh", "c"), ("x", "yl", "z")), P("z", ("x", "yl", "yh", "c")))
    out_specs = (in_specs[2], in_specs[0], in_specs[1])
    return jax.shard_map(body, mesh=fine, in_specs=in_specs, out_specs=out_specs, check_vma=False)
```

time: 272 us -> 200 us (0.74)
  the two profiles are of different devices: /device:TPU:63 before, /device:TPU:54 now
where the time goes in v5:
time: 200 us; the launch traced here: 199 us
  starting transfers between devices  71.2 us (36%)
  waiting for transfers between devices  69 us (34%)
  blocking collectives  21.5 us (11%)
  between operations  14.4 us (7%)
  matrix products  12.8 us (6%)
  local copies, waits for them, and re-layouts  7.12 us (4%)
  other arithmetic  2.97 us (1%)
    ppermute x2, waiting for transfers between devices, swap_z_g(): return lax.ppermute(value, ('z', 'yh', 'c'), pairs)  36.3 us
    ppermute x9, starting transfers between devices, along_x(): return lax.ppermute(value, 'x', [(i, (i + shift) % NX) for i in range(NX)])  30 us
    all_gather x1, blocking collectives, body(): grad_own = lax.all_gather(hidden_grad, 'yh', axis=0, tiled=True)  21.5 us
    all_to_all x2, starting transfers between devices, exchange_rows(): lax.all_to_all(value, ('z', 'yl', 'c'), split_axis=0, concat_axis=0, axis...  17.7 us
    dot_general x5, matrix products, dot(): lax.dot_general(a, b, (contract, ((), ())), preferred_element_type=jnp.fl...  12.8 us
    ppermute x9, waiting for transfers between devices, along_x(): return lax.ppermute(value, 'x', [(i, (i + shift) % NX) for i in range(NX)])  12.3 us
    ppermute x2, starting transfers between devices, swap_z_g(): return lax.ppermute(value, ('z', 'yh', 'c'), pairs)  11.9 us
    all_to_all x2, waiting for transfers between devices, exchange_rows(): lax.all_to_all(value, ('z', 'yl', 'c'), split_axis=0, concat_axis=0, axis...  9.25 us
  transfers between devices with their start and end apart: 19, of which 11 were waited for; matrix products, arithmetic and copies ran while one was open for 6% of the time, Pallas kernels for 0%

profile of v5, /device:TPU:54, one launch (start us, length us, event | category | flops | bytes accessed | tf_op | source)
XLA Modules:
  0.0 199.0 jit_solution(8975475311277214719)
XLA Ops:
  7.9 1.8 broadcast_in_dim.42
  9.8 10.5 %all-to-all-start = ((bf16[16,32,896]{2,1,0:T(8,128)(2,1)}), bf16[16,32,896]{2,1,0:T(8,128)(2,1)S(1)}, u32[]{:S(2)}, u32[]{:S(2)}) async-start(bf16[16,32,896]{2,1,0:T(8,128)(2,1)} %broadcast_in_dim.42), calls=%async_computation | async-start | bytes 1835008 | tf_op jit(solution)/shard_map/all_to_all | solution.py:48
  20.4 6.2 %collective-permute-start = (bf16[256,448]{1,0:T(8,128)(2,1)S(1)}, bf16[256,448]{1,0:T(8,128)(2,1)S(1)}, u32[]{:S(2)}, u32[]{:S(2)}) collective-permute-start(bf16[256,448]{1,0:T(8,128)(2,1)S(1)} %copy.25), channel_id=1, source_target_pairs={{0,0},{1,8},{2,16},{3,24},{4,32},{5,40},{6,48},{7,56},{8,1},{9,9},... | collective-permute-start | bytes 688136 | tf_op jit(solution)/shard_map/ppermute | solution.py:29
  26.6 26.2 %collective-permute-done = bf16[256,448]{1,0:T(8,128)(2,1)S(1)} collective-permute-done((bf16[256,448]{1,0:T(8,128)(2,1)S(1)}, bf16[256,448]{1,0:T(8,128)(2,1)S(1)}, u32[]{:S(2)}, u32[]{:S(2)}) %collective-permute-start) | collective-permute-done | bytes 229408 | tf_op jit(solution)/shard_map/ppermute | solution.py:29
  52.8 9.2 %all-to-all-done = bf16[16,32,896]{2,1,0:T(8,128)(2,1)S(1)} async-done(((bf16[16,32,896]{2,1,0:T(8,128)(2,1)}), bf16[16,32,896]{2,1,0:T(8,128)(2,1)S(1)}, u32[]{:S(2)}, u32[]{:S(2)}) %all-to-all-start) | async-done | bytes 917536 | tf_op jit(solution)/shard_map/all_to_all | solution.py:48
  62.1 3.4 %convolution_convert_fusion = bf16[256,1792]{1,0:T(8,128)(2,1)S(1)} fusion(bf16[1792,896]{1,0:T(8,128)(2,1)} %all-gather.5.cloned.1.call-done, bf16[2,256,896]{2,1,0:T(8,128)(2,1)S(1)} %bitcast.81), kind=kOutput, calls=%fused_computation.2 | convolution fusion | flops 822542336 | bytes 4587520 | tf_op jit(solution)/shard_map/dot_general | solution.py:54
  65.5 1.9 collective-permute-start.1
  67.5 2.4 %collective-permute-done.1 = bf16[256,1792]{1,0:T(8,128)(2,1)S(1)} collective-permute-done((bf16[256,1792]{1,0:T(8,128)(2,1)S(1)}, bf16[256,1792]{1,0:T(8,128)(2,1)S(1)}, u32[]{:S(2)}, u32[]{:S(2)}) %collective-permute-start.1) | collective-permute-done | bytes 917536 | tf_op jit(solution)/shard_map/ppermute | solution.py:24
  69.9 2.2 %fusion = bf16[256,1792]{1,0:T(8,128)(2,1)} fusion(bf16[1792,896]{1,0:T(8,128)(2,1)S(1)} %copy-done.2, bf16[256,1792]{1,0:T(8,128)(2,1)S(1)} %collective-permute-done.1, bf16[2,256,896]{2,1,0:T(8,128)(2,1)S(1)} %bitcast.82), kind=kOutput, calls=%fused_computation.1 | convolution fusion | flops 823459840 | bytes 5505024 | tf_op jit(solution)/shard_map/dot_general | solution.py:54
  72.1 5.8 %all-to-all-start.1 = ((bf16[4,64,1792]{2,1,0:T(8,128)(2,1)}), bf16[4,64,1792]{2,1,0:T(8,128)(2,1)S(1)}, u32[]{:S(2)}, u32[]{:S(2)}) async-start(bf16[4,64,1792]{2,1,0:T(8,128)(2,1)} %bitcast.6), calls=%async_computation.1 | async-start | bytes 1835008 | tf_op jit(solution)/shard_map/all_to_all | solution.py:75
  78.6 2.4 %collective-permute-start.2 = (bf16[64,448]{1,0:T(8,128)(2,1)S(1)}, bf16[64,448]{1,0:T(8,128)(2,1)S(1)}, u32[]{:S(2)}, u32[]{:S(2)}) collective-permute-start(bf16[64,448]{1,0:T(8,128)(2,1)S(1)} %get-tuple-element.49), channel_id=1, source_target_pairs={{0,128},{128,256},{256,384},{384,0},{1,129},{129,257},{257,385},{3... | collective-permute-start | bytes 172040 | tf_op jit(solution)/shard_map/ppermute | solution.py:20
  81.0 4.3 %collective-permute-start.3 = (bf16[64,448]{1,0:T(8,128)(2,1)S(1)}, bf16[64,448]{1,0:T(8,128)(2,1)S(1)}, u32[]{:S(2)}, u32[]{:S(2)}) collective-permute-start(bf16[64,448]{1,0:T(8,128)(2,1)S(1)} %get-tuple-element.48), channel_id=1, source_target_pairs={{0,256},{128,384},{256,0},{384,128},{1,257},{129,385},{257,1},{385... | collective-permute-start | bytes 172040 | tf_op jit(solution)/shard_map/ppermute | solution.py:20
  85.4 1.9 collective-permute-start.4
  87.3 1.4 collective-permute-done.3
  88.7 4.0 %collective-permute-done.4 = bf16[64,448]{1,0:T(8,128)(2,1)S(1)} collective-permute-done((bf16[64,448]{1,0:T(8,128)(2,1)S(1)}, bf16[64,448]{1,0:T(8,128)(2,1)S(1)}, u32[]{:S(2)}, u32[]{:S(2)}) %collective-permute-start.4) | collective-permute-done | bytes 57376 | tf_op jit(solution)/shard_map/ppermute | solution.py:20
  93.6 6.0 %all-to-all-done.1 = bf16[4,64,1792]{2,1,0:T(8,128)(2,1)S(1)} async-done(((bf16[4,64,1792]{2,1,0:T(8,128)(2,1)}), bf16[4,64,1792]{2,1,0:T(8,128)(2,1)S(1)}, u32[]{:S(2)}, u32[]{:S(2)}) %all-to-all-start.1) | async-done | bytes 917536 | tf_op jit(solution)/shard_map/all_to_all | solution.py:75
  100.8 21.5 %all_gather.17 = bf16[256,1792]{1,0:T(8,128)(2,1)S(1)} all-gather(bf16[64,1792]{1,0:T(8,128)(2,1)S(1)} %get-tuple-element.42), channel_id=1, replica_groups=mesh['x'=4,'yl'=2,'z'=8,'yh'=4,'c'=2] {'yh'}, dimensions={0}, use_global_device_ids=true | all-gather | bytes 1146880 | tf_op jit(solution)/shard_map/all_gather | solution.py:85
  122.2 1.9 collective-permute-start.5
  125.3 1.3 collective-permute-done.5
  130.2 2.0 %collective-permute-start.6 = (bf16[256,448]{0,1:T(8,128)(2,1)}, bf16[256,448]{0,1:T(8,128)(2,1)S(1)}, u32[]{:S(2)}, u32[]{:S(2)}) collective-permute-start(bf16[256,448]{0,1:T(8,128)(2,1)} %get-tuple-element.40), channel_id=1, source_target_pairs={{0,128},{128,256},{256,384},{384,0},{1,129},{129,257},{257,385},{3... | collective-permute-start | bytes 688136 | tf_op jit(solution)/shard_map/ppermute | solution.py:20
  132.2 5.8 %collective-permute-start.9 = (bf16[64,1792]{1,0:T(8,128)(2,1)}, bf16[64,1792]{1,0:T(8,128)(2,1)S(1)}, u32[]{:S(2)}, u32[]{:S(2)}) collective-permute-start(bf16[64,1792]{1,0:T(8,128)(2,1)} %get-tuple-element.25), channel_id=1, source_target_pairs={{0,0},{1,8},{2,16},{3,24},{4,32},{5,40},{6,48},{7,56},{8,1},{9,9},... | collective-permute-start | bytes 688136 | tf_op jit(solution)/shard_map/ppermute | solution.py:29
  138.0 2.7 %collective-permute-start.7 = (bf16[256,448]{0,1:T(8,128)(2,1)}, bf16[256,448]{0,1:T(8,128)(2,1)}, u32[]{:S(2)}, u32[]{:S(2)}) collective-permute-start(bf16[256,448]{0,1:T(8,128)(2,1)} %get-tuple-element.39), channel_id=1, source_target_pairs={{0,256},{128,384},{256,0},{384,128},{1,257},{129,385},{257,1},{385... | collective-permute-start | bytes 688136 | tf_op jit(solution)/shard_map/ppermute | solution.py:20
  140.7 3.3 %collective-permute-start.8 = (bf16[256,448]{0,1:T(8,128)(2,1)}, bf16[256,448]{0,1:T(8,128)(2,1)S(1)}, u32[]{:S(2)}, u32[]{:S(2)}) collective-permute-start(bf16[256,448]{0,1:T(8,128)(2,1)} %get-tuple-element.38), channel_id=1, source_target_pairs={{0,384},{128,0},{256,128},{384,256},{1,385},{129,1},{257,129},{385... | collective-permute-start | bytes 688136 | tf_op jit(solution)/shard_map/ppermute | solution.py:20
  144.0 7.2 %all-to-all-start.2 = ((bf16[16,32,896]{2,1,0:T(8,128)(2,1)}), bf16[16,32,896]{2,1,0:T(8,128)(2,1)S(1)}, u32[]{:S(2)}, u32[]{:S(2)}) async-start(bf16[16,32,896]{2,1,0:T(8,128)(2,1)} %bitcast.17), calls=%async_computation.2 | async-start | bytes 1835008 | tf_op jit(solution)/shard_map/all_to_all | solution.py:48
  152.3 1.5 collective-permute-done.8
  153.8 10.1 %collective-permute-done.9 = bf16[64,1792]{1,0:T(8,128)(2,1)S(1)} collective-permute-done((bf16[64,1792]{1,0:T(8,128)(2,1)}, bf16[64,1792]{1,0:T(8,128)(2,1)S(1)}, u32[]{:S(2)}, u32[]{:S(2)}) %collective-permute-start.9) | collective-permute-done | bytes 229408 | tf_op jit(solution)/shard_map/ppermute | solution.py:29
  163.9 1.9 collective-permute-start.13
  166.7 5.1 %collective-permute-start.10 = (bf16[64,448]{1,0:T(8,128)(2,1)S(1)}, bf16[64,448]{1,0:T(8,128)(2,1)S(1)}, u32[]{:S(2)}, u32[]{:S(2)}) collective-permute-start(bf16[64,448]{1,0:T(8,128)(2,1)S(1)} %bitcast.93), channel_id=1, source_target_pairs={{0,128},{128,256},{256,384},{384,0},{1,129},{129,257},{257,385},{3... | collective-permute-start | bytes 172040 | tf_op jit(solution)/shard_map/ppermute | solution.py:20
  171.9 6.3 %collective-permute-start.11 = (bf16[64,448]{1,0:T(8,128)(2,1)S(1)}, bf16[64,448]{1,0:T(8,128)(2,1)S(1)}, u32[]{:S(2)}, u32[]{:S(2)}) collective-permute-start(bf16[64,448]{1,0:T(8,128)(2,1)S(1)} %bitcast.92), channel_id=1, source_target_pairs={{0,256},{128,384},{256,0},{384,128},{1,257},{129,385},{257,1},{385... | collective-permute-start | bytes 172040 | tf_op jit(solution)/shard_map/ppermute | solution.py:20
  178.2 1.9 collective-permute-start.12
  180.7 4.9 %collective-permute-done.12 = bf16[64,448]{1,0:T(8,128)(2,1)S(1)} collective-permute-done((bf16[64,448]{1,0:T(8,128)(2,1)S(1)}, bf16[64,448]{1,0:T(8,128)(2,1)S(1)}, u32[]{:S(2)}, u32[]{:S(2)}) %collective-permute-start.12) | collective-permute-done | bytes 57376 | tf_op jit(solution)/shard_map/ppermute | solution.py:20
  187.2 5.0 %bitcast_convert_fusion = bf16[896,448]{0,1:T(8,128)(2,1)} fusion(bf16[4,2,256,896]{3,2,1,0:T(8,128)(2,1)} %bitcast.94, bf16[4,1,256,448]{2,3,1,0:T(8,128)(2,1)S(1)} %bitcast.95, bf16[4,1,256,448]{2,3,1,0:T(8,128)(2,1)S(1)} %bitcast.87), kind=kOutput, calls=%fused_computation.8 | convolution fusion | flops 1645486080 | bytes 6307840 | tf_op jit(solution)/shard_map/dot_general | solution.py:54
  (54 shorter events, 12.4 us)
Async XLA Ops:
  7.2 13.1 %copy-start.1 = (bf16[256,448]{0,1:T(8,128)(2,1)S(1)}, bf16[256,448]{0,1:T(8,128)(2,1)}, u32[]{:S(2)}) copy-start(bf16[256,448]{0,1:T(8,128)(2,1)} %param.5) | copy-start | bytes 688132
  7.2 54.9 %all-gather.5.cloned.1.call-start = ((), (), s32[]{:S(2)}) async-start(), calls=%async_computation.3 | async-start | bytes 4014080 | tf_op jit(solution)/shard_map/all_gather | solution.py:63
  9.8 52.3 %all-to-all-start = ((bf16[16,32,896]{2,1,0:T(8,128)(2,1)}), bf16[16,32,896]{2,1,0:T(8,128)(2,1)S(1)}, u32[]{:S(2)}, u32[]{:S(2)}) async-start(bf16[16,32,896]{2,1,0:T(8,128)(2,1)} %broadcast_in_dim.42), calls=%async_computation | async-start | bytes 1835008 | tf_op jit(solution)/shard_map/all_to_all | solution.py:48
  20.4 32.4 %collective-permute-start = (bf16[256,448]{1,0:T(8,128)(2,1)S(1)}, bf16[256,448]{1,0:T(8,128)(2,1)S(1)}, u32[]{:S(2)}, u32[]{:S(2)}) collective-permute-start(bf16[256,448]{1,0:T(8,128)(2,1)S(1)} %copy.25), channel_id=1, source_target_pairs={{0,0},{1,8},{2,16},{3,24},{4,32},{5,40},{6,48},{7,56},{8,1},{9,9},... | collective-permute-start | bytes 688136 | tf_op jit(solution)/shard_map/ppermute | solution.py:29
  62.1 10.0 %copy-start = (bf16[16,32,896]{2,1,0:T(8,128)(2,1)}, bf16[16,32,896]{2,1,0:T(8,128)(2,1)S(1)}, u32[]{:S(2)}) copy-start(bf16[16,32,896]{2,1,0:T(8,128)(2,1)S(1)} %all-to-all-done) | copy-start | bytes 2752516
  62.1 7.8 %copy-start.2 = (bf16[1792,896]{1,0:T(8,128)(2,1)S(1)}, bf16[1792,896]{1,0:T(8,128)(2,1)}, u32[]{:S(2)}) copy-start(bf16[1792,896]{1,0:T(8,128)(2,1)} %all-gather.5.cloned.1.call-done) | copy-start | bytes 9633796
  65.5 4.4 %collective-permute-start.1 = (bf16[256,1792]{1,0:T(8,128)(2,1)S(1)}, bf16[256,1792]{1,0:T(8,128)(2,1)S(1)}, u32[]{:S(2)}, u32[]{:S(2)}) collective-permute-start(bf16[256,1792]{1,0:T(8,128)(2,1)S(1)} %convolution_convert_fusion), channel_id=1, source_target_pairs={{0,1},{1,0},{2,3},{3,2},{4,5},{5,4},{6,7},{7,6},{8,9},{9,8},{10,11... | collective-permute-start | bytes 2752520 | tf_op jit(solution)/shard_map/ppermute | solution.py:24
  72.1 27.6 %all-to-all-start.1 = ((bf16[4,64,1792]{2,1,0:T(8,128)(2,1)}), bf16[4,64,1792]{2,1,0:T(8,128)(2,1)S(1)}, u32[]{:S(2)}, u32[]{:S(2)}) async-start(bf16[4,64,1792]{2,1,0:T(8,128)(2,1)} %bitcast.6), calls=%async_computation.1 | async-start | bytes 1835008 | tf_op jit(solution)/shard_map/all_to_all | solution.py:75
  77.8 109.3 %all-gather.7.cloned.1.call-start = ((), (), s32[]{:S(2)}) async-start(), calls=%async_computation.4 | async-start | bytes 4587520 | tf_op jit(solution)/shard_map/all_gather | solution.py:102
  78.6 8.7 %collective-permute-start.2 = (bf16[64,448]{1,0:T(8,128)(2,1)S(1)}, bf16[64,448]{1,0:T(8,128)(2,1)S(1)}, u32[]{:S(2)}, u32[]{:S(2)}) collective-permute-start(bf16[64,448]{1,0:T(8,128)(2,1)S(1)} %get-tuple-element.49), channel_id=1, source_target_pairs={{0,128},{128,256},{256,384},{384,0},{1,129},{129,257},{257,385},{3... | collective-permute-start | bytes 172040 | tf_op jit(solution)/shard_map/ppermute | solution.py:20
  81.0 7.7 %collective-permute-start.3 = (bf16[64,448]{1,0:T(8,128)(2,1)S(1)}, bf16[64,448]{1,0:T(8,128)(2,1)S(1)}, u32[]{:S(2)}, u32[]{:S(2)}) collective-permute-start(bf16[64,448]{1,0:T(8,128)(2,1)S(1)} %get-tuple-element.48), channel_id=1, source_target_pairs={{0,256},{128,384},{256,0},{384,128},{1,257},{129,385},{257,1},{385... | collective-permute-start | bytes 172040 | tf_op jit(solution)/shard_map/ppermute | solution.py:20
  85.4 7.4 %collective-permute-start.4 = (bf16[64,448]{1,0:T(8,128)(2,1)S(1)}, bf16[64,448]{1,0:T(8,128)(2,1)S(1)}, u32[]{:S(2)}, u32[]{:S(2)}) collective-permute-start(bf16[64,448]{1,0:T(8,128)(2,1)S(1)} %get-tuple-element.47), channel_id=1, source_target_pairs={{0,384},{128,0},{256,128},{384,256},{1,385},{129,1},{257,129},{385... | collective-permute-start | bytes 172040 | tf_op jit(solution)/shard_map/ppermute | solution.py:20
  99.6 24.5 %copy-start.3 = (bf16[1792,896]{1,0:T(8,128)(2,1)S(1)}, bf16[1792,896]{1,0:T(8,128)(2,1)}, u32[]{:S(2)}) copy-start(bf16[1792,896]{1,0:T(8,128)(2,1)} %all-gather.5.cloned.1.call-done) | copy-start | bytes 9633796
  122.2 4.4 %collective-permute-start.5 = (bf16[256,1792]{1,0:T(8,128)(2,1)S(1)}, bf16[256,1792]{1,0:T(8,128)(2,1)S(1)}, u32[]{:S(2)}, u32[]{:S(2)}) collective-permute-start(bf16[256,1792]{1,0:T(8,128)(2,1)S(1)} %all_gather.17), channel_id=1, source_target_pairs={{0,1},{1,0},{2,3},{3,2},{4,5},{5,4},{6,7},{7,6},{8,9},{9,8},{10,11... | collective-permute-start | bytes 2752520 | tf_op jit(solution)/shard_map/ppermute | solution.py:24
  130.2 21.1 %collective-permute-start.6 = (bf16[256,448]{0,1:T(8,128)(2,1)}, bf16[256,448]{0,1:T(8,128)(2,1)S(1)}, u32[]{:S(2)}, u32[]{:S(2)}) collective-permute-start(bf16[256,448]{0,1:T(8,128)(2,1)} %get-tuple-element.40), channel_id=1, source_target_pairs={{0,128},{128,256},{256,384},{384,0},{1,129},{129,257},{257,385},{3... | collective-permute-start | bytes 688136 | tf_op jit(solution)/shard_map/ppermute | solution.py:20
  132.2 31.7 %collective-permute-start.9 = (bf16[64,1792]{1,0:T(8,128)(2,1)}, bf16[64,1792]{1,0:T(8,128)(2,1)S(1)}, u32[]{:S(2)}, u32[]{:S(2)}) collective-permute-start(bf16[64,1792]{1,0:T(8,128)(2,1)} %get-tuple-element.25), channel_id=1, source_target_pairs={{0,0},{1,8},{2,16},{3,24},{4,32},{5,40},{6,48},{7,56},{8,1},{9,9},... | collective-permute-start | bytes 688136 | tf_op jit(solution)/shard_map/ppermute | solution.py:29
  138.0 13.3 %collective-permute-start.7 = (bf16[256,448]{0,1:T(8,128)(2,1)}, bf16[256,448]{0,1:T(8,128)(2,1)}, u32[]{:S(2)}, u32[]{:S(2)}) collective-permute-start(bf16[256,448]{0,1:T(8,128)(2,1)} %get-tuple-element.39), channel_id=1, source_target_pairs={{0,256},{128,384},{256,0},{384,128},{1,257},{129,385},{257,1},{385... | collective-permute-start | bytes 688136 | tf_op jit(solution)/shard_map/ppermute | solution.py:20
  140.7 13.1 %collective-permute-start.8 = (bf16[256,448]{0,1:T(8,128)(2,1)}, bf16[256,448]{0,1:T(8,128)(2,1)S(1)}, u32[]{:S(2)}, u32[]{:S(2)}) collective-permute-start(bf16[256,448]{0,1:T(8,128)(2,1)} %get-tuple-element.38), channel_id=1, source_target_pairs={{0,384},{128,0},{256,128},{384,256},{1,385},{129,1},{257,129},{385... | collective-permute-start | bytes 688136 | tf_op jit(solution)/shard_map/ppermute | solution.py:20
  144.0 42.4 %all-to-all-start.2 = ((bf16[16,32,896]{2,1,0:T(8,128)(2,1)}), bf16[16,32,896]{2,1,0:T(8,128)(2,1)S(1)}, u32[]{:S(2)}, u32[]{:S(2)}) async-start(bf16[16,32,896]{2,1,0:T(8,128)(2,1)} %bitcast.17), calls=%async_computation.2 | async-start | bytes 1835008 | tf_op jit(solution)/shard_map/all_to_all | solution.py:48
  163.9 23.2 %collective-permute-start.13 = (bf16[4,256,448]{1,2,0:T(8,128)(2,1)S(1)}, bf16[4,256,448]{1,2,0:T(8,128)(2,1)S(1)}, u32[]{:S(2)}, u32[]{:S(2)}) collective-permute-start(bf16[4,256,448]{1,2,0:T(8,128)(2,1)S(1)} %bitcast_dynamic-update-slice_fusion), channel_id=1, source_target_pairs={{0,1},{1,0},{2,3},{3,2},{4,5},{5,4},{6,7},{7,6},{8,9},{9,8},{10,11... | collective-permute-start | bytes 2752520 | tf_op jit(solution)/shard_map/ppermute | solution.py:24
  166.7 13.5 %collective-permute-start.10 = (bf16[64,448]{1,0:T(8,128)(2,1)S(1)}, bf16[64,448]{1,0:T(8,128)(2,1)S(1)}, u32[]{:S(2)}, u32[]{:S(2)}) collective-permute-start(bf16[64,448]{1,0:T(8,128)(2,1)S(1)} %bitcast.93), channel_id=1, source_target_pairs={{0,128},{128,256},{256,384},{384,0},{1,129},{129,257},{257,385},{3... | collective-permute-start | bytes 172040 | tf_op jit(solution)/shard_map/ppermute | solution.py:20
  171.9 8.8 %collective-permute-start.11 = (bf16[64,448]{1,0:T(8,128)(2,1)S(1)}, bf16[64,448]{1,0:T(8,128)(2,1)S(1)}, u32[]{:S(2)}, u32[]{:S(2)}) collective-permute-start(bf16[64,448]{1,0:T(8,128)(2,1)S(1)} %bitcast.92), channel_id=1, source_target_pairs={{0,256},{128,384},{256,0},{384,128},{1,257},{129,385},{257,1},{385... | collective-permute-start | bytes 172040 | tf_op jit(solution)/shard_map/ppermute | solution.py:20
  178.2 7.4 %collective-permute-start.12 = (bf16[64,448]{1,0:T(8,128)(2,1)S(1)}, bf16[64,448]{1,0:T(8,128)(2,1)S(1)}, u32[]{:S(2)}, u32[]{:S(2)}) collective-permute-start(bf16[64,448]{1,0:T(8,128)(2,1)S(1)} %bitcast.91), channel_id=1, source_target_pairs={{0,384},{128,0},{256,128},{384,256},{1,385},{129,1},{257,129},{385... | collective-permute-start | bytes 172040 | tf_op jit(solution)/shard_map/ppermute | solution.py:20
Sparse Core Ops, SparseCore 0:
  10.1 47.7 all-gather.4
  80.8 46.5 all-gather.6

commit v6 on v5

--- a/solution.py
+++ b/solution.py
@@ -65,7 +65,7 @@
     near = exchange_rows(jnp.broadcast_to(tokens[None], (16, rows, feats)))
     near = near.reshape(2, 4 * pair, feats)
 
-    near, cot, w_all = lax.optimization_barrier((near, swap_z_g(act_grad), w_all))
+    near, cot, w_all = lax.optimization_barrier((near, swap_z_g(act_grad.T), w_all))
     w_all = w_all.reshape(NX * cols, feats)
 
     sent = swap_cores(dot(near[1], w_all, ((1,), (1,))).astype(BF))
@@ -75,7 +75,7 @@
     parts = lax.all_to_all(partial_value, "yh", split_axis=0, concat_axis=0)
     hidden = jnp.sum(parts.astype(jnp.float32), axis=0)
 
-    cot = in_order(shift_blocks(cot.reshape(NX, pair, cols), here), here)
+    cot = in_order(shift_blocks(cot.T.reshape(NX, pair, cols), here), here)
     cot = cot.transpose(1, 0, 2).reshape(pair, NX * cols)
 
     activated, pullback = jax.vjp(gelu_tanh, hidden)
@@ -84,27 +84,26 @@
 
     grad_own = lax.all_gather(hidden_grad, "yh", axis=0, tiled=True)
     grad_own, activated = lax.optimization_barrier((grad_own, activated))
+    both = jnp.concatenate([grad_own, activated], axis=0)
+    both = both.reshape(5 * pair, NX, cols).transpose(1, 0, 2)
+    both = shift_blocks(both, here)
     grad_other = swap_cores(grad_own)
-    activated = swap_z_g(activated)
 
     ig_own = dot(grad_own, w_all, ((1,), (0,))).astype(BF)
-    ig_own, grad_other = lax.optimization_barrier((ig_own, grad_other))
+    ig_own, grad_other, *both = lax.optimization_barrier((ig_own, grad_other, *both))
     ig_other = dot(grad_other, w_all, ((1,), (0,))).astype(BF)
     ig = jnp.stack([ig_own, ig_other]).reshape(16, rows, feats)
-    ig, grad_own = lax.optimization_barrier((ig, grad_own))
+    out = in_order([part[4 * pair :] for part in both], here).reshape(NX * pair, cols)
+    ig, out, *both = lax.optimization_barrier((ig, out.T, *both))
+    out = swap_z_g(out).T
     ig = exchange_rows(ig)
     input_grad = jnp.sum(ig.astype(jnp.float32), axis=0).astype(BF)
 
-    far_own = grad_own.reshape(4 * pair, NX, cols).transpose(1, 0, 2)
-    far_own = in_order(shift_blocks(far_own, here), here)
-    far_own, activated = lax.optimization_barrier((far_own, activated))
+    far_own = in_order([part[: 4 * pair] for part in both], here)
     far_other = swap_cores(far_own)
     far = lax.all_gather(near, "x", axis=0, tiled=False)
     far_grad = jnp.stack([far_own, far_other], axis=1)
     weight_grad = dot(far.reshape(-1, feats), far_grad.reshape(-1, cols), ((0,), (0,))).astype(BF)
-
-    activated = activated.reshape(pair, NX, cols).transpose(1, 0, 2)
-    out = in_order(shift_blocks(activated, here), here).reshape(NX * pair, cols)
     return out, input_grad, weight_grad
 
 

time: 200 us -> 216 us (1.080)
  the two profiles are of different devices: /device:TPU:54 before, /device:TPU:1 now
where the time goes in v6:
time: 216 us; the launch traced here: 214 us
  waiting for transfers between devices  91.8 us (42%)
  starting transfers between devices  62.6 us (29%)
  blocking collectives  20.5 us (9%)
  matrix products  17 us (8%)
  between operations  14.4 us (7%)
  local copies, waits for them, and re-layouts  5.32 us (2%)
  other arithmetic  2.37 us (1%)
    ppermute x2, waiting for transfers between devices, swap_z_g(): return lax.ppermute(value, ('z', 'yh', 'c'), pairs)  68.3 us
    ppermute x6, starting transfers between devices, along_x(): return lax.ppermute(value, 'x', [(i, (i + shift) % NX) for i in range(NX)])  21.1 us
    all_gather x1, blocking collectives, body(): grad_own = lax.all_gather(hidden_grad, 'yh', axis=0, tiled=True)  20.5 us
    all_to_all x2, starting transfers between devices, exchange_rows(): lax.all_to_all(value, ('z', 'yl', 'c'), split_axis=0, concat_axis=0, axis...  20 us
    dot_general x5, matrix products, dot(): lax.dot_general(a, b, (contract, ((), ())), preferred_element_type=jnp.fl...  17 us
    ppermute x6, waiting for transfers between devices, along_x(): return lax.ppermute(value, 'x', [(i, (i + shift) % NX) for i in range(NX)])  10.9 us
    all_to_all x1, waiting for transfers between devices, body(): parts = lax.all_to_all(partial_value, 'yh', split_axis=0, concat_axis=0)  9.7 us
    ppermute x3, starting transfers between devices, swap_cores(): return lax.ppermute(value, 'c', [(0, 1), (1, 0)])  8.38 us
  transfers between devices with their start and end apart: 16, of which 8 were waited for; matrix products, arithmetic and copies ran while one was open for 7% of the time, Pallas kernels for 0%

profile of v6, /device:TPU:1, one launch (start us, length us, event | category | flops | bytes accessed | tf_op | source)
XLA Modules:
  0.0 214.0 jit_solution(16450519970350315023)
XLA Ops:
  7.9 1.8 broadcast_in_dim.45
  9.7 13.1 %all-to-all-start = ((bf16[16,32,896]{2,1,0:T(8,128)(2,1)}), bf16[16,32,896]{2,1,0:T(8,128)(2,1)S(1)}, u32[]{:S(2)}, u32[]{:S(2)}) async-start(bf16[16,32,896]{2,1,0:T(8,128)(2,1)} %broadcast_in_dim.45), calls=%async_computation | async-start | bytes 1835008 | tf_op jit(solution)/shard_map/all_to_all | solution.py:48
  23.0 3.3 %collective-permute-start = (bf16[448,256]{0,1:T(8,128)(2,1)S(1)}, bf16[448,256]{0,1:T(8,128)(2,1)S(1)}, u32[]{:S(2)}, u32[]{:S(2)}) collective-permute-start(bf16[448,256]{0,1:T(8,128)(2,1)S(1)} %bitcast.88), channel_id=1, source_target_pairs={{0,0},{1,8},{2,16},{3,24},{4,32},{5,40},{6,48},{7,56},{8,1},{9,9},... | collective-permute-start | bytes 688136 | tf_op jit(solution)/shard_map/ppermute | solution.py:29
  26.3 35.7 %collective-permute-done = bf16[448,256]{0,1:T(8,128)(2,1)S(1)} collective-permute-done((bf16[448,256]{0,1:T(8,128)(2,1)S(1)}, bf16[448,256]{0,1:T(8,128)(2,1)S(1)}, u32[]{:S(2)}, u32[]{:S(2)}) %collective-permute-start) | collective-permute-done | bytes 229408 | tf_op jit(solution)/shard_map/ppermute | solution.py:29
  62.1 3.4 %convolution_convert_fusion = bf16[256,1792]{1,0:T(8,128)(2,1)S(1)} fusion(bf16[1792,896]{1,0:T(8,128)(2,1)} %all-gather.5.cloned.1.call-done, bf16[2,256,896]{2,1,0:T(8,128)(2,1)S(1)} %bitcast.79), kind=kOutput, calls=%fused_computation.2 | convolution fusion | flops 822542336 | bytes 4587520 | tf_op jit(solution)/shard_map/dot_general | solution.py:54
  65.5 2.7 %collective-permute-start.1 = (bf16[256,1792]{1,0:T(8,128)(2,1)S(1)}, bf16[256,1792]{1,0:T(8,128)(2,1)S(1)}, u32[]{:S(2)}, u32[]{:S(2)}) collective-permute-start(bf16[256,1792]{1,0:T(8,128)(2,1)S(1)} %convolution_convert_fusion), channel_id=1, source_target_pairs={{0,1},{1,0},{2,3},{3,2},{4,5},{5,4},{6,7},{7,6},{8,9},{9,8},{10,11... | collective-permute-start | bytes 2752520 | tf_op jit(solution)/shard_map/ppermute | solution.py:24
  68.3 2.1 collective-permute-done.1
  70.4 2.2 %fusion = bf16[256,1792]{1,0:T(8,128)(2,1)} fusion(bf16[1792,896]{1,0:T(8,128)(2,1)S(1)} %copy-done.8, bf16[256,1792]{1,0:T(8,128)(2,1)S(1)} %collective-permute-done.1, bf16[2,256,896]{2,1,0:T(8,128)(2,1)S(1)} %bitcast.80), kind=kOutput, calls=%fused_computation.1 | convolution fusion | flops 823459840 | bytes 5505024 | tf_op jit(solution)/shard_map/dot_general | solution.py:54
  72.5 6.3 %all-to-all-start.1 = ((bf16[4,64,1792]{2,1,0:T(8,128)(2,1)}), bf16[4,64,1792]{2,1,0:T(8,128)(2,1)S(1)}, u32[]{:S(2)}, u32[]{:S(2)}) async-start(bf16[4,64,1792]{2,1,0:T(8,128)(2,1)} %bitcast.7), calls=%async_computation.1 | async-start | bytes 1835008 | tf_op jit(solution)/shard_map/all_to_all | solution.py:75
  78.9 3.1 %collective-permute-start.2 = (bf16[64,448]{1,0:T(8,128)(2,1)S(1)}, bf16[64,448]{1,0:T(8,128)(2,1)S(1)}, u32[]{:S(2)}, u32[]{:S(2)}) collective-permute-start(bf16[64,448]{1,0:T(8,128)(2,1)S(1)} %get-tuple-element.58), channel_id=1, source_target_pairs={{0,128},{128,256},{256,384},{384,0},{1,129},{129,257},{257,385},{3... | collective-permute-start | bytes 172040 | tf_op jit(solution)/shard_map/ppermute | solution.py:20
  82.0 4.4 %collective-permute-start.3 = (bf16[64,448]{1,0:T(8,128)(2,1)S(1)}, bf16[64,448]{1,0:T(8,128)(2,1)S(1)}, u32[]{:S(2)}, u32[]{:S(2)}) collective-permute-start(bf16[64,448]{1,0:T(8,128)(2,1)S(1)} %get-tuple-element.57), channel_id=1, source_target_pairs={{0,256},{128,384},{256,0},{384,128},{1,257},{129,385},{257,1},{385... | collective-permute-start | bytes 172040 | tf_op jit(solution)/shard_map/ppermute | solution.py:20
  86.4 3.1 %collective-permute-start.4 = (bf16[64,448]{1,0:T(8,128)(2,1)S(1)}, bf16[64,448]{1,0:T(8,128)(2,1)S(1)}, u32[]{:S(2)}, u32[]{:S(2)}) collective-permute-start(bf16[64,448]{1,0:T(8,128)(2,1)S(1)} %get-tuple-element.56), channel_id=1, source_target_pairs={{0,384},{128,0},{256,128},{384,256},{1,385},{129,1},{257,129},{385... | collective-permute-start | bytes 172040 | tf_op jit(solution)/shard_map/ppermute | solution.py:20
  89.5 2.2 %collective-permute-done.4 = bf16[64,448]{1,0:T(8,128)(2,1)S(1)} collective-permute-done((bf16[64,448]{1,0:T(8,128)(2,1)S(1)}, bf16[64,448]{1,0:T(8,128)(2,1)S(1)}, u32[]{:S(2)}, u32[]{:S(2)}) %collective-permute-start.4) | collective-permute-done | bytes 57376 | tf_op jit(solution)/shard_map/ppermute | solution.py:20
  92.6 9.7 %all-to-all-done.1 = bf16[4,64,1792]{2,1,0:T(8,128)(2,1)S(1)} async-done(((bf16[4,64,1792]{2,1,0:T(8,128)(2,1)}), bf16[4,64,1792]{2,1,0:T(8,128)(2,1)S(1)}, u32[]{:S(2)}, u32[]{:S(2)}) %all-to-all-start.1) | async-done | bytes 917536 | tf_op jit(solution)/shard_map/all_to_all | solution.py:75
  102.8 20.5 %all_gather.17 = bf16[256,1792]{1,0:T(8,128)(2,1)S(1)} all-gather(bf16[64,1792]{1,0:T(8,128)(2,1)S(1)} %get-tuple-element.55), channel_id=1, replica_groups=mesh['x'=4,'yl'=2,'z'=8,'yh'=4,'c'=2] {'yh'}, dimensions={0}, use_global_device_ids=true | all-gather | bytes 1146880 | tf_op jit(solution)/shard_map/all_gather | solution.py:85
  123.2 2.8 %collective-permute-start.5 = (bf16[256,1792]{1,0:T(8,128)(2,1)S(1)}, bf16[256,1792]{1,0:T(8,128)(2,1)}, u32[]{:S(2)}, u32[]{:S(2)}) collective-permute-start(bf16[256,1792]{1,0:T(8,128)(2,1)S(1)} %all_gather.17), channel_id=1, source_target_pairs={{0,1},{1,0},{2,3},{3,2},{4,5},{5,4},{6,7},{7,6},{8,9},{9,8},{10,11... | collective-permute-start | bytes 2752520 | tf_op jit(solution)/shard_map/ppermute | solution.py:24
  126.2 0.8 copy.42
  127.2 3.2 %collective-permute-start.6 = (bf16[320,448]{0,1:T(8,128)(2,1)S(1)}, bf16[320,448]{0,1:T(8,128)(2,1)S(1)}, u32[]{:S(2)}, u32[]{:S(2)}) collective-permute-start(bf16[320,448]{0,1:T(8,128)(2,1)S(1)} %get-tuple-element.52), channel_id=1, source_target_pairs={{0,128},{128,256},{256,384},{384,0},{1,129},{129,257},{257,385},{3... | collective-permute-start | bytes 860168 | tf_op jit(solution)/shard_map/ppermute | solution.py:20
  130.3 4.0 %collective-permute-start.7 = (bf16[320,448]{0,1:T(8,128)(2,1)S(1)}, bf16[320,448]{0,1:T(8,128)(2,1)S(1)}, u32[]{:S(2)}, u32[]{:S(2)}) collective-permute-start(bf16[320,448]{0,1:T(8,128)(2,1)S(1)} %get-tuple-element.51), channel_id=1, source_target_pairs={{0,256},{128,384},{256,0},{384,128},{1,257},{129,385},{257,1},{385... | collective-permute-start | bytes 860168 | tf_op jit(solution)/shard_map/ppermute | solution.py:20
  134.4 3.4 %collective-permute-start.8 = (bf16[320,448]{0,1:T(8,128)(2,1)S(1)}, bf16[320,448]{0,1:T(8,128)(2,1)S(1)}, u32[]{:S(2)}, u32[]{:S(2)}) collective-permute-start(bf16[320,448]{0,1:T(8,128)(2,1)S(1)} %get-tuple-element.50), channel_id=1, source_target_pairs={{0,384},{128,0},{256,128},{384,256},{1,385},{129,1},{257,129},{385... | collective-permute-start | bytes 860168 | tf_op jit(solution)/shard_map/ppermute | solution.py:20
  137.8 3.0 %convolution_convert_fusion.2 = bf16[256,896]{1,0:T(8,128)(2,1)S(1)} fusion(bf16[256,1792]{1,0:T(8,128)(2,1)S(1)} %all_gather.17, bf16[1792,896]{1,0:T(8,128)(2,1)} %all-gather.5.cloned.1.call-done), kind=kOutput, calls=%fused_computation.10 | convolution fusion | flops 822312960 | bytes 4587520 | tf_op jit(solution)/shard_map/dot_general | solution.py:54
  140.8 7.2 %collective-permute-done.7 = bf16[320,448]{0,1:T(8,128)(2,1)S(1)} collective-permute-done((bf16[320,448]{0,1:T(8,128)(2,1)S(1)}, bf16[320,448]{0,1:T(8,128)(2,1)S(1)}, u32[]{:S(2)}, u32[]{:S(2)}) %collective-permute-start.7) | collective-permute-done | bytes 286752 | tf_op jit(solution)/shard_map/ppermute | solution.py:20
  148.0 1.5 collective-permute-done.8
  150.1 3.4 %fusion.7 = bf16[1,256,896]{2,1,0:T(8,128)(2,1)S(1)} fusion(bf16[256,1792]{1,0:T(8,128)(2,1)} %collective-permute-done.5, bf16[1792,896]{1,0:T(8,128)(2,1)} %all-gather.5.cloned.1.call-done), kind=kOutput, calls=%fused_computation.11 | convolution fusion | flops 822312960 | bytes 4587520 | tf_op jit(solution)/shard_map/dot_general | solution.py:54
  153.6 1.0 pad_maximum_fusion.1
  154.6 7.0 %all-to-all-start.2 = ((bf16[16,32,896]{2,1,0:T(8,128)(2,1)}), bf16[16,32,896]{2,1,0:T(8,128)(2,1)S(1)}, u32[]{:S(2)}, u32[]{:S(2)}) async-start(bf16[16,32,896]{2,1,0:T(8,128)(2,1)} %bitcast.24), calls=%async_computation.2 | async-start | bytes 1835008 | tf_op jit(solution)/shard_map/all_to_all | solution.py:48
  161.8 2.8 %collective-permute-start.10 = (bf16[4,256,448]{1,2,0:T(8,128)(2,1)S(1)}, bf16[4,256,448]{1,2,0:T(8,128)(2,1)S(1)}, u32[]{:S(2)}, u32[]{:S(2)}) collective-permute-start(bf16[4,256,448]{1,2,0:T(8,128)(2,1)S(1)} %bitcast_dynamic-update-slice_fusion), channel_id=1, source_target_pairs={{0,1},{1,0},{2,3},{3,2},{4,5},{5,4},{6,7},{7,6},{8,9},{9,8},{10,11... | collective-permute-start | bytes 2752520 | tf_op jit(solution)/shard_map/ppermute | solution.py:24
  164.6 3.5 %collective-permute-start.9 = (bf16[448,256]{0,1:T(8,128)(2,1)S(1)}, bf16[448,256]{0,1:T(8,128)(2,1)S(1)}, u32[]{:S(2)}, u32[]{:S(2)}) collective-permute-start(bf16[448,256]{0,1:T(8,128)(2,1)S(1)} %bitcast.86), channel_id=1, source_target_pairs={{0,0},{1,8},{2,16},{3,24},{4,32},{5,40},{6,48},{7,56},{8,1},{9,9},... | collective-permute-start | bytes 688136 | tf_op jit(solution)/shard_map/ppermute | solution.py:29
  168.0 32.6 %collective-permute-done.9 = bf16[448,256]{0,1:T(8,128)(2,1)S(1)} collective-permute-done((bf16[448,256]{0,1:T(8,128)(2,1)S(1)}, bf16[448,256]{0,1:T(8,128)(2,1)S(1)}, u32[]{:S(2)}, u32[]{:S(2)}) %collective-permute-start.9) | collective-permute-done | bytes 229408 | tf_op jit(solution)/shard_map/ppermute | solution.py:29
  200.6 0.8 copy.40
  201.4 0.8 reduce_sum.22
  202.2 5.0 %bitcast_convert_fusion = bf16[896,448]{0,1:T(8,128)(2,1)} fusion(bf16[4,2,256,896]{3,2,1,0:T(8,128)(2,1)} %bitcast.89, bf16[4,1,256,448]{2,3,1,0:T(8,128)(2,1)S(1)} %bitcast.90, bf16[4,1,256,448]{2,3,1,0:T(8,128)(2,1)S(1)} %bitcast.82), kind=kOutput, calls=%fused_computation.8 | convolution fusion | flops 1645486080 | bytes 6307840 | tf_op jit(solution)/shard_map/dot_general | solution.py:54
  (60 shorter events, 3.2 us)
Async XLA Ops:
  7.2 15.6 %copy-start.7 = (bf16[256,448]{0,1:T(8,128)(2,1)S(1)}, bf16[256,448]{0,1:T(8,128)(2,1)}, u32[]{:S(2)}) copy-start(bf16[256,448]{0,1:T(8,128)(2,1)} %param.5) | copy-start | bytes 688132
  7.2 54.9 %all-gather.5.cloned.1.call-start = ((), (), s32[]{:S(2)}) async-start(), calls=%async_computation.3 | async-start | bytes 4014080 | tf_op jit(solution)/shard_map/all_gather | solution.py:63
  9.7 52.4 %all-to-all-start = ((bf16[16,32,896]{2,1,0:T(8,128)(2,1)}), bf16[16,32,896]{2,1,0:T(8,128)(2,1)S(1)}, u32[]{:S(2)}, u32[]{:S(2)}) async-start(bf16[16,32,896]{2,1,0:T(8,128)(2,1)} %broadcast_in_dim.45), calls=%async_computation | async-start | bytes 1835008 | tf_op jit(solution)/shard_map/all_to_all | solution.py:48
  23.0 39.1 %collective-permute-start = (bf16[448,256]{0,1:T(8,128)(2,1)S(1)}, bf16[448,256]{0,1:T(8,128)(2,1)S(1)}, u32[]{:S(2)}, u32[]{:S(2)}) collective-permute-start(bf16[448,256]{0,1:T(8,128)(2,1)S(1)} %bitcast.88), channel_id=1, source_target_pairs={{0,0},{1,8},{2,16},{3,24},{4,32},{5,40},{6,48},{7,56},{8,1},{9,9},... | collective-permute-start | bytes 688136 | tf_op jit(solution)/shard_map/ppermute | solution.py:29
  62.1 8.3 %copy-start = (bf16[16,32,896]{2,1,0:T(8,128)(2,1)}, bf16[16,32,896]{2,1,0:T(8,128)(2,1)S(1)}, u32[]{:S(2)}) copy-start(bf16[16,32,896]{2,1,0:T(8,128)(2,1)S(1)} %all-to-all-done) | copy-start | bytes 2752516
  62.1 8.3 %copy-start.8 = (bf16[1792,896]{1,0:T(8,128)(2,1)S(1)}, bf16[1792,896]{1,0:T(8,128)(2,1)}, u32[]{:S(2)}) copy-start(bf16[1792,896]{1,0:T(8,128)(2,1)} %all-gather.5.cloned.1.call-done) | copy-start | bytes 9633796
  65.5 4.8 %collective-permute-start.1 = (bf16[256,1792]{1,0:T(8,128)(2,1)S(1)}, bf16[256,1792]{1,0:T(8,128)(2,1)S(1)}, u32[]{:S(2)}, u32[]{:S(2)}) collective-permute-start(bf16[256,1792]{1,0:T(8,128)(2,1)S(1)} %convolution_convert_fusion), channel_id=1, source_target_pairs={{0,1},{1,0},{2,3},{3,2},{4,5},{5,4},{6,7},{7,6},{8,9},{9,8},{10,11... | collective-permute-start | bytes 2752520 | tf_op jit(solution)/shard_map/ppermute | solution.py:24
  72.5 29.7 %all-to-all-start.1 = ((bf16[4,64,1792]{2,1,0:T(8,128)(2,1)}), bf16[4,64,1792]{2,1,0:T(8,128)(2,1)S(1)}, u32[]{:S(2)}, u32[]{:S(2)}) async-start(bf16[4,64,1792]{2,1,0:T(8,128)(2,1)} %bitcast.7), calls=%async_computation.1 | async-start | bytes 1835008 | tf_op jit(solution)/shard_map/all_to_all | solution.py:75
  78.8 123.4 %all-gather.7.cloned.1.call-start = ((), (), s32[]{:S(2)}) async-start(), calls=%async_computation.4 | async-start | bytes 4587520 | tf_op jit(solution)/shard_map/all_gather | solution.py:104
  78.9 10.6 %collective-permute-start.2 = (bf16[64,448]{1,0:T(8,128)(2,1)S(1)}, bf16[64,448]{1,0:T(8,128)(2,1)S(1)}, u32[]{:S(2)}, u32[]{:S(2)}) collective-permute-start(bf16[64,448]{1,0:T(8,128)(2,1)S(1)} %get-tuple-element.58), channel_id=1, source_target_pairs={{0,128},{128,256},{256,384},{384,0},{1,129},{129,257},{257,385},{3... | collective-permute-start | bytes 172040 | tf_op jit(solution)/shard_map/ppermute | solution.py:20
  82.0 7.5 %collective-permute-start.3 = (bf16[64,448]{1,0:T(8,128)(2,1)S(1)}, bf16[64,448]{1,0:T(8,128)(2,1)S(1)}, u32[]{:S(2)}, u32[]{:S(2)}) collective-permute-start(bf16[64,448]{1,0:T(8,128)(2,1)S(1)} %get-tuple-element.57), channel_id=1, source_target_pairs={{0,256},{128,384},{256,0},{384,128},{1,257},{129,385},{257,1},{385... | collective-permute-start | bytes 172040 | tf_op jit(solution)/shard_map/ppermute | solution.py:20
  86.4 5.3 %collective-permute-start.4 = (bf16[64,448]{1,0:T(8,128)(2,1)S(1)}, bf16[64,448]{1,0:T(8,128)(2,1)S(1)}, u32[]{:S(2)}, u32[]{:S(2)}) collective-permute-start(bf16[64,448]{1,0:T(8,128)(2,1)S(1)} %get-tuple-element.56), channel_id=1, source_target_pairs={{0,384},{128,0},{256,128},{384,256},{1,385},{129,1},{257,129},{385... | collective-permute-start | bytes 172040 | tf_op jit(solution)/shard_map/ppermute | solution.py:20
  123.2 26.3 %collective-permute-start.5 = (bf16[256,1792]{1,0:T(8,128)(2,1)S(1)}, bf16[256,1792]{1,0:T(8,128)(2,1)}, u32[]{:S(2)}, u32[]{:S(2)}) collective-permute-start(bf16[256,1792]{1,0:T(8,128)(2,1)S(1)} %all_gather.17), channel_id=1, source_target_pairs={{0,1},{1,0},{2,3},{3,2},{4,5},{5,4},{6,7},{7,6},{8,9},{9,8},{10,11... | collective-permute-start | bytes 2752520 | tf_op jit(solution)/shard_map/ppermute | solution.py:24
  127.2 13.6 %collective-permute-start.6 = (bf16[320,448]{0,1:T(8,128)(2,1)S(1)}, bf16[320,448]{0,1:T(8,128)(2,1)S(1)}, u32[]{:S(2)}, u32[]{:S(2)}) collective-permute-start(bf16[320,448]{0,1:T(8,128)(2,1)S(1)} %get-tuple-element.52), channel_id=1, source_target_pairs={{0,128},{128,256},{256,384},{384,0},{1,129},{129,257},{257,385},{3... | collective-permute-start | bytes 860168 | tf_op jit(solution)/shard_map/ppermute | solution.py:20
  130.3 17.7 %collective-permute-start.7 = (bf16[320,448]{0,1:T(8,128)(2,1)S(1)}, bf16[320,448]{0,1:T(8,128)(2,1)S(1)}, u32[]{:S(2)}, u32[]{:S(2)}) collective-permute-start(bf16[320,448]{0,1:T(8,128)(2,1)S(1)} %get-tuple-element.51), channel_id=1, source_target_pairs={{0,256},{128,384},{256,0},{384,128},{1,257},{129,385},{257,1},{385... | collective-permute-start | bytes 860168 | tf_op jit(solution)/shard_map/ppermute | solution.py:20
  134.4 15.2 %collective-permute-start.8 = (bf16[320,448]{0,1:T(8,128)(2,1)S(1)}, bf16[320,448]{0,1:T(8,128)(2,1)S(1)}, u32[]{:S(2)}, u32[]{:S(2)}) collective-permute-start(bf16[320,448]{0,1:T(8,128)(2,1)S(1)} %get-tuple-element.50), channel_id=1, source_target_pairs={{0,384},{128,0},{256,128},{384,256},{1,385},{129,1},{257,129},{385... | collective-permute-start | bytes 860168 | tf_op jit(solution)/shard_map/ppermute | solution.py:20
  148.0 1.6 copy-start.1
  149.6 4.0 %copy-start.3 = (bf16[320,448]{0,1:T(8,128)(2,1)}, bf16[320,448]{0,1:T(8,128)(2,1)S(1)}, u32[]{:S(2)}) copy-start(bf16[320,448]{0,1:T(8,128)(2,1)S(1)} %collective-permute-done.8) | copy-start | bytes 860164
  150.1 3.4 %copy-start.5 = (bf16[4,64,448]{2,1,0:T(8,128)(2,1)}, bf16[4,64,448]{2,1,0:T(8,128)(2,1)S(1)}, u32[]{:S(2)}) copy-start(bf16[4,64,448]{2,1,0:T(8,128)(2,1)S(1)} %constant_dynamic-update-slice_fusion) | copy-start | bytes 688132
  154.6 7.1 %copy-start.2 = (bf16[320,448]{0,1:T(8,128)(2,1)S(1)}, bf16[320,448]{0,1:T(8,128)(2,1)}, u32[]{:S(2)}) copy-start(bf16[320,448]{0,1:T(8,128)(2,1)} %copy-done.1) | copy-start | bytes 860164
  154.6 7.1 %copy-start.4 = (bf16[320,448]{0,1:T(8,128)(2,1)S(1)}, bf16[320,448]{0,1:T(8,128)(2,1)}, u32[]{:S(2)}) copy-start(bf16[320,448]{0,1:T(8,128)(2,1)} %copy-done.3) | copy-start | bytes 860164
  154.6 46.9 %all-to-all-start.2 = ((bf16[16,32,896]{2,1,0:T(8,128)(2,1)}), bf16[16,32,896]{2,1,0:T(8,128)(2,1)S(1)}, u32[]{:S(2)}, u32[]{:S(2)}) async-start(bf16[16,32,896]{2,1,0:T(8,128)(2,1)} %bitcast.24), calls=%async_computation.2 | async-start | bytes 1835008 | tf_op jit(solution)/shard_map/all_to_all | solution.py:48
  161.5 3.0 %copy-start.6 = (bf16[4,64,448]{2,1,0:T(8,128)(2,1)S(1)}, bf16[4,64,448]{2,1,0:T(8,128)(2,1)}, u32[]{:S(2)}) copy-start(bf16[4,64,448]{2,1,0:T(8,128)(2,1)} %copy-done.5) | copy-start | bytes 688132
  161.8 40.4 %collective-permute-start.10 = (bf16[4,256,448]{1,2,0:T(8,128)(2,1)S(1)}, bf16[4,256,448]{1,2,0:T(8,128)(2,1)S(1)}, u32[]{:S(2)}, u32[]{:S(2)}) collective-permute-start(bf16[4,256,448]{1,2,0:T(8,128)(2,1)S(1)} %bitcast_dynamic-update-slice_fusion), channel_id=1, source_target_pairs={{0,1},{1,0},{2,3},{3,2},{4,5},{5,4},{6,7},{7,6},{8,9},{9,8},{10,11... | collective-permute-start | bytes 2752520 | tf_op jit(solution)/shard_map/ppermute | solution.py:24
  164.6 36.0 %collective-permute-start.9 = (bf16[448,256]{0,1:T(8,128)(2,1)S(1)}, bf16[448,256]{0,1:T(8,128)(2,1)S(1)}, u32[]{:S(2)}, u32[]{:S(2)}) collective-permute-start(bf16[448,256]{0,1:T(8,128)(2,1)S(1)} %bitcast.86), channel_id=1, source_target_pairs={{0,0},{1,8},{2,16},{3,24},{4,32},{5,40},{6,48},{7,56},{8,1},{9,9},... | collective-permute-start | bytes 688136 | tf_op jit(solution)/shard_map/ppermute | solution.py:29
Sparse Core Ops, SparseCore 0:
  10.1 50.8 all-gather.4
  82.1 48.7 all-gather.6

commit v7 on v5

--- a/solution.py
+++ b/solution.py
@@ -83,28 +83,25 @@
     activated = activated.astype(BF)
 
     grad_own = lax.all_gather(hidden_grad, "yh", axis=0, tiled=True)
-    grad_own, activated = lax.optimization_barrier((grad_own, activated))
+    grad_own, activated = lax.optimization_barrier((grad_own, swap_z_g(activated)))
     grad_other = swap_cores(grad_own)
-    activated = swap_z_g(activated)
 
     ig_own = dot(grad_own, w_all, ((1,), (0,))).astype(BF)
     ig_own, grad_other = lax.optimization_barrier((ig_own, grad_other))
     ig_other = dot(grad_other, w_all, ((1,), (0,))).astype(BF)
     ig = jnp.stack([ig_own, ig_other]).reshape(16, rows, feats)
-    ig, grad_own = lax.optimization_barrier((ig, grad_own))
     ig = exchange_rows(ig)
     input_grad = jnp.sum(ig.astype(jnp.float32), axis=0).astype(BF)
 
-    far_own = grad_own.reshape(4 * pair, NX, cols).transpose(1, 0, 2)
-    far_own = in_order(shift_blocks(far_own, here), here)
-    far_own, activated = lax.optimization_barrier((far_own, activated))
+    both = jnp.concatenate([grad_own, activated], axis=0)
+    both = both.reshape(5 * pair, NX, cols).transpose(1, 0, 2)
+    both = shift_blocks(both, here)
+    far_own = in_order([part[: 4 * pair] for part in both], here)
     far_other = swap_cores(far_own)
     far = lax.all_gather(near, "x", axis=0, tiled=False)
     far_grad = jnp.stack([far_own, far_other], axis=1)
     weight_grad = dot(far.reshape(-1, feats), far_grad.reshape(-1, cols), ((0,), (0,))).astype(BF)
-
-    activated = activated.reshape(pair, NX, cols).transpose(1, 0, 2)
-    out = in_order(shift_blocks(activated, here), here).reshape(NX * pair, cols)
+    out = in_order([part[4 * pair :] for part in both], here).reshape(NX * pair, cols)
     return out, input_grad, weight_grad
 
 

time: 200 us -> 209 us (1.045)
  the two profiles are of different devices: /device:TPU:54 before, /device:TPU:1 now
where the time goes in v7:
time: 209 us; the launch traced here: 205 us
  starting transfers between devices  60.9 us (29%)
  waiting for transfers between devices  60.4 us (29%)
  blocking collectives  35.4 us (17%)
  matrix products  16.3 us (8%)
  local copies, waits for them, and re-layouts  15.2 us (7%)
  between operations  14.4 us (7%)
  other arithmetic  2.37 us (1%)
    ppermute x2, waiting for transfers between devices, swap_z_g(): return lax.ppermute(value, ('z', 'yh', 'c'), pairs)  35.7 us
    all_gather x1, blocking collectives, body(): grad_own = lax.all_gather(hidden_grad, 'yh', axis=0, tiled=True)  35.4 us
    all_to_all x2, starting transfers between devices, exchange_rows(): lax.all_to_all(value, ('z', 'yl', 'c'), split_axis=0, concat_axis=0, axis...  21.8 us
    ppermute x6, starting transfers between devices, along_x(): return lax.ppermute(value, 'x', [(i, (i + shift) % NX) for i in range(NX)])  21 us
    dot_general x5, matrix products, dot(): lax.dot_general(a, b, (contract, ((), ())), preferred_element_type=jnp.fl...  16.3 us
    all_to_all x2, waiting for transfers between devices, exchange_rows(): lax.all_to_all(value, ('z', 'yl', 'c'), split_axis=0, concat_axis=0, axis...  10 us
    all_to_all x1, waiting for transfers between devices, body(): parts = lax.all_to_all(partial_value, 'yh', split_axis=0, concat_axis=0)  8.97 us
    ppermute x3, starting transfers between devices, swap_cores(): return lax.ppermute(value, 'c', [(0, 1), (1, 0)])  6.61 us
  transfers between devices with their start and end apart: 16, of which 6 were waited for; matrix products, arithmetic and copies ran while one was open for 11% of the time, Pallas kernels for 0%

profile of v7, /device:TPU:1, one launch (start us, length us, event | category | flops | bytes accessed | tf_op | source)
XLA Modules:
  0.0 205.1 jit_solution(11357303036697852256)
XLA Ops:
  7.9 1.8 broadcast_in_dim.41
  9.7 13.1 %all-to-all-start = ((bf16[16,32,896]{2,1,0:T(8,128)(2,1)}), bf16[16,32,896]{2,1,0:T(8,128)(2,1)S(1)}, u32[]{:S(2)}, u32[]{:S(2)}) async-start(bf16[16,32,896]{2,1,0:T(8,128)(2,1)} %broadcast_in_dim.41), calls=%async_computation | async-start | bytes 1835008 | tf_op jit(solution)/shard_map/all_to_all | solution.py:48
  23.0 3.3 %collective-permute-start = (bf16[256,448]{1,0:T(8,128)(2,1)S(1)}, bf16[256,448]{1,0:T(8,128)(2,1)S(1)}, u32[]{:S(2)}, u32[]{:S(2)}) collective-permute-start(bf16[256,448]{1,0:T(8,128)(2,1)S(1)} %copy.29), channel_id=1, source_target_pairs={{0,0},{1,8},{2,16},{3,24},{4,32},{5,40},{6,48},{7,56},{8,1},{9,9},... | collective-permute-start | bytes 688136 | tf_op jit(solution)/shard_map/ppermute | solution.py:29
  26.3 35.7 %collective-permute-done = bf16[256,448]{1,0:T(8,128)(2,1)S(1)} collective-permute-done((bf16[256,448]{1,0:T(8,128)(2,1)S(1)}, bf16[256,448]{1,0:T(8,128)(2,1)S(1)}, u32[]{:S(2)}, u32[]{:S(2)}) %collective-permute-start) | collective-permute-done | bytes 229408 | tf_op jit(solution)/shard_map/ppermute | solution.py:29
  62.1 3.4 %convolution_convert_fusion = bf16[256,1792]{1,0:T(8,128)(2,1)S(1)} fusion(bf16[1792,896]{1,0:T(8,128)(2,1)} %all-gather.5.cloned.1.call-done, bf16[2,256,896]{2,1,0:T(8,128)(2,1)S(1)} %bitcast.75), kind=kOutput, calls=%fused_computation.2 | convolution fusion | flops 822542336 | bytes 4587520 | tf_op jit(solution)/shard_map/dot_general | solution.py:54
  65.5 2.7 %collective-permute-start.1 = (bf16[256,1792]{1,0:T(8,128)(2,1)S(1)}, bf16[256,1792]{1,0:T(8,128)(2,1)S(1)}, u32[]{:S(2)}, u32[]{:S(2)}) collective-permute-start(bf16[256,1792]{1,0:T(8,128)(2,1)S(1)} %convolution_convert_fusion), channel_id=1, source_target_pairs={{0,1},{1,0},{2,3},{3,2},{4,5},{5,4},{6,7},{7,6},{8,9},{9,8},{10,11... | collective-permute-start | bytes 2752520 | tf_op jit(solution)/shard_map/ppermute | solution.py:24
  68.3 2.1 %collective-permute-done.1 = bf16[256,1792]{1,0:T(8,128)(2,1)S(1)} collective-permute-done((bf16[256,1792]{1,0:T(8,128)(2,1)S(1)}, bf16[256,1792]{1,0:T(8,128)(2,1)S(1)}, u32[]{:S(2)}, u32[]{:S(2)}) %collective-permute-start.1) | collective-permute-done | bytes 917536 | tf_op jit(solution)/shard_map/ppermute | solution.py:24
  70.4 2.2 %fusion = bf16[256,1792]{1,0:T(8,128)(2,1)} fusion(bf16[1792,896]{1,0:T(8,128)(2,1)S(1)} %copy-done.2, bf16[256,1792]{1,0:T(8,128)(2,1)S(1)} %collective-permute-done.1, bf16[2,256,896]{2,1,0:T(8,128)(2,1)S(1)} %bitcast.76), kind=kOutput, calls=%fused_computation.1 | convolution fusion | flops 823459840 | bytes 5505024 | tf_op jit(solution)/shard_map/dot_general | solution.py:54
  72.6 6.3 %all-to-all-start.1 = ((bf16[4,64,1792]{2,1,0:T(8,128)(2,1)}), bf16[4,64,1792]{2,1,0:T(8,128)(2,1)S(1)}, u32[]{:S(2)}, u32[]{:S(2)}) async-start(bf16[4,64,1792]{2,1,0:T(8,128)(2,1)} %bitcast.6), calls=%async_computation.1 | async-start | bytes 1835008 | tf_op jit(solution)/shard_map/all_to_all | solution.py:75
  79.6 3.1 %collective-permute-start.2 = (bf16[64,448]{1,0:T(8,128)(2,1)S(1)}, bf16[64,448]{1,0:T(8,128)(2,1)S(1)}, u32[]{:S(2)}, u32[]{:S(2)}) collective-permute-start(bf16[64,448]{1,0:T(8,128)(2,1)S(1)} %get-tuple-element.38), channel_id=1, source_target_pairs={{0,128},{128,256},{256,384},{384,0},{1,129},{129,257},{257,385},{3... | collective-permute-start | bytes 172040 | tf_op jit(solution)/shard_map/ppermute | solution.py:20
  82.8 4.4 %collective-permute-start.3 = (bf16[64,448]{1,0:T(8,128)(2,1)S(1)}, bf16[64,448]{1,0:T(8,128)(2,1)S(1)}, u32[]{:S(2)}, u32[]{:S(2)}) collective-permute-start(bf16[64,448]{1,0:T(8,128)(2,1)S(1)} %get-tuple-element.37), channel_id=1, source_target_pairs={{0,256},{128,384},{256,0},{384,128},{1,257},{129,385},{257,1},{385... | collective-permute-start | bytes 172040 | tf_op jit(solution)/shard_map/ppermute | solution.py:20
  87.1 3.1 %collective-permute-start.4 = (bf16[64,448]{1,0:T(8,128)(2,1)S(1)}, bf16[64,448]{1,0:T(8,128)(2,1)S(1)}, u32[]{:S(2)}, u32[]{:S(2)}) collective-permute-start(bf16[64,448]{1,0:T(8,128)(2,1)S(1)} %get-tuple-element.36), channel_id=1, source_target_pairs={{0,384},{128,0},{256,128},{384,256},{1,385},{129,1},{257,129},{385... | collective-permute-start | bytes 172040 | tf_op jit(solution)/shard_map/ppermute | solution.py:20
  90.2 2.2 %collective-permute-done.4 = bf16[64,448]{1,0:T(8,128)(2,1)S(1)} collective-permute-done((bf16[64,448]{1,0:T(8,128)(2,1)S(1)}, bf16[64,448]{1,0:T(8,128)(2,1)S(1)}, u32[]{:S(2)}, u32[]{:S(2)}) %collective-permute-start.4) | collective-permute-done | bytes 57376 | tf_op jit(solution)/shard_map/ppermute | solution.py:20
  93.3 9.0 %all-to-all-done.1 = bf16[4,64,1792]{2,1,0:T(8,128)(2,1)S(1)} async-done(((bf16[4,64,1792]{2,1,0:T(8,128)(2,1)}), bf16[4,64,1792]{2,1,0:T(8,128)(2,1)S(1)}, u32[]{:S(2)}, u32[]{:S(2)}) %all-to-all-start.1) | async-done | bytes 917536 | tf_op jit(solution)/shard_map/all_to_all | solution.py:75
  102.8 1.9 collective-permute-start.5
  104.7 35.4 %all_gather.17 = bf16[256,1792]{1,0:T(8,128)(2,1)S(1)} all-gather(bf16[64,1792]{1,0:T(8,128)(2,1)S(1)} %get-tuple-element.35), channel_id=1, replica_groups=mesh['x'=4,'yl'=2,'z'=8,'yh'=4,'c'=2] {'yh'}, dimensions={0}, use_global_device_ids=true | all-gather | bytes 1146880 | tf_op jit(solution)/shard_map/all_gather | solution.py:85
  140.1 1.9 collective-permute-start.9
  143.9 4.2 %collective-permute-start.6 = (bf16[320,448]{0,1:T(8,128)(2,1)}, bf16[320,448]{0,1:T(8,128)(2,1)}, u32[]{:S(2)}, u32[]{:S(2)}) collective-permute-start(bf16[320,448]{0,1:T(8,128)(2,1)} %get-tuple-element.32), channel_id=1, source_target_pairs={{0,128},{128,256},{256,384},{384,0},{1,129},{129,257},{257,385},{3... | collective-permute-start | bytes 860168 | tf_op jit(solution)/shard_map/ppermute | solution.py:20
  148.2 3.2 %collective-permute-start.7 = (bf16[320,448]{0,1:T(8,128)(2,1)S(1)}, bf16[320,448]{0,1:T(8,128)(2,1)}, u32[]{:S(2)}, u32[]{:S(2)}) collective-permute-start(bf16[320,448]{0,1:T(8,128)(2,1)S(1)} %get-tuple-element.31), channel_id=1, source_target_pairs={{0,256},{128,384},{256,0},{384,128},{1,257},{129,385},{257,1},{385... | collective-permute-start | bytes 860168 | tf_op jit(solution)/shard_map/ppermute | solution.py:20
  151.3 3.0 %collective-permute-start.8 = (bf16[320,448]{0,1:T(8,128)(2,1)S(1)}, bf16[320,448]{0,1:T(8,128)(2,1)}, u32[]{:S(2)}, u32[]{:S(2)}) collective-permute-start(bf16[320,448]{0,1:T(8,128)(2,1)S(1)} %get-tuple-element.30), channel_id=1, source_target_pairs={{0,384},{128,0},{256,128},{384,256},{1,385},{129,1},{257,129},{385... | collective-permute-start | bytes 860168 | tf_op jit(solution)/shard_map/ppermute | solution.py:20
  154.4 1.0 broadcast_in_dim.48
  156.2 3.2 %convolution_convert_fusion.2 = bf16[256,896]{1,0:T(8,128)(2,1)S(1)} fusion(bf16[256,1792]{1,0:T(8,128)(2,1)S(1)} %all_gather.17, bf16[1792,896]{1,0:T(8,128)(2,1)} %all-gather.5.cloned.1.call-done), kind=kOutput, calls=%fused_computation.10 | convolution fusion | flops 822312960 | bytes 4587520 | tf_op jit(solution)/shard_map/dot_general | solution.py:54
  159.3 2.3 %fusion.7 = bf16[1,256,896]{2,1,0:T(8,128)(2,1)S(1)} fusion(bf16[256,1792]{1,0:T(8,128)(2,1)} %collective-permute-done.9, bf16[1792,896]{1,0:T(8,128)(2,1)S(1)} %copy-done.3), kind=kOutput, calls=%fused_computation.11 | convolution fusion | flops 822312960 | bytes 4587520 | tf_op jit(solution)/shard_map/dot_general | solution.py:54
  161.7 1.0 pad_maximum_fusion.1
  162.7 8.7 %all-to-all-start.2 = ((bf16[16,32,896]{2,1,0:T(8,128)(2,1)}), bf16[16,32,896]{2,1,0:T(8,128)(2,1)S(1)}, u32[]{:S(2)}, u32[]{:S(2)}) async-start(bf16[16,32,896]{2,1,0:T(8,128)(2,1)} %bitcast.25), calls=%async_computation.2 | async-start | bytes 1835008 | tf_op jit(solution)/shard_map/all_to_all | solution.py:48
  171.4 1.6 fusion.21
  173.1 1.6 fusion.20
  174.7 1.7 fusion.19
  176.4 2.0 collective-permute-start.10
  178.3 0.9 slice_bitcast_fusion.5
  182.2 10.0 %all-to-all-done.2 = bf16[16,32,896]{2,1,0:T(8,128)(2,1)S(1)} async-done(((bf16[16,32,896]{2,1,0:T(8,128)(2,1)}), bf16[16,32,896]{2,1,0:T(8,128)(2,1)S(1)}, u32[]{:S(2)}, u32[]{:S(2)}) %all-to-all-start.2) | async-done | bytes 917536 | tf_op jit(solution)/shard_map/all_to_all | solution.py:48
  193.0 5.3 %bitcast_convert_fusion = bf16[896,448]{0,1:T(8,128)(2,1)} fusion(bf16[4,2,256,896]{3,2,1,0:T(8,128)(2,1)} %bitcast.82, bf16[4,1,256,448]{2,3,1,0:T(8,128)(2,1)S(1)} %bitcast.83, bf16[4,1,256,448]{2,3,1,0:T(8,128)(2,1)} %bitcast.31), kind=kOutput, calls=%fused_computation.8 | convolution fusion | flops 1645486080 | bytes 6307840 | tf_op jit(solution)/shard_map/dot_general | solution.py:54
  (52 shorter events, 9.4 us)
Async XLA Ops:
  7.2 15.6 %copy-start.1 = (bf16[256,448]{0,1:T(8,128)(2,1)S(1)}, bf16[256,448]{0,1:T(8,128)(2,1)}, u32[]{:S(2)}) copy-start(bf16[256,448]{0,1:T(8,128)(2,1)} %param.5) | copy-start | bytes 688132
  7.2 54.9 %all-gather.5.cloned.1.call-start = ((), (), s32[]{:S(2)}) async-start(), calls=%async_computation.3 | async-start | bytes 4014080 | tf_op jit(solution)/shard_map/all_gather | solution.py:63
  9.7 52.4 %all-to-all-start = ((bf16[16,32,896]{2,1,0:T(8,128)(2,1)}), bf16[16,32,896]{2,1,0:T(8,128)(2,1)S(1)}, u32[]{:S(2)}, u32[]{:S(2)}) async-start(bf16[16,32,896]{2,1,0:T(8,128)(2,1)} %broadcast_in_dim.41), calls=%async_computation | async-start | bytes 1835008 | tf_op jit(solution)/shard_map/all_to_all | solution.py:48
  23.0 39.1 %collective-permute-start = (bf16[256,448]{1,0:T(8,128)(2,1)S(1)}, bf16[256,448]{1,0:T(8,128)(2,1)S(1)}, u32[]{:S(2)}, u32[]{:S(2)}) collective-permute-start(bf16[256,448]{1,0:T(8,128)(2,1)S(1)} %copy.29), channel_id=1, source_target_pairs={{0,0},{1,8},{2,16},{3,24},{4,32},{5,40},{6,48},{7,56},{8,1},{9,9},... | collective-permute-start | bytes 688136 | tf_op jit(solution)/shard_map/ppermute | solution.py:29
  62.1 8.3 %copy-start = (bf16[16,32,896]{2,1,0:T(8,128)(2,1)}, bf16[16,32,896]{2,1,0:T(8,128)(2,1)S(1)}, u32[]{:S(2)}) copy-start(bf16[16,32,896]{2,1,0:T(8,128)(2,1)S(1)} %all-to-all-done) | copy-start | bytes 2752516
  62.1 8.3 %copy-start.2 = (bf16[1792,896]{1,0:T(8,128)(2,1)S(1)}, bf16[1792,896]{1,0:T(8,128)(2,1)}, u32[]{:S(2)}) copy-start(bf16[1792,896]{1,0:T(8,128)(2,1)} %all-gather.5.cloned.1.call-done) | copy-start | bytes 9633796
  65.5 4.8 %collective-permute-start.1 = (bf16[256,1792]{1,0:T(8,128)(2,1)S(1)}, bf16[256,1792]{1,0:T(8,128)(2,1)S(1)}, u32[]{:S(2)}, u32[]{:S(2)}) collective-permute-start(bf16[256,1792]{1,0:T(8,128)(2,1)S(1)} %convolution_convert_fusion), channel_id=1, source_target_pairs={{0,1},{1,0},{2,3},{3,2},{4,5},{5,4},{6,7},{7,6},{8,9},{9,8},{10,11... | collective-permute-start | bytes 2752520 | tf_op jit(solution)/shard_map/ppermute | solution.py:24
  72.6 29.7 %all-to-all-start.1 = ((bf16[4,64,1792]{2,1,0:T(8,128)(2,1)}), bf16[4,64,1792]{2,1,0:T(8,128)(2,1)S(1)}, u32[]{:S(2)}, u32[]{:S(2)}) async-start(bf16[4,64,1792]{2,1,0:T(8,128)(2,1)} %bitcast.6), calls=%async_computation.1 | async-start | bytes 1835008 | tf_op jit(solution)/shard_map/all_to_all | solution.py:75
  78.8 114.1 %all-gather.7.cloned.1.call-start = ((), (), s32[]{:S(2)}) async-start(), calls=%async_computation.4 | async-start | bytes 4587520 | tf_op jit(solution)/shard_map/all_gather | solution.py:101
  79.6 10.6 %collective-permute-start.2 = (bf16[64,448]{1,0:T(8,128)(2,1)S(1)}, bf16[64,448]{1,0:T(8,128)(2,1)S(1)}, u32[]{:S(2)}, u32[]{:S(2)}) collective-permute-start(bf16[64,448]{1,0:T(8,128)(2,1)S(1)} %get-tuple-element.38), channel_id=1, source_target_pairs={{0,128},{128,256},{256,384},{384,0},{1,129},{129,257},{257,385},{3... | collective-permute-start | bytes 172040 | tf_op jit(solution)/shard_map/ppermute | solution.py:20
  82.8 7.5 %collective-permute-start.3 = (bf16[64,448]{1,0:T(8,128)(2,1)S(1)}, bf16[64,448]{1,0:T(8,128)(2,1)S(1)}, u32[]{:S(2)}, u32[]{:S(2)}) collective-permute-start(bf16[64,448]{1,0:T(8,128)(2,1)S(1)} %get-tuple-element.37), channel_id=1, source_target_pairs={{0,256},{128,384},{256,0},{384,128},{1,257},{129,385},{257,1},{385... | collective-permute-start | bytes 172040 | tf_op jit(solution)/shard_map/ppermute | solution.py:20
  87.1 5.3 %collective-permute-start.4 = (bf16[64,448]{1,0:T(8,128)(2,1)S(1)}, bf16[64,448]{1,0:T(8,128)(2,1)S(1)}, u32[]{:S(2)}, u32[]{:S(2)}) collective-permute-start(bf16[64,448]{1,0:T(8,128)(2,1)S(1)} %get-tuple-element.36), channel_id=1, source_target_pairs={{0,384},{128,0},{256,128},{384,256},{1,385},{129,1},{257,129},{385... | collective-permute-start | bytes 172040 | tf_op jit(solution)/shard_map/ppermute | solution.py:20
  102.8 37.3 %collective-permute-start.5 = (bf16[64,1792]{1,0:T(8,128)(2,1)S(1)}, bf16[64,1792]{1,0:T(8,128)(2,1)S(1)}, u32[]{:S(2)}, u32[]{:S(2)}) collective-permute-start(bf16[64,1792]{1,0:T(8,128)(2,1)S(1)} %get-tuple-element.34), channel_id=1, source_target_pairs={{0,0},{1,8},{2,16},{3,24},{4,32},{5,40},{6,48},{7,56},{8,1},{9,9},... | collective-permute-start | bytes 688136 | tf_op jit(solution)/shard_map/ppermute | solution.py:29
  140.1 19.2 %collective-permute-start.9 = (bf16[256,1792]{1,0:T(8,128)(2,1)S(1)}, bf16[256,1792]{1,0:T(8,128)(2,1)}, u32[]{:S(2)}, u32[]{:S(2)}) collective-permute-start(bf16[256,1792]{1,0:T(8,128)(2,1)S(1)} %all_gather.17), channel_id=1, source_target_pairs={{0,1},{1,0},{2,3},{3,2},{4,5},{5,4},{6,7},{7,6},{8,9},{9,8},{10,11... | collective-permute-start | bytes 2752520 | tf_op jit(solution)/shard_map/ppermute | solution.py:24
  143.9 27.5 %collective-permute-start.6 = (bf16[320,448]{0,1:T(8,128)(2,1)}, bf16[320,448]{0,1:T(8,128)(2,1)}, u32[]{:S(2)}, u32[]{:S(2)}) collective-permute-start(bf16[320,448]{0,1:T(8,128)(2,1)} %get-tuple-element.32), channel_id=1, source_target_pairs={{0,128},{128,256},{256,384},{384,0},{1,129},{129,257},{257,385},{3... | collective-permute-start | bytes 860168 | tf_op jit(solution)/shard_map/ppermute | solution.py:20
  148.2 24.9 %collective-permute-start.7 = (bf16[320,448]{0,1:T(8,128)(2,1)S(1)}, bf16[320,448]{0,1:T(8,128)(2,1)}, u32[]{:S(2)}, u32[]{:S(2)}) collective-permute-start(bf16[320,448]{0,1:T(8,128)(2,1)S(1)} %get-tuple-element.31), channel_id=1, source_target_pairs={{0,256},{128,384},{256,0},{384,128},{1,257},{129,385},{257,1},{385... | collective-permute-start | bytes 860168 | tf_op jit(solution)/shard_map/ppermute | solution.py:20
  151.3 23.4 %collective-permute-start.8 = (bf16[320,448]{0,1:T(8,128)(2,1)S(1)}, bf16[320,448]{0,1:T(8,128)(2,1)}, u32[]{:S(2)}, u32[]{:S(2)}) collective-permute-start(bf16[320,448]{0,1:T(8,128)(2,1)S(1)} %get-tuple-element.30), channel_id=1, source_target_pairs={{0,384},{128,0},{256,128},{384,256},{1,385},{129,1},{257,129},{385... | collective-permute-start | bytes 860168 | tf_op jit(solution)/shard_map/ppermute | solution.py:20
  156.2 3.2 %copy-start.3 = (bf16[1792,896]{1,0:T(8,128)(2,1)S(1)}, bf16[1792,896]{1,0:T(8,128)(2,1)}, u32[]{:S(2)}) copy-start(bf16[1792,896]{1,0:T(8,128)(2,1)} %all-gather.5.cloned.1.call-done) | copy-start | bytes 9633796
  162.7 29.5 %all-to-all-start.2 = ((bf16[16,32,896]{2,1,0:T(8,128)(2,1)}), bf16[16,32,896]{2,1,0:T(8,128)(2,1)S(1)}, u32[]{:S(2)}, u32[]{:S(2)}) async-start(bf16[16,32,896]{2,1,0:T(8,128)(2,1)} %bitcast.25), calls=%async_computation.2 | async-start | bytes 1835008 | tf_op jit(solution)/shard_map/all_to_all | solution.py:48
  176.4 16.6 %collective-permute-start.10 = (bf16[4,256,448]{1,2,0:T(8,128)(2,1)}, bf16[4,256,448]{1,2,0:T(8,128)(2,1)S(1)}, u32[]{:S(2)}, u32[]{:S(2)}) collective-permute-start(bf16[4,256,448]{1,2,0:T(8,128)(2,1)} %fusion.19), channel_id=1, source_target_pairs={{0,1},{1,0},{2,3},{3,2},{4,5},{5,4},{6,7},{7,6},{8,9},{9,8},{10,11... | collective-permute-start | bytes 2752520 | tf_op jit(solution)/shard_map/ppermute | solution.py:24
Sparse Core Ops, SparseCore 0:
  10.1 50.8 all-gather.4
  81.7 48.6 all-gather.6

commit v8 on v7

v8 whole, which is shorter than its diff:
```python
import jax
import jax.numpy as jnp
from jax import lax
from jax.sharding import Mesh
from jax.sharding import PartitionSpec as P

AXES = ("x", "yl", "z", "yh", "c")
NX = 4
BF = jnp.bfloat16


def gelu_tanh(values):
    return jax.nn.gelu(values, approximate=True)


def along_x(value, shift):
    return lax.ppermute(value, "x", [(i, (i + shift) % NX) for i in range(NX)])


def swap_cores(value):
    return lax.ppermute(value, "c", [(0, 1), (1, 0)])


def turn(core, high):
    return 4 * core + high


def along_z(value, sign):
    pairs = []
    for z in range(8):
        for g in range(8):
            pairs.append((z * 8 + g, (z + sign * turn(g % 2, g // 2)) % 8 * 8 + g))
    return lax.ppermute(value, ("z", "yh", "c"), pairs)


def within_z(value, home):
    pairs = []
    for z in range(8):
        for g in range(8):
            pair = (z * 8 + g, z * 8 + (z - turn(g % 2, g // 2)) % 8)
            pairs.append(pair if home else pair[::-1])
    return lax.ppermute(value, ("z", "yh", "c"), pairs)


def shift_blocks(blocks, here):
    parts = []
    for r in range(NX):
        block = lax.dynamic_index_in_dim(blocks, (here + r) & (NX - 1), 0, keepdims=False)
        parts.append(along_x(block, r) if r else block)
    return parts


def in_order(parts, here, out=None):
    out = jnp.zeros((NX,) + parts[0].shape, BF) if out is None else out
    for r in range(NX):
        out = lax.dynamic_update_index_in_dim(out, parts[r], (here + (NX - r)) & (NX - 1), 0)
    return out


def cut(blocks, start, count):
    n, m = blocks.shape[1:]
    twice = jnp.concatenate([blocks, blocks], axis=0).reshape(16 * n, m)
    return lax.dynamic_slice_in_dim(twice, (start & 7) * n, count * n, 0)


def dot(a, b, contract):
    return lax.dot_general(a, b, (contract, ((), ())), preferred_element_type=jnp.float32)


def body(tokens, w_up, act_grad):
    rows, feats = tokens.shape
    cols = w_up.shape[1]
    pair = 2 * rows
    here = lax.axis_index("x").astype(jnp.uint32)
    first = lax.axis_index("z").astype(jnp.uint32) + 4 * lax.axis_index("c").astype(jnp.uint32)

    w_own = w_up.T
    w_all = jnp.zeros((NX, cols, feats), BF)
    for r in range(NX):
        block = along_x(w_own, -r) if r else w_own
        w_all = lax.dynamic_update_index_in_dim(w_all, block, (here + r) & (NX - 1), 0)

    near = lax.all_gather(tokens, "yl", axis=0, tiled=True)
    near = lax.all_gather(near, "z", axis=0, tiled=False)
    near, cot = lax.optimization_barrier((near, within_z(act_grad, False)))
    near = jnp.stack([cut(near, first, 4), cut(near, first + 4, 4)])
    w_all = w_all.reshape(NX * cols, feats)

    sent = swap_cores(dot(near[1], w_all, ((1,), (1,))).astype(BF))
    partial_value = (dot(near[0], w_all, ((1,), (1,))) + sent.astype(jnp.float32)).astype(BF)
    partial_value = partial_value.reshape(4, pair, NX * cols)
    partial_value, cot = lax.optimization_barrier((partial_value, cot))
    parts = lax.all_to_all(partial_value, "yh", split_axis=0, concat_axis=0)
    hidden = jnp.sum(parts.astype(jnp.float32), axis=0)

    cot = along_z(cot, -1)
    cot = in_order(shift_blocks(cot.reshape(NX, pair, cols), here), here)
    cot = cot.transpose(1, 0, 2).reshape(pair, NX * cols)

    activated, pullback = jax.vjp(gelu_tanh, hidden)
    hidden_grad = pullback(cot.astype(jnp.float32))[0].astype(BF)
    activated = activated.astype(BF)

    grad_own = lax.all_gather(hidden_grad, "yh", axis=0, tiled=True)
    grad_own, activated = lax.optimization_barrier((grad_own, along_z(activated, 1)))
    grad_other = swap_cores(grad_own)
    activated = within_z(activated, True)

    ig_own = dot(grad_own, w_all, ((1,), (0,))).astype(BF)
    ig_own, grad_other = lax.optimization_barrier((ig_own, grad_other))
    ig_other = dot(grad_other, w_all, ((1,), (0,))).astype(BF)
    ig = cut(jnp.stack([ig_own, ig_other]).reshape(8, pair, feats), 16 - first, 8)
    far_own = jnp.zeros((NX, 4 * pair, cols), BF)
    ig, activated, far_own = lax.optimization_barrier((ig.reshape(16, rows, feats), activated, far_own))
    ig = lax.all_to_all(ig, ("z", "yl"), split_axis=0, concat_axis=0)
    input_grad = jnp.sum(ig.astype(jnp.float32), axis=0).astype(BF)

    blocks = grad_own.reshape(4 * pair, NX, cols).transpose(1, 0, 2)
    far_own = in_order(shift_blocks(blocks, here), here, far_own)
    far_other = swap_cores(far_own)
    far = lax.all_gather(near, "x", axis=0, tiled=False)
    far_grad = jnp.stack([far_own, far_other], axis=1)
    weight_grad = dot(far.reshape(-1, feats), far_grad.reshape(-1, cols), ((0,), (0,))).astype(BF)

    out = activated.reshape(pair, NX, cols).transpose(1, 0, 2)
    out = in_order(shift_blocks(out, here), here).reshape(NX * pair, cols)
    return out, input_grad, weight_grad


def solution(mesh):
    fine = Mesh(mesh.devices.reshape(NX, 2, 8, 4, 2), AXES)
    in_specs = (P(("z", "x", "yl"), ("yh", "c")), P(("yh", "c"), ("x", "yl", "z")), P("z", ("x", "yl", "yh", "c")))
    out_specs = (in_specs[2], in_specs[0], in_specs[1])
    return jax.shard_map(body, mesh=fine, in_specs=in_specs, out_specs=out_specs, check_vma=False)
```

time: 209 us -> 210 us (level); the launches traced: 205 us -> 208 us
  waiting for transfers between devices: 60.4 us -> 13.5 us
  blocking collectives: 35.4 us -> 59.9 us
  starting transfers between devices: 60.9 us -> 81.8 us
  matrix products: 16.3 us -> 19.4 us
    all_gather x0 -> x2, blocking collectives: none -> 40 us  [the longest x1 34.2 us: body(): near = lax.all_gather(near, 'z', axis=0, tiled=False)]
    ppermute x2 -> x4, waiting for transfers between devices: 35.7 us -> 6.05 us  [the longest x2 6.05 us: along_z(): return lax.ppermute(value, ('z', 'yh', 'c'), pairs)]
    all_to_all x2 -> x1, starting transfers between devices: 21.8 us -> 3.63 us  [body(): ig = lax.all_to_all(ig, ('z', 'yl'), split_axis=0, concat_axis=0)]
    ppermute x6 -> x12, starting transfers between devices: 21 us -> 38.5 us  [along_x(): return lax.ppermute(value, 'x', [(i, (i + shift) % NX) for i in range(NX)])]
    ppermute x2 -> x4, starting transfers between devices: 5.23 us -> 21.8 us  [the longest x2 11.2 us: within_z(): return lax.ppermute(value, ('z', 'yh', 'c'), pairs)]
    all_gather x1, blocking collectives: 35.4 us -> 19.9 us  [body(): grad_own = lax.all_gather(hidden_grad, 'yh', axis=0, tiled=True)]
    all_to_all x2 -> x1, waiting for transfers between devices: 10 us -> 0.01 us  [body(): ig = lax.all_to_all(ig, ('z', 'yl'), split_axis=0, concat_axis=0)]
    all_to_all x1, waiting for transfers between devices: 8.97 us -> 0.68 us  [body(): parts = lax.all_to_all(partial_value, 'yh', split_axis=0, concat_axis=0)]
  transfers between devices with their start and end apart: 16 -> 22, of which waited for: 6 -> 7; matrix products, arithmetic and copies ran while one was open for 11% -> 13% of each run, Pallas kernels for 0% -> 0%
where the time goes in v8:
time: 210 us; the launch traced here: 208 us
  starting transfers between devices  81.8 us (39%)
  blocking collectives  59.9 us (29%)
  matrix products  19.4 us (9%)
  local copies, waits for them, and re-layouts  16.5 us (8%)
  between operations  14.5 us (7%)
  waiting for transfers between devices  13.5 us (6%)
  other arithmetic  2.77 us (1%)
    ppermute x12, starting transfers between devices, along_x(): return lax.ppermute(value, 'x', [(i, (i + shift) % NX) for i in range(NX)])  38.5 us
    all_gather x1, blocking collectives, body(): near = lax.all_gather(near, 'z', axis=0, tiled=False)  34.2 us
    all_gather x1, blocking collectives, body(): grad_own = lax.all_gather(hidden_grad, 'yh', axis=0, tiled=True)  19.9 us
    dot_general x5, matrix products, dot(): lax.dot_general(a, b, (contract, ((), ())), preferred_element_type=jnp.fl...  19.4 us
    ppermute x3, starting transfers between devices, swap_cores(): return lax.ppermute(value, 'c', [(0, 1), (1, 0)])  14.3 us
    ppermute x2, starting transfers between devices, within_z(): return lax.ppermute(value, ('z', 'yh', 'c'), pairs)  11.2 us
    ppermute x2, starting transfers between devices, along_z(): return lax.ppermute(value, ('z', 'yh', 'c'), pairs)  10.6 us
    dynamic_update_slice x4, local copies, waits for them, and re-layouts, body(): w_all = lax.dynamic_update_index_in_dim(w_all, block, here + r & NX - 1, 0)  7.29 us
  transfers between devices with their start and end apart: 22, of which 7 were waited for; matrix products, arithmetic and copies ran while one was open for 13% of the time, Pallas kernels for 0%

profile of v8, /device:TPU:1, one launch (start us, length us, event | category | flops | bytes accessed | tf_op | source)
XLA Modules:
  0.0 208.4 jit_solution(18443564017785493430)
XLA Ops:
  7.2 5.3 %collective-permute-start.1 = (bf16[448,896]{1,0:T(8,128)(2,1)}, bf16[448,896]{1,0:T(8,128)(2,1)}, u32[]{:S(2)}, u32[]{:S(2)}) collective-permute-start(bf16[448,896]{1,0:T(8,128)(2,1)} %bitcast.101), channel_id=1, source_target_pairs={{0,384},{128,0},{256,128},{384,256},{1,385},{129,1},{257,129},{385... | collective-permute-start | bytes 2408456 | tf_op jit(solution)/shard_map/ppermute | solution.py:17
  12.5 2.4 %collective-permute-start.2 = (bf16[448,896]{1,0:T(8,128)(2,1)}, bf16[448,896]{1,0:T(8,128)(2,1)}, u32[]{:S(2)}, u32[]{:S(2)}) collective-permute-start(bf16[448,896]{1,0:T(8,128)(2,1)} %bitcast.102), channel_id=1, source_target_pairs={{0,256},{128,384},{256,0},{384,128},{1,257},{129,385},{257,1},{385... | collective-permute-start | bytes 2408456 | tf_op jit(solution)/shard_map/ppermute | solution.py:17
  15.0 2.5 %collective-permute-start.3 = (bf16[448,896]{1,0:T(8,128)(2,1)}, bf16[448,896]{1,0:T(8,128)(2,1)}, u32[]{:S(2)}, u32[]{:S(2)}) collective-permute-start(bf16[448,896]{1,0:T(8,128)(2,1)} %bitcast.103), channel_id=1, source_target_pairs={{0,128},{128,256},{256,384},{384,0},{1,129},{129,257},{257,385},{3... | collective-permute-start | bytes 2408456 | tf_op jit(solution)/shard_map/ppermute | solution.py:17
  18.6 5.9 %collective-permute-start = (bf16[256,448]{1,0:T(8,128)(2,1)S(1)}, bf16[256,448]{1,0:T(8,128)(2,1)S(1)}, u32[]{:S(2)}, u32[]{:S(2)}) collective-permute-start(bf16[256,448]{1,0:T(8,128)(2,1)S(1)} %copy.25), channel_id=1, source_target_pairs={{0,0},{4,1},{7,2},{3,3},{6,4},{2,5},{5,6},{1,7},{9,8},{13,9},{8,10... | collective-permute-start | bytes 688136 | tf_op jit(solution)/shard_map/ppermute | solution.py:42
  24.5 5.8 %all_gather.18 = bf16[64,896]{1,0:T(8,128)(2,1)S(1)} all-gather(bf16[32,896]{1,0:T(8,128)(2,1)} %param.3), channel_id=1, replica_groups=mesh['x'=4,'yl'=2,'z'=8,'yh'=4,'c'=2] {'yl'}, dimensions={0}, use_global_device_ids=true | all-gather | bytes 172032 | tf_op jit(solution)/shard_map/all_gather | solution.py:83
  30.3 34.2 %all-gather = bf16[512,896]{1,0:T(8,128)(2,1)S(1)} all-gather(bf16[64,896]{1,0:T(8,128)(2,1)S(1)} %all_gather.18), channel_id=2, replica_groups=mesh['x'=4,'yl'=2,'z'=8,'yh'=4,'c'=2] {'z'}, dimensions={0}, use_global_device_ids=true | all-gather | bytes 1032192 | tf_op jit(solution)/shard_map/all_gather | solution.py:84
  67.6 2.1 %bitcast_dynamic-update-slice_fusion.3 = bf16[4,448,896]{2,1,0:T(8,128)(2,1)} fusion(bf16[4,448,896]{2,1,0:T(8,128)(2,1)} %bitcast_dynamic-update-slice_fusion, u32[]{:T(128)S(6)} %and.21, bf16[448,896]{1,0:T(8,128)(2,1)} %collective-permute-done.1), kind=kLoop, calls=%fused_computation.19 | loop fusion | bytes 1605636 | tf_op jit(solution)/shard_map/jit(dynamic_update_index_in_dim)/dynamic_update_slice | solution.py:81
  71.8 2.1 %bitcast_dynamic-update-slice_fusion.1 = bf16[4,448,896]{2,1,0:T(8,128)(2,1)} fusion(bf16[4,448,896]{2,1,0:T(8,128)(2,1)} %bitcast_dynamic-update-slice_fusion.2, u32[]{:T(128)S(6)} %and.23, bf16[448,896]{1,0:T(8,128)(2,1)} %collective-permute-done.3), kind=kLoop, calls=%fused_computation.17 | loop fusion | bytes 1605636 | tf_op jit(solution)/shard_map/jit(dynamic_update_index_in_dim)/dynamic_update_slice | solution.py:81
  73.9 4.0 %convolution_convert_fusion = bf16[256,1792]{1,0:T(8,128)(2,1)} fusion(bf16[1792,896]{1,0:T(8,128)(2,1)} %bitcast.7, bf16[1024,896]{1,0:T(8,128)(2,1)S(1)} %bitcast.90, u32[]{:T(128)S(6)} %mul.58), kind=kOutput, calls=%fused_computation.2 | convolution fusion | flops 822542336 | bytes 4587524 | tf_op jit(solution)/shard_map/dot_general | solution.py:67
  77.9 6.5 %collective-permute-start.4 = (bf16[256,1792]{1,0:T(8,128)(2,1)}, bf16[256,1792]{1,0:T(8,128)(2,1)S(1)}, u32[]{:S(2)}, u32[]{:S(2)}) collective-permute-start(bf16[256,1792]{1,0:T(8,128)(2,1)} %convolution_convert_fusion), channel_id=1, source_target_pairs={{0,1},{1,0},{2,3},{3,2},{4,5},{5,4},{6,7},{7,6},{8,9},{9,8},{10,11... | collective-permute-start | bytes 2752520 | tf_op jit(solution)/shard_map/ppermute | solution.py:21
  84.4 2.3 %collective-permute-done.4 = bf16[256,1792]{1,0:T(8,128)(2,1)S(1)} collective-permute-done((bf16[256,1792]{1,0:T(8,128)(2,1)}, bf16[256,1792]{1,0:T(8,128)(2,1)S(1)}, u32[]{:S(2)}, u32[]{:S(2)}) %collective-permute-start.4) | collective-permute-done | bytes 917536 | tf_op jit(solution)/shard_map/ppermute | solution.py:21
  86.7 4.0 %fusion = bf16[256,1792]{1,0:T(8,128)(2,1)} fusion(bf16[1792,896]{1,0:T(8,128)(2,1)} %bitcast.7, bf16[256,1792]{1,0:T(8,128)(2,1)S(1)} %collective-permute-done.4, bf16[1024,896]{1,0:T(8,128)(2,1)S(1)} %bitcast.91, u32[]{:T(128)S(6)} %mul.57), kind=kOutput, calls=%fused_computation.1 | convolution fusion | flops 823459840 | bytes 5505028 | tf_op jit(solution)/shard_map/dot_general | solution.py:67
  90.8 4.1 %collective-permute-start.5 = (bf16[256,448]{1,0:T(8,128)(2,1)S(1)}, bf16[256,448]{1,0:T(8,128)(2,1)S(1)}, u32[]{:S(2)}, u32[]{:S(2)}) collective-permute-start(bf16[256,448]{1,0:T(8,128)(2,1)S(1)} %collective-permute-done), channel_id=1, source_target_pairs={{0,0},{1,33},{2,58},{3,27},{4,52},{5,21},{6,46},{7,15},{8,8},{9,41... | collective-permute-start | bytes 688136 | tf_op jit(solution)/shard_map/ppermute | solution.py:33
  94.9 3.5 %all-to-all-start = ((bf16[4,64,1792]{2,1,0:T(8,128)(2,1)}), bf16[4,64,1792]{2,1,0:T(8,128)(2,1)S(1)}, u32[]{:S(2)}, u32[]{:S(2)}) async-start(bf16[4,64,1792]{2,1,0:T(8,128)(2,1)} %bitcast.99), calls=%async_computation | async-start | bytes 1835008 | tf_op jit(solution)/shard_map/all_to_all | solution.py:93
  98.6 6.0 %collective-permute-done.5 = bf16[256,448]{1,0:T(8,128)(2,1)S(1)} collective-permute-done((bf16[256,448]{1,0:T(8,128)(2,1)S(1)}, bf16[256,448]{1,0:T(8,128)(2,1)S(1)}, u32[]{:S(2)}, u32[]{:S(2)}) %collective-permute-start.5) | collective-permute-done | bytes 229408 | tf_op jit(solution)/shard_map/ppermute | solution.py:33
  104.7 3.6 %collective-permute-start.6 = (bf16[64,448]{1,0:T(8,128)(2,1)S(1)}, bf16[64,448]{1,0:T(8,128)(2,1)S(1)}, u32[]{:S(2)}, u32[]{:S(2)}) collective-permute-start(bf16[64,448]{1,0:T(8,128)(2,1)S(1)} %get-tuple-element.47), channel_id=1, source_target_pairs={{0,128},{128,256},{256,384},{384,0},{1,129},{129,257},{257,385},{3... | collective-permute-start | bytes 172040 | tf_op jit(solution)/shard_map/ppermute | solution.py:17
  109.3 3.6 %collective-permute-start.7 = (bf16[64,448]{1,0:T(8,128)(2,1)S(1)}, bf16[64,448]{1,0:T(8,128)(2,1)S(1)}, u32[]{:S(2)}, u32[]{:S(2)}) collective-permute-start(bf16[64,448]{1,0:T(8,128)(2,1)S(1)} %get-tuple-element.46), channel_id=1, source_target_pairs={{0,256},{128,384},{256,0},{384,128},{1,257},{129,385},{257,1},{385... | collective-permute-start | bytes 172040 | tf_op jit(solution)/shard_map/ppermute | solution.py:17
  113.0 2.7 %collective-permute-start.8 = (bf16[64,448]{1,0:T(8,128)(2,1)S(1)}, bf16[64,448]{1,0:T(8,128)(2,1)S(1)}, u32[]{:S(2)}, u32[]{:S(2)}) collective-permute-start(bf16[64,448]{1,0:T(8,128)(2,1)S(1)} %get-tuple-element.45), channel_id=1, source_target_pairs={{0,384},{128,0},{256,128},{384,256},{1,385},{129,1},{257,129},{385... | collective-permute-start | bytes 172040 | tf_op jit(solution)/shard_map/ppermute | solution.py:17
  120.3 6.5 %collective-permute-start.9 = (bf16[64,1792]{1,0:T(8,128)(2,1)S(1)}, bf16[64,1792]{1,0:T(8,128)(2,1)}, u32[]{:S(2)}, u32[]{:S(2)}) collective-permute-start(bf16[64,1792]{1,0:T(8,128)(2,1)S(1)} %get-tuple-element.39), channel_id=1, source_target_pairs={{0,0},{1,33},{2,10},{3,43},{4,20},{5,53},{6,30},{7,63},{8,8},{9,41... | collective-permute-start | bytes 688136 | tf_op jit(solution)/shard_map/ppermute | solution.py:33
  126.8 19.9 %all_gather.21 = bf16[256,1792]{1,0:T(8,128)(2,1)S(1)} all-gather(bf16[64,1792]{1,0:T(8,128)(2,1)S(1)} %get-tuple-element.40), channel_id=1, replica_groups=mesh['x'=4,'yl'=2,'z'=8,'yh'=4,'c'=2] {'yh'}, dimensions={0}, use_global_device_ids=true | all-gather | bytes 1146880 | tf_op jit(solution)/shard_map/all_gather | solution.py:104
  146.8 2.6 %collective-permute-start.10 = (bf16[256,1792]{1,0:T(8,128)(2,1)S(1)}, bf16[256,1792]{1,0:T(8,128)(2,1)}, u32[]{:S(2)}, u32[]{:S(2)}) collective-permute-start(bf16[256,1792]{1,0:T(8,128)(2,1)S(1)} %all_gather.21), channel_id=1, source_target_pairs={{0,1},{1,0},{2,3},{3,2},{4,5},{5,4},{6,7},{7,6},{8,9},{9,8},{10,11... | collective-permute-start | bytes 2752520 | tf_op jit(solution)/shard_map/ppermute | solution.py:21
  149.9 5.3 %collective-permute-start.11 = (bf16[64,1792]{1,0:T(8,128)(2,1)}, bf16[64,1792]{1,0:T(8,128)(2,1)S(1)}, u32[]{:S(2)}, u32[]{:S(2)}) collective-permute-start(bf16[64,1792]{1,0:T(8,128)(2,1)} %collective-permute-done.9), channel_id=1, source_target_pairs={{0,0},{1,4},{2,7},{3,3},{4,6},{5,2},{6,5},{7,1},{8,9},{9,13},{10,8... | collective-permute-start | bytes 688136 | tf_op jit(solution)/shard_map/ppermute | solution.py:42
  158.0 4.7 %collective-permute-start.16 = (bf16[256,448]{0,1:T(8,128)(2,1)}, bf16[256,448]{0,1:T(8,128)(2,1)S(1)}, u32[]{:S(2)}, u32[]{:S(2)}) collective-permute-start(bf16[256,448]{0,1:T(8,128)(2,1)} %get-tuple-element.37), channel_id=1, source_target_pairs={{0,256},{128,384},{256,0},{384,128},{1,257},{129,385},{257,1},{385... | collective-permute-start | bytes 688136 | tf_op jit(solution)/shard_map/ppermute | solution.py:17
  162.7 2.3 %collective-permute-start.17 = (bf16[256,448]{0,1:T(8,128)(2,1)}, bf16[256,448]{0,1:T(8,128)(2,1)S(1)}, u32[]{:S(2)}, u32[]{:S(2)}) collective-permute-start(bf16[256,448]{0,1:T(8,128)(2,1)} %get-tuple-element.36), channel_id=1, source_target_pairs={{0,384},{128,0},{256,128},{384,256},{1,385},{129,1},{257,129},{385... | collective-permute-start | bytes 688136 | tf_op jit(solution)/shard_map/ppermute | solution.py:17
  165.0 3.0 %convolution_convert_fusion.2 = bf16[256,896]{1,0:T(8,128)(2,1)S(1)} fusion(bf16[256,1792]{1,0:T(8,128)(2,1)S(1)} %all_gather.21, bf16[1792,896]{1,0:T(8,128)(2,1)} %bitcast.7), kind=kOutput, calls=%fused_computation.12 | convolution fusion | flops 822312960 | bytes 4587520 | tf_op jit(solution)/shard_map/dot_general | solution.py:67
  168.0 3.3 %fusion.7 = bf16[1,256,896]{2,1,0:T(8,128)(2,1)S(1)} fusion(bf16[256,1792]{1,0:T(8,128)(2,1)} %collective-permute-done.10, bf16[1792,896]{1,0:T(8,128)(2,1)} %bitcast.7), kind=kOutput, calls=%fused_computation.13 | convolution fusion | flops 822312960 | bytes 4587520 | tf_op jit(solution)/shard_map/dot_general | solution.py:67
  172.6 3.6 %all-to-all-start.1 = ((bf16[16,32,896]{2,1,0:T(8,128)(2,1)}), bf16[16,32,896]{2,1,0:T(8,128)(2,1)S(1)}, u32[]{:S(2)}, u32[]{:S(2)}) async-start(bf16[16,32,896]{2,1,0:T(8,128)(2,1)} %bitcast.21), calls=%async_computation.1 | async-start | bytes 1835008 | tf_op jit(solution)/shard_map/all_to_all | solution.py:115
  177.4 5.2 %collective-permute-start.18 = (bf16[4,256,448]{1,2,0:T(8,128)(2,1)S(1)}, bf16[4,256,448]{1,2,0:T(8,128)(2,1)S(1)}, u32[]{:S(2)}, u32[]{:S(2)}) collective-permute-start(bf16[4,256,448]{1,2,0:T(8,128)(2,1)S(1)} %bitcast_dynamic-update-slice_fusion.4), channel_id=1, source_target_pairs={{0,1},{1,0},{2,3},{3,2},{4,5},{5,4},{6,7},{7,6},{8,9},{9,8},{10,11... | collective-permute-start | bytes 2752520 | tf_op jit(solution)/shard_map/ppermute | solution.py:21
  183.5 3.2 %collective-permute-start.12 = (bf16[64,448]{1,0:T(8,128)(2,1)S(1)}, bf16[64,448]{1,0:T(8,128)(2,1)S(1)}, u32[]{:S(2)}, u32[]{:S(2)}) collective-permute-start(bf16[64,448]{1,0:T(8,128)(2,1)S(1)} %bitcast.108), channel_id=1, source_target_pairs={{0,128},{128,256},{256,384},{384,0},{1,129},{129,257},{257,385},{3... | collective-permute-start | bytes 172040 | tf_op jit(solution)/shard_map/ppermute | solution.py:17
  186.7 3.0 %collective-permute-start.13 = (bf16[64,448]{1,0:T(8,128)(2,1)S(1)}, bf16[64,448]{1,0:T(8,128)(2,1)S(1)}, u32[]{:S(2)}, u32[]{:S(2)}) collective-permute-start(bf16[64,448]{1,0:T(8,128)(2,1)S(1)} %bitcast.107), channel_id=1, source_target_pairs={{0,256},{128,384},{256,0},{384,128},{1,257},{129,385},{257,1},{385... | collective-permute-start | bytes 172040 | tf_op jit(solution)/shard_map/ppermute | solution.py:17
  189.7 3.3 %collective-permute-start.14 = (bf16[64,448]{1,0:T(8,128)(2,1)S(1)}, bf16[64,448]{1,0:T(8,128)(2,1)S(1)}, u32[]{:S(2)}, u32[]{:S(2)}) collective-permute-start(bf16[64,448]{1,0:T(8,128)(2,1)S(1)} %bitcast.106), channel_id=1, source_target_pairs={{0,384},{128,0},{256,128},{384,256},{1,385},{129,1},{257,129},{385... | collective-permute-start | bytes 172040 | tf_op jit(solution)/shard_map/ppermute | solution.py:17
  195.8 5.0 %bitcast_convert_fusion = bf16[896,448]{0,1:T(8,128)(2,1)} fusion(bf16[4,2,256,896]{3,2,1,0:T(8,128)(2,1)} %bitcast.109, bf16[4,1,256,448]{2,3,1,0:T(8,128)(2,1)S(1)} %bitcast.110, bf16[4,1,256,448]{2,3,1,0:T(8,128)(2,1)S(1)} %bitcast.100), kind=kOutput, calls=%fused_computation.10 | convolution fusion | flops 1645486080 | bytes 6307840 | tf_op jit(solution)/shard_map/dot_general | solution.py:67
  (64 shorter events, 22.2 us)
Async XLA Ops:
  7.2 59.3 %copy-start = (bf16[896,448]{0,1:T(8,128)(2,1)S(1)}, bf16[896,448]{0,1:T(8,128)(2,1)}, u32[]{:S(2)}) copy-start(bf16[896,448]{0,1:T(8,128)(2,1)} %param.4) | copy-start | bytes 2408452
  7.2 60.4 %collective-permute-start.1 = (bf16[448,896]{1,0:T(8,128)(2,1)}, bf16[448,896]{1,0:T(8,128)(2,1)}, u32[]{:S(2)}, u32[]{:S(2)}) collective-permute-start(bf16[448,896]{1,0:T(8,128)(2,1)} %bitcast.101), channel_id=1, source_target_pairs={{0,384},{128,0},{256,128},{384,256},{1,385},{129,1},{257,129},{385... | collective-permute-start | bytes 2408456 | tf_op jit(solution)/shard_map/ppermute | solution.py:17
  12.5 57.2 %collective-permute-start.2 = (bf16[448,896]{1,0:T(8,128)(2,1)}, bf16[448,896]{1,0:T(8,128)(2,1)}, u32[]{:S(2)}, u32[]{:S(2)}) collective-permute-start(bf16[448,896]{1,0:T(8,128)(2,1)} %bitcast.102), channel_id=1, source_target_pairs={{0,256},{128,384},{256,0},{384,128},{1,257},{129,385},{257,1},{385... | collective-permute-start | bytes 2408456 | tf_op jit(solution)/shard_map/ppermute | solution.py:17
  15.0 56.8 %collective-permute-start.3 = (bf16[448,896]{1,0:T(8,128)(2,1)}, bf16[448,896]{1,0:T(8,128)(2,1)}, u32[]{:S(2)}, u32[]{:S(2)}) collective-permute-start(bf16[448,896]{1,0:T(8,128)(2,1)} %bitcast.103), channel_id=1, source_target_pairs={{0,128},{128,256},{256,384},{384,0},{1,129},{129,257},{257,385},{3... | collective-permute-start | bytes 2408456 | tf_op jit(solution)/shard_map/ppermute | solution.py:17
  18.6 48.8 %collective-permute-start = (bf16[256,448]{1,0:T(8,128)(2,1)S(1)}, bf16[256,448]{1,0:T(8,128)(2,1)S(1)}, u32[]{:S(2)}, u32[]{:S(2)}) collective-permute-start(bf16[256,448]{1,0:T(8,128)(2,1)S(1)} %copy.25), channel_id=1, source_target_pairs={{0,0},{4,1},{7,2},{3,3},{6,4},{2,5},{5,6},{1,7},{9,8},{13,9},{8,10... | collective-permute-start | bytes 688136 | tf_op jit(solution)/shard_map/ppermute | solution.py:42
  77.9 8.8 %collective-permute-start.4 = (bf16[256,1792]{1,0:T(8,128)(2,1)}, bf16[256,1792]{1,0:T(8,128)(2,1)S(1)}, u32[]{:S(2)}, u32[]{:S(2)}) collective-permute-start(bf16[256,1792]{1,0:T(8,128)(2,1)} %convolution_convert_fusion), channel_id=1, source_target_pairs={{0,1},{1,0},{2,3},{3,2},{4,5},{5,4},{6,7},{7,6},{8,9},{9,8},{10,11... | collective-permute-start | bytes 2752520 | tf_op jit(solution)/shard_map/ppermute | solution.py:21
  90.8 13.9 %collective-permute-start.5 = (bf16[256,448]{1,0:T(8,128)(2,1)S(1)}, bf16[256,448]{1,0:T(8,128)(2,1)S(1)}, u32[]{:S(2)}, u32[]{:S(2)}) collective-permute-start(bf16[256,448]{1,0:T(8,128)(2,1)S(1)} %collective-permute-done), channel_id=1, source_target_pairs={{0,0},{1,33},{2,58},{3,27},{4,52},{5,21},{6,46},{7,15},{8,8},{9,41... | collective-permute-start | bytes 688136 | tf_op jit(solution)/shard_map/ppermute | solution.py:33
  94.9 24.9 %all-to-all-start = ((bf16[4,64,1792]{2,1,0:T(8,128)(2,1)}), bf16[4,64,1792]{2,1,0:T(8,128)(2,1)S(1)}, u32[]{:S(2)}, u32[]{:S(2)}) async-start(bf16[4,64,1792]{2,1,0:T(8,128)(2,1)} %bitcast.99), calls=%async_computation | async-start | bytes 1835008 | tf_op jit(solution)/shard_map/all_to_all | solution.py:93
  98.4 97.4 %all-gather.4.cloned.1.call-start = ((), (), s32[]{:S(2)}) async-start(), calls=%async_computation.2 | async-start | bytes 4587520 | tf_op jit(solution)/shard_map/all_gather | solution.py:121
  104.7 11.0 %collective-permute-start.6 = (bf16[64,448]{1,0:T(8,128)(2,1)S(1)}, bf16[64,448]{1,0:T(8,128)(2,1)S(1)}, u32[]{:S(2)}, u32[]{:S(2)}) collective-permute-start(bf16[64,448]{1,0:T(8,128)(2,1)S(1)} %get-tuple-element.47), channel_id=1, source_target_pairs={{0,128},{128,256},{256,384},{384,0},{1,129},{129,257},{257,385},{3... | collective-permute-start | bytes 172040 | tf_op jit(solution)/shard_map/ppermute | solution.py:17
  109.3 6.8 %collective-permute-start.7 = (bf16[64,448]{1,0:T(8,128)(2,1)S(1)}, bf16[64,448]{1,0:T(8,128)(2,1)S(1)}, u32[]{:S(2)}, u32[]{:S(2)}) collective-permute-start(bf16[64,448]{1,0:T(8,128)(2,1)S(1)} %get-tuple-element.46), channel_id=1, source_target_pairs={{0,256},{128,384},{256,0},{384,128},{1,257},{129,385},{257,1},{385... | collective-permute-start | bytes 172040 | tf_op jit(solution)/shard_map/ppermute | solution.py:17
  113.0 5.3 %collective-permute-start.8 = (bf16[64,448]{1,0:T(8,128)(2,1)S(1)}, bf16[64,448]{1,0:T(8,128)(2,1)S(1)}, u32[]{:S(2)}, u32[]{:S(2)}) collective-permute-start(bf16[64,448]{1,0:T(8,128)(2,1)S(1)} %get-tuple-element.45), channel_id=1, source_target_pairs={{0,384},{128,0},{256,128},{384,256},{1,385},{129,1},{257,129},{385... | collective-permute-start | bytes 172040 | tf_op jit(solution)/shard_map/ppermute | solution.py:17
  120.3 26.5 %collective-permute-start.9 = (bf16[64,1792]{1,0:T(8,128)(2,1)S(1)}, bf16[64,1792]{1,0:T(8,128)(2,1)}, u32[]{:S(2)}, u32[]{:S(2)}) collective-permute-start(bf16[64,1792]{1,0:T(8,128)(2,1)S(1)} %get-tuple-element.39), channel_id=1, source_target_pairs={{0,0},{1,33},{2,10},{3,43},{4,20},{5,53},{6,30},{7,63},{8,8},{9,41... | collective-permute-start | bytes 688136 | tf_op jit(solution)/shard_map/ppermute | solution.py:33
  146.8 21.3 %collective-permute-start.10 = (bf16[256,1792]{1,0:T(8,128)(2,1)S(1)}, bf16[256,1792]{1,0:T(8,128)(2,1)}, u32[]{:S(2)}, u32[]{:S(2)}) collective-permute-start(bf16[256,1792]{1,0:T(8,128)(2,1)S(1)} %all_gather.21), channel_id=1, source_target_pairs={{0,1},{1,0},{2,3},{3,2},{4,5},{5,4},{6,7},{7,6},{8,9},{9,8},{10,11... | collective-permute-start | bytes 2752520 | tf_op jit(solution)/shard_map/ppermute | solution.py:21
  149.9 22.8 %collective-permute-start.11 = (bf16[64,1792]{1,0:T(8,128)(2,1)}, bf16[64,1792]{1,0:T(8,128)(2,1)S(1)}, u32[]{:S(2)}, u32[]{:S(2)}) collective-permute-start(bf16[64,1792]{1,0:T(8,128)(2,1)} %collective-permute-done.9), channel_id=1, source_target_pairs={{0,0},{1,4},{2,7},{3,3},{4,6},{5,2},{6,5},{7,1},{8,9},{9,13},{10,8... | collective-permute-start | bytes 688136 | tf_op jit(solution)/shard_map/ppermute | solution.py:42
  156.1 20.3 %collective-permute-start.15 = (bf16[256,448]{0,1:T(8,128)(2,1)}, bf16[256,448]{0,1:T(8,128)(2,1)}, u32[]{:S(2)}, u32[]{:S(2)}) collective-permute-start(bf16[256,448]{0,1:T(8,128)(2,1)} %get-tuple-element.38), channel_id=1, source_target_pairs={{0,128},{128,256},{256,384},{384,0},{1,129},{129,257},{257,385},{3... | collective-permute-start | bytes 688136 | tf_op jit(solution)/shard_map/ppermute | solution.py:17
  158.0 19.4 %collective-permute-start.16 = (bf16[256,448]{0,1:T(8,128)(2,1)}, bf16[256,448]{0,1:T(8,128)(2,1)S(1)}, u32[]{:S(2)}, u32[]{:S(2)}) collective-permute-start(bf16[256,448]{0,1:T(8,128)(2,1)} %get-tuple-element.37), channel_id=1, source_target_pairs={{0,256},{128,384},{256,0},{384,128},{1,257},{129,385},{257,1},{385... | collective-permute-start | bytes 688136 | tf_op jit(solution)/shard_map/ppermute | solution.py:17
  162.7 14.7 %collective-permute-start.17 = (bf16[256,448]{0,1:T(8,128)(2,1)}, bf16[256,448]{0,1:T(8,128)(2,1)S(1)}, u32[]{:S(2)}, u32[]{:S(2)}) collective-permute-start(bf16[256,448]{0,1:T(8,128)(2,1)} %get-tuple-element.36), channel_id=1, source_target_pairs={{0,384},{128,0},{256,128},{384,256},{1,385},{129,1},{257,129},{385... | collective-permute-start | bytes 688136 | tf_op jit(solution)/shard_map/ppermute | solution.py:17
  172.6 28.2 %all-to-all-start.1 = ((bf16[16,32,896]{2,1,0:T(8,128)(2,1)}), bf16[16,32,896]{2,1,0:T(8,128)(2,1)S(1)}, u32[]{:S(2)}, u32[]{:S(2)}) async-start(bf16[16,32,896]{2,1,0:T(8,128)(2,1)} %bitcast.21), calls=%async_computation.1 | async-start | bytes 1835008 | tf_op jit(solution)/shard_map/all_to_all | solution.py:115
  177.4 18.4 %collective-permute-start.18 = (bf16[4,256,448]{1,2,0:T(8,128)(2,1)S(1)}, bf16[4,256,448]{1,2,0:T(8,128)(2,1)S(1)}, u32[]{:S(2)}, u32[]{:S(2)}) collective-permute-start(bf16[4,256,448]{1,2,0:T(8,128)(2,1)S(1)} %bitcast_dynamic-update-slice_fusion.4), channel_id=1, source_target_pairs={{0,1},{1,0},{2,3},{3,2},{4,5},{5,4},{6,7},{7,6},{8,9},{9,8},{10,11... | collective-permute-start | bytes 2752520 | tf_op jit(solution)/shard_map/ppermute | solution.py:21
  183.5 9.5 %collective-permute-start.12 = (bf16[64,448]{1,0:T(8,128)(2,1)S(1)}, bf16[64,448]{1,0:T(8,128)(2,1)S(1)}, u32[]{:S(2)}, u32[]{:S(2)}) collective-permute-start(bf16[64,448]{1,0:T(8,128)(2,1)S(1)} %bitcast.108), channel_id=1, source_target_pairs={{0,128},{128,256},{256,384},{384,0},{1,129},{129,257},{257,385},{3... | collective-permute-start | bytes 172040 | tf_op jit(solution)/shard_map/ppermute | solution.py:17
  186.7 6.5 %collective-permute-start.13 = (bf16[64,448]{1,0:T(8,128)(2,1)S(1)}, bf16[64,448]{1,0:T(8,128)(2,1)S(1)}, u32[]{:S(2)}, u32[]{:S(2)}) collective-permute-start(bf16[64,448]{1,0:T(8,128)(2,1)S(1)} %bitcast.107), channel_id=1, source_target_pairs={{0,256},{128,384},{256,0},{384,128},{1,257},{129,385},{257,1},{385... | collective-permute-start | bytes 172040 | tf_op jit(solution)/shard_map/ppermute | solution.py:17
  189.7 5.3 %collective-permute-start.14 = (bf16[64,448]{1,0:T(8,128)(2,1)S(1)}, bf16[64,448]{1,0:T(8,128)(2,1)S(1)}, u32[]{:S(2)}, u32[]{:S(2)}) collective-permute-start(bf16[64,448]{1,0:T(8,128)(2,1)S(1)} %bitcast.106), channel_id=1, source_target_pairs={{0,384},{128,0},{256,128},{384,256},{1,385},{129,1},{257,129},{385... | collective-permute-start | bytes 172040 | tf_op jit(solution)/shard_map/ppermute | solution.py:17
Sparse Core Ops, SparseCore 0:
  109.5 45.2 all-gather.3

commit v9 on v8

--- a/solution.py
+++ b/solution.py
@@ -74,15 +74,12 @@
     here = lax.axis_index("x").astype(jnp.uint32)
     first = lax.axis_index("z").astype(jnp.uint32) + 4 * lax.axis_index("c").astype(jnp.uint32)
 
-    w_own = w_up.T
-    w_all = jnp.zeros((NX, cols, feats), BF)
-    for r in range(NX):
-        block = along_x(w_own, -r) if r else w_own
-        w_all = lax.dynamic_update_index_in_dim(w_all, block, (here + r) & (NX - 1), 0)
+    w_all = lax.all_gather(w_up.T, "x", axis=0, tiled=False)
 
-    near = lax.all_gather(tokens, "yl", axis=0, tiled=True)
-    near = lax.all_gather(near, "z", axis=0, tiled=False)
-    near, cot = lax.optimization_barrier((near, within_z(act_grad, False)))
+    near = jnp.broadcast_to(tokens[None], (16, rows, feats))
+    near = lax.all_to_all(near, ("z", "yl"), split_axis=0, concat_axis=0).reshape(8, pair, feats)
+    cot = along_z(within_z(act_grad, False), -1)
+    near, cot, w_all = lax.optimization_barrier((near, cot, w_all))
     near = jnp.stack([cut(near, first, 4), cut(near, first + 4, 4)])
     w_all = w_all.reshape(NX * cols, feats)
 
@@ -93,7 +90,6 @@
     parts = lax.all_to_all(partial_value, "yh", split_axis=0, concat_axis=0)
     hidden = jnp.sum(parts.astype(jnp.float32), axis=0)
 
-    cot = along_z(cot, -1)
     cot = in_order(shift_blocks(cot.reshape(NX, pair, cols), here), here)
     cot = cot.transpose(1, 0, 2).reshape(pair, NX * cols)
 
@@ -104,26 +100,26 @@
     grad_own = lax.all_gather(hidden_grad, "yh", axis=0, tiled=True)
     grad_own, activated = lax.optimization_barrier((grad_own, along_z(activated, 1)))
     grad_other = swap_cores(grad_own)
-    activated = within_z(activated, True)
 
     ig_own = dot(grad_own, w_all, ((1,), (0,))).astype(BF)
     ig_own, grad_other = lax.optimization_barrier((ig_own, grad_other))
     ig_other = dot(grad_other, w_all, ((1,), (0,))).astype(BF)
     ig = cut(jnp.stack([ig_own, ig_other]).reshape(8, pair, feats), 16 - first, 8)
-    far_own = jnp.zeros((NX, 4 * pair, cols), BF)
-    ig, activated, far_own = lax.optimization_barrier((ig.reshape(16, rows, feats), activated, far_own))
+    ig, grad_own, activated = lax.optimization_barrier((ig.reshape(16, rows, feats), grad_own, activated))
     ig = lax.all_to_all(ig, ("z", "yl"), split_axis=0, concat_axis=0)
-    input_grad = jnp.sum(ig.astype(jnp.float32), axis=0).astype(BF)
 
-    blocks = grad_own.reshape(4 * pair, NX, cols).transpose(1, 0, 2)
-    far_own = in_order(shift_blocks(blocks, here), here, far_own)
+    far = lax.all_gather(near, "x", axis=0, tiled=False)
+    far, grad_own, activated = lax.optimization_barrier((far, grad_own, activated))
+    both = jnp.concatenate([grad_own, activated], axis=0)
+    both = shift_blocks(both.reshape(5 * pair, NX, cols).transpose(1, 0, 2), here)
+    far_own = in_order([part[: 4 * pair] for part in both], here)
     far_other = swap_cores(far_own)
-    far = lax.all_gather(near, "x", axis=0, tiled=False)
     far_grad = jnp.stack([far_own, far_other], axis=1)
     weight_grad = dot(far.reshape(-1, feats), far_grad.reshape(-1, cols), ((0,), (0,))).astype(BF)
-
-    out = activated.reshape(pair, NX, cols).transpose(1, 0, 2)
-    out = in_order(shift_blocks(out, here), here).reshape(NX * pair, cols)
+    out = in_order([part[4 * pair :] for part in both], here).reshape(NX * pair, cols)
+    out = within_z(out, True)
+    ig, weight_grad = lax.optimization_barrier((ig, weight_grad))
+    input_grad = jnp.sum(ig.astype(jnp.float32), axis=0).astype(BF)
     return out, input_grad, weight_grad
 
 

time: 210 us -> 199 us (0.948)
  the two profiles are of different devices: /device:TPU:1 before, /device:TPU:81 now
where the time goes in v9:
time: 199 us; the launch traced here: 198 us
  waiting for transfers between devices  69.3 us (35%)
  starting transfers between devices  68.5 us (34%)
  blocking collectives  17.9 us (9%)
  matrix products  14.7 us (7%)
  between operations  14.5 us (7%)
  local copies, waits for them, and re-layouts  10.8 us (5%)
  other arithmetic  2.84 us (1%)
    ppermute x2, waiting for transfers between devices, within_z(): return lax.ppermute(value, ('z', 'yh', 'c'), pairs)  28.6 us
    ppermute x6, starting transfers between devices, along_x(): return lax.ppermute(value, 'x', [(i, (i + shift) % NX) for i in range(NX)])  18.6 us
    all_gather x1, blocking collectives, body(): grad_own = lax.all_gather(hidden_grad, 'yh', axis=0, tiled=True)  17.9 us
    ppermute x6, waiting for transfers between devices, along_x(): return lax.ppermute(value, 'x', [(i, (i + shift) % NX) for i in range(NX)])  15.5 us
    dot_general x5, matrix products, dot(): lax.dot_general(a, b, (contract, ((), ())), preferred_element_type=jnp.fl...  14.7 us
    ppermute x2, starting transfers between devices, along_z(): return lax.ppermute(value, ('z', 'yh', 'c'), pairs)  11.4 us
    all_to_all x1, starting transfers between devices, body(): lax.all_to_all(near, ('z', 'yl'), split_axis=0, concat_axis=0)  10.4 us
    all_to_all x1, waiting for transfers between devices, body(): parts = lax.all_to_all(partial_value, 'yh', split_axis=0, concat_axis=0)  9.77 us
  transfers between devices with their start and end apart: 18, of which 11 were waited for; matrix products, arithmetic and copies ran while one was open for 13% of the time, Pallas kernels for 0%

profile of v9, /device:TPU:81, one launch (start us, length us, event | category | flops | bytes accessed | tf_op | source)
XLA Modules:
  0.0 198.5 jit_solution(816623318243128417)
XLA Ops:
  7.9 1.8 broadcast_in_dim.41
  9.7 10.4 %all-to-all-start = ((bf16[16,32,896]{2,1,0:T(8,128)(2,1)}), bf16[16,32,896]{2,1,0:T(8,128)(2,1)S(1)}, u32[]{:S(2)}, u32[]{:S(2)}) async-start(bf16[16,32,896]{2,1,0:T(8,128)(2,1)} %broadcast_in_dim.41), calls=%async_computation | async-start | bytes 1835008 | tf_op jit(solution)/shard_map/all_to_all | solution.py:80
  20.4 4.5 %collective-permute-start = (bf16[256,448]{1,0:T(8,128)(2,1)S(1)}, bf16[256,448]{1,0:T(8,128)(2,1)S(1)}, u32[]{:S(2)}, u32[]{:S(2)}) collective-permute-start(bf16[256,448]{1,0:T(8,128)(2,1)S(1)} %copy.29), channel_id=1, source_target_pairs={{0,0},{4,1},{7,2},{3,3},{6,4},{2,5},{5,6},{1,7},{9,8},{13,9},{8,10... | collective-permute-start | bytes 688136 | tf_op jit(solution)/shard_map/ppermute | solution.py:42
  24.9 16.5 %collective-permute-done = bf16[256,448]{1,0:T(8,128)(2,1)S(1)} collective-permute-done((bf16[256,448]{1,0:T(8,128)(2,1)S(1)}, bf16[256,448]{1,0:T(8,128)(2,1)S(1)}, u32[]{:S(2)}, u32[]{:S(2)}) %collective-permute-start) | collective-permute-done | bytes 229408 | tf_op jit(solution)/shard_map/ppermute | solution.py:42
  41.4 5.3 %collective-permute-start.1 = (bf16[256,448]{1,0:T(8,128)(2,1)S(1)}, bf16[256,448]{1,0:T(8,128)(2,1)S(1)}, u32[]{:S(2)}, u32[]{:S(2)}) collective-permute-start(bf16[256,448]{1,0:T(8,128)(2,1)S(1)} %collective-permute-done), channel_id=1, source_target_pairs={{0,0},{1,33},{2,58},{3,27},{4,52},{5,21},{6,46},{7,15},{8,8},{9,41... | collective-permute-start | bytes 688136 | tf_op jit(solution)/shard_map/ppermute | solution.py:33
  46.7 8.2 %collective-permute-done.1 = bf16[256,448]{1,0:T(8,128)(2,1)S(1)} collective-permute-done((bf16[256,448]{1,0:T(8,128)(2,1)S(1)}, bf16[256,448]{1,0:T(8,128)(2,1)S(1)}, u32[]{:S(2)}, u32[]{:S(2)}) %collective-permute-start.1) | collective-permute-done | bytes 229408 | tf_op jit(solution)/shard_map/ppermute | solution.py:33
  54.9 4.4 %all-gather.5.cloned.1.call-done = bf16[1792,896]{1,0:T(8,128)(2,1)} async-done(((bf16[448,896]{1,0:T(8,128)(2,1)}), bf16[1792,896]{1,0:T(8,128)(2,1)}) %all-gather.5.cloned.1.call-update) | async-done | bytes 3211280 | tf_op jit(solution)/shard_map/all_gather | solution.py:77
  60.7 3.2 %convolution_convert_fusion = bf16[256,1792]{1,0:T(8,128)(2,1)S(1)} fusion(bf16[1792,896]{1,0:T(8,128)(2,1)} %all-gather.5.cloned.1.call-done, bf16[1024,896]{1,0:T(8,128)(2,1)S(1)} %bitcast.77, u32[]{:T(128)S(6)} %mul.58), kind=kOutput, calls=%fused_computation.2 | convolution fusion | flops 822542336 | bytes 4587524 | tf_op jit(solution)/shard_map/dot_general | solution.py:67
  63.9 2.6 %collective-permute-start.2 = (bf16[256,1792]{1,0:T(8,128)(2,1)S(1)}, bf16[256,1792]{1,0:T(8,128)(2,1)S(1)}, u32[]{:S(2)}, u32[]{:S(2)}) collective-permute-start(bf16[256,1792]{1,0:T(8,128)(2,1)S(1)} %convolution_convert_fusion), channel_id=1, source_target_pairs={{0,1},{1,0},{2,3},{3,2},{4,5},{5,4},{6,7},{7,6},{8,9},{9,8},{10,11... | collective-permute-start | bytes 2752520 | tf_op jit(solution)/shard_map/ppermute | solution.py:21
  66.5 2.1 %collective-permute-done.2 = bf16[256,1792]{1,0:T(8,128)(2,1)S(1)} collective-permute-done((bf16[256,1792]{1,0:T(8,128)(2,1)S(1)}, bf16[256,1792]{1,0:T(8,128)(2,1)S(1)}, u32[]{:S(2)}, u32[]{:S(2)}) %collective-permute-start.2) | collective-permute-done | bytes 917536 | tf_op jit(solution)/shard_map/ppermute | solution.py:21
  68.5 2.2 %fusion = bf16[256,1792]{1,0:T(8,128)(2,1)} fusion(bf16[1792,896]{1,0:T(8,128)(2,1)S(1)} %copy-done.1, bf16[256,1792]{1,0:T(8,128)(2,1)S(1)} %collective-permute-done.2, bf16[1024,896]{1,0:T(8,128)(2,1)S(1)} %bitcast.78, u32[]{:T(128)S(6)} %mul.57), kind=kOutput, calls=%fused_computation.1 | convolution fusion | flops 823459840 | bytes 5505028 | tf_op jit(solution)/shard_map/dot_general | solution.py:67
  70.7 6.7 %all-to-all-start.1 = ((bf16[4,64,1792]{2,1,0:T(8,128)(2,1)}), bf16[4,64,1792]{2,1,0:T(8,128)(2,1)S(1)}, u32[]{:S(2)}, u32[]{:S(2)}) async-start(bf16[4,64,1792]{2,1,0:T(8,128)(2,1)} %bitcast.8), calls=%async_computation.1 | async-start | bytes 1835008 | tf_op jit(solution)/shard_map/all_to_all | solution.py:90
  77.4 2.3 %collective-permute-start.3 = (bf16[64,448]{1,0:T(8,128)(2,1)S(1)}, bf16[64,448]{1,0:T(8,128)(2,1)S(1)}, u32[]{:S(2)}, u32[]{:S(2)}) collective-permute-start(bf16[64,448]{1,0:T(8,128)(2,1)S(1)} %get-tuple-element.56), channel_id=1, source_target_pairs={{0,128},{128,256},{256,384},{384,0},{1,129},{129,257},{257,385},{3... | collective-permute-start | bytes 172040 | tf_op jit(solution)/shard_map/ppermute | solution.py:17
  79.8 3.4 %collective-permute-start.4 = (bf16[64,448]{1,0:T(8,128)(2,1)S(1)}, bf16[64,448]{1,0:T(8,128)(2,1)S(1)}, u32[]{:S(2)}, u32[]{:S(2)}) collective-permute-start(bf16[64,448]{1,0:T(8,128)(2,1)S(1)} %get-tuple-element.55), channel_id=1, source_target_pairs={{0,256},{128,384},{256,0},{384,128},{1,257},{129,385},{257,1},{385... | collective-permute-start | bytes 172040 | tf_op jit(solution)/shard_map/ppermute | solution.py:17
  83.2 3.7 %collective-permute-start.5 = (bf16[64,448]{1,0:T(8,128)(2,1)S(1)}, bf16[64,448]{1,0:T(8,128)(2,1)S(1)}, u32[]{:S(2)}, u32[]{:S(2)}) collective-permute-start(bf16[64,448]{1,0:T(8,128)(2,1)S(1)} %get-tuple-element.54), channel_id=1, source_target_pairs={{0,384},{128,0},{256,128},{384,256},{1,385},{129,1},{257,129},{385... | collective-permute-start | bytes 172040 | tf_op jit(solution)/shard_map/ppermute | solution.py:17
  88.2 2.7 %collective-permute-done.5 = bf16[64,448]{1,0:T(8,128)(2,1)S(1)} collective-permute-done((bf16[64,448]{1,0:T(8,128)(2,1)S(1)}, bf16[64,448]{1,0:T(8,128)(2,1)S(1)}, u32[]{:S(2)}, u32[]{:S(2)}) %collective-permute-start.5) | collective-permute-done | bytes 57376 | tf_op jit(solution)/shard_map/ppermute | solution.py:17
  91.8 9.8 %all-to-all-done.1 = bf16[4,64,1792]{2,1,0:T(8,128)(2,1)S(1)} async-done(((bf16[4,64,1792]{2,1,0:T(8,128)(2,1)}), bf16[4,64,1792]{2,1,0:T(8,128)(2,1)S(1)}, u32[]{:S(2)}, u32[]{:S(2)}) %all-to-all-start.1) | async-done | bytes 917536 | tf_op jit(solution)/shard_map/all_to_all | solution.py:90
  102.0 6.1 %collective-permute-start.6 = (bf16[64,1792]{1,0:T(8,128)(2,1)S(1)}, bf16[64,1792]{1,0:T(8,128)(2,1)S(1)}, u32[]{:S(2)}, u32[]{:S(2)}) collective-permute-start(bf16[64,1792]{1,0:T(8,128)(2,1)S(1)} %get-tuple-element.52), channel_id=1, source_target_pairs={{0,0},{1,33},{2,10},{3,43},{4,20},{5,53},{6,30},{7,63},{8,8},{9,41... | collective-permute-start | bytes 688136 | tf_op jit(solution)/shard_map/ppermute | solution.py:33
  108.1 17.9 %all_gather.19 = bf16[256,1792]{1,0:T(8,128)(2,1)S(1)} all-gather(bf16[64,1792]{1,0:T(8,128)(2,1)S(1)} %get-tuple-element.53), channel_id=1, replica_groups=mesh['x'=4,'yl'=2,'z'=8,'yh'=4,'c'=2] {'yh'}, dimensions={0}, use_global_device_ids=true | all-gather | bytes 1146880 | tf_op jit(solution)/shard_map/all_gather | solution.py:100
  126.1 3.2 %collective-permute-start.7 = (bf16[256,1792]{1,0:T(8,128)(2,1)S(1)}, bf16[256,1792]{1,0:T(8,128)(2,1)S(1)}, u32[]{:S(2)}, u32[]{:S(2)}) collective-permute-start(bf16[256,1792]{1,0:T(8,128)(2,1)S(1)} %all_gather.19), channel_id=1, source_target_pairs={{0,1},{1,0},{2,3},{3,2},{4,5},{5,4},{6,7},{7,6},{8,9},{9,8},{10,11... | collective-permute-start | bytes 2752520 | tf_op jit(solution)/shard_map/ppermute | solution.py:21
  129.3 3.2 %convolution_convert_fusion.2 = bf16[256,896]{1,0:T(8,128)(2,1)S(1)} fusion(bf16[256,1792]{1,0:T(8,128)(2,1)S(1)} %all_gather.19, bf16[1792,896]{1,0:T(8,128)(2,1)} %all-gather.5.cloned.1.call-done), kind=kOutput, calls=%fused_computation.12 | convolution fusion | flops 822312960 | bytes 4587520 | tf_op jit(solution)/shard_map/dot_general | solution.py:67
  134.9 4.8 %all-to-all-start.2 = ((bf16[16,32,896]{2,1,0:T(8,128)(2,1)}), bf16[16,32,896]{2,1,0:T(8,128)(2,1)S(1)}, u32[]{:S(2)}, u32[]{:S(2)}) async-start(bf16[16,32,896]{2,1,0:T(8,128)(2,1)} %bitcast.21), calls=%async_computation.2 | async-start | bytes 1835008 | tf_op jit(solution)/shard_map/all_to_all | solution.py:109
  141.6 2.1 %collective-permute-start.8 = (bf16[320,448]{0,1:T(8,128)(2,1)}, bf16[320,448]{0,1:T(8,128)(2,1)S(1)}, u32[]{:S(2)}, u32[]{:S(2)}) collective-permute-start(bf16[320,448]{0,1:T(8,128)(2,1)} %get-tuple-element.50), channel_id=1, source_target_pairs={{0,128},{128,256},{256,384},{384,0},{1,129},{129,257},{257,385},{3... | collective-permute-start | bytes 860168 | tf_op jit(solution)/shard_map/ppermute | solution.py:17
  143.7 4.0 %collective-permute-start.9 = (bf16[320,448]{0,1:T(8,128)(2,1)S(1)}, bf16[320,448]{0,1:T(8,128)(2,1)}, u32[]{:S(2)}, u32[]{:S(2)}) collective-permute-start(bf16[320,448]{0,1:T(8,128)(2,1)S(1)} %get-tuple-element.49), channel_id=1, source_target_pairs={{0,256},{128,384},{256,0},{384,128},{1,257},{129,385},{257,1},{385... | collective-permute-start | bytes 860168 | tf_op jit(solution)/shard_map/ppermute | solution.py:17
  147.7 3.1 %collective-permute-start.10 = (bf16[320,448]{0,1:T(8,128)(2,1)S(1)}, bf16[320,448]{0,1:T(8,128)(2,1)}, u32[]{:S(2)}, u32[]{:S(2)}) collective-permute-start(bf16[320,448]{0,1:T(8,128)(2,1)S(1)} %get-tuple-element.48), channel_id=1, source_target_pairs={{0,384},{128,0},{256,128},{384,256},{1,385},{129,1},{257,129},{385... | collective-permute-start | bytes 860168 | tf_op jit(solution)/shard_map/ppermute | solution.py:17
  151.0 3.3 %collective-permute-done.8 = bf16[320,448]{0,1:T(8,128)(2,1)S(1)} collective-permute-done((bf16[320,448]{0,1:T(8,128)(2,1)}, bf16[320,448]{0,1:T(8,128)(2,1)S(1)}, u32[]{:S(2)}, u32[]{:S(2)}) %collective-permute-start.8) | collective-permute-done | bytes 286752 | tf_op jit(solution)/shard_map/ppermute | solution.py:17
  154.3 6.7 %collective-permute-done.9 = bf16[320,448]{0,1:T(8,128)(2,1)} collective-permute-done((bf16[320,448]{0,1:T(8,128)(2,1)S(1)}, bf16[320,448]{0,1:T(8,128)(2,1)}, u32[]{:S(2)}, u32[]{:S(2)}) %collective-permute-start.9) | collective-permute-done | bytes 286752 | tf_op jit(solution)/shard_map/ppermute | solution.py:17
  162.0 1.5 collective-permute-done.10
  164.4 3.6 %collective-permute-start.12 = (bf16[4,256,448]{1,2,0:T(8,128)(2,1)S(1)}, bf16[4,256,448]{1,2,0:T(8,128)(2,1)S(1)}, u32[]{:S(2)}, u32[]{:S(2)}) collective-permute-start(bf16[4,256,448]{1,2,0:T(8,128)(2,1)S(1)} %fusion.17), channel_id=1, source_target_pairs={{0,1},{1,0},{2,3},{3,2},{4,5},{5,4},{6,7},{7,6},{8,9},{9,8},{10,11... | collective-permute-start | bytes 2752520 | tf_op jit(solution)/shard_map/ppermute | solution.py:21
  170.2 2.7 %collective-permute-start.11 = (bf16[256,448]{1,0:T(8,128)(2,1)S(1)}, bf16[256,448]{1,0:T(8,128)(2,1)S(1)}, u32[]{:S(2)}, u32[]{:S(2)}) collective-permute-start(bf16[256,448]{1,0:T(8,128)(2,1)S(1)} %bitcast.86), channel_id=1, source_target_pairs={{0,0},{1,4},{2,7},{3,3},{4,6},{5,2},{6,5},{7,1},{8,9},{9,13},{10,8... | collective-permute-start | bytes 688136 | tf_op jit(solution)/shard_map/ppermute | solution.py:42
  172.9 12.1 %collective-permute-done.11 = bf16[256,448]{1,0:T(8,128)(2,1)S(1)} collective-permute-done((bf16[256,448]{1,0:T(8,128)(2,1)S(1)}, bf16[256,448]{1,0:T(8,128)(2,1)S(1)}, u32[]{:S(2)}, u32[]{:S(2)}) %collective-permute-start.11) | collective-permute-done | bytes 229408 | tf_op jit(solution)/shard_map/ppermute | solution.py:42
  185.9 5.0 %bitcast_convert_fusion = bf16[896,448]{0,1:T(8,128)(2,1)} fusion(bf16[4,2,256,896]{3,2,1,0:T(8,128)(2,1)} %bitcast.87, bf16[4,1,256,448]{2,3,1,0:T(8,128)(2,1)S(1)} %bitcast.88, bf16[4,1,256,448]{2,3,1,0:T(8,128)(2,1)S(1)} %bitcast.82), kind=kOutput, calls=%fused_computation.10 | convolution fusion | flops 1645486080 | bytes 6307840 | tf_op jit(solution)/shard_map/dot_general | solution.py:67
  (59 shorter events, 15.0 us)
Async XLA Ops:
  7.2 13.1 %copy-start = (bf16[256,448]{0,1:T(8,128)(2,1)S(1)}, bf16[256,448]{0,1:T(8,128)(2,1)}, u32[]{:S(2)}) copy-start(bf16[256,448]{0,1:T(8,128)(2,1)} %param.5) | copy-start | bytes 688132
  7.2 52.1 %all-gather.5.cloned.1.call-start = ((), (), s32[]{:S(2)}) async-start(), calls=%async_computation.3 | async-start | bytes 4014080 | tf_op jit(solution)/shard_map/all_gather | solution.py:77
  9.7 45.2 %all-to-all-start = ((bf16[16,32,896]{2,1,0:T(8,128)(2,1)}), bf16[16,32,896]{2,1,0:T(8,128)(2,1)S(1)}, u32[]{:S(2)}, u32[]{:S(2)}) async-start(bf16[16,32,896]{2,1,0:T(8,128)(2,1)} %broadcast_in_dim.41), calls=%async_computation | async-start | bytes 1835008 | tf_op jit(solution)/shard_map/all_to_all | solution.py:80
  20.2 119.6 %all-gather.7.cloned.1.call-start = ((), (), s32[]{:S(2)}) async-start(), calls=%async_computation.4 | async-start | bytes 4587520 | tf_op jit(solution)/shard_map/all_gather | solution.py:111
  20.4 21.0 %collective-permute-start = (bf16[256,448]{1,0:T(8,128)(2,1)S(1)}, bf16[256,448]{1,0:T(8,128)(2,1)S(1)}, u32[]{:S(2)}, u32[]{:S(2)}) collective-permute-start(bf16[256,448]{1,0:T(8,128)(2,1)S(1)} %copy.29), channel_id=1, source_target_pairs={{0,0},{4,1},{7,2},{3,3},{6,4},{2,5},{5,6},{1,7},{9,8},{13,9},{8,10... | collective-permute-start | bytes 688136 | tf_op jit(solution)/shard_map/ppermute | solution.py:42
  41.4 13.5 %collective-permute-start.1 = (bf16[256,448]{1,0:T(8,128)(2,1)S(1)}, bf16[256,448]{1,0:T(8,128)(2,1)S(1)}, u32[]{:S(2)}, u32[]{:S(2)}) collective-permute-start(bf16[256,448]{1,0:T(8,128)(2,1)S(1)} %collective-permute-done), channel_id=1, source_target_pairs={{0,0},{1,33},{2,58},{3,27},{4,52},{5,21},{6,46},{7,15},{8,8},{9,41... | collective-permute-start | bytes 688136 | tf_op jit(solution)/shard_map/ppermute | solution.py:33
  60.6 7.9 %copy-start.1 = (bf16[1792,896]{1,0:T(8,128)(2,1)S(1)}, bf16[1792,896]{1,0:T(8,128)(2,1)}, u32[]{:S(2)}) copy-start(bf16[1792,896]{1,0:T(8,128)(2,1)} %all-gather.5.cloned.1.call-done) | copy-start | bytes 9633796
  63.9 4.7 %collective-permute-start.2 = (bf16[256,1792]{1,0:T(8,128)(2,1)S(1)}, bf16[256,1792]{1,0:T(8,128)(2,1)S(1)}, u32[]{:S(2)}, u32[]{:S(2)}) collective-permute-start(bf16[256,1792]{1,0:T(8,128)(2,1)S(1)} %convolution_convert_fusion), channel_id=1, source_target_pairs={{0,1},{1,0},{2,3},{3,2},{4,5},{5,4},{6,7},{7,6},{8,9},{9,8},{10,11... | collective-permute-start | bytes 2752520 | tf_op jit(solution)/shard_map/ppermute | solution.py:21
  70.7 30.8 %all-to-all-start.1 = ((bf16[4,64,1792]{2,1,0:T(8,128)(2,1)}), bf16[4,64,1792]{2,1,0:T(8,128)(2,1)S(1)}, u32[]{:S(2)}, u32[]{:S(2)}) async-start(bf16[4,64,1792]{2,1,0:T(8,128)(2,1)} %bitcast.8), calls=%async_computation.1 | async-start | bytes 1835008 | tf_op jit(solution)/shard_map/all_to_all | solution.py:90
  77.4 9.5 %collective-permute-start.3 = (bf16[64,448]{1,0:T(8,128)(2,1)S(1)}, bf16[64,448]{1,0:T(8,128)(2,1)S(1)}, u32[]{:S(2)}, u32[]{:S(2)}) collective-permute-start(bf16[64,448]{1,0:T(8,128)(2,1)S(1)} %get-tuple-element.56), channel_id=1, source_target_pairs={{0,128},{128,256},{256,384},{384,0},{1,129},{129,257},{257,385},{3... | collective-permute-start | bytes 172040 | tf_op jit(solution)/shard_map/ppermute | solution.py:17
  79.8 8.4 %collective-permute-start.4 = (bf16[64,448]{1,0:T(8,128)(2,1)S(1)}, bf16[64,448]{1,0:T(8,128)(2,1)S(1)}, u32[]{:S(2)}, u32[]{:S(2)}) collective-permute-start(bf16[64,448]{1,0:T(8,128)(2,1)S(1)} %get-tuple-element.55), channel_id=1, source_target_pairs={{0,256},{128,384},{256,0},{384,128},{1,257},{129,385},{257,1},{385... | collective-permute-start | bytes 172040 | tf_op jit(solution)/shard_map/ppermute | solution.py:17
  83.2 7.7 %collective-permute-start.5 = (bf16[64,448]{1,0:T(8,128)(2,1)S(1)}, bf16[64,448]{1,0:T(8,128)(2,1)S(1)}, u32[]{:S(2)}, u32[]{:S(2)}) collective-permute-start(bf16[64,448]{1,0:T(8,128)(2,1)S(1)} %get-tuple-element.54), channel_id=1, source_target_pairs={{0,384},{128,0},{256,128},{384,256},{1,385},{129,1},{257,129},{385... | collective-permute-start | bytes 172040 | tf_op jit(solution)/shard_map/ppermute | solution.py:17
  102.0 24.1 %collective-permute-start.6 = (bf16[64,1792]{1,0:T(8,128)(2,1)S(1)}, bf16[64,1792]{1,0:T(8,128)(2,1)S(1)}, u32[]{:S(2)}, u32[]{:S(2)}) collective-permute-start(bf16[64,1792]{1,0:T(8,128)(2,1)S(1)} %get-tuple-element.52), channel_id=1, source_target_pairs={{0,0},{1,33},{2,10},{3,43},{4,20},{5,53},{6,30},{7,63},{8,8},{9,41... | collective-permute-start | bytes 688136 | tf_op jit(solution)/shard_map/ppermute | solution.py:33
  126.1 6.4 %collective-permute-start.7 = (bf16[256,1792]{1,0:T(8,128)(2,1)S(1)}, bf16[256,1792]{1,0:T(8,128)(2,1)S(1)}, u32[]{:S(2)}, u32[]{:S(2)}) collective-permute-start(bf16[256,1792]{1,0:T(8,128)(2,1)S(1)} %all_gather.19), channel_id=1, source_target_pairs={{0,1},{1,0},{2,3},{3,2},{4,5},{5,4},{6,7},{7,6},{8,9},{9,8},{10,11... | collective-permute-start | bytes 2752520 | tf_op jit(solution)/shard_map/ppermute | solution.py:21
  129.3 3.2 %copy-start.2 = (bf16[1792,896]{1,0:T(8,128)(2,1)S(1)}, bf16[1792,896]{1,0:T(8,128)(2,1)}, u32[]{:S(2)}) copy-start(bf16[1792,896]{1,0:T(8,128)(2,1)} %all-gather.5.cloned.1.call-done) | copy-start | bytes 9633796
  134.9 55.9 %all-to-all-start.2 = ((bf16[16,32,896]{2,1,0:T(8,128)(2,1)}), bf16[16,32,896]{2,1,0:T(8,128)(2,1)S(1)}, u32[]{:S(2)}, u32[]{:S(2)}) async-start(bf16[16,32,896]{2,1,0:T(8,128)(2,1)} %bitcast.21), calls=%async_computation.2 | async-start | bytes 1835008 | tf_op jit(solution)/shard_map/all_to_all | solution.py:109
  141.6 12.7 %collective-permute-start.8 = (bf16[320,448]{0,1:T(8,128)(2,1)}, bf16[320,448]{0,1:T(8,128)(2,1)S(1)}, u32[]{:S(2)}, u32[]{:S(2)}) collective-permute-start(bf16[320,448]{0,1:T(8,128)(2,1)} %get-tuple-element.50), channel_id=1, source_target_pairs={{0,128},{128,256},{256,384},{384,0},{1,129},{129,257},{257,385},{3... | collective-permute-start | bytes 860168 | tf_op jit(solution)/shard_map/ppermute | solution.py:17
  143.7 17.4 %collective-permute-start.9 = (bf16[320,448]{0,1:T(8,128)(2,1)S(1)}, bf16[320,448]{0,1:T(8,128)(2,1)}, u32[]{:S(2)}, u32[]{:S(2)}) collective-permute-start(bf16[320,448]{0,1:T(8,128)(2,1)S(1)} %get-tuple-element.49), channel_id=1, source_target_pairs={{0,256},{128,384},{256,0},{384,128},{1,257},{129,385},{257,1},{385... | collective-permute-start | bytes 860168 | tf_op jit(solution)/shard_map/ppermute | solution.py:17
  147.7 15.8 %collective-permute-start.10 = (bf16[320,448]{0,1:T(8,128)(2,1)S(1)}, bf16[320,448]{0,1:T(8,128)(2,1)}, u32[]{:S(2)}, u32[]{:S(2)}) collective-permute-start(bf16[320,448]{0,1:T(8,128)(2,1)S(1)} %get-tuple-element.48), channel_id=1, source_target_pairs={{0,384},{128,0},{256,128},{384,256},{1,385},{129,1},{257,129},{385... | collective-permute-start | bytes 860168 | tf_op jit(solution)/shard_map/ppermute | solution.py:17
  164.4 21.4 %collective-permute-start.12 = (bf16[4,256,448]{1,2,0:T(8,128)(2,1)S(1)}, bf16[4,256,448]{1,2,0:T(8,128)(2,1)S(1)}, u32[]{:S(2)}, u32[]{:S(2)}) collective-permute-start(bf16[4,256,448]{1,2,0:T(8,128)(2,1)S(1)} %fusion.17), channel_id=1, source_target_pairs={{0,1},{1,0},{2,3},{3,2},{4,5},{5,4},{6,7},{7,6},{8,9},{9,8},{10,11... | collective-permute-start | bytes 2752520 | tf_op jit(solution)/shard_map/ppermute | solution.py:21
  170.2 14.8 %collective-permute-start.11 = (bf16[256,448]{1,0:T(8,128)(2,1)S(1)}, bf16[256,448]{1,0:T(8,128)(2,1)S(1)}, u32[]{:S(2)}, u32[]{:S(2)}) collective-permute-start(bf16[256,448]{1,0:T(8,128)(2,1)S(1)} %bitcast.86), channel_id=1, source_target_pairs={{0,0},{1,4},{2,7},{3,3},{4,6},{5,2},{6,5},{7,1},{8,9},{9,13},{10,8... | collective-permute-start | bytes 688136 | tf_op jit(solution)/shard_map/ppermute | solution.py:42
Sparse Core Ops, SparseCore 0:
  10.1 49.1 all-gather.4
  61.4 52.2 all-gather.6

commit v10 on v9

--- a/solution.py
+++ b/solution.py
@@ -117,8 +117,7 @@
     far_grad = jnp.stack([far_own, far_other], axis=1)
     weight_grad = dot(far.reshape(-1, feats), far_grad.reshape(-1, cols), ((0,), (0,))).astype(BF)
     out = in_order([part[4 * pair :] for part in both], here).reshape(NX * pair, cols)
-    out = within_z(out, True)
-    ig, weight_grad = lax.optimization_barrier((ig, weight_grad))
+    ig, weight_grad, out = lax.optimization_barrier((ig, weight_grad, within_z(out, True)))
     input_grad = jnp.sum(ig.astype(jnp.float32), axis=0).astype(BF)
     return out, input_grad, weight_grad
 

time: 199 us -> 193 us (0.970)
  waiting for transfers between devices: 69.3 us -> 65.2 us
    ppermute x2, waiting for transfers between devices: 28.6 us -> 23.4 us  [within_z(): return lax.ppermute(value, ('z', 'yh', 'c'), pairs)]
  transfers between devices with their start and end apart: 18 -> 18, of which waited for: 11 -> 11; matrix products, arithmetic and copies ran while one was open for 13% -> 12% of each run, Pallas kernels for 0% -> 0%
where the time goes in v10:
time: 193 us
  starting transfers between devices  68.2 us (35%)
  waiting for transfers between devices  65.2 us (34%)
  blocking collectives  17.9 us (9%)
  matrix products  14.9 us (8%)
  between operations  14.5 us (8%)
  local copies, waits for them, and re-layouts  8.94 us (5%)
  other arithmetic  2.85 us (1%)
    ppermute x2, waiting for transfers between devices, within_z(): return lax.ppermute(value, ('z', 'yh', 'c'), pairs)  23.4 us
    ppermute x6, starting transfers between devices, along_x(): return lax.ppermute(value, 'x', [(i, (i + shift) % NX) for i in range(NX)])  18.5 us
    all_gather x1, blocking collectives, body(): grad_own = lax.all_gather(hidden_grad, 'yh', axis=0, tiled=True)  17.9 us
    ppermute x6, waiting for transfers between devices, along_x(): return lax.ppermute(value, 'x', [(i, (i + shift) % NX) for i in range(NX)])  16.6 us
    dot_general x5, matrix products, dot(): lax.dot_general(a, b, (contract, ((), ())), preferred_element_type=jnp.fl...  14.9 us
    ppermute x2, starting transfers between devices, along_z(): return lax.ppermute(value, ('z', 'yh', 'c'), pairs)  11.4 us
    all_to_all x1, starting transfers between devices, body(): lax.all_to_all(near, ('z', 'yl'), split_axis=0, concat_axis=0)  10.4 us
    all_to_all x1, waiting for transfers between devices, body(): parts = lax.all_to_all(partial_value, 'yh', split_axis=0, concat_axis=0)  9.78 us
  transfers between devices with their start and end apart: 18, of which 11 were waited for; matrix products, arithmetic and copies ran while one was open for 12% of the time, Pallas kernels for 0%

profile of v10, /device:TPU:81, one launch (start us, length us, event | category | flops | bytes accessed | tf_op | source)
XLA Modules:
  0.0 192.5 jit_solution(16459437763181559381)
XLA Ops:
  7.9 1.8 broadcast_in_dim.41
  9.8 10.4 %all-to-all-start = ((bf16[16,32,896]{2,1,0:T(8,128)(2,1)}), bf16[16,32,896]{2,1,0:T(8,128)(2,1)S(1)}, u32[]{:S(2)}, u32[]{:S(2)}) async-start(bf16[16,32,896]{2,1,0:T(8,128)(2,1)} %broadcast_in_dim.41), calls=%async_computation | async-start | bytes 1835008 | tf_op jit(solution)/shard_map/all_to_all | solution.py:80
  20.4 4.5 %collective-permute-start = (bf16[256,448]{1,0:T(8,128)(2,1)S(1)}, bf16[256,448]{1,0:T(8,128)(2,1)S(1)}, u32[]{:S(2)}, u32[]{:S(2)}) collective-permute-start(bf16[256,448]{1,0:T(8,128)(2,1)S(1)} %copy.29), channel_id=1, source_target_pairs={{0,0},{4,1},{7,2},{3,3},{6,4},{2,5},{5,6},{1,7},{9,8},{13,9},{8,10... | collective-permute-start | bytes 688136 | tf_op jit(solution)/shard_map/ppermute | solution.py:42
  24.9 16.5 %collective-permute-done = bf16[256,448]{1,0:T(8,128)(2,1)S(1)} collective-permute-done((bf16[256,448]{1,0:T(8,128)(2,1)S(1)}, bf16[256,448]{1,0:T(8,128)(2,1)S(1)}, u32[]{:S(2)}, u32[]{:S(2)}) %collective-permute-start) | collective-permute-done | bytes 229408 | tf_op jit(solution)/shard_map/ppermute | solution.py:42
  41.4 5.3 %collective-permute-start.1 = (bf16[256,448]{1,0:T(8,128)(2,1)S(1)}, bf16[256,448]{1,0:T(8,128)(2,1)S(1)}, u32[]{:S(2)}, u32[]{:S(2)}) collective-permute-start(bf16[256,448]{1,0:T(8,128)(2,1)S(1)} %collective-permute-done), channel_id=1, source_target_pairs={{0,0},{1,33},{2,58},{3,27},{4,52},{5,21},{6,46},{7,15},{8,8},{9,41... | collective-permute-start | bytes 688136 | tf_op jit(solution)/shard_map/ppermute | solution.py:33
  46.7 8.2 %collective-permute-done.1 = bf16[256,448]{1,0:T(8,128)(2,1)S(1)} collective-permute-done((bf16[256,448]{1,0:T(8,128)(2,1)S(1)}, bf16[256,448]{1,0:T(8,128)(2,1)S(1)}, u32[]{:S(2)}, u32[]{:S(2)}) %collective-permute-start.1) | collective-permute-done | bytes 229408 | tf_op jit(solution)/shard_map/ppermute | solution.py:33
  54.9 4.4 %all-gather.5.cloned.1.call-done = bf16[1792,896]{1,0:T(8,128)(2,1)} async-done(((bf16[448,896]{1,0:T(8,128)(2,1)}), bf16[1792,896]{1,0:T(8,128)(2,1)}) %all-gather.5.cloned.1.call-update) | async-done | bytes 3211280 | tf_op jit(solution)/shard_map/all_gather | solution.py:77
  60.7 3.2 %convolution_convert_fusion = bf16[256,1792]{1,0:T(8,128)(2,1)S(1)} fusion(bf16[1792,896]{1,0:T(8,128)(2,1)} %all-gather.5.cloned.1.call-done, bf16[1024,896]{1,0:T(8,128)(2,1)S(1)} %bitcast.77, u32[]{:T(128)S(6)} %mul.58), kind=kOutput, calls=%fused_computation.2 | convolution fusion | flops 822542336 | bytes 4587524 | tf_op jit(solution)/shard_map/dot_general | solution.py:67
  63.9 2.6 %collective-permute-start.2 = (bf16[256,1792]{1,0:T(8,128)(2,1)S(1)}, bf16[256,1792]{1,0:T(8,128)(2,1)S(1)}, u32[]{:S(2)}, u32[]{:S(2)}) collective-permute-start(bf16[256,1792]{1,0:T(8,128)(2,1)S(1)} %convolution_convert_fusion), channel_id=1, source_target_pairs={{0,1},{1,0},{2,3},{3,2},{4,5},{5,4},{6,7},{7,6},{8,9},{9,8},{10,11... | collective-permute-start | bytes 2752520 | tf_op jit(solution)/shard_map/ppermute | solution.py:21
  66.5 2.1 %collective-permute-done.2 = bf16[256,1792]{1,0:T(8,128)(2,1)S(1)} collective-permute-done((bf16[256,1792]{1,0:T(8,128)(2,1)S(1)}, bf16[256,1792]{1,0:T(8,128)(2,1)S(1)}, u32[]{:S(2)}, u32[]{:S(2)}) %collective-permute-start.2) | collective-permute-done | bytes 917536 | tf_op jit(solution)/shard_map/ppermute | solution.py:21
  68.5 2.2 %fusion = bf16[256,1792]{1,0:T(8,128)(2,1)} fusion(bf16[1792,896]{1,0:T(8,128)(2,1)S(1)} %copy-done.3, bf16[256,1792]{1,0:T(8,128)(2,1)S(1)} %collective-permute-done.2, bf16[1024,896]{1,0:T(8,128)(2,1)S(1)} %bitcast.78, u32[]{:T(128)S(6)} %mul.57), kind=kOutput, calls=%fused_computation.1 | convolution fusion | flops 823459840 | bytes 5505028 | tf_op jit(solution)/shard_map/dot_general | solution.py:67
  70.7 6.7 %all-to-all-start.1 = ((bf16[4,64,1792]{2,1,0:T(8,128)(2,1)}), bf16[4,64,1792]{2,1,0:T(8,128)(2,1)S(1)}, u32[]{:S(2)}, u32[]{:S(2)}) async-start(bf16[4,64,1792]{2,1,0:T(8,128)(2,1)} %bitcast.5), calls=%async_computation.1 | async-start | bytes 1835008 | tf_op jit(solution)/shard_map/all_to_all | solution.py:90
  77.5 2.3 %collective-permute-start.3 = (bf16[64,448]{1,0:T(8,128)(2,1)S(1)}, bf16[64,448]{1,0:T(8,128)(2,1)S(1)}, u32[]{:S(2)}, u32[]{:S(2)}) collective-permute-start(bf16[64,448]{1,0:T(8,128)(2,1)S(1)} %get-tuple-element.58), channel_id=1, source_target_pairs={{0,128},{128,256},{256,384},{384,0},{1,129},{129,257},{257,385},{3... | collective-permute-start | bytes 172040 | tf_op jit(solution)/shard_map/ppermute | solution.py:17
  79.8 3.4 %collective-permute-start.4 = (bf16[64,448]{1,0:T(8,128)(2,1)S(1)}, bf16[64,448]{1,0:T(8,128)(2,1)S(1)}, u32[]{:S(2)}, u32[]{:S(2)}) collective-permute-start(bf16[64,448]{1,0:T(8,128)(2,1)S(1)} %get-tuple-element.57), channel_id=1, source_target_pairs={{0,256},{128,384},{256,0},{384,128},{1,257},{129,385},{257,1},{385... | collective-permute-start | bytes 172040 | tf_op jit(solution)/shard_map/ppermute | solution.py:17
  83.2 3.7 %collective-permute-start.5 = (bf16[64,448]{1,0:T(8,128)(2,1)S(1)}, bf16[64,448]{1,0:T(8,128)(2,1)S(1)}, u32[]{:S(2)}, u32[]{:S(2)}) collective-permute-start(bf16[64,448]{1,0:T(8,128)(2,1)S(1)} %get-tuple-element.56), channel_id=1, source_target_pairs={{0,384},{128,0},{256,128},{384,256},{1,385},{129,1},{257,129},{385... | collective-permute-start | bytes 172040 | tf_op jit(solution)/shard_map/ppermute | solution.py:17
  88.2 2.7 %collective-permute-done.5 = bf16[64,448]{1,0:T(8,128)(2,1)S(1)} collective-permute-done((bf16[64,448]{1,0:T(8,128)(2,1)S(1)}, bf16[64,448]{1,0:T(8,128)(2,1)S(1)}, u32[]{:S(2)}, u32[]{:S(2)}) %collective-permute-start.5) | collective-permute-done | bytes 57376 | tf_op jit(solution)/shard_map/ppermute | solution.py:17
  91.8 9.8 %all-to-all-done.1 = bf16[4,64,1792]{2,1,0:T(8,128)(2,1)S(1)} async-done(((bf16[4,64,1792]{2,1,0:T(8,128)(2,1)}), bf16[4,64,1792]{2,1,0:T(8,128)(2,1)S(1)}, u32[]{:S(2)}, u32[]{:S(2)}) %all-to-all-start.1) | async-done | bytes 917536 | tf_op jit(solution)/shard_map/all_to_all | solution.py:90
  102.0 6.1 %collective-permute-start.6 = (bf16[64,1792]{1,0:T(8,128)(2,1)S(1)}, bf16[64,1792]{1,0:T(8,128)(2,1)S(1)}, u32[]{:S(2)}, u32[]{:S(2)}) collective-permute-start(bf16[64,1792]{1,0:T(8,128)(2,1)S(1)} %get-tuple-element.54), channel_id=1, source_target_pairs={{0,0},{1,33},{2,10},{3,43},{4,20},{5,53},{6,30},{7,63},{8,8},{9,41... | collective-permute-start | bytes 688136 | tf_op jit(solution)/shard_map/ppermute | solution.py:33
  108.1 17.9 %all_gather.17 = bf16[256,1792]{1,0:T(8,128)(2,1)S(1)} all-gather(bf16[64,1792]{1,0:T(8,128)(2,1)S(1)} %get-tuple-element.55), channel_id=1, replica_groups=mesh['x'=4,'yl'=2,'z'=8,'yh'=4,'c'=2] {'yh'}, dimensions={0}, use_global_device_ids=true | all-gather | bytes 1146880 | tf_op jit(solution)/shard_map/all_gather | solution.py:100
  126.1 3.2 %collective-permute-start.7 = (bf16[256,1792]{1,0:T(8,128)(2,1)S(1)}, bf16[256,1792]{1,0:T(8,128)(2,1)S(1)}, u32[]{:S(2)}, u32[]{:S(2)}) collective-permute-start(bf16[256,1792]{1,0:T(8,128)(2,1)S(1)} %all_gather.17), channel_id=1, source_target_pairs={{0,1},{1,0},{2,3},{3,2},{4,5},{5,4},{6,7},{7,6},{8,9},{9,8},{10,11... | collective-permute-start | bytes 2752520 | tf_op jit(solution)/shard_map/ppermute | solution.py:21
  129.3 3.2 %convolution_convert_fusion.2 = bf16[256,896]{1,0:T(8,128)(2,1)S(1)} fusion(bf16[256,1792]{1,0:T(8,128)(2,1)S(1)} %all_gather.17, bf16[1792,896]{1,0:T(8,128)(2,1)} %all-gather.5.cloned.1.call-done), kind=kOutput, calls=%fused_computation.12 | convolution fusion | flops 822312960 | bytes 4587520 | tf_op jit(solution)/shard_map/dot_general | solution.py:67
  134.9 4.7 %all-to-all-start.2 = ((bf16[16,32,896]{2,1,0:T(8,128)(2,1)}), bf16[16,32,896]{2,1,0:T(8,128)(2,1)S(1)}, u32[]{:S(2)}, u32[]{:S(2)}) async-start(bf16[16,32,896]{2,1,0:T(8,128)(2,1)} %bitcast.18), calls=%async_computation.2 | async-start | bytes 1835008 | tf_op jit(solution)/shard_map/all_to_all | solution.py:109
  141.6 2.2 %collective-permute-start.8 = (bf16[320,448]{0,1:T(8,128)(2,1)}, bf16[320,448]{0,1:T(8,128)(2,1)S(1)}, u32[]{:S(2)}, u32[]{:S(2)}) collective-permute-start(bf16[320,448]{0,1:T(8,128)(2,1)} %get-tuple-element.52), channel_id=1, source_target_pairs={{0,128},{128,256},{256,384},{384,0},{1,129},{129,257},{257,385},{3... | collective-permute-start | bytes 860168 | tf_op jit(solution)/shard_map/ppermute | solution.py:17
  143.8 3.8 %collective-permute-start.9 = (bf16[320,448]{0,1:T(8,128)(2,1)S(1)}, bf16[320,448]{0,1:T(8,128)(2,1)S(1)}, u32[]{:S(2)}, u32[]{:S(2)}) collective-permute-start(bf16[320,448]{0,1:T(8,128)(2,1)S(1)} %get-tuple-element.51), channel_id=1, source_target_pairs={{0,256},{128,384},{256,0},{384,128},{1,257},{129,385},{257,1},{385... | collective-permute-start | bytes 860168 | tf_op jit(solution)/shard_map/ppermute | solution.py:17
  147.6 3.1 %collective-permute-start.10 = (bf16[320,448]{0,1:T(8,128)(2,1)S(1)}, bf16[320,448]{0,1:T(8,128)(2,1)S(1)}, u32[]{:S(2)}, u32[]{:S(2)}) collective-permute-start(bf16[320,448]{0,1:T(8,128)(2,1)S(1)} %get-tuple-element.50), channel_id=1, source_target_pairs={{0,384},{128,0},{256,128},{384,256},{1,385},{129,1},{257,129},{385... | collective-permute-start | bytes 860168 | tf_op jit(solution)/shard_map/ppermute | solution.py:17
  150.9 3.6 %collective-permute-done.8 = bf16[320,448]{0,1:T(8,128)(2,1)S(1)} collective-permute-done((bf16[320,448]{0,1:T(8,128)(2,1)}, bf16[320,448]{0,1:T(8,128)(2,1)S(1)}, u32[]{:S(2)}, u32[]{:S(2)}) %collective-permute-start.8) | collective-permute-done | bytes 286752 | tf_op jit(solution)/shard_map/ppermute | solution.py:17
  154.5 6.4 %collective-permute-done.9 = bf16[320,448]{0,1:T(8,128)(2,1)S(1)} collective-permute-done((bf16[320,448]{0,1:T(8,128)(2,1)S(1)}, bf16[320,448]{0,1:T(8,128)(2,1)S(1)}, u32[]{:S(2)}, u32[]{:S(2)}) %collective-permute-start.9) | collective-permute-done | bytes 286752 | tf_op jit(solution)/shard_map/ppermute | solution.py:17
  160.9 2.7 %collective-permute-done.10 = bf16[320,448]{0,1:T(8,128)(2,1)S(1)} collective-permute-done((bf16[320,448]{0,1:T(8,128)(2,1)S(1)}, bf16[320,448]{0,1:T(8,128)(2,1)S(1)}, u32[]{:S(2)}, u32[]{:S(2)}) %collective-permute-start.10) | collective-permute-done | bytes 286752 | tf_op jit(solution)/shard_map/ppermute | solution.py:17
  163.6 3.5 %collective-permute-start.11 = (bf16[4,256,448]{1,2,0:T(8,128)(2,1)S(1)}, bf16[4,256,448]{1,2,0:T(8,128)(2,1)}, u32[]{:S(2)}, u32[]{:S(2)}) collective-permute-start(bf16[4,256,448]{1,2,0:T(8,128)(2,1)S(1)} %fusion.17), channel_id=1, source_target_pairs={{0,1},{1,0},{2,3},{3,2},{4,5},{5,4},{6,7},{7,6},{8,9},{9,8},{10,11... | collective-permute-start | bytes 2752520 | tf_op jit(solution)/shard_map/ppermute | solution.py:21
  169.3 2.6 %collective-permute-start.12 = (bf16[256,448]{1,0:T(8,128)(2,1)S(1)}, bf16[256,448]{1,0:T(8,128)(2,1)S(1)}, u32[]{:S(2)}, u32[]{:S(2)}) collective-permute-start(bf16[256,448]{1,0:T(8,128)(2,1)S(1)} %bitcast.86), channel_id=1, source_target_pairs={{0,0},{1,4},{2,7},{3,3},{4,6},{5,2},{6,5},{7,1},{8,9},{9,13},{10,8... | collective-permute-start | bytes 688136 | tf_op jit(solution)/shard_map/ppermute | solution.py:42
  171.9 5.3 %bitcast_convert_fusion = bf16[896,448]{0,1:T(8,128)(2,1)} fusion(bf16[4,2,256,896]{3,2,1,0:T(8,128)(2,1)} %bitcast.87, bf16[4,1,256,448]{2,3,1,0:T(8,128)(2,1)} %bitcast.31, bf16[4,1,256,448]{2,3,1,0:T(8,128)(2,1)S(1)} %bitcast.82), kind=kOutput, calls=%fused_computation.10 | convolution fusion | flops 1645486080 | bytes 6307840 | tf_op jit(solution)/shard_map/dot_general | solution.py:67
  177.2 6.9 %collective-permute-done.12 = bf16[256,448]{1,0:T(8,128)(2,1)S(1)} collective-permute-done((bf16[256,448]{1,0:T(8,128)(2,1)S(1)}, bf16[256,448]{1,0:T(8,128)(2,1)S(1)}, u32[]{:S(2)}, u32[]{:S(2)}) %collective-permute-start.12) | collective-permute-done | bytes 229408 | tf_op jit(solution)/shard_map/ppermute | solution.py:42
  (63 shorter events, 13.1 us)
Async XLA Ops:
  7.2 13.1 %copy-start.2 = (bf16[256,448]{0,1:T(8,128)(2,1)S(1)}, bf16[256,448]{0,1:T(8,128)(2,1)}, u32[]{:S(2)}) copy-start(bf16[256,448]{0,1:T(8,128)(2,1)} %param.5) | copy-start | bytes 688132
  7.2 52.1 %all-gather.5.cloned.1.call-start = ((), (), s32[]{:S(2)}) async-start(), calls=%async_computation.3 | async-start | bytes 4014080 | tf_op jit(solution)/shard_map/all_gather | solution.py:77
  9.8 45.2 %all-to-all-start = ((bf16[16,32,896]{2,1,0:T(8,128)(2,1)}), bf16[16,32,896]{2,1,0:T(8,128)(2,1)S(1)}, u32[]{:S(2)}, u32[]{:S(2)}) async-start(bf16[16,32,896]{2,1,0:T(8,128)(2,1)} %broadcast_in_dim.41), calls=%async_computation | async-start | bytes 1835008 | tf_op jit(solution)/shard_map/all_to_all | solution.py:80
  20.2 119.5 %all-gather.7.cloned.1.call-start = ((), (), s32[]{:S(2)}) async-start(), calls=%async_computation.4 | async-start | bytes 4587520 | tf_op jit(solution)/shard_map/all_gather | solution.py:111
  20.4 21.0 %collective-permute-start = (bf16[256,448]{1,0:T(8,128)(2,1)S(1)}, bf16[256,448]{1,0:T(8,128)(2,1)S(1)}, u32[]{:S(2)}, u32[]{:S(2)}) collective-permute-start(bf16[256,448]{1,0:T(8,128)(2,1)S(1)} %copy.29), channel_id=1, source_target_pairs={{0,0},{4,1},{7,2},{3,3},{6,4},{2,5},{5,6},{1,7},{9,8},{13,9},{8,10... | collective-permute-start | bytes 688136 | tf_op jit(solution)/shard_map/ppermute | solution.py:42
  41.4 13.5 %collective-permute-start.1 = (bf16[256,448]{1,0:T(8,128)(2,1)S(1)}, bf16[256,448]{1,0:T(8,128)(2,1)S(1)}, u32[]{:S(2)}, u32[]{:S(2)}) collective-permute-start(bf16[256,448]{1,0:T(8,128)(2,1)S(1)} %collective-permute-done), channel_id=1, source_target_pairs={{0,0},{1,33},{2,58},{3,27},{4,52},{5,21},{6,46},{7,15},{8,8},{9,41... | collective-permute-start | bytes 688136 | tf_op jit(solution)/shard_map/ppermute | solution.py:33
  60.6 7.9 %copy-start.3 = (bf16[1792,896]{1,0:T(8,128)(2,1)S(1)}, bf16[1792,896]{1,0:T(8,128)(2,1)}, u32[]{:S(2)}) copy-start(bf16[1792,896]{1,0:T(8,128)(2,1)} %all-gather.5.cloned.1.call-done) | copy-start | bytes 9633796
  63.9 4.7 %collective-permute-start.2 = (bf16[256,1792]{1,0:T(8,128)(2,1)S(1)}, bf16[256,1792]{1,0:T(8,128)(2,1)S(1)}, u32[]{:S(2)}, u32[]{:S(2)}) collective-permute-start(bf16[256,1792]{1,0:T(8,128)(2,1)S(1)} %convolution_convert_fusion), channel_id=1, source_target_pairs={{0,1},{1,0},{2,3},{3,2},{4,5},{5,4},{6,7},{7,6},{8,9},{9,8},{10,11... | collective-permute-start | bytes 2752520 | tf_op jit(solution)/shard_map/ppermute | solution.py:21
  70.7 30.8 %all-to-all-start.1 = ((bf16[4,64,1792]{2,1,0:T(8,128)(2,1)}), bf16[4,64,1792]{2,1,0:T(8,128)(2,1)S(1)}, u32[]{:S(2)}, u32[]{:S(2)}) async-start(bf16[4,64,1792]{2,1,0:T(8,128)(2,1)} %bitcast.5), calls=%async_computation.1 | async-start | bytes 1835008 | tf_op jit(solution)/shard_map/all_to_all | solution.py:90
  77.5 9.5 %collective-permute-start.3 = (bf16[64,448]{1,0:T(8,128)(2,1)S(1)}, bf16[64,448]{1,0:T(8,128)(2,1)S(1)}, u32[]{:S(2)}, u32[]{:S(2)}) collective-permute-start(bf16[64,448]{1,0:T(8,128)(2,1)S(1)} %get-tuple-element.58), channel_id=1, source_target_pairs={{0,128},{128,256},{256,384},{384,0},{1,129},{129,257},{257,385},{3... | collective-permute-start | bytes 172040 | tf_op jit(solution)/shard_map/ppermute | solution.py:17
  79.8 8.4 %collective-permute-start.4 = (bf16[64,448]{1,0:T(8,128)(2,1)S(1)}, bf16[64,448]{1,0:T(8,128)(2,1)S(1)}, u32[]{:S(2)}, u32[]{:S(2)}) collective-permute-start(bf16[64,448]{1,0:T(8,128)(2,1)S(1)} %get-tuple-element.57), channel_id=1, source_target_pairs={{0,256},{128,384},{256,0},{384,128},{1,257},{129,385},{257,1},{385... | collective-permute-start | bytes 172040 | tf_op jit(solution)/shard_map/ppermute | solution.py:17
  83.2 7.7 %collective-permute-start.5 = (bf16[64,448]{1,0:T(8,128)(2,1)S(1)}, bf16[64,448]{1,0:T(8,128)(2,1)S(1)}, u32[]{:S(2)}, u32[]{:S(2)}) collective-permute-start(bf16[64,448]{1,0:T(8,128)(2,1)S(1)} %get-tuple-element.56), channel_id=1, source_target_pairs={{0,384},{128,0},{256,128},{384,256},{1,385},{129,1},{257,129},{385... | collective-permute-start | bytes 172040 | tf_op jit(solution)/shard_map/ppermute | solution.py:17
  102.0 24.1 %collective-permute-start.6 = (bf16[64,1792]{1,0:T(8,128)(2,1)S(1)}, bf16[64,1792]{1,0:T(8,128)(2,1)S(1)}, u32[]{:S(2)}, u32[]{:S(2)}) collective-permute-start(bf16[64,1792]{1,0:T(8,128)(2,1)S(1)} %get-tuple-element.54), channel_id=1, source_target_pairs={{0,0},{1,33},{2,10},{3,43},{4,20},{5,53},{6,30},{7,63},{8,8},{9,41... | collective-permute-start | bytes 688136 | tf_op jit(solution)/shard_map/ppermute | solution.py:33
  126.1 6.4 %collective-permute-start.7 = (bf16[256,1792]{1,0:T(8,128)(2,1)S(1)}, bf16[256,1792]{1,0:T(8,128)(2,1)S(1)}, u32[]{:S(2)}, u32[]{:S(2)}) collective-permute-start(bf16[256,1792]{1,0:T(8,128)(2,1)S(1)} %all_gather.17), channel_id=1, source_target_pairs={{0,1},{1,0},{2,3},{3,2},{4,5},{5,4},{6,7},{7,6},{8,9},{9,8},{10,11... | collective-permute-start | bytes 2752520 | tf_op jit(solution)/shard_map/ppermute | solution.py:21
  129.3 3.2 %copy-start.4 = (bf16[1792,896]{1,0:T(8,128)(2,1)S(1)}, bf16[1792,896]{1,0:T(8,128)(2,1)}, u32[]{:S(2)}) copy-start(bf16[1792,896]{1,0:T(8,128)(2,1)} %all-gather.5.cloned.1.call-done) | copy-start | bytes 9633796
  134.9 42.3 %all-to-all-start.2 = ((bf16[16,32,896]{2,1,0:T(8,128)(2,1)}), bf16[16,32,896]{2,1,0:T(8,128)(2,1)S(1)}, u32[]{:S(2)}, u32[]{:S(2)}) async-start(bf16[16,32,896]{2,1,0:T(8,128)(2,1)} %bitcast.18), calls=%async_computation.2 | async-start | bytes 1835008 | tf_op jit(solution)/shard_map/all_to_all | solution.py:109
  141.6 12.9 %collective-permute-start.8 = (bf16[320,448]{0,1:T(8,128)(2,1)}, bf16[320,448]{0,1:T(8,128)(2,1)S(1)}, u32[]{:S(2)}, u32[]{:S(2)}) collective-permute-start(bf16[320,448]{0,1:T(8,128)(2,1)} %get-tuple-element.52), channel_id=1, source_target_pairs={{0,128},{128,256},{256,384},{384,0},{1,129},{129,257},{257,385},{3... | collective-permute-start | bytes 860168 | tf_op jit(solution)/shard_map/ppermute | solution.py:17
  143.8 17.1 %collective-permute-start.9 = (bf16[320,448]{0,1:T(8,128)(2,1)S(1)}, bf16[320,448]{0,1:T(8,128)(2,1)S(1)}, u32[]{:S(2)}, u32[]{:S(2)}) collective-permute-start(bf16[320,448]{0,1:T(8,128)(2,1)S(1)} %get-tuple-element.51), channel_id=1, source_target_pairs={{0,256},{128,384},{256,0},{384,128},{1,257},{129,385},{257,1},{385... | collective-permute-start | bytes 860168 | tf_op jit(solution)/shard_map/ppermute | solution.py:17
  147.6 16.0 %collective-permute-start.10 = (bf16[320,448]{0,1:T(8,128)(2,1)S(1)}, bf16[320,448]{0,1:T(8,128)(2,1)S(1)}, u32[]{:S(2)}, u32[]{:S(2)}) collective-permute-start(bf16[320,448]{0,1:T(8,128)(2,1)S(1)} %get-tuple-element.50), channel_id=1, source_target_pairs={{0,384},{128,0},{256,128},{384,256},{1,385},{129,1},{257,129},{385... | collective-permute-start | bytes 860168 | tf_op jit(solution)/shard_map/ppermute | solution.py:17
  160.9 2.7 %copy-start = (bf16[320,448]{0,1:T(8,128)(2,1)}, bf16[320,448]{0,1:T(8,128)(2,1)S(1)}, u32[]{:S(2)}) copy-start(bf16[320,448]{0,1:T(8,128)(2,1)S(1)} %collective-permute-done.9) | copy-start | bytes 860164
  163.6 3.5 %copy-start.1 = (bf16[320,448]{0,1:T(8,128)(2,1)}, bf16[320,448]{0,1:T(8,128)(2,1)S(1)}, u32[]{:S(2)}) copy-start(bf16[320,448]{0,1:T(8,128)(2,1)S(1)} %collective-permute-done.10) | copy-start | bytes 860164
  163.6 8.3 %collective-permute-start.11 = (bf16[4,256,448]{1,2,0:T(8,128)(2,1)S(1)}, bf16[4,256,448]{1,2,0:T(8,128)(2,1)}, u32[]{:S(2)}, u32[]{:S(2)}) collective-permute-start(bf16[4,256,448]{1,2,0:T(8,128)(2,1)S(1)} %fusion.17), channel_id=1, source_target_pairs={{0,1},{1,0},{2,3},{3,2},{4,5},{5,4},{6,7},{7,6},{8,9},{9,8},{10,11... | collective-permute-start | bytes 2752520 | tf_op jit(solution)/shard_map/ppermute | solution.py:21
  169.3 14.8 %collective-permute-start.12 = (bf16[256,448]{1,0:T(8,128)(2,1)S(1)}, bf16[256,448]{1,0:T(8,128)(2,1)S(1)}, u32[]{:S(2)}, u32[]{:S(2)}) collective-permute-start(bf16[256,448]{1,0:T(8,128)(2,1)S(1)} %bitcast.86), channel_id=1, source_target_pairs={{0,0},{1,4},{2,7},{3,3},{4,6},{5,2},{6,5},{7,1},{8,9},{9,13},{10,8... | collective-permute-start | bytes 688136 | tf_op jit(solution)/shard_map/ppermute | solution.py:42
Sparse Core Ops, SparseCore 0:
  10.1 49.1 all-gather.4
  61.4 52.2 all-gather.6

commit v11 on v9

--- a/solution.py
+++ b/solution.py
@@ -97,27 +97,31 @@
     hidden_grad = pullback(cot.astype(jnp.float32))[0].astype(BF)
     activated = activated.astype(BF)
 
+    both = jnp.concatenate([hidden_grad, activated], axis=0)
+    both = lax.optimization_barrier(both.reshape(2 * pair, NX, cols).transpose(1, 0, 2))
+    both = shift_blocks(both, here)
     grad_own = lax.all_gather(hidden_grad, "yh", axis=0, tiled=True)
-    grad_own, activated = lax.optimization_barrier((grad_own, along_z(activated, 1)))
+    grad_own, *both = lax.optimization_barrier((grad_own, *both))
     grad_other = swap_cores(grad_own)
+    both = in_order(both, here)
+    out = along_z(both[:, pair:].reshape(NX * pair, cols), 1)
 
     ig_own = dot(grad_own, w_all, ((1,), (0,))).astype(BF)
     ig_own, grad_other = lax.optimization_barrier((ig_own, grad_other))
     ig_other = dot(grad_other, w_all, ((1,), (0,))).astype(BF)
     ig = cut(jnp.stack([ig_own, ig_other]).reshape(8, pair, feats), 16 - first, 8)
-    ig, grad_own, activated = lax.optimization_barrier((ig.reshape(16, rows, feats), grad_own, activated))
+    far_own = both[:, :pair]
+    ig, far_own = lax.optimization_barrier((ig.reshape(16, rows, feats), far_own))
     ig = lax.all_to_all(ig, ("z", "yl"), split_axis=0, concat_axis=0)
 
+    far_own, out = lax.optimization_barrier((far_own, out))
+    out = within_z(out, True)
+    far_own = lax.all_gather(far_own, "yh", axis=0, tiled=False)
+    far_own, out = lax.optimization_barrier((far_own, out))
+    far_other = swap_cores(far_own)
+    far_grad = jnp.stack([far_own, far_other]).transpose(2, 0, 1, 3, 4)
     far = lax.all_gather(near, "x", axis=0, tiled=False)
-    far, grad_own, activated = lax.optimization_barrier((far, grad_own, activated))
-    both = jnp.concatenate([grad_own, activated], axis=0)
-    both = shift_blocks(both.reshape(5 * pair, NX, cols).transpose(1, 0, 2), here)
-    far_own = in_order([part[: 4 * pair] for part in both], here)
-    far_other = swap_cores(far_own)
-    far_grad = jnp.stack([far_own, far_other], axis=1)
     weight_grad = dot(far.reshape(-1, feats), far_grad.reshape(-1, cols), ((0,), (0,))).astype(BF)
-    out = in_order([part[4 * pair :] for part in both], here).reshape(NX * pair, cols)
-    out = within_z(out, True)
     ig, weight_grad = lax.optimization_barrier((ig, weight_grad))
     input_grad = jnp.sum(ig.astype(jnp.float32), axis=0).astype(BF)
     return out, input_grad, weight_grad

time: 199 us -> 223 us (1.12)
  the two profiles are of different devices: /device:TPU:81 before, /device:TPU:1 now
where the time goes in v11:
time: 223 us; the launch traced here: 222 us
  starting transfers between devices  72 us (32%)
  blocking collectives  56.8 us (25%)
  waiting for transfers between devices  50.9 us (23%)
  matrix products  17.2 us (8%)
  between operations  14.5 us (7%)
  local copies, waits for them, and re-layouts  6.63 us (3%)
  other arithmetic  3.51 us (2%)
    all_gather x1, blocking collectives, body(): far_own = lax.all_gather(far_own, 'yh', axis=0, tiled=False)  38.8 us
    ppermute x2, waiting for transfers between devices, within_z(): return lax.ppermute(value, ('z', 'yh', 'c'), pairs)  21.4 us
    ppermute x6, starting transfers between devices, along_x(): return lax.ppermute(value, 'x', [(i, (i + shift) % NX) for i in range(NX)])  18.8 us
    all_gather x1, blocking collectives, body(): grad_own = lax.all_gather(hidden_grad, 'yh', axis=0, tiled=True)  18 us
    dot_general x5, matrix products, dot(): lax.dot_general(a, b, (contract, ((), ())), preferred_element_type=jnp.fl...  17.2 us
    all_to_all x1, starting transfers between devices, body(): lax.all_to_all(near, ('z', 'yl'), split_axis=0, concat_axis=0)  12 us
    ppermute x2, waiting for transfers between devices, along_z(): return lax.ppermute(value, ('z', 'yh', 'c'), pairs)  11.6 us
    ppermute x3, starting transfers between devices, swap_cores(): return lax.ppermute(value, 'c', [(0, 1), (1, 0)])  11.1 us
  transfers between devices with their start and end apart: 18, of which 8 were waited for; matrix products, arithmetic and copies ran while one was open for 8% of the time, Pallas kernels for 0%

profile of v11, /device:TPU:1, one launch (start us, length us, event | category | flops | bytes accessed | tf_op | source)
XLA Modules:
  0.0 221.5 jit_solution(1265485908614567437)
XLA Ops:
  7.9 1.8 broadcast_in_dim.37
  9.7 12.0 %all-to-all-start = ((bf16[16,32,896]{2,1,0:T(8,128)(2,1)}), bf16[16,32,896]{2,1,0:T(8,128)(2,1)S(1)}, u32[]{:S(2)}, u32[]{:S(2)}) async-start(bf16[16,32,896]{2,1,0:T(8,128)(2,1)} %broadcast_in_dim.37), calls=%async_computation | async-start | bytes 1835008 | tf_op jit(solution)/shard_map/all_to_all | solution.py:80
  21.9 5.0 %collective-permute-start = (bf16[256,448]{1,0:T(8,128)(2,1)S(1)}, bf16[256,448]{1,0:T(8,128)(2,1)S(1)}, u32[]{:S(2)}, u32[]{:S(2)}) collective-permute-start(bf16[256,448]{1,0:T(8,128)(2,1)S(1)} %copy.59), channel_id=1, source_target_pairs={{0,0},{4,1},{7,2},{3,3},{6,4},{2,5},{5,6},{1,7},{9,8},{13,9},{8,10... | collective-permute-start | bytes 688136 | tf_op jit(solution)/shard_map/ppermute | solution.py:42
  26.9 21.4 %collective-permute-done = bf16[256,448]{1,0:T(8,128)(2,1)S(1)} collective-permute-done((bf16[256,448]{1,0:T(8,128)(2,1)S(1)}, bf16[256,448]{1,0:T(8,128)(2,1)S(1)}, u32[]{:S(2)}, u32[]{:S(2)}) %collective-permute-start) | collective-permute-done | bytes 229408 | tf_op jit(solution)/shard_map/ppermute | solution.py:42
  48.3 1.9 collective-permute-start.1
  50.2 9.1 %collective-permute-done.1 = bf16[256,448]{1,0:T(8,128)(2,1)S(1)} collective-permute-done((bf16[256,448]{1,0:T(8,128)(2,1)S(1)}, bf16[256,448]{1,0:T(8,128)(2,1)S(1)}, u32[]{:S(2)}, u32[]{:S(2)}) %collective-permute-start.1) | collective-permute-done | bytes 229408 | tf_op jit(solution)/shard_map/ppermute | solution.py:33
  59.3 1.7 all-gather.6.cloned.1.call-done
  61.2 4.0 %convolution_convert_fusion = bf16[256,1792]{1,0:T(8,128)(2,1)} fusion(bf16[1792,896]{1,0:T(8,128)(2,1)} %all-gather.6.cloned.1.call-done, bf16[1024,896]{1,0:T(8,128)(2,1)S(1)} %bitcast.61, u32[]{:T(128)S(6)} %mul.102), kind=kOutput, calls=%fused_computation.2 | convolution fusion | flops 822542336 | bytes 4587524 | tf_op jit(solution)/shard_map/dot_general | solution.py:67
  65.2 2.6 %collective-permute-start.2 = (bf16[256,1792]{1,0:T(8,128)(2,1)}, bf16[256,1792]{1,0:T(8,128)(2,1)S(1)}, u32[]{:S(2)}, u32[]{:S(2)}) collective-permute-start(bf16[256,1792]{1,0:T(8,128)(2,1)} %convolution_convert_fusion), channel_id=1, source_target_pairs={{0,1},{1,0},{2,3},{3,2},{4,5},{5,4},{6,7},{7,6},{8,9},{9,8},{10,11... | collective-permute-start | bytes 2752520 | tf_op jit(solution)/shard_map/ppermute | solution.py:21
  67.8 2.3 %collective-permute-done.2 = bf16[256,1792]{1,0:T(8,128)(2,1)S(1)} collective-permute-done((bf16[256,1792]{1,0:T(8,128)(2,1)}, bf16[256,1792]{1,0:T(8,128)(2,1)S(1)}, u32[]{:S(2)}, u32[]{:S(2)}) %collective-permute-start.2) | collective-permute-done | bytes 917536 | tf_op jit(solution)/shard_map/ppermute | solution.py:21
  70.1 4.0 %fusion = bf16[256,1792]{1,0:T(8,128)(2,1)} fusion(bf16[1792,896]{1,0:T(8,128)(2,1)} %all-gather.6.cloned.1.call-done, bf16[256,1792]{1,0:T(8,128)(2,1)S(1)} %collective-permute-done.2, bf16[1024,896]{1,0:T(8,128)(2,1)S(1)} %bitcast.62, u32[]{:T(128)S(6)} %mul.101), kind=kOutput, calls=%fused_computation.1 | convolution fusion | flops 823459840 | bytes 5505028 | tf_op jit(solution)/shard_map/dot_general | solution.py:67
  74.2 6.5 %all-to-all-start.1 = ((bf16[4,64,1792]{2,1,0:T(8,128)(2,1)}), bf16[4,64,1792]{2,1,0:T(8,128)(2,1)S(1)}, u32[]{:S(2)}, u32[]{:S(2)}) async-start(bf16[4,64,1792]{2,1,0:T(8,128)(2,1)} %bitcast.69), calls=%async_computation.1 | async-start | bytes 1835008 | tf_op jit(solution)/shard_map/all_to_all | solution.py:90
  80.8 2.3 %collective-permute-start.3 = (bf16[64,448]{1,0:T(8,128)(2,1)S(1)}, bf16[64,448]{1,0:T(8,128)(2,1)S(1)}, u32[]{:S(2)}, u32[]{:S(2)}) collective-permute-start(bf16[64,448]{1,0:T(8,128)(2,1)S(1)} %get-tuple-element.70), channel_id=1, source_target_pairs={{0,128},{128,256},{256,384},{384,0},{1,129},{129,257},{257,385},{3... | collective-permute-start | bytes 172040 | tf_op jit(solution)/shard_map/ppermute | solution.py:17
  84.1 3.4 %collective-permute-start.4 = (bf16[64,448]{1,0:T(8,128)(2,1)S(1)}, bf16[64,448]{1,0:T(8,128)(2,1)S(1)}, u32[]{:S(2)}, u32[]{:S(2)}) collective-permute-start(bf16[64,448]{1,0:T(8,128)(2,1)S(1)} %get-tuple-element.69), channel_id=1, source_target_pairs={{0,256},{128,384},{256,0},{384,128},{1,257},{129,385},{257,1},{385... | collective-permute-start | bytes 172040 | tf_op jit(solution)/shard_map/ppermute | solution.py:17
  87.5 3.7 %collective-permute-start.5 = (bf16[64,448]{1,0:T(8,128)(2,1)S(1)}, bf16[64,448]{1,0:T(8,128)(2,1)S(1)}, u32[]{:S(2)}, u32[]{:S(2)}) collective-permute-start(bf16[64,448]{1,0:T(8,128)(2,1)S(1)} %get-tuple-element.68), channel_id=1, source_target_pairs={{0,384},{128,0},{256,128},{384,256},{1,385},{129,1},{257,129},{385... | collective-permute-start | bytes 172040 | tf_op jit(solution)/shard_map/ppermute | solution.py:17
  91.3 1.6 collective-permute-done.5
  93.8 10.2 %all-to-all-done.1 = bf16[4,64,1792]{2,1,0:T(8,128)(2,1)S(1)} async-done(((bf16[4,64,1792]{2,1,0:T(8,128)(2,1)}), bf16[4,64,1792]{2,1,0:T(8,128)(2,1)S(1)}, u32[]{:S(2)}, u32[]{:S(2)}) %all-to-all-start.1) | async-done | bytes 917536 | tf_op jit(solution)/shard_map/all_to_all | solution.py:90
  105.3 2.3 %collective-permute-start.6 = (bf16[128,448]{0,1:T(8,128)(2,1)S(1)}, bf16[128,448]{0,1:T(8,128)(2,1)S(1)}, u32[]{:S(2)}, u32[]{:S(2)}) collective-permute-start(bf16[128,448]{0,1:T(8,128)(2,1)S(1)} %bitcast.77), channel_id=1, source_target_pairs={{0,128},{128,256},{256,384},{384,0},{1,129},{129,257},{257,385},{3... | collective-permute-start | bytes 344072 | tf_op jit(solution)/shard_map/ppermute | solution.py:17
  107.8 3.1 %collective-permute-start.7 = (bf16[128,448]{0,1:T(8,128)(2,1)S(1)}, bf16[128,448]{0,1:T(8,128)(2,1)S(1)}, u32[]{:S(2)}, u32[]{:S(2)}) collective-permute-start(bf16[128,448]{0,1:T(8,128)(2,1)S(1)} %bitcast.78), channel_id=1, source_target_pairs={{0,256},{128,384},{256,0},{384,128},{1,257},{129,385},{257,1},{385... | collective-permute-start | bytes 344072 | tf_op jit(solution)/shard_map/ppermute | solution.py:17
  111.0 4.0 %collective-permute-start.8 = (bf16[128,448]{0,1:T(8,128)(2,1)S(1)}, bf16[128,448]{0,1:T(8,128)(2,1)S(1)}, u32[]{:S(2)}, u32[]{:S(2)}) collective-permute-start(bf16[128,448]{0,1:T(8,128)(2,1)S(1)} %bitcast.79), channel_id=1, source_target_pairs={{0,384},{128,0},{256,128},{384,256},{1,385},{129,1},{257,129},{385... | collective-permute-start | bytes 344072 | tf_op jit(solution)/shard_map/ppermute | solution.py:17
  115.3 18.0 %all_gather.23 = bf16[256,1792]{1,0:T(8,128)(2,1)S(1)} all-gather(bf16[64,1792]{1,0:T(8,128)(2,1)S(1)} %fusion.15), channel_id=1, replica_groups=mesh['x'=4,'yl'=2,'z'=8,'yh'=4,'c'=2] {'yh'}, dimensions={0}, use_global_device_ids=true | all-gather | bytes 1146880 | tf_op jit(solution)/shard_map/all_gather | solution.py:103
  134.0 6.0 %collective-permute-start.9 = (bf16[256,1792]{1,0:T(8,128)(2,1)S(1)}, bf16[256,1792]{1,0:T(8,128)(2,1)S(1)}, u32[]{:S(2)}, u32[]{:S(2)}) collective-permute-start(bf16[256,1792]{1,0:T(8,128)(2,1)S(1)} %all_gather.23), channel_id=1, source_target_pairs={{0,1},{1,0},{2,3},{3,2},{4,5},{5,4},{6,7},{7,6},{8,9},{9,8},{10,11... | collective-permute-start | bytes 2752520 | tf_op jit(solution)/shard_map/ppermute | solution.py:21
  140.2 6.0 %collective-permute-start.10 = (bf16[256,448]{1,0:T(8,128)(2,1)S(1)}, bf16[256,448]{1,0:T(8,128)(2,1)S(1)}, u32[]{:S(2)}, u32[]{:S(2)}) collective-permute-start(bf16[256,448]{1,0:T(8,128)(2,1)S(1)} %bitcast.73), channel_id=1, source_target_pairs={{0,0},{1,33},{2,10},{3,43},{4,20},{5,53},{6,30},{7,63},{8,8},{9,41... | collective-permute-start | bytes 688136 | tf_op jit(solution)/shard_map/ppermute | solution.py:33
  146.2 3.0 %convolution_convert_fusion.3 = bf16[256,896]{1,0:T(8,128)(2,1)S(1)} fusion(bf16[256,1792]{1,0:T(8,128)(2,1)S(1)} %all_gather.23, bf16[1792,896]{1,0:T(8,128)(2,1)} %all-gather.6.cloned.1.call-done), kind=kOutput, calls=%fused_computation.9 | convolution fusion | flops 822312960 | bytes 4587520 | tf_op jit(solution)/shard_map/dot_general | solution.py:67
  149.3 1.1 fusion.1
  151.7 2.5 %collective-permute-done.10 = bf16[256,448]{1,0:T(8,128)(2,1)S(1)} collective-permute-done((bf16[256,448]{1,0:T(8,128)(2,1)S(1)}, bf16[256,448]{1,0:T(8,128)(2,1)S(1)}, u32[]{:S(2)}, u32[]{:S(2)}) %collective-permute-start.10) | collective-permute-done | bytes 229408 | tf_op jit(solution)/shard_map/ppermute | solution.py:33
  154.3 1.9 collective-permute-start.11
  156.2 8.8 %all-to-all-start.2 = ((bf16[16,32,896]{2,1,0:T(8,128)(2,1)}), bf16[16,32,896]{2,1,0:T(8,128)(2,1)S(1)}, u32[]{:S(2)}, u32[]{:S(2)}) async-start(bf16[16,32,896]{2,1,0:T(8,128)(2,1)} %bitcast.23), calls=%async_computation.2 | async-start | bytes 1835008 | tf_op jit(solution)/shard_map/all_to_all | solution.py:115
  165.0 38.8 %all-gather.1 = bf16[16,64,448]{2,1,0:T(8,128)(2,1)S(1)} all-gather(bf16[4,64,448]{2,1,0:T(8,128)(2,1)S(1)} %get-tuple-element.36), channel_id=3, replica_groups=mesh['x'=4,'yl'=2,'z'=8,'yh'=4,'c'=2] {'yh'}, dimensions={0}, use_global_device_ids=true | all-gather | bytes 1146880 | tf_op jit(solution)/shard_map/all_gather | solution.py:119
  203.8 2.5 %collective-permute-start.12 = (bf16[4,4,64,448]{3,2,1,0:T(8,128)(2,1)S(1)}, bf16[4,4,64,448]{3,2,1,0:T(8,128)(2,1)S(1)}, u32[]{:S(2)}, u32[]{:S(2)}) collective-permute-start(bf16[4,4,64,448]{3,2,1,0:T(8,128)(2,1)S(1)} %bitcast.59), channel_id=1, source_target_pairs={{0,1},{1,0},{2,3},{3,2},{4,5},{5,4},{6,7},{7,6},{8,9},{9,8},{10,11... | collective-permute-start | bytes 2752520 | tf_op jit(solution)/shard_map/ppermute | solution.py:21
  207.2 1.3 collective-permute-done.12
  208.9 5.0 %convolution_convert_fusion.1 = bf16[896,448]{0,1:T(8,128)(2,1)} fusion(bf16[2048,896]{1,0:T(8,128)(2,1)} %bitcast.80, bf16[2048,448]{1,0:T(8,128)(2,1)S(1)} %bitcast.67), kind=kOutput, calls=%fused_computation.7 | convolution fusion | flops 1644568576 | bytes 6307840 | tf_op jit(solution)/shard_map/dot_general | solution.py:67
  (57 shorter events, 9.1 us)
Async XLA Ops:
  7.2 14.6 %copy-start = (bf16[256,448]{0,1:T(8,128)(2,1)S(1)}, bf16[256,448]{0,1:T(8,128)(2,1)}, u32[]{:S(2)}) copy-start(bf16[256,448]{0,1:T(8,128)(2,1)} %param.5) | copy-start | bytes 688132
  7.2 53.9 %all-gather.6.cloned.1.call-start = ((), (), s32[]{:S(2)}) async-start(), calls=%async_computation.3 | async-start | bytes 4014080 | tf_op jit(solution)/shard_map/all_gather | solution.py:77
  9.7 49.6 %all-to-all-start = ((bf16[16,32,896]{2,1,0:T(8,128)(2,1)}), bf16[16,32,896]{2,1,0:T(8,128)(2,1)S(1)}, u32[]{:S(2)}, u32[]{:S(2)}) async-start(bf16[16,32,896]{2,1,0:T(8,128)(2,1)} %broadcast_in_dim.37), calls=%async_computation | async-start | bytes 1835008 | tf_op jit(solution)/shard_map/all_to_all | solution.py:80
  21.9 26.4 %collective-permute-start = (bf16[256,448]{1,0:T(8,128)(2,1)S(1)}, bf16[256,448]{1,0:T(8,128)(2,1)S(1)}, u32[]{:S(2)}, u32[]{:S(2)}) collective-permute-start(bf16[256,448]{1,0:T(8,128)(2,1)S(1)} %copy.59), channel_id=1, source_target_pairs={{0,0},{4,1},{7,2},{3,3},{6,4},{2,5},{5,6},{1,7},{9,8},{13,9},{8,10... | collective-permute-start | bytes 688136 | tf_op jit(solution)/shard_map/ppermute | solution.py:42
  48.3 11.0 %collective-permute-start.1 = (bf16[256,448]{1,0:T(8,128)(2,1)S(1)}, bf16[256,448]{1,0:T(8,128)(2,1)S(1)}, u32[]{:S(2)}, u32[]{:S(2)}) collective-permute-start(bf16[256,448]{1,0:T(8,128)(2,1)S(1)} %collective-permute-done), channel_id=1, source_target_pairs={{0,0},{1,33},{2,58},{3,27},{4,52},{5,21},{6,46},{7,15},{8,8},{9,41... | collective-permute-start | bytes 688136 | tf_op jit(solution)/shard_map/ppermute | solution.py:33
  65.2 4.9 %collective-permute-start.2 = (bf16[256,1792]{1,0:T(8,128)(2,1)}, bf16[256,1792]{1,0:T(8,128)(2,1)S(1)}, u32[]{:S(2)}, u32[]{:S(2)}) collective-permute-start(bf16[256,1792]{1,0:T(8,128)(2,1)} %convolution_convert_fusion), channel_id=1, source_target_pairs={{0,1},{1,0},{2,3},{3,2},{4,5},{5,4},{6,7},{7,6},{8,9},{9,8},{10,11... | collective-permute-start | bytes 2752520 | tf_op jit(solution)/shard_map/ppermute | solution.py:21
  74.2 29.8 %all-to-all-start.1 = ((bf16[4,64,1792]{2,1,0:T(8,128)(2,1)}), bf16[4,64,1792]{2,1,0:T(8,128)(2,1)S(1)}, u32[]{:S(2)}, u32[]{:S(2)}) async-start(bf16[4,64,1792]{2,1,0:T(8,128)(2,1)} %bitcast.69), calls=%async_computation.1 | async-start | bytes 1835008 | tf_op jit(solution)/shard_map/all_to_all | solution.py:90
  80.6 128.3 %all-gather.8.cloned.1.call-start = ((), (), s32[]{:S(2)}) async-start(), calls=%async_computation.4 | async-start | bytes 4587520 | tf_op jit(solution)/shard_map/all_gather | solution.py:123
  80.8 10.5 %collective-permute-start.3 = (bf16[64,448]{1,0:T(8,128)(2,1)S(1)}, bf16[64,448]{1,0:T(8,128)(2,1)S(1)}, u32[]{:S(2)}, u32[]{:S(2)}) collective-permute-start(bf16[64,448]{1,0:T(8,128)(2,1)S(1)} %get-tuple-element.70), channel_id=1, source_target_pairs={{0,128},{128,256},{256,384},{384,0},{1,129},{129,257},{257,385},{3... | collective-permute-start | bytes 172040 | tf_op jit(solution)/shard_map/ppermute | solution.py:17
  84.1 7.1 %collective-permute-start.4 = (bf16[64,448]{1,0:T(8,128)(2,1)S(1)}, bf16[64,448]{1,0:T(8,128)(2,1)S(1)}, u32[]{:S(2)}, u32[]{:S(2)}) collective-permute-start(bf16[64,448]{1,0:T(8,128)(2,1)S(1)} %get-tuple-element.69), channel_id=1, source_target_pairs={{0,256},{128,384},{256,0},{384,128},{1,257},{129,385},{257,1},{385... | collective-permute-start | bytes 172040 | tf_op jit(solution)/shard_map/ppermute | solution.py:17
  87.5 5.4 %collective-permute-start.5 = (bf16[64,448]{1,0:T(8,128)(2,1)S(1)}, bf16[64,448]{1,0:T(8,128)(2,1)S(1)}, u32[]{:S(2)}, u32[]{:S(2)}) collective-permute-start(bf16[64,448]{1,0:T(8,128)(2,1)S(1)} %get-tuple-element.68), channel_id=1, source_target_pairs={{0,384},{128,0},{256,128},{384,256},{1,385},{129,1},{257,129},{385... | collective-permute-start | bytes 172040 | tf_op jit(solution)/shard_map/ppermute | solution.py:17
  105.3 28.2 %collective-permute-start.6 = (bf16[128,448]{0,1:T(8,128)(2,1)S(1)}, bf16[128,448]{0,1:T(8,128)(2,1)S(1)}, u32[]{:S(2)}, u32[]{:S(2)}) collective-permute-start(bf16[128,448]{0,1:T(8,128)(2,1)S(1)} %bitcast.77), channel_id=1, source_target_pairs={{0,128},{128,256},{256,384},{384,0},{1,129},{129,257},{257,385},{3... | collective-permute-start | bytes 344072 | tf_op jit(solution)/shard_map/ppermute | solution.py:17
  107.8 25.7 %collective-permute-start.7 = (bf16[128,448]{0,1:T(8,128)(2,1)S(1)}, bf16[128,448]{0,1:T(8,128)(2,1)S(1)}, u32[]{:S(2)}, u32[]{:S(2)}) collective-permute-start(bf16[128,448]{0,1:T(8,128)(2,1)S(1)} %bitcast.78), channel_id=1, source_target_pairs={{0,256},{128,384},{256,0},{384,128},{1,257},{129,385},{257,1},{385... | collective-permute-start | bytes 344072 | tf_op jit(solution)/shard_map/ppermute | solution.py:17
  111.0 22.5 %collective-permute-start.8 = (bf16[128,448]{0,1:T(8,128)(2,1)S(1)}, bf16[128,448]{0,1:T(8,128)(2,1)S(1)}, u32[]{:S(2)}, u32[]{:S(2)}) collective-permute-start(bf16[128,448]{0,1:T(8,128)(2,1)S(1)} %bitcast.79), channel_id=1, source_target_pairs={{0,384},{128,0},{256,128},{384,256},{1,385},{129,1},{257,129},{385... | collective-permute-start | bytes 344072 | tf_op jit(solution)/shard_map/ppermute | solution.py:17
  134.0 15.3 %collective-permute-start.9 = (bf16[256,1792]{1,0:T(8,128)(2,1)S(1)}, bf16[256,1792]{1,0:T(8,128)(2,1)S(1)}, u32[]{:S(2)}, u32[]{:S(2)}) collective-permute-start(bf16[256,1792]{1,0:T(8,128)(2,1)S(1)} %all_gather.23), channel_id=1, source_target_pairs={{0,1},{1,0},{2,3},{3,2},{4,5},{5,4},{6,7},{7,6},{8,9},{9,8},{10,11... | collective-permute-start | bytes 2752520 | tf_op jit(solution)/shard_map/ppermute | solution.py:21
  140.2 9.1 %copy-start.1 = (bf16[1792,896]{1,0:T(8,128)(2,1)S(1)}, bf16[1792,896]{1,0:T(8,128)(2,1)}, u32[]{:S(2)}) copy-start(bf16[1792,896]{1,0:T(8,128)(2,1)} %all-gather.6.cloned.1.call-done) | copy-start | bytes 9633796
  140.2 14.1 %collective-permute-start.10 = (bf16[256,448]{1,0:T(8,128)(2,1)S(1)}, bf16[256,448]{1,0:T(8,128)(2,1)S(1)}, u32[]{:S(2)}, u32[]{:S(2)}) collective-permute-start(bf16[256,448]{1,0:T(8,128)(2,1)S(1)} %bitcast.73), channel_id=1, source_target_pairs={{0,0},{1,33},{2,10},{3,43},{4,20},{5,53},{6,30},{7,63},{8,8},{9,41... | collective-permute-start | bytes 688136 | tf_op jit(solution)/shard_map/ppermute | solution.py:33
  154.3 49.5 %collective-permute-start.11 = (bf16[256,448]{1,0:T(8,128)(2,1)S(1)}, bf16[256,448]{1,0:T(8,128)(2,1)S(1)}, u32[]{:S(2)}, u32[]{:S(2)}) collective-permute-start(bf16[256,448]{1,0:T(8,128)(2,1)S(1)} %collective-permute-done.10), channel_id=1, source_target_pairs={{0,0},{1,4},{2,7},{3,3},{4,6},{5,2},{6,5},{7,1},{8,9},{9,13},{10,8... | collective-permute-start | bytes 688136 | tf_op jit(solution)/shard_map/ppermute | solution.py:42
  156.2 57.8 %all-to-all-start.2 = ((bf16[16,32,896]{2,1,0:T(8,128)(2,1)}), bf16[16,32,896]{2,1,0:T(8,128)(2,1)S(1)}, u32[]{:S(2)}, u32[]{:S(2)}) async-start(bf16[16,32,896]{2,1,0:T(8,128)(2,1)} %bitcast.23), calls=%async_computation.2 | async-start | bytes 1835008 | tf_op jit(solution)/shard_map/all_to_all | solution.py:115
  203.8 4.6 %collective-permute-start.12 = (bf16[4,4,64,448]{3,2,1,0:T(8,128)(2,1)S(1)}, bf16[4,4,64,448]{3,2,1,0:T(8,128)(2,1)S(1)}, u32[]{:S(2)}, u32[]{:S(2)}) collective-permute-start(bf16[4,4,64,448]{3,2,1,0:T(8,128)(2,1)S(1)} %bitcast.59), channel_id=1, source_target_pairs={{0,1},{1,0},{2,3},{3,2},{4,5},{5,4},{6,7},{7,6},{8,9},{9,8},{10,11... | collective-permute-start | bytes 2752520 | tf_op jit(solution)/shard_map/ppermute | solution.py:21
Sparse Core Ops, SparseCore 0:
  10.1 50.8 all-gather.5
  84.3 55.7 all-gather.7

commit v12 on v10

--- a/solution.py
+++ b/solution.py
@@ -100,12 +100,13 @@
     grad_own = lax.all_gather(hidden_grad, "yh", axis=0, tiled=True)
     grad_own, activated = lax.optimization_barrier((grad_own, along_z(activated, 1)))
     grad_other = swap_cores(grad_own)
+    activated = within_z(activated, True)
 
     ig_own = dot(grad_own, w_all, ((1,), (0,))).astype(BF)
     ig_own, grad_other = lax.optimization_barrier((ig_own, grad_other))
     ig_other = dot(grad_other, w_all, ((1,), (0,))).astype(BF)
     ig = cut(jnp.stack([ig_own, ig_other]).reshape(8, pair, feats), 16 - first, 8)
-    ig, grad_own, activated = lax.optimization_barrier((ig.reshape(16, rows, feats), grad_own, activated))
+    ig, grad_own = lax.optimization_barrier((ig.reshape(16, rows, feats), grad_own))
     ig = lax.all_to_all(ig, ("z", "yl"), split_axis=0, concat_axis=0)
 
     far = lax.all_gather(near, "x", axis=0, tiled=False)
@@ -117,7 +118,7 @@
     far_grad = jnp.stack([far_own, far_other], axis=1)
     weight_grad = dot(far.reshape(-1, feats), far_grad.reshape(-1, cols), ((0,), (0,))).astype(BF)
     out = in_order([part[4 * pair :] for part in both], here).reshape(NX * pair, cols)
-    ig, weight_grad, out = lax.optimization_barrier((ig, weight_grad, within_z(out, True)))
+    ig, weight_grad, out = lax.optimization_barrier((ig, weight_grad, out))
     input_grad = jnp.sum(ig.astype(jnp.float32), axis=0).astype(BF)
     return out, input_grad, weight_grad
 

time: 193 us -> 190 us (0.984)
  the two profiles are of different devices: /device:TPU:81 before, /device:TPU:1 now
where the time goes in v12:
time: 190 us; the launch traced here: 189 us
  starting transfers between devices  69.4 us (37%)
  waiting for transfers between devices  60.5 us (32%)
  blocking collectives  18.2 us (10%)
  matrix products  14.5 us (8%)
  between operations  14.5 us (8%)
  local copies, waits for them, and re-layouts  8.94 us (5%)
  other arithmetic  2.85 us (2%)
    ppermute x2, waiting for transfers between devices, within_z(): return lax.ppermute(value, ('z', 'yh', 'c'), pairs)  21.4 us
    ppermute x6, starting transfers between devices, along_x(): return lax.ppermute(value, 'x', [(i, (i + shift) % NX) for i in range(NX)])  18.7 us
    all_gather x1, blocking collectives, body(): grad_own = lax.all_gather(hidden_grad, 'yh', axis=0, tiled=True)  18.2 us
    ppermute x6, waiting for transfers between devices, along_x(): return lax.ppermute(value, 'x', [(i, (i + shift) % NX) for i in range(NX)])  16.5 us
    dot_general x5, matrix products, dot(): lax.dot_general(a, b, (contract, ((), ())), preferred_element_type=jnp.fl...  14.5 us
    all_to_all x1, starting transfers between devices, body(): lax.all_to_all(near, ('z', 'yl'), split_axis=0, concat_axis=0)  12 us
    ppermute x2, starting transfers between devices, within_z(): return lax.ppermute(value, ('z', 'yh', 'c'), pairs)  10 us
    ppermute x2, starting transfers between devices, along_z(): return lax.ppermute(value, ('z', 'yh', 'c'), pairs)  9.64 us
  transfers between devices with their start and end apart: 18, of which 10 were waited for; matrix products, arithmetic and copies ran while one was open for 12% of the time, Pallas kernels for 0%

profile of v12, /device:TPU:1, one launch (start us, length us, event | category | flops | bytes accessed | tf_op | source)
XLA Modules:
  0.0 188.9 jit_solution(12012324327594956503)
XLA Ops:
  7.9 1.8 broadcast_in_dim.41
  9.8 12.0 %all-to-all-start = ((bf16[16,32,896]{2,1,0:T(8,128)(2,1)}), bf16[16,32,896]{2,1,0:T(8,128)(2,1)S(1)}, u32[]{:S(2)}, u32[]{:S(2)}) async-start(bf16[16,32,896]{2,1,0:T(8,128)(2,1)} %broadcast_in_dim.41), calls=%async_computation | async-start | bytes 1835008 | tf_op jit(solution)/shard_map/all_to_all | solution.py:80
  21.9 5.0 %collective-permute-start = (bf16[256,448]{1,0:T(8,128)(2,1)S(1)}, bf16[256,448]{1,0:T(8,128)(2,1)S(1)}, u32[]{:S(2)}, u32[]{:S(2)}) collective-permute-start(bf16[256,448]{1,0:T(8,128)(2,1)S(1)} %copy.29), channel_id=1, source_target_pairs={{0,0},{4,1},{7,2},{3,3},{6,4},{2,5},{5,6},{1,7},{9,8},{13,9},{8,10... | collective-permute-start | bytes 688136 | tf_op jit(solution)/shard_map/ppermute | solution.py:42
  26.9 21.4 %collective-permute-done = bf16[256,448]{1,0:T(8,128)(2,1)S(1)} collective-permute-done((bf16[256,448]{1,0:T(8,128)(2,1)S(1)}, bf16[256,448]{1,0:T(8,128)(2,1)S(1)}, u32[]{:S(2)}, u32[]{:S(2)}) %collective-permute-start) | collective-permute-done | bytes 229408 | tf_op jit(solution)/shard_map/ppermute | solution.py:42
  48.3 1.9 %collective-permute-start.1 = (bf16[256,448]{1,0:T(8,128)(2,1)S(1)}, bf16[256,448]{1,0:T(8,128)(2,1)S(1)}, u32[]{:S(2)}, u32[]{:S(2)}) collective-permute-start(bf16[256,448]{1,0:T(8,128)(2,1)S(1)} %collective-permute-done), channel_id=1, source_target_pairs={{0,0},{1,33},{2,58},{3,27},{4,52},{5,21},{6,46},{7,15},{8,8},{9,41... | collective-permute-start | bytes 688136 | tf_op jit(solution)/shard_map/ppermute | solution.py:33
  50.2 9.1 %collective-permute-done.1 = bf16[256,448]{1,0:T(8,128)(2,1)S(1)} collective-permute-done((bf16[256,448]{1,0:T(8,128)(2,1)S(1)}, bf16[256,448]{1,0:T(8,128)(2,1)S(1)}, u32[]{:S(2)}, u32[]{:S(2)}) %collective-permute-start.1) | collective-permute-done | bytes 229408 | tf_op jit(solution)/shard_map/ppermute | solution.py:33
  59.3 1.7 all-gather.5.cloned.1.call-done
  62.4 3.2 %convolution_convert_fusion = bf16[256,1792]{1,0:T(8,128)(2,1)S(1)} fusion(bf16[1792,896]{1,0:T(8,128)(2,1)} %all-gather.5.cloned.1.call-done, bf16[1024,896]{1,0:T(8,128)(2,1)S(1)} %bitcast.77, u32[]{:T(128)S(6)} %mul.58), kind=kOutput, calls=%fused_computation.2 | convolution fusion | flops 822542336 | bytes 4587524 | tf_op jit(solution)/shard_map/dot_general | solution.py:67
  65.6 2.6 %collective-permute-start.2 = (bf16[256,1792]{1,0:T(8,128)(2,1)S(1)}, bf16[256,1792]{1,0:T(8,128)(2,1)S(1)}, u32[]{:S(2)}, u32[]{:S(2)}) collective-permute-start(bf16[256,1792]{1,0:T(8,128)(2,1)S(1)} %convolution_convert_fusion), channel_id=1, source_target_pairs={{0,1},{1,0},{2,3},{3,2},{4,5},{5,4},{6,7},{7,6},{8,9},{9,8},{10,11... | collective-permute-start | bytes 2752520 | tf_op jit(solution)/shard_map/ppermute | solution.py:21
  68.2 2.1 %collective-permute-done.2 = bf16[256,1792]{1,0:T(8,128)(2,1)S(1)} collective-permute-done((bf16[256,1792]{1,0:T(8,128)(2,1)S(1)}, bf16[256,1792]{1,0:T(8,128)(2,1)S(1)}, u32[]{:S(2)}, u32[]{:S(2)}) %collective-permute-start.2) | collective-permute-done | bytes 917536 | tf_op jit(solution)/shard_map/ppermute | solution.py:21
  70.3 2.2 %fusion = bf16[256,1792]{1,0:T(8,128)(2,1)} fusion(bf16[1792,896]{1,0:T(8,128)(2,1)S(1)} %copy-done.3, bf16[256,1792]{1,0:T(8,128)(2,1)S(1)} %collective-permute-done.2, bf16[1024,896]{1,0:T(8,128)(2,1)S(1)} %bitcast.78, u32[]{:T(128)S(6)} %mul.57), kind=kOutput, calls=%fused_computation.1 | convolution fusion | flops 823459840 | bytes 5505028 | tf_op jit(solution)/shard_map/dot_general | solution.py:67
  72.5 6.4 %all-to-all-start.1 = ((bf16[4,64,1792]{2,1,0:T(8,128)(2,1)}), bf16[4,64,1792]{2,1,0:T(8,128)(2,1)S(1)}, u32[]{:S(2)}, u32[]{:S(2)}) async-start(bf16[4,64,1792]{2,1,0:T(8,128)(2,1)} %bitcast.5), calls=%async_computation.1 | async-start | bytes 1835008 | tf_op jit(solution)/shard_map/all_to_all | solution.py:90
  79.0 2.3 %collective-permute-start.3 = (bf16[64,448]{1,0:T(8,128)(2,1)S(1)}, bf16[64,448]{1,0:T(8,128)(2,1)S(1)}, u32[]{:S(2)}, u32[]{:S(2)}) collective-permute-start(bf16[64,448]{1,0:T(8,128)(2,1)S(1)} %get-tuple-element.56), channel_id=1, source_target_pairs={{0,128},{128,256},{256,384},{384,0},{1,129},{129,257},{257,385},{3... | collective-permute-start | bytes 172040 | tf_op jit(solution)/shard_map/ppermute | solution.py:17
  81.3 3.4 %collective-permute-start.4 = (bf16[64,448]{1,0:T(8,128)(2,1)S(1)}, bf16[64,448]{1,0:T(8,128)(2,1)S(1)}, u32[]{:S(2)}, u32[]{:S(2)}) collective-permute-start(bf16[64,448]{1,0:T(8,128)(2,1)S(1)} %get-tuple-element.55), channel_id=1, source_target_pairs={{0,256},{128,384},{256,0},{384,128},{1,257},{129,385},{257,1},{385... | collective-permute-start | bytes 172040 | tf_op jit(solution)/shard_map/ppermute | solution.py:17
  84.7 3.7 %collective-permute-start.5 = (bf16[64,448]{1,0:T(8,128)(2,1)S(1)}, bf16[64,448]{1,0:T(8,128)(2,1)S(1)}, u32[]{:S(2)}, u32[]{:S(2)}) collective-permute-start(bf16[64,448]{1,0:T(8,128)(2,1)S(1)} %get-tuple-element.54), channel_id=1, source_target_pairs={{0,384},{128,0},{256,128},{384,256},{1,385},{129,1},{257,129},{385... | collective-permute-start | bytes 172040 | tf_op jit(solution)/shard_map/ppermute | solution.py:17
  88.4 1.3 collective-permute-done.4
  89.7 2.8 %collective-permute-done.5 = bf16[64,448]{1,0:T(8,128)(2,1)S(1)} collective-permute-done((bf16[64,448]{1,0:T(8,128)(2,1)S(1)}, bf16[64,448]{1,0:T(8,128)(2,1)S(1)}, u32[]{:S(2)}, u32[]{:S(2)}) %collective-permute-start.5) | collective-permute-done | bytes 57376 | tf_op jit(solution)/shard_map/ppermute | solution.py:17
  93.4 9.0 %all-to-all-done.1 = bf16[4,64,1792]{2,1,0:T(8,128)(2,1)S(1)} async-done(((bf16[4,64,1792]{2,1,0:T(8,128)(2,1)}), bf16[4,64,1792]{2,1,0:T(8,128)(2,1)S(1)}, u32[]{:S(2)}, u32[]{:S(2)}) %all-to-all-start.1) | async-done | bytes 917536 | tf_op jit(solution)/shard_map/all_to_all | solution.py:90
  102.8 7.7 %collective-permute-start.6 = (bf16[64,1792]{1,0:T(8,128)(2,1)S(1)}, bf16[64,1792]{1,0:T(8,128)(2,1)S(1)}, u32[]{:S(2)}, u32[]{:S(2)}) collective-permute-start(bf16[64,1792]{1,0:T(8,128)(2,1)S(1)} %get-tuple-element.52), channel_id=1, source_target_pairs={{0,0},{1,33},{2,10},{3,43},{4,20},{5,53},{6,30},{7,63},{8,8},{9,41... | collective-permute-start | bytes 688136 | tf_op jit(solution)/shard_map/ppermute | solution.py:33
  110.6 18.2 %all_gather.17 = bf16[256,1792]{1,0:T(8,128)(2,1)S(1)} all-gather(bf16[64,1792]{1,0:T(8,128)(2,1)S(1)} %get-tuple-element.53), channel_id=1, replica_groups=mesh['x'=4,'yl'=2,'z'=8,'yh'=4,'c'=2] {'yh'}, dimensions={0}, use_global_device_ids=true | all-gather | bytes 1146880 | tf_op jit(solution)/shard_map/all_gather | solution.py:100
  128.8 2.7 %collective-permute-start.7 = (bf16[256,1792]{1,0:T(8,128)(2,1)S(1)}, bf16[256,1792]{1,0:T(8,128)(2,1)S(1)}, u32[]{:S(2)}, u32[]{:S(2)}) collective-permute-start(bf16[256,1792]{1,0:T(8,128)(2,1)S(1)} %all_gather.17), channel_id=1, source_target_pairs={{0,1},{1,0},{2,3},{3,2},{4,5},{5,4},{6,7},{7,6},{8,9},{9,8},{10,11... | collective-permute-start | bytes 2752520 | tf_op jit(solution)/shard_map/ppermute | solution.py:21
  131.5 5.0 %collective-permute-start.8 = (bf16[64,1792]{1,0:T(8,128)(2,1)S(1)}, bf16[64,1792]{1,0:T(8,128)(2,1)S(1)}, u32[]{:S(2)}, u32[]{:S(2)}) collective-permute-start(bf16[64,1792]{1,0:T(8,128)(2,1)S(1)} %collective-permute-done.6), channel_id=1, source_target_pairs={{0,0},{1,4},{2,7},{3,3},{4,6},{5,2},{6,5},{7,1},{8,9},{9,13},{10,8... | collective-permute-start | bytes 688136 | tf_op jit(solution)/shard_map/ppermute | solution.py:42
  136.6 3.0 %convolution_convert_fusion.2 = bf16[256,896]{1,0:T(8,128)(2,1)S(1)} fusion(bf16[256,1792]{1,0:T(8,128)(2,1)S(1)} %all_gather.17, bf16[1792,896]{1,0:T(8,128)(2,1)} %all-gather.5.cloned.1.call-done), kind=kOutput, calls=%fused_computation.12 | convolution fusion | flops 822312960 | bytes 4587520 | tf_op jit(solution)/shard_map/dot_general | solution.py:67
  142.1 3.8 %all-to-all-start.2 = ((bf16[16,32,896]{2,1,0:T(8,128)(2,1)}), bf16[16,32,896]{2,1,0:T(8,128)(2,1)S(1)}, u32[]{:S(2)}, u32[]{:S(2)}) async-start(bf16[16,32,896]{2,1,0:T(8,128)(2,1)} %bitcast.18), calls=%async_computation.2 | async-start | bytes 1835008 | tf_op jit(solution)/shard_map/all_to_all | solution.py:110
  147.8 2.3 %collective-permute-start.9 = (bf16[320,448]{0,1:T(8,128)(2,1)}, bf16[320,448]{0,1:T(8,128)(2,1)S(1)}, u32[]{:S(2)}, u32[]{:S(2)}) collective-permute-start(bf16[320,448]{0,1:T(8,128)(2,1)} %get-tuple-element.50), channel_id=1, source_target_pairs={{0,128},{128,256},{256,384},{384,0},{1,129},{129,257},{257,385},{3... | collective-permute-start | bytes 860168 | tf_op jit(solution)/shard_map/ppermute | solution.py:17
  150.1 4.5 %collective-permute-start.10 = (bf16[320,448]{0,1:T(8,128)(2,1)S(1)}, bf16[320,448]{0,1:T(8,128)(2,1)S(1)}, u32[]{:S(2)}, u32[]{:S(2)}) collective-permute-start(bf16[320,448]{0,1:T(8,128)(2,1)S(1)} %get-tuple-element.49), channel_id=1, source_target_pairs={{0,256},{128,384},{256,0},{384,128},{1,257},{129,385},{257,1},{385... | collective-permute-start | bytes 860168 | tf_op jit(solution)/shard_map/ppermute | solution.py:17
  154.6 2.5 %collective-permute-start.11 = (bf16[320,448]{0,1:T(8,128)(2,1)S(1)}, bf16[320,448]{0,1:T(8,128)(2,1)S(1)}, u32[]{:S(2)}, u32[]{:S(2)}) collective-permute-start(bf16[320,448]{0,1:T(8,128)(2,1)S(1)} %get-tuple-element.48), channel_id=1, source_target_pairs={{0,384},{128,0},{256,128},{384,256},{1,385},{129,1},{257,129},{385... | collective-permute-start | bytes 860168 | tf_op jit(solution)/shard_map/ppermute | solution.py:17
  157.3 3.6 %collective-permute-done.9 = bf16[320,448]{0,1:T(8,128)(2,1)S(1)} collective-permute-done((bf16[320,448]{0,1:T(8,128)(2,1)}, bf16[320,448]{0,1:T(8,128)(2,1)S(1)}, u32[]{:S(2)}, u32[]{:S(2)}) %collective-permute-start.9) | collective-permute-done | bytes 286752 | tf_op jit(solution)/shard_map/ppermute | solution.py:17
  160.9 5.9 %collective-permute-done.10 = bf16[320,448]{0,1:T(8,128)(2,1)S(1)} collective-permute-done((bf16[320,448]{0,1:T(8,128)(2,1)S(1)}, bf16[320,448]{0,1:T(8,128)(2,1)S(1)}, u32[]{:S(2)}, u32[]{:S(2)}) %collective-permute-start.10) | collective-permute-done | bytes 286752 | tf_op jit(solution)/shard_map/ppermute | solution.py:17
  166.8 2.9 %collective-permute-done.11 = bf16[320,448]{0,1:T(8,128)(2,1)S(1)} collective-permute-done((bf16[320,448]{0,1:T(8,128)(2,1)S(1)}, bf16[320,448]{0,1:T(8,128)(2,1)S(1)}, u32[]{:S(2)}, u32[]{:S(2)}) %collective-permute-start.11) | collective-permute-done | bytes 286752 | tf_op jit(solution)/shard_map/ppermute | solution.py:17
  169.8 3.5 %collective-permute-start.12 = (bf16[4,256,448]{1,2,0:T(8,128)(2,1)S(1)}, bf16[4,256,448]{1,2,0:T(8,128)(2,1)S(1)}, u32[]{:S(2)}, u32[]{:S(2)}) collective-permute-start(bf16[4,256,448]{1,2,0:T(8,128)(2,1)S(1)} %fusion.17), channel_id=1, source_target_pairs={{0,1},{1,0},{2,3},{3,2},{4,5},{5,4},{6,7},{7,6},{8,9},{9,8},{10,11... | collective-permute-start | bytes 2752520 | tf_op jit(solution)/shard_map/ppermute | solution.py:21
  175.5 5.0 %bitcast_convert_fusion = bf16[896,448]{0,1:T(8,128)(2,1)} fusion(bf16[4,2,256,896]{3,2,1,0:T(8,128)(2,1)} %bitcast.87, bf16[4,1,256,448]{2,3,1,0:T(8,128)(2,1)S(1)} %bitcast.88, bf16[4,1,256,448]{2,3,1,0:T(8,128)(2,1)S(1)} %bitcast.83), kind=kOutput, calls=%fused_computation.10 | convolution fusion | flops 1645486080 | bytes 6307840 | tf_op jit(solution)/shard_map/dot_general | solution.py:67
  (63 shorter events, 11.9 us)
Async XLA Ops:
  7.2 14.6 %copy-start.2 = (bf16[256,448]{0,1:T(8,128)(2,1)S(1)}, bf16[256,448]{0,1:T(8,128)(2,1)}, u32[]{:S(2)}) copy-start(bf16[256,448]{0,1:T(8,128)(2,1)} %param.5) | copy-start | bytes 688132
  7.2 53.9 %all-gather.5.cloned.1.call-start = ((), (), s32[]{:S(2)}) async-start(), calls=%async_computation.3 | async-start | bytes 4014080 | tf_op jit(solution)/shard_map/all_gather | solution.py:77
  9.8 49.6 %all-to-all-start = ((bf16[16,32,896]{2,1,0:T(8,128)(2,1)}), bf16[16,32,896]{2,1,0:T(8,128)(2,1)S(1)}, u32[]{:S(2)}, u32[]{:S(2)}) async-start(bf16[16,32,896]{2,1,0:T(8,128)(2,1)} %broadcast_in_dim.41), calls=%async_computation | async-start | bytes 1835008 | tf_op jit(solution)/shard_map/all_to_all | solution.py:80
  21.7 124.1 %all-gather.7.cloned.1.call-start = ((), (), s32[]{:S(2)}) async-start(), calls=%async_computation.4 | async-start | bytes 4587520 | tf_op jit(solution)/shard_map/all_gather | solution.py:112
  21.9 26.4 %collective-permute-start = (bf16[256,448]{1,0:T(8,128)(2,1)S(1)}, bf16[256,448]{1,0:T(8,128)(2,1)S(1)}, u32[]{:S(2)}, u32[]{:S(2)}) collective-permute-start(bf16[256,448]{1,0:T(8,128)(2,1)S(1)} %copy.29), channel_id=1, source_target_pairs={{0,0},{4,1},{7,2},{3,3},{6,4},{2,5},{5,6},{1,7},{9,8},{13,9},{8,10... | collective-permute-start | bytes 688136 | tf_op jit(solution)/shard_map/ppermute | solution.py:42
  48.3 11.0 %collective-permute-start.1 = (bf16[256,448]{1,0:T(8,128)(2,1)S(1)}, bf16[256,448]{1,0:T(8,128)(2,1)S(1)}, u32[]{:S(2)}, u32[]{:S(2)}) collective-permute-start(bf16[256,448]{1,0:T(8,128)(2,1)S(1)} %collective-permute-done), channel_id=1, source_target_pairs={{0,0},{1,33},{2,58},{3,27},{4,52},{5,21},{6,46},{7,15},{8,8},{9,41... | collective-permute-start | bytes 688136 | tf_op jit(solution)/shard_map/ppermute | solution.py:33
  62.4 7.9 %copy-start.3 = (bf16[1792,896]{1,0:T(8,128)(2,1)S(1)}, bf16[1792,896]{1,0:T(8,128)(2,1)}, u32[]{:S(2)}) copy-start(bf16[1792,896]{1,0:T(8,128)(2,1)} %all-gather.5.cloned.1.call-done) | copy-start | bytes 9633796
  65.6 4.7 %collective-permute-start.2 = (bf16[256,1792]{1,0:T(8,128)(2,1)S(1)}, bf16[256,1792]{1,0:T(8,128)(2,1)S(1)}, u32[]{:S(2)}, u32[]{:S(2)}) collective-permute-start(bf16[256,1792]{1,0:T(8,128)(2,1)S(1)} %convolution_convert_fusion), channel_id=1, source_target_pairs={{0,1},{1,0},{2,3},{3,2},{4,5},{5,4},{6,7},{7,6},{8,9},{9,8},{10,11... | collective-permute-start | bytes 2752520 | tf_op jit(solution)/shard_map/ppermute | solution.py:21
  72.5 29.9 %all-to-all-start.1 = ((bf16[4,64,1792]{2,1,0:T(8,128)(2,1)}), bf16[4,64,1792]{2,1,0:T(8,128)(2,1)S(1)}, u32[]{:S(2)}, u32[]{:S(2)}) async-start(bf16[4,64,1792]{2,1,0:T(8,128)(2,1)} %bitcast.5), calls=%async_computation.1 | async-start | bytes 1835008 | tf_op jit(solution)/shard_map/all_to_all | solution.py:90
  79.0 9.5 %collective-permute-start.3 = (bf16[64,448]{1,0:T(8,128)(2,1)S(1)}, bf16[64,448]{1,0:T(8,128)(2,1)S(1)}, u32[]{:S(2)}, u32[]{:S(2)}) collective-permute-start(bf16[64,448]{1,0:T(8,128)(2,1)S(1)} %get-tuple-element.56), channel_id=1, source_target_pairs={{0,128},{128,256},{256,384},{384,0},{1,129},{129,257},{257,385},{3... | collective-permute-start | bytes 172040 | tf_op jit(solution)/shard_map/ppermute | solution.py:17
  81.3 8.4 %collective-permute-start.4 = (bf16[64,448]{1,0:T(8,128)(2,1)S(1)}, bf16[64,448]{1,0:T(8,128)(2,1)S(1)}, u32[]{:S(2)}, u32[]{:S(2)}) collective-permute-start(bf16[64,448]{1,0:T(8,128)(2,1)S(1)} %get-tuple-element.55), channel_id=1, source_target_pairs={{0,256},{128,384},{256,0},{384,128},{1,257},{129,385},{257,1},{385... | collective-permute-start | bytes 172040 | tf_op jit(solution)/shard_map/ppermute | solution.py:17
  84.7 7.8 %collective-permute-start.5 = (bf16[64,448]{1,0:T(8,128)(2,1)S(1)}, bf16[64,448]{1,0:T(8,128)(2,1)S(1)}, u32[]{:S(2)}, u32[]{:S(2)}) collective-permute-start(bf16[64,448]{1,0:T(8,128)(2,1)S(1)} %get-tuple-element.54), channel_id=1, source_target_pairs={{0,384},{128,0},{256,128},{384,256},{1,385},{129,1},{257,129},{385... | collective-permute-start | bytes 172040 | tf_op jit(solution)/shard_map/ppermute | solution.py:17
  102.8 26.0 %collective-permute-start.6 = (bf16[64,1792]{1,0:T(8,128)(2,1)S(1)}, bf16[64,1792]{1,0:T(8,128)(2,1)S(1)}, u32[]{:S(2)}, u32[]{:S(2)}) collective-permute-start(bf16[64,1792]{1,0:T(8,128)(2,1)S(1)} %get-tuple-element.52), channel_id=1, source_target_pairs={{0,0},{1,33},{2,10},{3,43},{4,20},{5,53},{6,30},{7,63},{8,8},{9,41... | collective-permute-start | bytes 688136 | tf_op jit(solution)/shard_map/ppermute | solution.py:33
  128.8 10.8 %collective-permute-start.7 = (bf16[256,1792]{1,0:T(8,128)(2,1)S(1)}, bf16[256,1792]{1,0:T(8,128)(2,1)S(1)}, u32[]{:S(2)}, u32[]{:S(2)}) collective-permute-start(bf16[256,1792]{1,0:T(8,128)(2,1)S(1)} %all_gather.17), channel_id=1, source_target_pairs={{0,1},{1,0},{2,3},{3,2},{4,5},{5,4},{6,7},{7,6},{8,9},{9,8},{10,11... | collective-permute-start | bytes 2752520 | tf_op jit(solution)/shard_map/ppermute | solution.py:21
  131.5 8.1 %copy-start.4 = (bf16[1792,896]{1,0:T(8,128)(2,1)S(1)}, bf16[1792,896]{1,0:T(8,128)(2,1)}, u32[]{:S(2)}) copy-start(bf16[1792,896]{1,0:T(8,128)(2,1)} %all-gather.5.cloned.1.call-done) | copy-start | bytes 9633796
  131.5 14.3 %collective-permute-start.8 = (bf16[64,1792]{1,0:T(8,128)(2,1)S(1)}, bf16[64,1792]{1,0:T(8,128)(2,1)S(1)}, u32[]{:S(2)}, u32[]{:S(2)}) collective-permute-start(bf16[64,1792]{1,0:T(8,128)(2,1)S(1)} %collective-permute-done.6), channel_id=1, source_target_pairs={{0,0},{1,4},{2,7},{3,3},{4,6},{5,2},{6,5},{7,1},{8,9},{9,13},{10,8... | collective-permute-start | bytes 688136 | tf_op jit(solution)/shard_map/ppermute | solution.py:42
  142.1 38.4 %all-to-all-start.2 = ((bf16[16,32,896]{2,1,0:T(8,128)(2,1)}), bf16[16,32,896]{2,1,0:T(8,128)(2,1)S(1)}, u32[]{:S(2)}, u32[]{:S(2)}) async-start(bf16[16,32,896]{2,1,0:T(8,128)(2,1)} %bitcast.18), calls=%async_computation.2 | async-start | bytes 1835008 | tf_op jit(solution)/shard_map/all_to_all | solution.py:110
  147.8 13.1 %collective-permute-start.9 = (bf16[320,448]{0,1:T(8,128)(2,1)}, bf16[320,448]{0,1:T(8,128)(2,1)S(1)}, u32[]{:S(2)}, u32[]{:S(2)}) collective-permute-start(bf16[320,448]{0,1:T(8,128)(2,1)} %get-tuple-element.50), channel_id=1, source_target_pairs={{0,128},{128,256},{256,384},{384,0},{1,129},{129,257},{257,385},{3... | collective-permute-start | bytes 860168 | tf_op jit(solution)/shard_map/ppermute | solution.py:17
  150.1 16.7 %collective-permute-start.10 = (bf16[320,448]{0,1:T(8,128)(2,1)S(1)}, bf16[320,448]{0,1:T(8,128)(2,1)S(1)}, u32[]{:S(2)}, u32[]{:S(2)}) collective-permute-start(bf16[320,448]{0,1:T(8,128)(2,1)S(1)} %get-tuple-element.49), channel_id=1, source_target_pairs={{0,256},{128,384},{256,0},{384,128},{1,257},{129,385},{257,1},{385... | collective-permute-start | bytes 860168 | tf_op jit(solution)/shard_map/ppermute | solution.py:17
  154.6 15.1 %collective-permute-start.11 = (bf16[320,448]{0,1:T(8,128)(2,1)S(1)}, bf16[320,448]{0,1:T(8,128)(2,1)S(1)}, u32[]{:S(2)}, u32[]{:S(2)}) collective-permute-start(bf16[320,448]{0,1:T(8,128)(2,1)S(1)} %get-tuple-element.48), channel_id=1, source_target_pairs={{0,384},{128,0},{256,128},{384,256},{1,385},{129,1},{257,129},{385... | collective-permute-start | bytes 860168 | tf_op jit(solution)/shard_map/ppermute | solution.py:17
  166.8 3.0 %copy-start = (bf16[320,448]{0,1:T(8,128)(2,1)}, bf16[320,448]{0,1:T(8,128)(2,1)S(1)}, u32[]{:S(2)}) copy-start(bf16[320,448]{0,1:T(8,128)(2,1)S(1)} %collective-permute-done.10) | copy-start | bytes 860164
  169.8 3.5 %copy-start.1 = (bf16[320,448]{0,1:T(8,128)(2,1)}, bf16[320,448]{0,1:T(8,128)(2,1)S(1)}, u32[]{:S(2)}) copy-start(bf16[320,448]{0,1:T(8,128)(2,1)S(1)} %collective-permute-done.11) | copy-start | bytes 860164
  169.8 5.7 %collective-permute-start.12 = (bf16[4,256,448]{1,2,0:T(8,128)(2,1)S(1)}, bf16[4,256,448]{1,2,0:T(8,128)(2,1)S(1)}, u32[]{:S(2)}, u32[]{:S(2)}) collective-permute-start(bf16[4,256,448]{1,2,0:T(8,128)(2,1)S(1)} %fusion.17), channel_id=1, source_target_pairs={{0,1},{1,0},{2,3},{3,2},{4,5},{5,4},{6,7},{7,6},{8,9},{9,8},{10,11... | collective-permute-start | bytes 2752520 | tf_op jit(solution)/shard_map/ppermute | solution.py:21
Sparse Core Ops, SparseCore 0:
  10.1 50.8 all-gather.4
  63.1 52.2 all-gather.6

commit v13 on v12

--- a/solution.py
+++ b/solution.py
@@ -6,6 +6,7 @@
 
 AXES = ("x", "yl", "z", "yh", "c")
 NX = 4
+SPLIT = 512
 BF = jnp.bfloat16
 
 
@@ -74,24 +75,35 @@
     here = lax.axis_index("x").astype(jnp.uint32)
     first = lax.axis_index("z").astype(jnp.uint32) + 4 * lax.axis_index("c").astype(jnp.uint32)
 
-    w_all = lax.all_gather(w_up.T, "x", axis=0, tiled=False)
+    w_low = lax.all_gather(w_up.T[:, :SPLIT], "x", axis=0, tiled=True)
+    w_own = w_up.T[:, SPLIT:]
+    w_high = jnp.zeros((NX,) + w_own.shape, BF)
+    for r in range(NX):
+        block = along_x(w_own, -r) if r else w_own
+        w_high = lax.dynamic_update_index_in_dim(w_high, block, (here + r) & (NX - 1), 0)
+    w_high = w_high.reshape(NX * cols, feats - SPLIT)
 
     near = jnp.broadcast_to(tokens[None], (16, rows, feats))
     near = lax.all_to_all(near, ("z", "yl"), split_axis=0, concat_axis=0).reshape(8, pair, feats)
-    cot = along_z(within_z(act_grad, False), -1)
-    near, cot, w_all = lax.optimization_barrier((near, cot, w_all))
+    near, cot = lax.optimization_barrier((near, within_z(act_grad, False)))
+    cot = along_z(cot, -1)
     near = jnp.stack([cut(near, first, 4), cut(near, first + 4, 4)])
-    w_all = w_all.reshape(NX * cols, feats)
 
-    sent = swap_cores(dot(near[1], w_all, ((1,), (1,))).astype(BF))
-    partial_value = (dot(near[0], w_all, ((1,), (1,))) + sent.astype(jnp.float32)).astype(BF)
+    def hidden_part(part):
+        low = dot(part[:, :SPLIT], w_low, ((1,), (1,)))
+        return low + dot(part[:, SPLIT:], w_high, ((1,), (1,)))
+
+    sent = swap_cores(hidden_part(near[1]).astype(BF))
+    partial_value = (hidden_part(near[0]) + sent.astype(jnp.float32)).astype(BF)
     partial_value = partial_value.reshape(4, pair, NX * cols)
-    partial_value, cot = lax.optimization_barrier((partial_value, cot))
+    partial_value, w_low, w_high = lax.optimization_barrier((partial_value, w_low, w_high))
+    w_all = jnp.concatenate([w_low, w_high], axis=1)
     parts = lax.all_to_all(partial_value, "yh", split_axis=0, concat_axis=0)
     hidden = jnp.sum(parts.astype(jnp.float32), axis=0)
 
     cot = in_order(shift_blocks(cot.reshape(NX, pair, cols), here), here)
     cot = cot.transpose(1, 0, 2).reshape(pair, NX * cols)
+    cot, w_all = lax.optimization_barrier((cot, w_all))
 
     activated, pullback = jax.vjp(gelu_tanh, hidden)
     hidden_grad = pullback(cot.astype(jnp.float32))[0].astype(BF)

time: 190 us -> 199 us (1.047)
  waiting for transfers between devices: 60.5 us -> 35.1 us
  starting transfers between devices: 69.4 us -> 81.2 us
  local copies, waits for them, and re-layouts: 8.94 us -> 16.2 us
  blocking collectives: 18.2 us -> 25.3 us
  other arithmetic: 2.85 us -> 7.68 us
  matrix products: 14.5 us -> 17.3 us
    ppermute x2, waiting for transfers between devices: 21.4 us -> 0.01 us  [within_z(): return lax.ppermute(value, ('z', 'yh', 'c'), pairs)]
    ppermute x6 -> x9, waiting for transfers between devices: 16.5 us -> 32 us  [along_x(): return lax.ppermute(value, 'x', [(i, (i + shift) % NX) for i in range(NX)])]
    ppermute x6 -> x9, starting transfers between devices: 18.7 us -> 31.2 us  [along_x(): return lax.ppermute(value, 'x', [(i, (i + shift) % NX) for i in range(NX)])]
    ppermute x2, waiting for transfers between devices: 9.09 us -> 0.01 us  [along_z(): return lax.ppermute(value, ('z', 'yh', 'c'), pairs)]
    all_to_all x1, waiting for transfers between devices: 8.99 us -> 0.01 us  [body(): parts = lax.all_to_all(partial_value, 'yh', split_axis=0, concat_axis=0)]
    all_gather x1, blocking collectives: 18.2 us -> 25.3 us  [body(): grad_own = lax.all_gather(hidden_grad, 'yh', axis=0, tiled=True)]
    dynamic_update_slice x0 -> x4, local copies, waits for them, and re-layouts: none -> 3.16 us  [body(): lax.dynamic_update_index_in_dim(w_high, block, here + r & NX - 1, 0)]
    dot_general x5 -> x7, matrix products: 14.5 us -> 17.3 us  [dot(): lax.dot_general(a, b, (contract, ((), ())), preferred_element_type=jnp.fl...]
  transfers between devices with their start and end apart: 18 -> 21, of which waited for: 10 -> 8; matrix products, arithmetic and copies ran while one was open for 12% -> 19% of each run, Pallas kernels for 0% -> 0%
where the time goes in v13:
time: 199 us; the launch traced here: 197 us
  starting transfers between devices  81.2 us (41%)
  waiting for transfers between devices  35.1 us (18%)
  blocking collectives  25.3 us (13%)
  matrix products  17.3 us (9%)
  local copies, waits for them, and re-layouts  16.2 us (8%)
  between operations  14.7 us (7%)
  other arithmetic  7.68 us (4%)
    ppermute x9, waiting for transfers between devices, along_x(): return lax.ppermute(value, 'x', [(i, (i + shift) % NX) for i in range(NX)])  32 us
    ppermute x9, starting transfers between devices, along_x(): return lax.ppermute(value, 'x', [(i, (i + shift) % NX) for i in range(NX)])  31.2 us
    all_gather x1, blocking collectives, body(): grad_own = lax.all_gather(hidden_grad, 'yh', axis=0, tiled=True)  25.3 us
    dot_general x7, matrix products, dot(): lax.dot_general(a, b, (contract, ((), ())), preferred_element_type=jnp.fl...  17.3 us
    all_to_all x1, starting transfers between devices, body(): lax.all_to_all(near, ('z', 'yl'), split_axis=0, concat_axis=0)  12 us
    ppermute x2, starting transfers between devices, within_z(): return lax.ppermute(value, ('z', 'yh', 'c'), pairs)  10.1 us
    ppermute x2, starting transfers between devices, along_z(): return lax.ppermute(value, ('z', 'yh', 'c'), pairs)  9.68 us
    ppermute x3, starting transfers between devices, swap_cores(): return lax.ppermute(value, 'c', [(0, 1), (1, 0)])  9.36 us
  transfers between devices with their start and end apart: 21, of which 8 were waited for; matrix products, arithmetic and copies ran while one was open for 19% of the time, Pallas kernels for 0%

profile of v13, /device:TPU:1, one launch (start us, length us, event | category | flops | bytes accessed | tf_op | source)
XLA Modules:
  0.0 197.4 jit_solution(3113331454678651975)
XLA Ops:
  9.1 1.9 broadcast_in_dim.57
  11.0 12.0 %all-to-all-start = ((bf16[16,32,896]{2,1,0:T(8,128)(2,1)}), bf16[16,32,896]{2,1,0:T(8,128)(2,1)S(1)}, u32[]{:S(2)}, u32[]{:S(2)}) async-start(bf16[16,32,896]{2,1,0:T(8,128)(2,1)} %broadcast_in_dim.57), calls=%async_computation | async-start | bytes 1835008 | tf_op jit(solution)/shard_map/all_to_all | solution.py:87
  23.1 4.4 %collective-permute-start.5 = (bf16[448,384]{1,0:T(8,128)(2,1)S(1)}, bf16[448,384]{1,0:T(8,128)(2,1)}, u32[]{:S(2)}, u32[]{:S(2)}) collective-permute-start(bf16[448,384]{1,0:T(8,128)(2,1)S(1)} %slice.59), channel_id=1, source_target_pairs={{0,384},{128,0},{256,128},{384,256},{1,385},{129,1},{257,129},{385... | collective-permute-start | bytes 1032200 | tf_op jit(solution)/shard_map/ppermute | solution.py:18
  27.5 2.4 %collective-permute-start.6 = (bf16[448,384]{1,0:T(8,128)(2,1)S(1)}, bf16[448,384]{1,0:T(8,128)(2,1)}, u32[]{:S(2)}, u32[]{:S(2)}) collective-permute-start(bf16[448,384]{1,0:T(8,128)(2,1)S(1)} %slice.59), channel_id=1, source_target_pairs={{0,256},{128,384},{256,0},{384,128},{1,257},{129,385},{257,1},{385... | collective-permute-start | bytes 1032200 | tf_op jit(solution)/shard_map/ppermute | solution.py:18
  29.9 2.5 %collective-permute-start.7 = (bf16[448,384]{1,0:T(8,128)(2,1)S(1)}, bf16[448,384]{1,0:T(8,128)(2,1)}, u32[]{:S(2)}, u32[]{:S(2)}) collective-permute-start(bf16[448,384]{1,0:T(8,128)(2,1)S(1)} %slice.59), channel_id=1, source_target_pairs={{0,128},{128,256},{256,384},{384,0},{1,129},{129,257},{257,385},{3... | collective-permute-start | bytes 1032200 | tf_op jit(solution)/shard_map/ppermute | solution.py:18
  33.3 5.0 %collective-permute-start = (bf16[256,448]{1,0:T(8,128)(2,1)}, bf16[256,448]{1,0:T(8,128)(2,1)}, u32[]{:S(2)}, u32[]{:S(2)}) collective-permute-start(bf16[256,448]{1,0:T(8,128)(2,1)} %copy.29), channel_id=1, source_target_pairs={{0,0},{4,1},{7,2},{3,3},{6,4},{2,5},{5,6},{1,7},{9,8},{13,9},{8,10... | collective-permute-start | bytes 688136 | tf_op jit(solution)/shard_map/ppermute | solution.py:43
  39.6 3.3 %collective-permute-done.6 = bf16[448,384]{1,0:T(8,128)(2,1)} collective-permute-done((bf16[448,384]{1,0:T(8,128)(2,1)S(1)}, bf16[448,384]{1,0:T(8,128)(2,1)}, u32[]{:S(2)}, u32[]{:S(2)}) %collective-permute-start.6) | collective-permute-done | bytes 344096 | tf_op jit(solution)/shard_map/ppermute | solution.py:18
  43.9 11.6 %collective-permute-done.7 = bf16[448,384]{1,0:T(8,128)(2,1)} collective-permute-done((bf16[448,384]{1,0:T(8,128)(2,1)S(1)}, bf16[448,384]{1,0:T(8,128)(2,1)}, u32[]{:S(2)}, u32[]{:S(2)}) %collective-permute-start.7) | collective-permute-done | bytes 344096 | tf_op jit(solution)/shard_map/ppermute | solution.py:18
  60.5 3.0 %all-gather.4.cloned.1.call-done = bf16[1792,512]{1,0:T(8,128)(2,1)} async-done(((bf16[448,512]{1,0:T(8,128)(2,1)}), bf16[1792,512]{1,0:T(8,128)(2,1)}) %all-gather.4.cloned.1.call-update) | async-done | bytes 1835024 | tf_op jit(solution)/shard_map/all_gather | solution.py:78
  63.4 2.2 %fusion.20 = f32[256,1792]{1,0:T(8,128)S(1)} fusion(bf16[1792,512]{1,0:T(8,128)(2,1)} %all-gather.4.cloned.1.call-done, bf16[1024,896]{1,0:T(8,128)(2,1)S(1)} %bitcast.87, u32[]{:T(128)S(6)} %mul.58), kind=kOutput, calls=%fused_computation.45 | convolution fusion | flops 469762048 | bytes 3932164 | tf_op jit(solution)/shard_map/dot_general | solution.py:68
  67.4 2.4 %collective-permute-start.8 = (bf16[256,1792]{1,0:T(8,128)(2,1)S(1)}, bf16[256,1792]{1,0:T(8,128)(2,1)S(1)}, u32[]{:S(2)}, u32[]{:S(2)}) collective-permute-start(bf16[256,1792]{1,0:T(8,128)(2,1)S(1)} %fusion.2), channel_id=1, source_target_pairs={{0,1},{1,0},{2,3},{3,2},{4,5},{5,4},{6,7},{7,6},{8,9},{9,8},{10,11... | collective-permute-start | bytes 2752520 | tf_op jit(solution)/shard_map/ppermute | solution.py:22
  69.7 7.2 %collective-permute-start.1 = (bf16[256,448]{1,0:T(8,128)(2,1)}, bf16[256,448]{1,0:T(8,128)(2,1)S(1)}, u32[]{:S(2)}, u32[]{:S(2)}) collective-permute-start(bf16[256,448]{1,0:T(8,128)(2,1)} %collective-permute-done), channel_id=1, source_target_pairs={{0,0},{1,33},{2,58},{3,27},{4,52},{5,21},{6,46},{7,15},{8,8},{9,41... | collective-permute-start | bytes 688136 | tf_op jit(solution)/shard_map/ppermute | solution.py:34
  78.6 2.6 %fusion.1 = bf16[256,1792]{1,0:T(8,128)(2,1)} fusion(f32[256,1792]{1,0:T(8,128)S(1)} %fusion.22, bf16[1792,384]{1,0:T(8,128)(2,1)S(1)} %bitcast.84, bf16[256,1792]{1,0:T(8,128)(2,1)S(1)} %collective-permute-done.8, bf16[1024,896]{1,0:T(8,128)(2,1)} %bitcast.90, u32[]{:T(128)S(6)} %mul.57, u32[]{:T(128)S(6)} %convert.1), kind=kOutput, calls=%fused_computation.4 | convolution fusion | flops 354156544 | bytes 5242888 | tf_op jit(solution)/shard_map/dot_general | solution.py:68
  81.2 4.2 %all-to-all-start.1 = ((bf16[4,64,1792]{2,1,0:T(8,128)(2,1)}), bf16[4,64,1792]{2,1,0:T(8,128)(2,1)}, u32[]{:S(2)}, u32[]{:S(2)}) async-start(bf16[4,64,1792]{2,1,0:T(8,128)(2,1)} %bitcast.94), calls=%async_computation.1 | async-start | bytes 1835008 | tf_op jit(solution)/shard_map/all_to_all | solution.py:101
  85.5 2.2 %collective-permute-start.2 = (bf16[64,448]{1,0:T(8,128)(2,1)S(1)}, bf16[64,448]{1,0:T(8,128)(2,1)S(1)}, u32[]{:S(2)}, u32[]{:S(2)}) collective-permute-start(bf16[64,448]{1,0:T(8,128)(2,1)S(1)} %get-tuple-element.60), channel_id=1, source_target_pairs={{0,128},{128,256},{256,384},{384,0},{1,129},{129,257},{257,385},{3... | collective-permute-start | bytes 172040 | tf_op jit(solution)/shard_map/ppermute | solution.py:18
  87.6 7.5 %collective-permute-start.3 = (bf16[64,448]{1,0:T(8,128)(2,1)S(1)}, bf16[64,448]{1,0:T(8,128)(2,1)S(1)}, u32[]{:S(2)}, u32[]{:S(2)}) collective-permute-start(bf16[64,448]{1,0:T(8,128)(2,1)S(1)} %get-tuple-element.59), channel_id=1, source_target_pairs={{0,256},{128,384},{256,0},{384,128},{1,257},{129,385},{257,1},{385... | collective-permute-start | bytes 172040 | tf_op jit(solution)/shard_map/ppermute | solution.py:18
  95.1 1.9 collective-permute-start.4
  97.1 3.0 %collective-permute-done.3 = bf16[64,448]{1,0:T(8,128)(2,1)S(1)} collective-permute-done((bf16[64,448]{1,0:T(8,128)(2,1)S(1)}, bf16[64,448]{1,0:T(8,128)(2,1)S(1)}, u32[]{:S(2)}, u32[]{:S(2)}) %collective-permute-start.3) | collective-permute-done | bytes 57376 | tf_op jit(solution)/shard_map/ppermute | solution.py:18
  100.1 2.4 %collective-permute-done.4 = bf16[64,448]{1,0:T(8,128)(2,1)S(1)} collective-permute-done((bf16[64,448]{1,0:T(8,128)(2,1)S(1)}, bf16[64,448]{1,0:T(8,128)(2,1)S(1)}, u32[]{:S(2)}, u32[]{:S(2)}) %collective-permute-start.4) | collective-permute-done | bytes 57376 | tf_op jit(solution)/shard_map/ppermute | solution.py:18
  103.6 2.0 %pad_maximum_fusion = bf16[1792,896]{1,0:T(8,128)(2,1)} fusion(bf16[1792,384]{1,0:T(8,128)(2,1)S(1)} %bitcast.85, bf16[1792,512]{1,0:T(8,128)(2,1)S(1)} %copy-done), kind=kLoop, calls=%fused_computation | loop fusion | flops 6422528 | bytes 6422528 | tf_op jit(solution)/shard_map/concatenate | solution.py:100
  107.4 2.5 %collective-permute-start.9 = (bf16[64,1792]{1,0:T(8,128)(2,1)S(1)}, bf16[64,1792]{1,0:T(8,128)(2,1)S(1)}, u32[]{:S(2)}, u32[]{:S(2)}) collective-permute-start(bf16[64,1792]{1,0:T(8,128)(2,1)S(1)} %get-tuple-element.56), channel_id=1, source_target_pairs={{0,0},{1,33},{2,10},{3,43},{4,20},{5,53},{6,30},{7,63},{8,8},{9,41... | collective-permute-start | bytes 688136 | tf_op jit(solution)/shard_map/ppermute | solution.py:34
  109.9 25.3 %all_gather.13 = bf16[256,1792]{1,0:T(8,128)(2,1)S(1)} all-gather(bf16[64,1792]{1,0:T(8,128)(2,1)S(1)} %get-tuple-element.57), channel_id=1, replica_groups=mesh['x'=4,'yl'=2,'z'=8,'yh'=4,'c'=2] {'yh'}, dimensions={0}, use_global_device_ids=true | all-gather | bytes 1146880 | tf_op jit(solution)/shard_map/all_gather | solution.py:112
  135.2 3.2 %collective-permute-start.10 = (bf16[256,1792]{1,0:T(8,128)(2,1)S(1)}, bf16[256,1792]{1,0:T(8,128)(2,1)S(1)}, u32[]{:S(2)}, u32[]{:S(2)}) collective-permute-start(bf16[256,1792]{1,0:T(8,128)(2,1)S(1)} %all_gather.13), channel_id=1, source_target_pairs={{0,1},{1,0},{2,3},{3,2},{4,5},{5,4},{6,7},{7,6},{8,9},{9,8},{10,11... | collective-permute-start | bytes 2752520 | tf_op jit(solution)/shard_map/ppermute | solution.py:22
  138.4 5.1 %collective-permute-start.11 = (bf16[64,1792]{1,0:T(8,128)(2,1)S(1)}, bf16[64,1792]{1,0:T(8,128)(2,1)S(1)}, u32[]{:S(2)}, u32[]{:S(2)}) collective-permute-start(bf16[64,1792]{1,0:T(8,128)(2,1)S(1)} %collective-permute-done.9), channel_id=1, source_target_pairs={{0,0},{1,4},{2,7},{3,3},{4,6},{5,2},{6,5},{7,1},{8,9},{9,13},{10,8... | collective-permute-start | bytes 688136 | tf_op jit(solution)/shard_map/ppermute | solution.py:43
  143.5 3.0 %convolution_convert_fusion.1 = bf16[256,896]{1,0:T(8,128)(2,1)S(1)} fusion(bf16[256,1792]{1,0:T(8,128)(2,1)S(1)} %all_gather.13, bf16[1792,896]{1,0:T(8,128)(2,1)} %pad_maximum_fusion), kind=kOutput, calls=%fused_computation.15 | convolution fusion | flops 822312960 | bytes 4587520 | tf_op jit(solution)/shard_map/dot_general | solution.py:68
  149.0 4.6 %all-to-all-start.2 = ((bf16[16,32,896]{2,1,0:T(8,128)(2,1)}), bf16[16,32,896]{2,1,0:T(8,128)(2,1)S(1)}, u32[]{:S(2)}, u32[]{:S(2)}) async-start(bf16[16,32,896]{2,1,0:T(8,128)(2,1)} %bitcast.21), calls=%async_computation.2 | async-start | bytes 1835008 | tf_op jit(solution)/shard_map/all_to_all | solution.py:122
  157.5 6.5 %collective-permute-start.13 = (bf16[320,448]{0,1:T(8,128)(2,1)S(1)}, bf16[320,448]{0,1:T(8,128)(2,1)S(1)}, u32[]{:S(2)}, u32[]{:S(2)}) collective-permute-start(bf16[320,448]{0,1:T(8,128)(2,1)S(1)} %get-tuple-element.53), channel_id=1, source_target_pairs={{0,256},{128,384},{256,0},{384,128},{1,257},{129,385},{257,1},{385... | collective-permute-start | bytes 860168 | tf_op jit(solution)/shard_map/ppermute | solution.py:18
  164.0 1.9 collective-permute-start.14
  167.4 8.2 %collective-permute-done.13 = bf16[320,448]{0,1:T(8,128)(2,1)S(1)} collective-permute-done((bf16[320,448]{0,1:T(8,128)(2,1)S(1)}, bf16[320,448]{0,1:T(8,128)(2,1)S(1)}, u32[]{:S(2)}, u32[]{:S(2)}) %collective-permute-start.13) | collective-permute-done | bytes 286752 | tf_op jit(solution)/shard_map/ppermute | solution.py:18
  175.7 2.2 %collective-permute-done.14 = bf16[320,448]{0,1:T(8,128)(2,1)S(1)} collective-permute-done((bf16[320,448]{0,1:T(8,128)(2,1)S(1)}, bf16[320,448]{0,1:T(8,128)(2,1)S(1)}, u32[]{:S(2)}, u32[]{:S(2)}) %collective-permute-start.14) | collective-permute-done | bytes 286752 | tf_op jit(solution)/shard_map/ppermute | solution.py:18
  177.9 3.8 %collective-permute-start.15 = (bf16[4,256,448]{1,2,0:T(8,128)(2,1)S(1)}, bf16[4,256,448]{1,2,0:T(8,128)(2,1)S(1)}, u32[]{:S(2)}, u32[]{:S(2)}) collective-permute-start(bf16[4,256,448]{1,2,0:T(8,128)(2,1)S(1)} %fusion.24), channel_id=1, source_target_pairs={{0,1},{1,0},{2,3},{3,2},{4,5},{5,4},{6,7},{7,6},{8,9},{9,8},{10,11... | collective-permute-start | bytes 2752520 | tf_op jit(solution)/shard_map/ppermute | solution.py:22
  184.0 5.0 %bitcast_convert_fusion = bf16[896,448]{0,1:T(8,128)(2,1)} fusion(bf16[4,2,256,896]{3,2,1,0:T(8,128)(2,1)} %bitcast.104, bf16[4,1,256,448]{2,3,1,0:T(8,128)(2,1)S(1)} %bitcast.105, bf16[4,1,256,448]{2,3,1,0:T(8,128)(2,1)S(1)} %bitcast.101), kind=kOutput, calls=%fused_computation.13 | convolution fusion | flops 1645486080 | bytes 6307840 | tf_op jit(solution)/shard_map/dot_general | solution.py:68
  (86 shorter events, 27.9 us)
Async XLA Ops:
  7.2 56.2 %all-gather.4.cloned.1.call-start = ((), (), s32[]{:S(2)}) async-start(), calls=%async_computation.3 | async-start | bytes 2293760 | tf_op jit(solution)/shard_map/all_gather | solution.py:78
  9.0 14.0 %copy-start.4 = (bf16[896,448]{0,1:T(8,128)(2,1)S(1)}, bf16[896,448]{0,1:T(8,128)(2,1)}, u32[]{:S(2)}) copy-start(bf16[896,448]{0,1:T(8,128)(2,1)} %param.4) | copy-start | bytes 2408452
  9.1 23.4 %copy-start.8 = (bf16[256,448]{0,1:T(8,128)(2,1)S(1)}, bf16[256,448]{0,1:T(8,128)(2,1)}, u32[]{:S(2)}) copy-start(bf16[256,448]{0,1:T(8,128)(2,1)} %param.5) | copy-start | bytes 688132
  11.0 45.5 %all-to-all-start = ((bf16[16,32,896]{2,1,0:T(8,128)(2,1)}), bf16[16,32,896]{2,1,0:T(8,128)(2,1)S(1)}, u32[]{:S(2)}, u32[]{:S(2)}) async-start(bf16[16,32,896]{2,1,0:T(8,128)(2,1)} %broadcast_in_dim.57), calls=%async_computation | async-start | bytes 1835008 | tf_op jit(solution)/shard_map/all_to_all | solution.py:87
  23.0 130.7 %all-gather.6.cloned.1.call-start = ((), (), s32[]{:S(2)}) async-start(), calls=%async_computation.4 | async-start | bytes 4587520 | tf_op jit(solution)/shard_map/all_gather | solution.py:124
  23.1 15.4 %collective-permute-start.5 = (bf16[448,384]{1,0:T(8,128)(2,1)S(1)}, bf16[448,384]{1,0:T(8,128)(2,1)}, u32[]{:S(2)}, u32[]{:S(2)}) collective-permute-start(bf16[448,384]{1,0:T(8,128)(2,1)S(1)} %slice.59), channel_id=1, source_target_pairs={{0,384},{128,0},{256,128},{384,256},{1,385},{129,1},{257,129},{385... | collective-permute-start | bytes 1032200 | tf_op jit(solution)/shard_map/ppermute | solution.py:18
  27.5 15.4 %collective-permute-start.6 = (bf16[448,384]{1,0:T(8,128)(2,1)S(1)}, bf16[448,384]{1,0:T(8,128)(2,1)}, u32[]{:S(2)}, u32[]{:S(2)}) collective-permute-start(bf16[448,384]{1,0:T(8,128)(2,1)S(1)} %slice.59), channel_id=1, source_target_pairs={{0,256},{128,384},{256,0},{384,128},{1,257},{129,385},{257,1},{385... | collective-permute-start | bytes 1032200 | tf_op jit(solution)/shard_map/ppermute | solution.py:18
  29.9 25.6 %collective-permute-start.7 = (bf16[448,384]{1,0:T(8,128)(2,1)S(1)}, bf16[448,384]{1,0:T(8,128)(2,1)}, u32[]{:S(2)}, u32[]{:S(2)}) collective-permute-start(bf16[448,384]{1,0:T(8,128)(2,1)S(1)} %slice.59), channel_id=1, source_target_pairs={{0,128},{128,256},{256,384},{384,0},{1,129},{129,257},{257,385},{3... | collective-permute-start | bytes 1032200 | tf_op jit(solution)/shard_map/ppermute | solution.py:18
  33.3 23.2 %collective-permute-start = (bf16[256,448]{1,0:T(8,128)(2,1)}, bf16[256,448]{1,0:T(8,128)(2,1)}, u32[]{:S(2)}, u32[]{:S(2)}) collective-permute-start(bf16[256,448]{1,0:T(8,128)(2,1)} %copy.29), channel_id=1, source_target_pairs={{0,0},{4,1},{7,2},{3,3},{6,4},{2,5},{5,6},{1,7},{9,8},{13,9},{8,10... | collective-permute-start | bytes 688136 | tf_op jit(solution)/shard_map/ppermute | solution.py:43
  56.5 1.0 copy-start.2
  59.2 4.3 %copy-start.1 = (bf16[16,64,896]{2,1,0:T(8,128)(2,1)}, bf16[16,64,896]{2,1,0:T(8,128)(2,1)S(1)}, u32[]{:S(2)}) copy-start(bf16[16,64,896]{2,1,0:T(8,128)(2,1)S(1)} %pad_maximum_fusion.1) | copy-start | bytes 5505028
  65.6 11.3 %copy-start = (bf16[1792,512]{1,0:T(8,128)(2,1)S(1)}, bf16[1792,512]{1,0:T(8,128)(2,1)}, u32[]{:S(2)}) copy-start(bf16[1792,512]{1,0:T(8,128)(2,1)} %all-gather.4.cloned.1.call-done) | copy-start | bytes 5505028
  67.4 11.2 %collective-permute-start.8 = (bf16[256,1792]{1,0:T(8,128)(2,1)S(1)}, bf16[256,1792]{1,0:T(8,128)(2,1)S(1)}, u32[]{:S(2)}, u32[]{:S(2)}) collective-permute-start(bf16[256,1792]{1,0:T(8,128)(2,1)S(1)} %fusion.2), channel_id=1, source_target_pairs={{0,1},{1,0},{2,3},{3,2},{4,5},{5,4},{6,7},{7,6},{8,9},{9,8},{10,11... | collective-permute-start | bytes 2752520 | tf_op jit(solution)/shard_map/ppermute | solution.py:22
  69.7 15.6 %collective-permute-start.1 = (bf16[256,448]{1,0:T(8,128)(2,1)}, bf16[256,448]{1,0:T(8,128)(2,1)S(1)}, u32[]{:S(2)}, u32[]{:S(2)}) collective-permute-start(bf16[256,448]{1,0:T(8,128)(2,1)} %collective-permute-done), channel_id=1, source_target_pairs={{0,0},{1,33},{2,58},{3,27},{4,52},{5,21},{6,46},{7,15},{8,8},{9,41... | collective-permute-start | bytes 688136 | tf_op jit(solution)/shard_map/ppermute | solution.py:34
  81.2 24.5 %all-to-all-start.1 = ((bf16[4,64,1792]{2,1,0:T(8,128)(2,1)}), bf16[4,64,1792]{2,1,0:T(8,128)(2,1)}, u32[]{:S(2)}, u32[]{:S(2)}) async-start(bf16[4,64,1792]{2,1,0:T(8,128)(2,1)} %bitcast.94), calls=%async_computation.1 | async-start | bytes 1835008 | tf_op jit(solution)/shard_map/all_to_all | solution.py:101
  85.5 11.6 %collective-permute-start.2 = (bf16[64,448]{1,0:T(8,128)(2,1)S(1)}, bf16[64,448]{1,0:T(8,128)(2,1)S(1)}, u32[]{:S(2)}, u32[]{:S(2)}) collective-permute-start(bf16[64,448]{1,0:T(8,128)(2,1)S(1)} %get-tuple-element.60), channel_id=1, source_target_pairs={{0,128},{128,256},{256,384},{384,0},{1,129},{129,257},{257,385},{3... | collective-permute-start | bytes 172040 | tf_op jit(solution)/shard_map/ppermute | solution.py:18
  87.6 12.4 %collective-permute-start.3 = (bf16[64,448]{1,0:T(8,128)(2,1)S(1)}, bf16[64,448]{1,0:T(8,128)(2,1)S(1)}, u32[]{:S(2)}, u32[]{:S(2)}) collective-permute-start(bf16[64,448]{1,0:T(8,128)(2,1)S(1)} %get-tuple-element.59), channel_id=1, source_target_pairs={{0,256},{128,384},{256,0},{384,128},{1,257},{129,385},{257,1},{385... | collective-permute-start | bytes 172040 | tf_op jit(solution)/shard_map/ppermute | solution.py:18
  95.1 7.3 %collective-permute-start.4 = (bf16[64,448]{1,0:T(8,128)(2,1)S(1)}, bf16[64,448]{1,0:T(8,128)(2,1)S(1)}, u32[]{:S(2)}, u32[]{:S(2)}) collective-permute-start(bf16[64,448]{1,0:T(8,128)(2,1)S(1)} %get-tuple-element.58), channel_id=1, source_target_pairs={{0,384},{128,0},{256,128},{384,256},{1,385},{129,1},{257,129},{385... | collective-permute-start | bytes 172040 | tf_op jit(solution)/shard_map/ppermute | solution.py:18
  103.6 3.4 %copy-start.5 = (bf16[64,1792]{1,0:T(8,128)(2,1)S(1)}, bf16[64,1792]{1,0:T(8,128)(2,1)}, u32[]{:S(2)}) copy-start(bf16[64,1792]{1,0:T(8,128)(2,1)} %reshape.56) | copy-start | bytes 688132
  107.4 27.8 %collective-permute-start.9 = (bf16[64,1792]{1,0:T(8,128)(2,1)S(1)}, bf16[64,1792]{1,0:T(8,128)(2,1)S(1)}, u32[]{:S(2)}, u32[]{:S(2)}) collective-permute-start(bf16[64,1792]{1,0:T(8,128)(2,1)S(1)} %get-tuple-element.56), channel_id=1, source_target_pairs={{0,0},{1,33},{2,10},{3,43},{4,20},{5,53},{6,30},{7,63},{8,8},{9,41... | collective-permute-start | bytes 688136 | tf_op jit(solution)/shard_map/ppermute | solution.py:34
  135.2 11.3 %collective-permute-start.10 = (bf16[256,1792]{1,0:T(8,128)(2,1)S(1)}, bf16[256,1792]{1,0:T(8,128)(2,1)S(1)}, u32[]{:S(2)}, u32[]{:S(2)}) collective-permute-start(bf16[256,1792]{1,0:T(8,128)(2,1)S(1)} %all_gather.13), channel_id=1, source_target_pairs={{0,1},{1,0},{2,3},{3,2},{4,5},{5,4},{6,7},{7,6},{8,9},{9,8},{10,11... | collective-permute-start | bytes 2752520 | tf_op jit(solution)/shard_map/ppermute | solution.py:22
  138.4 8.2 %copy-start.3 = (bf16[1792,896]{1,0:T(8,128)(2,1)S(1)}, bf16[1792,896]{1,0:T(8,128)(2,1)}, u32[]{:S(2)}) copy-start(bf16[1792,896]{1,0:T(8,128)(2,1)} %pad_maximum_fusion) | copy-start | bytes 9633796
  138.4 15.2 %collective-permute-start.11 = (bf16[64,1792]{1,0:T(8,128)(2,1)S(1)}, bf16[64,1792]{1,0:T(8,128)(2,1)S(1)}, u32[]{:S(2)}, u32[]{:S(2)}) collective-permute-start(bf16[64,1792]{1,0:T(8,128)(2,1)S(1)} %collective-permute-done.9), channel_id=1, source_target_pairs={{0,0},{1,4},{2,7},{3,3},{4,6},{5,2},{6,5},{7,1},{8,9},{9,13},{10,8... | collective-permute-start | bytes 688136 | tf_op jit(solution)/shard_map/ppermute | solution.py:43
  149.0 40.0 %all-to-all-start.2 = ((bf16[16,32,896]{2,1,0:T(8,128)(2,1)}), bf16[16,32,896]{2,1,0:T(8,128)(2,1)S(1)}, u32[]{:S(2)}, u32[]{:S(2)}) async-start(bf16[16,32,896]{2,1,0:T(8,128)(2,1)} %bitcast.21), calls=%async_computation.2 | async-start | bytes 1835008 | tf_op jit(solution)/shard_map/all_to_all | solution.py:122
  155.6 11.9 %collective-permute-start.12 = (bf16[320,448]{0,1:T(8,128)(2,1)}, bf16[320,448]{0,1:T(8,128)(2,1)S(1)}, u32[]{:S(2)}, u32[]{:S(2)}) collective-permute-start(bf16[320,448]{0,1:T(8,128)(2,1)} %get-tuple-element.54), channel_id=1, source_target_pairs={{0,128},{128,256},{256,384},{384,0},{1,129},{129,257},{257,385},{3... | collective-permute-start | bytes 860168 | tf_op jit(solution)/shard_map/ppermute | solution.py:18
  157.5 18.2 %collective-permute-start.13 = (bf16[320,448]{0,1:T(8,128)(2,1)S(1)}, bf16[320,448]{0,1:T(8,128)(2,1)S(1)}, u32[]{:S(2)}, u32[]{:S(2)}) collective-permute-start(bf16[320,448]{0,1:T(8,128)(2,1)S(1)} %get-tuple-element.53), channel_id=1, source_target_pairs={{0,256},{128,384},{256,0},{384,128},{1,257},{129,385},{257,1},{385... | collective-permute-start | bytes 860168 | tf_op jit(solution)/shard_map/ppermute | solution.py:18
  164.0 13.9 %collective-permute-start.14 = (bf16[320,448]{0,1:T(8,128)(2,1)S(1)}, bf16[320,448]{0,1:T(8,128)(2,1)S(1)}, u32[]{:S(2)}, u32[]{:S(2)}) collective-permute-start(bf16[320,448]{0,1:T(8,128)(2,1)S(1)} %get-tuple-element.52), channel_id=1, source_target_pairs={{0,384},{128,0},{256,128},{384,256},{1,385},{129,1},{257,129},{385... | collective-permute-start | bytes 860168 | tf_op jit(solution)/shard_map/ppermute | solution.py:18
  175.7 2.2 %copy-start.6 = (bf16[320,448]{0,1:T(8,128)(2,1)}, bf16[320,448]{0,1:T(8,128)(2,1)S(1)}, u32[]{:S(2)}) copy-start(bf16[320,448]{0,1:T(8,128)(2,1)S(1)} %collective-permute-done.13) | copy-start | bytes 860164
  177.9 3.9 %copy-start.7 = (bf16[320,448]{0,1:T(8,128)(2,1)}, bf16[320,448]{0,1:T(8,128)(2,1)S(1)}, u32[]{:S(2)}) copy-start(bf16[320,448]{0,1:T(8,128)(2,1)S(1)} %collective-permute-done.14) | copy-start | bytes 860164
  177.9 6.1 %collective-permute-start.15 = (bf16[4,256,448]{1,2,0:T(8,128)(2,1)S(1)}, bf16[4,256,448]{1,2,0:T(8,128)(2,1)S(1)}, u32[]{:S(2)}, u32[]{:S(2)}) collective-permute-start(bf16[4,256,448]{1,2,0:T(8,128)(2,1)S(1)} %fusion.24), channel_id=1, source_target_pairs={{0,1},{1,0},{2,3},{3,2},{4,5},{5,4},{6,7},{7,6},{8,9},{9,8},{10,11... | collective-permute-start | bytes 2752520 | tf_op jit(solution)/shard_map/ppermute | solution.py:22
Sparse Core Ops, SparseCore 0:
  10.7 52.6 all-gather.3
  65.5 52.0 all-gather.5

commit v14 on v12

--- a/solution.py
+++ b/solution.py
@@ -79,12 +79,13 @@
     near = jnp.broadcast_to(tokens[None], (16, rows, feats))
     near = lax.all_to_all(near, ("z", "yl"), split_axis=0, concat_axis=0).reshape(8, pair, feats)
     cot = along_z(within_z(act_grad, False), -1)
-    near, cot, w_all = lax.optimization_barrier((near, cot, w_all))
+    near, cot = lax.optimization_barrier((near, cot))
     near = jnp.stack([cut(near, first, 4), cut(near, first + 4, 4)])
     w_all = w_all.reshape(NX * cols, feats)
 
     sent = swap_cores(dot(near[1], w_all, ((1,), (1,))).astype(BF))
-    partial_value = (dot(near[0], w_all, ((1,), (1,))) + sent.astype(jnp.float32)).astype(BF)
+    partial_value, sent = lax.optimization_barrier((dot(near[0], w_all, ((1,), (1,))), sent))
+    partial_value = (partial_value + sent.astype(jnp.float32)).astype(BF)
     partial_value = partial_value.reshape(4, pair, NX * cols)
     partial_value, cot = lax.optimization_barrier((partial_value, cot))
     parts = lax.all_to_all(partial_value, "yh", split_axis=0, concat_axis=0)

time: 190 us -> 197 us (1.037)
  waiting for transfers between devices: 60.5 us -> 53.5 us
  starting transfers between devices: 69.4 us -> 74.6 us
  local copies, waits for them, and re-layouts: 8.94 us -> 12.6 us
  other arithmetic: 2.85 us -> 5.16 us
    ppermute x6, waiting for transfers between devices: 16.5 us -> 3.93 us  [along_x(): return lax.ppermute(value, 'x', [(i, (i + shift) % NX) for i in range(NX)])]
    all_to_all x1, waiting for transfers between devices: 0.01 us -> 7.8 us  [body(): ig = lax.all_to_all(ig, ('z', 'yl'), split_axis=0, concat_axis=0)]
    all_to_all x1, starting transfers between devices: 3.79 us -> 7.77 us  [body(): ig = lax.all_to_all(ig, ('z', 'yl'), split_axis=0, concat_axis=0)]
    dynamic_update_slice x11, local copies, waits for them, and re-layouts: 0.14 us -> 2.96 us  [in_order(): lax.dynamic_update_index_in_dim(out, parts[r], here + (NX - r) & NX - 1, 0)]
    convert_element_type x0 -> x1, other arithmetic: none -> 2.33 us  [body(): partial_value = (partial_value + sent.astype(jnp.float32)).astype(BF)]
    ppermute x3, waiting for transfers between devices: 2.08 us -> 0.01 us  [swap_cores(): return lax.ppermute(value, 'c', [(0, 1), (1, 0)])]
  transfers between devices with their start and end apart: 18 -> 18, of which waited for: 10 -> 7; matrix products, arithmetic and copies ran while one was open for 12% -> 14% of each run, Pallas kernels for 0% -> 0%
where the time goes in v14:
time: 197 us; the launch traced here: 195 us
  starting transfers between devices  74.6 us (38%)
  waiting for transfers between devices  53.5 us (27%)
  blocking collectives  18.4 us (9%)
  matrix products  16.2 us (8%)
  between operations  14.5 us (7%)
  local copies, waits for them, and re-layouts  12.6 us (6%)
  other arithmetic  5.16 us (3%)
    ppermute x2, waiting for transfers between devices, within_z(): return lax.ppermute(value, ('z', 'yh', 'c'), pairs)  21.4 us
    ppermute x6, starting transfers between devices, along_x(): return lax.ppermute(value, 'x', [(i, (i + shift) % NX) for i in range(NX)])  18.8 us
    all_gather x1, blocking collectives, body(): grad_own = lax.all_gather(hidden_grad, 'yh', axis=0, tiled=True)  18.4 us
    dot_general x5, matrix products, dot(): lax.dot_general(a, b, (contract, ((), ())), preferred_element_type=jnp.fl...  16.2 us
    all_to_all x1, starting transfers between devices, body(): lax.all_to_all(near, ('z', 'yl'), split_axis=0, concat_axis=0)  12 us
    ppermute x2, starting transfers between devices, within_z(): return lax.ppermute(value, ('z', 'yh', 'c'), pairs)  10.7 us
    ppermute x2, starting transfers between devices, along_z(): return lax.ppermute(value, ('z', 'yh', 'c'), pairs)  9.62 us
    ppermute x3, starting transfers between devices, swap_cores(): return lax.ppermute(value, 'c', [(0, 1), (1, 0)])  9.21 us
  transfers between devices with their start and end apart: 18, of which 7 were waited for; matrix products, arithmetic and copies ran while one was open for 14% of the time, Pallas kernels for 0%

profile of v14, /device:TPU:1, one launch (start us, length us, event | category | flops | bytes accessed | tf_op | source)
XLA Modules:
  0.0 194.9 jit_solution(8309128121503752846)
XLA Ops:
  7.9 1.8 broadcast_in_dim.41
  9.7 12.0 %all-to-all-start = ((bf16[16,32,896]{2,1,0:T(8,128)(2,1)}), bf16[16,32,896]{2,1,0:T(8,128)(2,1)S(1)}, u32[]{:S(2)}, u32[]{:S(2)}) async-start(bf16[16,32,896]{2,1,0:T(8,128)(2,1)} %broadcast_in_dim.41), calls=%async_computation | async-start | bytes 1835008 | tf_op jit(solution)/shard_map/all_to_all | solution.py:80
  21.9 5.0 %collective-permute-start = (bf16[256,448]{1,0:T(8,128)(2,1)S(1)}, bf16[256,448]{1,0:T(8,128)(2,1)S(1)}, u32[]{:S(2)}, u32[]{:S(2)}) collective-permute-start(bf16[256,448]{1,0:T(8,128)(2,1)S(1)} %copy.29), channel_id=1, source_target_pairs={{0,0},{4,1},{7,2},{3,3},{6,4},{2,5},{5,6},{1,7},{9,8},{13,9},{8,10... | collective-permute-start | bytes 688136 | tf_op jit(solution)/shard_map/ppermute | solution.py:42
  26.9 21.4 %collective-permute-done = bf16[256,448]{1,0:T(8,128)(2,1)S(1)} collective-permute-done((bf16[256,448]{1,0:T(8,128)(2,1)S(1)}, bf16[256,448]{1,0:T(8,128)(2,1)S(1)}, u32[]{:S(2)}, u32[]{:S(2)}) %collective-permute-start) | collective-permute-done | bytes 229408 | tf_op jit(solution)/shard_map/ppermute | solution.py:42
  48.3 1.9 collective-permute-start.1
  50.2 9.1 %collective-permute-done.1 = bf16[256,448]{1,0:T(8,128)(2,1)S(1)} collective-permute-done((bf16[256,448]{1,0:T(8,128)(2,1)S(1)}, bf16[256,448]{1,0:T(8,128)(2,1)S(1)}, u32[]{:S(2)}, u32[]{:S(2)}) %collective-permute-start.1) | collective-permute-done | bytes 229408 | tf_op jit(solution)/shard_map/ppermute | solution.py:33
  59.6 1.4 all-gather.5.cloned.1.call-done
  61.0 4.0 %convolution_convert_fusion = bf16[256,1792]{1,0:T(8,128)(2,1)} fusion(bf16[1792,896]{1,0:T(8,128)(2,1)} %all-gather.5.cloned.1.call-done, bf16[1024,896]{1,0:T(8,128)(2,1)S(1)} %bitcast.74, u32[]{:T(128)S(6)} %mul.58), kind=kOutput, calls=%fused_computation | convolution fusion | flops 822542336 | bytes 4587524 | tf_op jit(solution)/shard_map/dot_general | solution.py:67
  65.0 2.6 %collective-permute-start.2 = (bf16[256,1792]{1,0:T(8,128)(2,1)}, bf16[256,1792]{1,0:T(8,128)(2,1)}, u32[]{:S(2)}, u32[]{:S(2)}) collective-permute-start(bf16[256,1792]{1,0:T(8,128)(2,1)} %convolution_convert_fusion), channel_id=1, source_target_pairs={{0,1},{1,0},{2,3},{3,2},{4,5},{5,4},{6,7},{7,6},{8,9},{9,8},{10,11... | collective-permute-start | bytes 2752520 | tf_op jit(solution)/shard_map/ppermute | solution.py:21
  67.6 1.0 pad_maximum_fusion.4
  68.7 3.1 %fusion.15 = f32[256,1792]{1,0:T(8,128)S(1)} fusion(bf16[1792,896]{1,0:T(8,128)(2,1)} %all-gather.5.cloned.1.call-done, bf16[1024,896]{1,0:T(8,128)(2,1)S(1)} %bitcast.75, u32[]{:T(128)S(6)} %mul.57), kind=kOutput, calls=%fused_computation.30 | convolution fusion | flops 822083584 | bytes 5505028 | tf_op jit(solution)/shard_map/dot_general | solution.py:67
  71.7 2.3 %add_convert_fusion = bf16[256,1792]{1,0:T(8,128)(2,1)} fusion(f32[256,1792]{1,0:T(8,128)S(1)} %fusion.15, bf16[256,1792]{1,0:T(8,128)(2,1)} %collective-permute-done.2), kind=kLoop, calls=%fused_computation.8 | loop fusion | flops 1376256 | bytes 3670016 | tf_op jit(solution)/shard_map/convert_element_type | solution.py:88
  74.1 6.4 %all-to-all-start.1 = ((bf16[4,64,1792]{2,1,0:T(8,128)(2,1)}), bf16[4,64,1792]{2,1,0:T(8,128)(2,1)S(1)}, u32[]{:S(2)}, u32[]{:S(2)}) async-start(bf16[4,64,1792]{2,1,0:T(8,128)(2,1)} %bitcast.3), calls=%async_computation.1 | async-start | bytes 1835008 | tf_op jit(solution)/shard_map/all_to_all | solution.py:91
  80.6 2.3 %collective-permute-start.3 = (bf16[64,448]{1,0:T(8,128)(2,1)S(1)}, bf16[64,448]{1,0:T(8,128)(2,1)S(1)}, u32[]{:S(2)}, u32[]{:S(2)}) collective-permute-start(bf16[64,448]{1,0:T(8,128)(2,1)S(1)} %get-tuple-element.58), channel_id=1, source_target_pairs={{0,128},{128,256},{256,384},{384,0},{1,129},{129,257},{257,385},{3... | collective-permute-start | bytes 172040 | tf_op jit(solution)/shard_map/ppermute | solution.py:17
  82.9 3.4 %collective-permute-start.4 = (bf16[64,448]{1,0:T(8,128)(2,1)S(1)}, bf16[64,448]{1,0:T(8,128)(2,1)S(1)}, u32[]{:S(2)}, u32[]{:S(2)}) collective-permute-start(bf16[64,448]{1,0:T(8,128)(2,1)S(1)} %get-tuple-element.57), channel_id=1, source_target_pairs={{0,256},{128,384},{256,0},{384,128},{1,257},{129,385},{257,1},{385... | collective-permute-start | bytes 172040 | tf_op jit(solution)/shard_map/ppermute | solution.py:17
  86.3 3.7 %collective-permute-start.5 = (bf16[64,448]{1,0:T(8,128)(2,1)S(1)}, bf16[64,448]{1,0:T(8,128)(2,1)S(1)}, u32[]{:S(2)}, u32[]{:S(2)}) collective-permute-start(bf16[64,448]{1,0:T(8,128)(2,1)S(1)} %get-tuple-element.56), channel_id=1, source_target_pairs={{0,384},{128,0},{256,128},{384,256},{1,385},{129,1},{257,129},{385... | collective-permute-start | bytes 172040 | tf_op jit(solution)/shard_map/ppermute | solution.py:17
  90.1 1.1 collective-permute-done.4
  91.1 2.9 %collective-permute-done.5 = bf16[64,448]{1,0:T(8,128)(2,1)S(1)} collective-permute-done((bf16[64,448]{1,0:T(8,128)(2,1)S(1)}, bf16[64,448]{1,0:T(8,128)(2,1)S(1)}, u32[]{:S(2)}, u32[]{:S(2)}) %collective-permute-start.5) | collective-permute-done | bytes 57376 | tf_op jit(solution)/shard_map/ppermute | solution.py:17
  94.9 9.1 %all-to-all-done.1 = bf16[4,64,1792]{2,1,0:T(8,128)(2,1)S(1)} async-done(((bf16[4,64,1792]{2,1,0:T(8,128)(2,1)}), bf16[4,64,1792]{2,1,0:T(8,128)(2,1)S(1)}, u32[]{:S(2)}, u32[]{:S(2)}) %all-to-all-start.1) | async-done | bytes 917536 | tf_op jit(solution)/shard_map/all_to_all | solution.py:91
  104.5 7.7 %collective-permute-start.6 = (bf16[64,1792]{1,0:T(8,128)(2,1)S(1)}, bf16[64,1792]{1,0:T(8,128)(2,1)S(1)}, u32[]{:S(2)}, u32[]{:S(2)}) collective-permute-start(bf16[64,1792]{1,0:T(8,128)(2,1)S(1)} %get-tuple-element.54), channel_id=1, source_target_pairs={{0,0},{1,33},{2,10},{3,43},{4,20},{5,53},{6,30},{7,63},{8,8},{9,41... | collective-permute-start | bytes 688136 | tf_op jit(solution)/shard_map/ppermute | solution.py:33
  112.2 18.4 %all_gather.17 = bf16[256,1792]{1,0:T(8,128)(2,1)S(1)} all-gather(bf16[64,1792]{1,0:T(8,128)(2,1)S(1)} %get-tuple-element.55), channel_id=1, replica_groups=mesh['x'=4,'yl'=2,'z'=8,'yh'=4,'c'=2] {'yh'}, dimensions={0}, use_global_device_ids=true | all-gather | bytes 1146880 | tf_op jit(solution)/shard_map/all_gather | solution.py:101
  130.6 2.6 %collective-permute-start.7 = (bf16[256,1792]{1,0:T(8,128)(2,1)S(1)}, bf16[256,1792]{1,0:T(8,128)(2,1)S(1)}, u32[]{:S(2)}, u32[]{:S(2)}) collective-permute-start(bf16[256,1792]{1,0:T(8,128)(2,1)S(1)} %all_gather.17), channel_id=1, source_target_pairs={{0,1},{1,0},{2,3},{3,2},{4,5},{5,4},{6,7},{7,6},{8,9},{9,8},{10,11... | collective-permute-start | bytes 2752520 | tf_op jit(solution)/shard_map/ppermute | solution.py:21
  133.2 5.7 %collective-permute-start.8 = (bf16[64,1792]{1,0:T(8,128)(2,1)S(1)}, bf16[64,1792]{1,0:T(8,128)(2,1)S(1)}, u32[]{:S(2)}, u32[]{:S(2)}) collective-permute-start(bf16[64,1792]{1,0:T(8,128)(2,1)S(1)} %collective-permute-done.6), channel_id=1, source_target_pairs={{0,0},{1,4},{2,7},{3,3},{4,6},{5,2},{6,5},{7,1},{8,9},{9,13},{10,8... | collective-permute-start | bytes 688136 | tf_op jit(solution)/shard_map/ppermute | solution.py:42
  138.9 3.0 %convolution_convert_fusion.2 = bf16[256,896]{1,0:T(8,128)(2,1)S(1)} fusion(bf16[256,1792]{1,0:T(8,128)(2,1)S(1)} %all_gather.17, bf16[1792,896]{1,0:T(8,128)(2,1)} %all-gather.5.cloned.1.call-done), kind=kOutput, calls=%fused_computation.11 | convolution fusion | flops 822312960 | bytes 4587520 | tf_op jit(solution)/shard_map/dot_general | solution.py:67
  141.9 1.1 fusion.6
  146.3 2.3 %collective-permute-start.9 = (bf16[320,448]{0,1:T(8,128)(2,1)}, bf16[320,448]{0,1:T(8,128)(2,1)}, u32[]{:S(2)}, u32[]{:S(2)}) collective-permute-start(bf16[320,448]{0,1:T(8,128)(2,1)} %get-tuple-element.52), channel_id=1, source_target_pairs={{0,128},{128,256},{256,384},{384,0},{1,129},{129,257},{257,385},{3... | collective-permute-start | bytes 860168 | tf_op jit(solution)/shard_map/ppermute | solution.py:17
  148.6 3.2 %collective-permute-start.10 = (bf16[320,448]{0,1:T(8,128)(2,1)S(1)}, bf16[320,448]{0,1:T(8,128)(2,1)}, u32[]{:S(2)}, u32[]{:S(2)}) collective-permute-start(bf16[320,448]{0,1:T(8,128)(2,1)S(1)} %get-tuple-element.51), channel_id=1, source_target_pairs={{0,256},{128,384},{256,0},{384,128},{1,257},{129,385},{257,1},{385... | collective-permute-start | bytes 860168 | tf_op jit(solution)/shard_map/ppermute | solution.py:17
  151.7 4.0 %collective-permute-start.11 = (bf16[320,448]{0,1:T(8,128)(2,1)S(1)}, bf16[320,448]{0,1:T(8,128)(2,1)}, u32[]{:S(2)}, u32[]{:S(2)}) collective-permute-start(bf16[320,448]{0,1:T(8,128)(2,1)S(1)} %get-tuple-element.50), channel_id=1, source_target_pairs={{0,384},{128,0},{256,128},{384,256},{1,385},{129,1},{257,129},{385... | collective-permute-start | bytes 860168 | tf_op jit(solution)/shard_map/ppermute | solution.py:17
  155.7 7.8 %all-to-all-start.2 = ((bf16[16,32,896]{2,1,0:T(8,128)(2,1)}), bf16[16,32,896]{2,1,0:T(8,128)(2,1)S(1)}, u32[]{:S(2)}, u32[]{:S(2)}) async-start(bf16[16,32,896]{2,1,0:T(8,128)(2,1)} %bitcast.16), calls=%async_computation.2 | async-start | bytes 1835008 | tf_op jit(solution)/shard_map/all_to_all | solution.py:111
  166.5 4.1 %collective-permute-start.12 = (bf16[4,256,448]{1,2,0:T(8,128)(2,1)S(1)}, bf16[4,256,448]{1,2,0:T(8,128)(2,1)S(1)}, u32[]{:S(2)}, u32[]{:S(2)}) collective-permute-start(bf16[4,256,448]{1,2,0:T(8,128)(2,1)S(1)} %fusion.17), channel_id=1, source_target_pairs={{0,1},{1,0},{2,3},{3,2},{4,5},{5,4},{6,7},{7,6},{8,9},{9,8},{10,11... | collective-permute-start | bytes 2752520 | tf_op jit(solution)/shard_map/ppermute | solution.py:21
  173.7 5.0 %bitcast_convert_fusion = bf16[896,448]{0,1:T(8,128)(2,1)} fusion(bf16[4,2,256,896]{3,2,1,0:T(8,128)(2,1)} %bitcast.85, bf16[4,1,256,448]{2,3,1,0:T(8,128)(2,1)S(1)} %bitcast.86, bf16[4,1,256,448]{2,3,1,0:T(8,128)(2,1)S(1)} %bitcast.81), kind=kOutput, calls=%fused_computation.9 | convolution fusion | flops 1645486080 | bytes 6307840 | tf_op jit(solution)/shard_map/dot_general | solution.py:67
  178.7 7.8 %all-to-all-done.2 = bf16[16,32,896]{2,1,0:T(8,128)(2,1)S(1)} async-done(((bf16[16,32,896]{2,1,0:T(8,128)(2,1)}), bf16[16,32,896]{2,1,0:T(8,128)(2,1)S(1)}, u32[]{:S(2)}, u32[]{:S(2)}) %all-to-all-start.2) | async-done | bytes 917536 | tf_op jit(solution)/shard_map/all_to_all | solution.py:111
  (58 shorter events, 13.4 us)
Async XLA Ops:
  7.2 14.6 %copy-start.1 = (bf16[256,448]{0,1:T(8,128)(2,1)S(1)}, bf16[256,448]{0,1:T(8,128)(2,1)}, u32[]{:S(2)}) copy-start(bf16[256,448]{0,1:T(8,128)(2,1)} %param.5) | copy-start | bytes 688132
  7.2 53.9 %all-gather.5.cloned.1.call-start = ((), (), s32[]{:S(2)}) async-start(), calls=%async_computation.3 | async-start | bytes 4014080 | tf_op jit(solution)/shard_map/all_gather | solution.py:77
  9.7 49.6 %all-to-all-start = ((bf16[16,32,896]{2,1,0:T(8,128)(2,1)}), bf16[16,32,896]{2,1,0:T(8,128)(2,1)S(1)}, u32[]{:S(2)}, u32[]{:S(2)}) async-start(bf16[16,32,896]{2,1,0:T(8,128)(2,1)} %broadcast_in_dim.41), calls=%async_computation | async-start | bytes 1835008 | tf_op jit(solution)/shard_map/all_to_all | solution.py:80
  21.7 122.6 %all-gather.7.cloned.1.call-start = ((), (), s32[]{:S(2)}) async-start(), calls=%async_computation.4 | async-start | bytes 4587520 | tf_op jit(solution)/shard_map/all_gather | solution.py:113
  21.9 26.4 %collective-permute-start = (bf16[256,448]{1,0:T(8,128)(2,1)S(1)}, bf16[256,448]{1,0:T(8,128)(2,1)S(1)}, u32[]{:S(2)}, u32[]{:S(2)}) collective-permute-start(bf16[256,448]{1,0:T(8,128)(2,1)S(1)} %copy.29), channel_id=1, source_target_pairs={{0,0},{4,1},{7,2},{3,3},{6,4},{2,5},{5,6},{1,7},{9,8},{13,9},{8,10... | collective-permute-start | bytes 688136 | tf_op jit(solution)/shard_map/ppermute | solution.py:42
  48.3 11.0 %collective-permute-start.1 = (bf16[256,448]{1,0:T(8,128)(2,1)S(1)}, bf16[256,448]{1,0:T(8,128)(2,1)S(1)}, u32[]{:S(2)}, u32[]{:S(2)}) collective-permute-start(bf16[256,448]{1,0:T(8,128)(2,1)S(1)} %collective-permute-done), channel_id=1, source_target_pairs={{0,0},{1,33},{2,58},{3,27},{4,52},{5,21},{6,46},{7,15},{8,8},{9,41... | collective-permute-start | bytes 688136 | tf_op jit(solution)/shard_map/ppermute | solution.py:33
  65.0 6.7 %collective-permute-start.2 = (bf16[256,1792]{1,0:T(8,128)(2,1)}, bf16[256,1792]{1,0:T(8,128)(2,1)}, u32[]{:S(2)}, u32[]{:S(2)}) collective-permute-start(bf16[256,1792]{1,0:T(8,128)(2,1)} %convolution_convert_fusion), channel_id=1, source_target_pairs={{0,1},{1,0},{2,3},{3,2},{4,5},{5,4},{6,7},{7,6},{8,9},{9,8},{10,11... | collective-permute-start | bytes 2752520 | tf_op jit(solution)/shard_map/ppermute | solution.py:21
  74.1 29.9 %all-to-all-start.1 = ((bf16[4,64,1792]{2,1,0:T(8,128)(2,1)}), bf16[4,64,1792]{2,1,0:T(8,128)(2,1)S(1)}, u32[]{:S(2)}, u32[]{:S(2)}) async-start(bf16[4,64,1792]{2,1,0:T(8,128)(2,1)} %bitcast.3), calls=%async_computation.1 | async-start | bytes 1835008 | tf_op jit(solution)/shard_map/all_to_all | solution.py:91
  80.6 9.5 %collective-permute-start.3 = (bf16[64,448]{1,0:T(8,128)(2,1)S(1)}, bf16[64,448]{1,0:T(8,128)(2,1)S(1)}, u32[]{:S(2)}, u32[]{:S(2)}) collective-permute-start(bf16[64,448]{1,0:T(8,128)(2,1)S(1)} %get-tuple-element.58), channel_id=1, source_target_pairs={{0,128},{128,256},{256,384},{384,0},{1,129},{129,257},{257,385},{3... | collective-permute-start | bytes 172040 | tf_op jit(solution)/shard_map/ppermute | solution.py:17
  82.9 8.2 %collective-permute-start.4 = (bf16[64,448]{1,0:T(8,128)(2,1)S(1)}, bf16[64,448]{1,0:T(8,128)(2,1)S(1)}, u32[]{:S(2)}, u32[]{:S(2)}) collective-permute-start(bf16[64,448]{1,0:T(8,128)(2,1)S(1)} %get-tuple-element.57), channel_id=1, source_target_pairs={{0,256},{128,384},{256,0},{384,128},{1,257},{129,385},{257,1},{385... | collective-permute-start | bytes 172040 | tf_op jit(solution)/shard_map/ppermute | solution.py:17
  86.3 7.7 %collective-permute-start.5 = (bf16[64,448]{1,0:T(8,128)(2,1)S(1)}, bf16[64,448]{1,0:T(8,128)(2,1)S(1)}, u32[]{:S(2)}, u32[]{:S(2)}) collective-permute-start(bf16[64,448]{1,0:T(8,128)(2,1)S(1)} %get-tuple-element.56), channel_id=1, source_target_pairs={{0,384},{128,0},{256,128},{384,256},{1,385},{129,1},{257,129},{385... | collective-permute-start | bytes 172040 | tf_op jit(solution)/shard_map/ppermute | solution.py:17
  104.5 26.1 %collective-permute-start.6 = (bf16[64,1792]{1,0:T(8,128)(2,1)S(1)}, bf16[64,1792]{1,0:T(8,128)(2,1)S(1)}, u32[]{:S(2)}, u32[]{:S(2)}) collective-permute-start(bf16[64,1792]{1,0:T(8,128)(2,1)S(1)} %get-tuple-element.54), channel_id=1, source_target_pairs={{0,0},{1,33},{2,10},{3,43},{4,20},{5,53},{6,30},{7,63},{8,8},{9,41... | collective-permute-start | bytes 688136 | tf_op jit(solution)/shard_map/ppermute | solution.py:33
  130.6 11.3 %collective-permute-start.7 = (bf16[256,1792]{1,0:T(8,128)(2,1)S(1)}, bf16[256,1792]{1,0:T(8,128)(2,1)S(1)}, u32[]{:S(2)}, u32[]{:S(2)}) collective-permute-start(bf16[256,1792]{1,0:T(8,128)(2,1)S(1)} %all_gather.17), channel_id=1, source_target_pairs={{0,1},{1,0},{2,3},{3,2},{4,5},{5,4},{6,7},{7,6},{8,9},{9,8},{10,11... | collective-permute-start | bytes 2752520 | tf_op jit(solution)/shard_map/ppermute | solution.py:21
  133.1 8.8 %copy-start = (bf16[1792,896]{1,0:T(8,128)(2,1)S(1)}, bf16[1792,896]{1,0:T(8,128)(2,1)}, u32[]{:S(2)}) copy-start(bf16[1792,896]{1,0:T(8,128)(2,1)} %all-gather.5.cloned.1.call-done) | copy-start | bytes 9633796
  133.2 11.2 %collective-permute-start.8 = (bf16[64,1792]{1,0:T(8,128)(2,1)S(1)}, bf16[64,1792]{1,0:T(8,128)(2,1)S(1)}, u32[]{:S(2)}, u32[]{:S(2)}) collective-permute-start(bf16[64,1792]{1,0:T(8,128)(2,1)S(1)} %collective-permute-done.6), channel_id=1, source_target_pairs={{0,0},{1,4},{2,7},{3,3},{4,6},{5,2},{6,5},{7,1},{8,9},{9,13},{10,8... | collective-permute-start | bytes 688136 | tf_op jit(solution)/shard_map/ppermute | solution.py:42
  146.3 17.4 %collective-permute-start.9 = (bf16[320,448]{0,1:T(8,128)(2,1)}, bf16[320,448]{0,1:T(8,128)(2,1)}, u32[]{:S(2)}, u32[]{:S(2)}) collective-permute-start(bf16[320,448]{0,1:T(8,128)(2,1)} %get-tuple-element.52), channel_id=1, source_target_pairs={{0,128},{128,256},{256,384},{384,0},{1,129},{129,257},{257,385},{3... | collective-permute-start | bytes 860168 | tf_op jit(solution)/shard_map/ppermute | solution.py:17
  148.6 16.1 %collective-permute-start.10 = (bf16[320,448]{0,1:T(8,128)(2,1)S(1)}, bf16[320,448]{0,1:T(8,128)(2,1)}, u32[]{:S(2)}, u32[]{:S(2)}) collective-permute-start(bf16[320,448]{0,1:T(8,128)(2,1)S(1)} %get-tuple-element.51), channel_id=1, source_target_pairs={{0,256},{128,384},{256,0},{384,128},{1,257},{129,385},{257,1},{385... | collective-permute-start | bytes 860168 | tf_op jit(solution)/shard_map/ppermute | solution.py:17
  151.7 13.8 %collective-permute-start.11 = (bf16[320,448]{0,1:T(8,128)(2,1)S(1)}, bf16[320,448]{0,1:T(8,128)(2,1)}, u32[]{:S(2)}, u32[]{:S(2)}) collective-permute-start(bf16[320,448]{0,1:T(8,128)(2,1)S(1)} %get-tuple-element.50), channel_id=1, source_target_pairs={{0,384},{128,0},{256,128},{384,256},{1,385},{129,1},{257,129},{385... | collective-permute-start | bytes 860168 | tf_op jit(solution)/shard_map/ppermute | solution.py:17
  155.7 30.8 %all-to-all-start.2 = ((bf16[16,32,896]{2,1,0:T(8,128)(2,1)}), bf16[16,32,896]{2,1,0:T(8,128)(2,1)S(1)}, u32[]{:S(2)}, u32[]{:S(2)}) async-start(bf16[16,32,896]{2,1,0:T(8,128)(2,1)} %bitcast.16), calls=%async_computation.2 | async-start | bytes 1835008 | tf_op jit(solution)/shard_map/all_to_all | solution.py:111
  166.5 7.2 %collective-permute-start.12 = (bf16[4,256,448]{1,2,0:T(8,128)(2,1)S(1)}, bf16[4,256,448]{1,2,0:T(8,128)(2,1)S(1)}, u32[]{:S(2)}, u32[]{:S(2)}) collective-permute-start(bf16[4,256,448]{1,2,0:T(8,128)(2,1)S(1)} %fusion.17), channel_id=1, source_target_pairs={{0,1},{1,0},{2,3},{3,2},{4,5},{5,4},{6,7},{7,6},{8,9},{9,8},{10,11... | collective-permute-start | bytes 2752520 | tf_op jit(solution)/shard_map/ppermute | solution.py:21
Sparse Core Ops, SparseCore 0:
  10.1 50.8 all-gather.4
  68.8 51.0 all-gather.6

commit v15 on v12

--- a/solution.py
+++ b/solution.py
@@ -79,8 +79,9 @@
     near = jnp.broadcast_to(tokens[None], (16, rows, feats))
     near = lax.all_to_all(near, ("z", "yl"), split_axis=0, concat_axis=0).reshape(8, pair, feats)
     cot = along_z(within_z(act_grad, False), -1)
+    near, cot = lax.optimization_barrier((near, cot))
+    near = jnp.stack([cut(near, first, 4), cut(near, first + 4, 4)])
     near, cot, w_all = lax.optimization_barrier((near, cot, w_all))
-    near = jnp.stack([cut(near, first, 4), cut(near, first + 4, 4)])
     w_all = w_all.reshape(NX * cols, feats)
 
     sent = swap_cores(dot(near[1], w_all, ((1,), (1,))).astype(BF))
@@ -97,10 +98,11 @@
     hidden_grad = pullback(cot.astype(jnp.float32))[0].astype(BF)
     activated = activated.astype(BF)
 
-    grad_own = lax.all_gather(hidden_grad, "yh", axis=0, tiled=True)
-    grad_own, activated = lax.optimization_barrier((grad_own, along_z(activated, 1)))
+    grad_own = jnp.broadcast_to(hidden_grad[None], (4, pair, NX * cols))
+    grad_own = lax.all_to_all(grad_own, "yh", split_axis=0, concat_axis=0).reshape(4 * pair, NX * cols)
+    activated = within_z(along_z(activated, 1), True)
+    grad_own, activated = lax.optimization_barrier((grad_own, activated))
     grad_other = swap_cores(grad_own)
-    activated = within_z(activated, True)
 
     ig_own = dot(grad_own, w_all, ((1,), (0,))).astype(BF)
     ig_own, grad_other = lax.optimization_barrier((ig_own, grad_other))

time: 190 us -> 197 us (1.037)
  blocking collectives: 18.2 us -> 0 us
  starting transfers between devices: 69.4 us -> 82.1 us
  waiting for transfers between devices: 60.5 us -> 70.4 us
  matrix products: 14.5 us -> 16.5 us
    all_gather x1 -> x0, blocking collectives: 18.2 us -> none  [body(): grad_own = lax.all_gather(hidden_grad, 'yh', axis=0, tiled=True)]
    ppermute x2, waiting for transfers between devices: 21.4 us -> 28.1 us  [within_z(): return lax.ppermute(value, ('z', 'yh', 'c'), pairs)]
    all_to_all x1, starting transfers between devices: 3.79 us -> 9.44 us  [body(): ig = lax.all_to_all(ig, ('z', 'yl'), split_axis=0, concat_axis=0)]
    all_to_all x0 -> x1, starting transfers between devices: none -> 4.44 us  [body(): lax.all_to_all(grad_own, 'yh', split_axis=0, concat_axis=0)]
    ppermute x2, waiting for transfers between devices: 9.09 us -> 12.6 us  [along_z(): return lax.ppermute(value, ('z', 'yh', 'c'), pairs)]
    ppermute x2, starting transfers between devices: 10 us -> 13.5 us  [within_z(): return lax.ppermute(value, ('z', 'yh', 'c'), pairs)]
    dot_general x5, matrix products: 14.5 us -> 16.5 us  [dot(): lax.dot_general(a, b, (contract, ((), ())), preferred_element_type=jnp.fl...]
  transfers between devices with their start and end apart: 18 -> 19, of which waited for: 10 -> 12; matrix products, arithmetic and copies ran while one was open for 12% -> 12% of each run, Pallas kernels for 0% -> 0%
where the time goes in v15:
time: 197 us; the launch traced here: 195 us
  starting transfers between devices  82.1 us (42%)
  waiting for transfers between devices  70.4 us (36%)
  matrix products  16.5 us (8%)
  between operations  14.5 us (7%)
  local copies, waits for them, and re-layouts  9.97 us (5%)
    ppermute x2, waiting for transfers between devices, within_z(): return lax.ppermute(value, ('z', 'yh', 'c'), pairs)  28.1 us
    ppermute x6, starting transfers between devices, along_x(): return lax.ppermute(value, 'x', [(i, (i + shift) % NX) for i in range(NX)])  18.8 us
    ppermute x6, waiting for transfers between devices, along_x(): return lax.ppermute(value, 'x', [(i, (i + shift) % NX) for i in range(NX)])  16.6 us
    dot_general x5, matrix products, dot(): lax.dot_general(a, b, (contract, ((), ())), preferred_element_type=jnp.fl...  16.5 us
    ppermute x2, starting transfers between devices, within_z(): return lax.ppermute(value, ('z', 'yh', 'c'), pairs)  13.5 us
    ppermute x2, waiting for transfers between devices, along_z(): return lax.ppermute(value, ('z', 'yh', 'c'), pairs)  12.6 us
    all_to_all x1, starting transfers between devices, body(): lax.all_to_all(near, ('z', 'yl'), split_axis=0, concat_axis=0)  12 us
    ppermute x2, starting transfers between devices, along_z(): return lax.ppermute(value, ('z', 'yh', 'c'), pairs)  9.62 us
  transfers between devices with their start and end apart: 19, of which 12 were waited for; matrix products, arithmetic and copies ran while one was open for 12% of the time, Pallas kernels for 0%

profile of v15, /device:TPU:1, one launch (start us, length us, event | category | flops | bytes accessed | tf_op | source)
XLA Modules:
  0.0 195.4 jit_solution(12659654605142413212)
XLA Ops:
  7.9 1.8 broadcast_in_dim.47
  9.7 12.0 %all-to-all-start = ((bf16[16,32,896]{2,1,0:T(8,128)(2,1)}), bf16[16,32,896]{2,1,0:T(8,128)(2,1)S(1)}, u32[]{:S(2)}, u32[]{:S(2)}) async-start(bf16[16,32,896]{2,1,0:T(8,128)(2,1)} %broadcast_in_dim.47), calls=%async_computation | async-start | bytes 1835008 | tf_op jit(solution)/shard_map/all_to_all | solution.py:80
  21.9 5.0 %collective-permute-start = (bf16[256,448]{1,0:T(8,128)(2,1)S(1)}, bf16[256,448]{1,0:T(8,128)(2,1)S(1)}, u32[]{:S(2)}, u32[]{:S(2)}) collective-permute-start(bf16[256,448]{1,0:T(8,128)(2,1)S(1)} %copy.22), channel_id=1, source_target_pairs={{0,0},{4,1},{7,2},{3,3},{6,4},{2,5},{5,6},{1,7},{9,8},{13,9},{8,10... | collective-permute-start | bytes 688136 | tf_op jit(solution)/shard_map/ppermute | solution.py:42
  26.9 21.4 %collective-permute-done = bf16[256,448]{1,0:T(8,128)(2,1)S(1)} collective-permute-done((bf16[256,448]{1,0:T(8,128)(2,1)S(1)}, bf16[256,448]{1,0:T(8,128)(2,1)S(1)}, u32[]{:S(2)}, u32[]{:S(2)}) %collective-permute-start) | collective-permute-done | bytes 229408 | tf_op jit(solution)/shard_map/ppermute | solution.py:42
  48.3 1.9 collective-permute-start.1
  50.2 9.1 %collective-permute-done.1 = bf16[256,448]{1,0:T(8,128)(2,1)S(1)} collective-permute-done((bf16[256,448]{1,0:T(8,128)(2,1)S(1)}, bf16[256,448]{1,0:T(8,128)(2,1)S(1)}, u32[]{:S(2)}, u32[]{:S(2)}) %collective-permute-start.1) | collective-permute-done | bytes 229408 | tf_op jit(solution)/shard_map/ppermute | solution.py:33
  61.0 3.1 %convolution_convert_fusion = bf16[256,1792]{1,0:T(8,128)(2,1)S(1)} fusion(bf16[1792,896]{1,0:T(8,128)(2,1)} %all-gather.5.cloned.1.call-done, bf16[2,256,896]{2,1,0:T(8,128)(2,1)S(1)} %pad_maximum_fusion.3), kind=kOutput, calls=%fused_computation | convolution fusion | flops 822542336 | bytes 4587520 | tf_op jit(solution)/shard_map/dot_general | solution.py:67
  64.1 2.6 %collective-permute-start.2 = (bf16[256,1792]{1,0:T(8,128)(2,1)S(1)}, bf16[256,1792]{1,0:T(8,128)(2,1)S(1)}, u32[]{:S(2)}, u32[]{:S(2)}) collective-permute-start(bf16[256,1792]{1,0:T(8,128)(2,1)S(1)} %convolution_convert_fusion), channel_id=1, source_target_pairs={{0,1},{1,0},{2,3},{3,2},{4,5},{5,4},{6,7},{7,6},{8,9},{9,8},{10,11... | collective-permute-start | bytes 2752520 | tf_op jit(solution)/shard_map/ppermute | solution.py:21
  66.7 2.1 %collective-permute-done.2 = bf16[256,1792]{1,0:T(8,128)(2,1)S(1)} collective-permute-done((bf16[256,1792]{1,0:T(8,128)(2,1)S(1)}, bf16[256,1792]{1,0:T(8,128)(2,1)S(1)}, u32[]{:S(2)}, u32[]{:S(2)}) %collective-permute-start.2) | collective-permute-done | bytes 917536 | tf_op jit(solution)/shard_map/ppermute | solution.py:21
  68.8 4.2 %add_convert_fusion = bf16[256,1792]{1,0:T(8,128)(2,1)} fusion(bf16[256,1792]{1,0:T(8,128)(2,1)S(1)} %collective-permute-done.2, bf16[1792,896]{1,0:T(8,128)(2,1)} %all-gather.5.cloned.1.call-done, bf16[2,256,896]{2,1,0:T(8,128)(2,1)} %copy-done), kind=kOutput, calls=%fused_computation.8 | convolution fusion | flops 823459840 | bytes 5505024 | tf_op jit(solution)/shard_map/dot_general | solution.py:67
  73.0 6.4 %all-to-all-start.1 = ((bf16[4,64,1792]{2,1,0:T(8,128)(2,1)}), bf16[4,64,1792]{2,1,0:T(8,128)(2,1)S(1)}, u32[]{:S(2)}, u32[]{:S(2)}) async-start(bf16[4,64,1792]{2,1,0:T(8,128)(2,1)} %bitcast.9), calls=%async_computation.1 | async-start | bytes 1835008 | tf_op jit(solution)/shard_map/all_to_all | solution.py:91
  79.5 2.3 %collective-permute-start.3 = (bf16[64,448]{1,0:T(8,128)(2,1)S(1)}, bf16[64,448]{1,0:T(8,128)(2,1)S(1)}, u32[]{:S(2)}, u32[]{:S(2)}) collective-permute-start(bf16[64,448]{1,0:T(8,128)(2,1)S(1)} %get-tuple-element.57), channel_id=1, source_target_pairs={{0,128},{128,256},{256,384},{384,0},{1,129},{129,257},{257,385},{3... | collective-permute-start | bytes 172040 | tf_op jit(solution)/shard_map/ppermute | solution.py:17
  81.8 3.4 %collective-permute-start.4 = (bf16[64,448]{1,0:T(8,128)(2,1)S(1)}, bf16[64,448]{1,0:T(8,128)(2,1)S(1)}, u32[]{:S(2)}, u32[]{:S(2)}) collective-permute-start(bf16[64,448]{1,0:T(8,128)(2,1)S(1)} %get-tuple-element.56), channel_id=1, source_target_pairs={{0,256},{128,384},{256,0},{384,128},{1,257},{129,385},{257,1},{385... | collective-permute-start | bytes 172040 | tf_op jit(solution)/shard_map/ppermute | solution.py:17
  85.2 3.7 %collective-permute-start.5 = (bf16[64,448]{1,0:T(8,128)(2,1)S(1)}, bf16[64,448]{1,0:T(8,128)(2,1)S(1)}, u32[]{:S(2)}, u32[]{:S(2)}) collective-permute-start(bf16[64,448]{1,0:T(8,128)(2,1)S(1)} %get-tuple-element.55), channel_id=1, source_target_pairs={{0,384},{128,0},{256,128},{384,256},{1,385},{129,1},{257,129},{385... | collective-permute-start | bytes 172040 | tf_op jit(solution)/shard_map/ppermute | solution.py:17
  90.0 3.0 %collective-permute-done.5 = bf16[64,448]{1,0:T(8,128)(2,1)S(1)} collective-permute-done((bf16[64,448]{1,0:T(8,128)(2,1)S(1)}, bf16[64,448]{1,0:T(8,128)(2,1)S(1)}, u32[]{:S(2)}, u32[]{:S(2)}) %collective-permute-start.5) | collective-permute-done | bytes 57376 | tf_op jit(solution)/shard_map/ppermute | solution.py:17
  93.9 9.0 %all-to-all-done.1 = bf16[4,64,1792]{2,1,0:T(8,128)(2,1)S(1)} async-done(((bf16[4,64,1792]{2,1,0:T(8,128)(2,1)}), bf16[4,64,1792]{2,1,0:T(8,128)(2,1)S(1)}, u32[]{:S(2)}, u32[]{:S(2)}) %all-to-all-start.1) | async-done | bytes 917536 | tf_op jit(solution)/shard_map/all_to_all | solution.py:91
  104.4 4.4 %all-to-all-start.2 = ((bf16[4,64,1792]{2,1,0:T(8,128)(2,1)}), bf16[4,64,1792]{2,1,0:T(8,128)(2,1)S(1)}, u32[]{:S(2)}, u32[]{:S(2)}) async-start(bf16[4,64,1792]{2,1,0:T(8,128)(2,1)} %broadcast_in_dim.51), calls=%async_computation.2 | async-start | bytes 1835008 | tf_op jit(solution)/shard_map/all_to_all | solution.py:102
  108.8 7.7 %collective-permute-start.6 = (bf16[64,1792]{1,0:T(8,128)(2,1)S(1)}, bf16[64,1792]{1,0:T(8,128)(2,1)S(1)}, u32[]{:S(2)}, u32[]{:S(2)}) collective-permute-start(bf16[64,1792]{1,0:T(8,128)(2,1)S(1)} %get-tuple-element.53), channel_id=1, source_target_pairs={{0,0},{1,33},{2,10},{3,43},{4,20},{5,53},{6,30},{7,63},{8,8},{9,41... | collective-permute-start | bytes 688136 | tf_op jit(solution)/shard_map/ppermute | solution.py:33
  116.6 3.5 %collective-permute-done.6 = bf16[64,1792]{1,0:T(8,128)(2,1)S(1)} collective-permute-done((bf16[64,1792]{1,0:T(8,128)(2,1)S(1)}, bf16[64,1792]{1,0:T(8,128)(2,1)S(1)}, u32[]{:S(2)}, u32[]{:S(2)}) %collective-permute-start.6) | collective-permute-done | bytes 229408 | tf_op jit(solution)/shard_map/ppermute | solution.py:33
  120.1 8.5 %collective-permute-start.7 = (bf16[64,1792]{1,0:T(8,128)(2,1)S(1)}, bf16[64,1792]{1,0:T(8,128)(2,1)S(1)}, u32[]{:S(2)}, u32[]{:S(2)}) collective-permute-start(bf16[64,1792]{1,0:T(8,128)(2,1)S(1)} %collective-permute-done.6), channel_id=1, source_target_pairs={{0,0},{1,4},{2,7},{3,3},{4,6},{5,2},{6,5},{7,1},{8,9},{9,13},{10,8... | collective-permute-start | bytes 688136 | tf_op jit(solution)/shard_map/ppermute | solution.py:42
  128.6 6.7 %collective-permute-done.7 = bf16[64,1792]{1,0:T(8,128)(2,1)S(1)} collective-permute-done((bf16[64,1792]{1,0:T(8,128)(2,1)S(1)}, bf16[64,1792]{1,0:T(8,128)(2,1)S(1)}, u32[]{:S(2)}, u32[]{:S(2)}) %collective-permute-start.7) | collective-permute-done | bytes 229408 | tf_op jit(solution)/shard_map/ppermute | solution.py:42
  135.3 1.9 collective-permute-start.8
  137.2 3.2 %convolution_convert_fusion.2 = bf16[256,896]{1,0:T(8,128)(2,1)S(1)} fusion(bf16[256,1792]{1,0:T(8,128)(2,1)S(1)} %bitcast.88, bf16[1792,896]{1,0:T(8,128)(2,1)} %all-gather.5.cloned.1.call-done), kind=kOutput, calls=%fused_computation.11 | convolution fusion | flops 822312960 | bytes 4587520 | tf_op jit(solution)/shard_map/dot_general | solution.py:67
  142.9 9.4 %all-to-all-start.3 = ((bf16[16,32,896]{2,1,0:T(8,128)(2,1)}), bf16[16,32,896]{2,1,0:T(8,128)(2,1)S(1)}, u32[]{:S(2)}, u32[]{:S(2)}) async-start(bf16[16,32,896]{2,1,0:T(8,128)(2,1)} %bitcast.23), calls=%async_computation.3 | async-start | bytes 1835008 | tf_op jit(solution)/shard_map/all_to_all | solution.py:112
  154.3 2.2 %collective-permute-start.9 = (bf16[320,448]{0,1:T(8,128)(2,1)}, bf16[320,448]{0,1:T(8,128)(2,1)S(1)}, u32[]{:S(2)}, u32[]{:S(2)}) collective-permute-start(bf16[320,448]{0,1:T(8,128)(2,1)} %get-tuple-element.51), channel_id=1, source_target_pairs={{0,128},{128,256},{256,384},{384,0},{1,129},{129,257},{257,385},{3... | collective-permute-start | bytes 860168 | tf_op jit(solution)/shard_map/ppermute | solution.py:17
  156.5 4.3 %collective-permute-start.10 = (bf16[320,448]{0,1:T(8,128)(2,1)S(1)}, bf16[320,448]{0,1:T(8,128)(2,1)S(1)}, u32[]{:S(2)}, u32[]{:S(2)}) collective-permute-start(bf16[320,448]{0,1:T(8,128)(2,1)S(1)} %get-tuple-element.50), channel_id=1, source_target_pairs={{0,256},{128,384},{256,0},{384,128},{1,257},{129,385},{257,1},{385... | collective-permute-start | bytes 860168 | tf_op jit(solution)/shard_map/ppermute | solution.py:17
  160.8 2.8 %collective-permute-start.11 = (bf16[320,448]{0,1:T(8,128)(2,1)S(1)}, bf16[320,448]{0,1:T(8,128)(2,1)S(1)}, u32[]{:S(2)}, u32[]{:S(2)}) collective-permute-start(bf16[320,448]{0,1:T(8,128)(2,1)S(1)} %get-tuple-element.49), channel_id=1, source_target_pairs={{0,384},{128,0},{256,128},{384,256},{1,385},{129,1},{257,129},{385... | collective-permute-start | bytes 860168 | tf_op jit(solution)/shard_map/ppermute | solution.py:17
  163.8 3.7 %collective-permute-done.9 = bf16[320,448]{0,1:T(8,128)(2,1)S(1)} collective-permute-done((bf16[320,448]{0,1:T(8,128)(2,1)}, bf16[320,448]{0,1:T(8,128)(2,1)S(1)}, u32[]{:S(2)}, u32[]{:S(2)}) %collective-permute-start.9) | collective-permute-done | bytes 286752 | tf_op jit(solution)/shard_map/ppermute | solution.py:17
  167.5 6.3 %collective-permute-done.10 = bf16[320,448]{0,1:T(8,128)(2,1)S(1)} collective-permute-done((bf16[320,448]{0,1:T(8,128)(2,1)S(1)}, bf16[320,448]{0,1:T(8,128)(2,1)S(1)}, u32[]{:S(2)}, u32[]{:S(2)}) %collective-permute-start.10) | collective-permute-done | bytes 286752 | tf_op jit(solution)/shard_map/ppermute | solution.py:17
  173.8 2.5 %collective-permute-done.11 = bf16[320,448]{0,1:T(8,128)(2,1)S(1)} collective-permute-done((bf16[320,448]{0,1:T(8,128)(2,1)S(1)}, bf16[320,448]{0,1:T(8,128)(2,1)S(1)}, u32[]{:S(2)}, u32[]{:S(2)}) %collective-permute-start.11) | collective-permute-done | bytes 286752 | tf_op jit(solution)/shard_map/ppermute | solution.py:17
  176.4 3.3 %collective-permute-start.12 = (bf16[4,256,448]{1,2,0:T(8,128)(2,1)S(1)}, bf16[4,256,448]{1,2,0:T(8,128)(2,1)S(1)}, u32[]{:S(2)}, u32[]{:S(2)}) collective-permute-start(bf16[4,256,448]{1,2,0:T(8,128)(2,1)S(1)} %fusion.21), channel_id=1, source_target_pairs={{0,1},{1,0},{2,3},{3,2},{4,5},{5,4},{6,7},{7,6},{8,9},{9,8},{10,11... | collective-permute-start | bytes 2752520 | tf_op jit(solution)/shard_map/ppermute | solution.py:21
  181.9 5.0 %bitcast_convert_fusion = bf16[896,448]{0,1:T(8,128)(2,1)} fusion(bf16[4,2,256,896]{3,2,1,0:T(8,128)(2,1)} %bitcast.97, bf16[4,1,256,448]{2,3,1,0:T(8,128)(2,1)S(1)} %bitcast.98, bf16[4,1,256,448]{2,3,1,0:T(8,128)(2,1)S(1)} %bitcast.93), kind=kOutput, calls=%fused_computation.9 | convolution fusion | flops 1645486080 | bytes 6307840 | tf_op jit(solution)/shard_map/dot_general | solution.py:67
  (65 shorter events, 14.4 us)
Async XLA Ops:
  7.2 14.6 %copy-start.3 = (bf16[256,448]{0,1:T(8,128)(2,1)S(1)}, bf16[256,448]{0,1:T(8,128)(2,1)}, u32[]{:S(2)}) copy-start(bf16[256,448]{0,1:T(8,128)(2,1)} %param.5) | copy-start | bytes 688132
  7.2 53.9 %all-gather.5.cloned.1.call-start = ((), (), s32[]{:S(2)}) async-start(), calls=%async_computation.4 | async-start | bytes 4014080 | tf_op jit(solution)/shard_map/all_gather | solution.py:77
  9.7 49.6 %all-to-all-start = ((bf16[16,32,896]{2,1,0:T(8,128)(2,1)}), bf16[16,32,896]{2,1,0:T(8,128)(2,1)S(1)}, u32[]{:S(2)}, u32[]{:S(2)}) async-start(bf16[16,32,896]{2,1,0:T(8,128)(2,1)} %broadcast_in_dim.47), calls=%async_computation | async-start | bytes 1835008 | tf_op jit(solution)/shard_map/all_to_all | solution.py:80
  21.7 130.6 %all-gather.7.cloned.1.call-start = ((), (), s32[]{:S(2)}) async-start(), calls=%async_computation.5 | async-start | bytes 4587520 | tf_op jit(solution)/shard_map/all_gather | solution.py:114
  21.9 26.4 %collective-permute-start = (bf16[256,448]{1,0:T(8,128)(2,1)S(1)}, bf16[256,448]{1,0:T(8,128)(2,1)S(1)}, u32[]{:S(2)}, u32[]{:S(2)}) collective-permute-start(bf16[256,448]{1,0:T(8,128)(2,1)S(1)} %copy.22), channel_id=1, source_target_pairs={{0,0},{4,1},{7,2},{3,3},{6,4},{2,5},{5,6},{1,7},{9,8},{13,9},{8,10... | collective-permute-start | bytes 688136 | tf_op jit(solution)/shard_map/ppermute | solution.py:42
  48.3 11.0 %collective-permute-start.1 = (bf16[256,448]{1,0:T(8,128)(2,1)S(1)}, bf16[256,448]{1,0:T(8,128)(2,1)S(1)}, u32[]{:S(2)}, u32[]{:S(2)}) collective-permute-start(bf16[256,448]{1,0:T(8,128)(2,1)S(1)} %collective-permute-done), channel_id=1, source_target_pairs={{0,0},{1,33},{2,58},{3,27},{4,52},{5,21},{6,46},{7,15},{8,8},{9,41... | collective-permute-start | bytes 688136 | tf_op jit(solution)/shard_map/ppermute | solution.py:33
  59.7 4.4 %copy-start = (bf16[2,256,896]{2,1,0:T(8,128)(2,1)}, bf16[2,256,896]{2,1,0:T(8,128)(2,1)S(1)}, u32[]{:S(2)}) copy-start(bf16[2,256,896]{2,1,0:T(8,128)(2,1)S(1)} %pad_maximum_fusion.3) | copy-start | bytes 2752516
  64.1 4.7 %collective-permute-start.2 = (bf16[256,1792]{1,0:T(8,128)(2,1)S(1)}, bf16[256,1792]{1,0:T(8,128)(2,1)S(1)}, u32[]{:S(2)}, u32[]{:S(2)}) collective-permute-start(bf16[256,1792]{1,0:T(8,128)(2,1)S(1)} %convolution_convert_fusion), channel_id=1, source_target_pairs={{0,1},{1,0},{2,3},{3,2},{4,5},{5,4},{6,7},{7,6},{8,9},{9,8},{10,11... | collective-permute-start | bytes 2752520 | tf_op jit(solution)/shard_map/ppermute | solution.py:21
  73.0 29.9 %all-to-all-start.1 = ((bf16[4,64,1792]{2,1,0:T(8,128)(2,1)}), bf16[4,64,1792]{2,1,0:T(8,128)(2,1)S(1)}, u32[]{:S(2)}, u32[]{:S(2)}) async-start(bf16[4,64,1792]{2,1,0:T(8,128)(2,1)} %bitcast.9), calls=%async_computation.1 | async-start | bytes 1835008 | tf_op jit(solution)/shard_map/all_to_all | solution.py:91
  79.5 9.5 %collective-permute-start.3 = (bf16[64,448]{1,0:T(8,128)(2,1)S(1)}, bf16[64,448]{1,0:T(8,128)(2,1)S(1)}, u32[]{:S(2)}, u32[]{:S(2)}) collective-permute-start(bf16[64,448]{1,0:T(8,128)(2,1)S(1)} %get-tuple-element.57), channel_id=1, source_target_pairs={{0,128},{128,256},{256,384},{384,0},{1,129},{129,257},{257,385},{3... | collective-permute-start | bytes 172040 | tf_op jit(solution)/shard_map/ppermute | solution.py:17
  81.8 8.2 %collective-permute-start.4 = (bf16[64,448]{1,0:T(8,128)(2,1)S(1)}, bf16[64,448]{1,0:T(8,128)(2,1)S(1)}, u32[]{:S(2)}, u32[]{:S(2)}) collective-permute-start(bf16[64,448]{1,0:T(8,128)(2,1)S(1)} %get-tuple-element.56), channel_id=1, source_target_pairs={{0,256},{128,384},{256,0},{384,128},{1,257},{129,385},{257,1},{385... | collective-permute-start | bytes 172040 | tf_op jit(solution)/shard_map/ppermute | solution.py:17
  85.2 7.8 %collective-permute-start.5 = (bf16[64,448]{1,0:T(8,128)(2,1)S(1)}, bf16[64,448]{1,0:T(8,128)(2,1)S(1)}, u32[]{:S(2)}, u32[]{:S(2)}) collective-permute-start(bf16[64,448]{1,0:T(8,128)(2,1)S(1)} %get-tuple-element.55), channel_id=1, source_target_pairs={{0,384},{128,0},{256,128},{384,256},{1,385},{129,1},{257,129},{385... | collective-permute-start | bytes 172040 | tf_op jit(solution)/shard_map/ppermute | solution.py:17
  104.4 30.9 %all-to-all-start.2 = ((bf16[4,64,1792]{2,1,0:T(8,128)(2,1)}), bf16[4,64,1792]{2,1,0:T(8,128)(2,1)S(1)}, u32[]{:S(2)}, u32[]{:S(2)}) async-start(bf16[4,64,1792]{2,1,0:T(8,128)(2,1)} %broadcast_in_dim.51), calls=%async_computation.2 | async-start | bytes 1835008 | tf_op jit(solution)/shard_map/all_to_all | solution.py:102
  108.8 11.2 %collective-permute-start.6 = (bf16[64,1792]{1,0:T(8,128)(2,1)S(1)}, bf16[64,1792]{1,0:T(8,128)(2,1)S(1)}, u32[]{:S(2)}, u32[]{:S(2)}) collective-permute-start(bf16[64,1792]{1,0:T(8,128)(2,1)S(1)} %get-tuple-element.53), channel_id=1, source_target_pairs={{0,0},{1,33},{2,10},{3,43},{4,20},{5,53},{6,30},{7,63},{8,8},{9,41... | collective-permute-start | bytes 688136 | tf_op jit(solution)/shard_map/ppermute | solution.py:33
  120.1 15.3 %collective-permute-start.7 = (bf16[64,1792]{1,0:T(8,128)(2,1)S(1)}, bf16[64,1792]{1,0:T(8,128)(2,1)S(1)}, u32[]{:S(2)}, u32[]{:S(2)}) collective-permute-start(bf16[64,1792]{1,0:T(8,128)(2,1)S(1)} %collective-permute-done.6), channel_id=1, source_target_pairs={{0,0},{1,4},{2,7},{3,3},{4,6},{5,2},{6,5},{7,1},{8,9},{9,13},{10,8... | collective-permute-start | bytes 688136 | tf_op jit(solution)/shard_map/ppermute | solution.py:42
  135.3 5.1 %collective-permute-start.8 = (bf16[256,1792]{1,0:T(8,128)(2,1)S(1)}, bf16[256,1792]{1,0:T(8,128)(2,1)S(1)}, u32[]{:S(2)}, u32[]{:S(2)}) collective-permute-start(bf16[256,1792]{1,0:T(8,128)(2,1)S(1)} %bitcast.87), channel_id=1, source_target_pairs={{0,1},{1,0},{2,3},{3,2},{4,5},{5,4},{6,7},{7,6},{8,9},{9,8},{10,11... | collective-permute-start | bytes 2752520 | tf_op jit(solution)/shard_map/ppermute | solution.py:21
  137.2 3.2 %copy-start.4 = (bf16[1792,896]{1,0:T(8,128)(2,1)S(1)}, bf16[1792,896]{1,0:T(8,128)(2,1)}, u32[]{:S(2)}) copy-start(bf16[1792,896]{1,0:T(8,128)(2,1)} %all-gather.5.cloned.1.call-done) | copy-start | bytes 9633796
  142.9 44.1 %all-to-all-start.3 = ((bf16[16,32,896]{2,1,0:T(8,128)(2,1)}), bf16[16,32,896]{2,1,0:T(8,128)(2,1)S(1)}, u32[]{:S(2)}, u32[]{:S(2)}) async-start(bf16[16,32,896]{2,1,0:T(8,128)(2,1)} %bitcast.23), calls=%async_computation.3 | async-start | bytes 1835008 | tf_op jit(solution)/shard_map/all_to_all | solution.py:112
  154.3 13.2 %collective-permute-start.9 = (bf16[320,448]{0,1:T(8,128)(2,1)}, bf16[320,448]{0,1:T(8,128)(2,1)S(1)}, u32[]{:S(2)}, u32[]{:S(2)}) collective-permute-start(bf16[320,448]{0,1:T(8,128)(2,1)} %get-tuple-element.51), channel_id=1, source_target_pairs={{0,128},{128,256},{256,384},{384,0},{1,129},{129,257},{257,385},{3... | collective-permute-start | bytes 860168 | tf_op jit(solution)/shard_map/ppermute | solution.py:17
  156.5 17.3 %collective-permute-start.10 = (bf16[320,448]{0,1:T(8,128)(2,1)S(1)}, bf16[320,448]{0,1:T(8,128)(2,1)S(1)}, u32[]{:S(2)}, u32[]{:S(2)}) collective-permute-start(bf16[320,448]{0,1:T(8,128)(2,1)S(1)} %get-tuple-element.50), channel_id=1, source_target_pairs={{0,256},{128,384},{256,0},{384,128},{1,257},{129,385},{257,1},{385... | collective-permute-start | bytes 860168 | tf_op jit(solution)/shard_map/ppermute | solution.py:17
  160.8 15.5 %collective-permute-start.11 = (bf16[320,448]{0,1:T(8,128)(2,1)S(1)}, bf16[320,448]{0,1:T(8,128)(2,1)S(1)}, u32[]{:S(2)}, u32[]{:S(2)}) collective-permute-start(bf16[320,448]{0,1:T(8,128)(2,1)S(1)} %get-tuple-element.49), channel_id=1, source_target_pairs={{0,384},{128,0},{256,128},{384,256},{1,385},{129,1},{257,129},{385... | collective-permute-start | bytes 860168 | tf_op jit(solution)/shard_map/ppermute | solution.py:17
  173.8 2.6 %copy-start.1 = (bf16[320,448]{0,1:T(8,128)(2,1)}, bf16[320,448]{0,1:T(8,128)(2,1)S(1)}, u32[]{:S(2)}) copy-start(bf16[320,448]{0,1:T(8,128)(2,1)S(1)} %collective-permute-done.10) | copy-start | bytes 860164
  176.4 3.4 %copy-start.2 = (bf16[320,448]{0,1:T(8,128)(2,1)}, bf16[320,448]{0,1:T(8,128)(2,1)S(1)}, u32[]{:S(2)}) copy-start(bf16[320,448]{0,1:T(8,128)(2,1)S(1)} %collective-permute-done.11) | copy-start | bytes 860164
  176.4 5.6 %collective-permute-start.12 = (bf16[4,256,448]{1,2,0:T(8,128)(2,1)S(1)}, bf16[4,256,448]{1,2,0:T(8,128)(2,1)S(1)}, u32[]{:S(2)}, u32[]{:S(2)}) collective-permute-start(bf16[4,256,448]{1,2,0:T(8,128)(2,1)S(1)} %fusion.21), channel_id=1, source_target_pairs={{0,1},{1,0},{2,3},{3,2},{4,5},{5,4},{6,7},{7,6},{8,9},{9,8},{10,11... | collective-permute-start | bytes 2752520 | tf_op jit(solution)/shard_map/ppermute | solution.py:21
Sparse Core Ops, SparseCore 0:
  10.1 50.8 all-gather.4
  66.8 51.2 all-gather.6

commit v16 on v12

--- a/solution.py
+++ b/solution.py
@@ -79,8 +79,9 @@
     near = jnp.broadcast_to(tokens[None], (16, rows, feats))
     near = lax.all_to_all(near, ("z", "yl"), split_axis=0, concat_axis=0).reshape(8, pair, feats)
     cot = along_z(within_z(act_grad, False), -1)
+    near, cot = lax.optimization_barrier((near, cot))
+    near = jnp.stack([cut(near, first, 4), cut(near, first + 4, 4)])
     near, cot, w_all = lax.optimization_barrier((near, cot, w_all))
-    near = jnp.stack([cut(near, first, 4), cut(near, first + 4, 4)])
     w_all = w_all.reshape(NX * cols, feats)
 
     sent = swap_cores(dot(near[1], w_all, ((1,), (1,))).astype(BF))

time: 190 us -> 189 us (level)
  transfers between devices with their start and end apart: 18 -> 18, of which waited for: 10 -> 10; matrix products, arithmetic and copies ran while one was open for 12% -> 13% of each run, Pallas kernels for 0% -> 0%
where the time goes in v16:
time: 189 us; the launch traced here: 188 us
  starting transfers between devices  69.4 us (37%)
  waiting for transfers between devices  59.5 us (31%)
  blocking collectives  18.6 us (10%)
  matrix products  14.6 us (8%)
  between operations  14.5 us (8%)
  local copies, waits for them, and re-layouts  8.92 us (5%)
  other arithmetic  2.84 us (2%)
    ppermute x2, waiting for transfers between devices, within_z(): return lax.ppermute(value, ('z', 'yh', 'c'), pairs)  21.4 us
    all_gather x1, blocking collectives, body(): grad_own = lax.all_gather(hidden_grad, 'yh', axis=0, tiled=True)  18.6 us
    ppermute x6, starting transfers between devices, along_x(): return lax.ppermute(value, 'x', [(i, (i + shift) % NX) for i in range(NX)])  18.4 us
    ppermute x6, waiting for transfers between devices, along_x(): return lax.ppermute(value, 'x', [(i, (i + shift) % NX) for i in range(NX)])  16.8 us
    dot_general x5, matrix products, dot(): lax.dot_general(a, b, (contract, ((), ())), preferred_element_type=jnp.fl...  14.6 us
    all_to_all x1, starting transfers between devices, body(): lax.all_to_all(near, ('z', 'yl'), split_axis=0, concat_axis=0)  12 us
    ppermute x2, starting transfers between devices, within_z(): return lax.ppermute(value, ('z', 'yh', 'c'), pairs)  10.3 us
    ppermute x2, starting transfers between devices, along_z(): return lax.ppermute(value, ('z', 'yh', 'c'), pairs)  9.64 us
  transfers between devices with their start and end apart: 18, of which 10 were waited for; matrix products, arithmetic and copies ran while one was open for 13% of the time, Pallas kernels for 0%

profile of v16, /device:TPU:1, one launch (start us, length us, event | category | flops | bytes accessed | tf_op | source)
XLA Modules:
  0.0 188.4 jit_solution(1423612411603267358)
XLA Ops:
  7.9 1.8 broadcast_in_dim.41
  9.7 12.0 %all-to-all-start = ((bf16[16,32,896]{2,1,0:T(8,128)(2,1)}), bf16[16,32,896]{2,1,0:T(8,128)(2,1)S(1)}, u32[]{:S(2)}, u32[]{:S(2)}) async-start(bf16[16,32,896]{2,1,0:T(8,128)(2,1)} %broadcast_in_dim.41), calls=%async_computation | async-start | bytes 1835008 | tf_op jit(solution)/shard_map/all_to_all | solution.py:80
  21.9 5.0 %collective-permute-start = (bf16[256,448]{1,0:T(8,128)(2,1)S(1)}, bf16[256,448]{1,0:T(8,128)(2,1)S(1)}, u32[]{:S(2)}, u32[]{:S(2)}) collective-permute-start(bf16[256,448]{1,0:T(8,128)(2,1)S(1)} %copy.29), channel_id=1, source_target_pairs={{0,0},{4,1},{7,2},{3,3},{6,4},{2,5},{5,6},{1,7},{9,8},{13,9},{8,10... | collective-permute-start | bytes 688136 | tf_op jit(solution)/shard_map/ppermute | solution.py:42
  26.9 21.4 %collective-permute-done = bf16[256,448]{1,0:T(8,128)(2,1)S(1)} collective-permute-done((bf16[256,448]{1,0:T(8,128)(2,1)S(1)}, bf16[256,448]{1,0:T(8,128)(2,1)S(1)}, u32[]{:S(2)}, u32[]{:S(2)}) %collective-permute-start) | collective-permute-done | bytes 229408 | tf_op jit(solution)/shard_map/ppermute | solution.py:42
  48.3 1.9 %collective-permute-start.1 = (bf16[256,448]{1,0:T(8,128)(2,1)S(1)}, bf16[256,448]{1,0:T(8,128)(2,1)S(1)}, u32[]{:S(2)}, u32[]{:S(2)}) collective-permute-start(bf16[256,448]{1,0:T(8,128)(2,1)S(1)} %collective-permute-done), channel_id=1, source_target_pairs={{0,0},{1,33},{2,58},{3,27},{4,52},{5,21},{6,46},{7,15},{8,8},{9,41... | collective-permute-start | bytes 688136 | tf_op jit(solution)/shard_map/ppermute | solution.py:33
  50.2 9.1 %collective-permute-done.1 = bf16[256,448]{1,0:T(8,128)(2,1)S(1)} collective-permute-done((bf16[256,448]{1,0:T(8,128)(2,1)S(1)}, bf16[256,448]{1,0:T(8,128)(2,1)S(1)}, u32[]{:S(2)}, u32[]{:S(2)}) %collective-permute-start.1) | collective-permute-done | bytes 229408 | tf_op jit(solution)/shard_map/ppermute | solution.py:33
  61.1 3.3 %convolution_convert_fusion = bf16[256,1792]{1,0:T(8,128)(2,1)S(1)} fusion(bf16[1792,896]{1,0:T(8,128)(2,1)} %all-gather.5.cloned.1.call-done, bf16[2,256,896]{2,1,0:T(8,128)(2,1)} %pad_maximum_fusion.3), kind=kOutput, calls=%fused_computation | convolution fusion | flops 822542336 | bytes 4587520 | tf_op jit(solution)/shard_map/dot_general | solution.py:67
  64.4 2.6 %collective-permute-start.2 = (bf16[256,1792]{1,0:T(8,128)(2,1)S(1)}, bf16[256,1792]{1,0:T(8,128)(2,1)S(1)}, u32[]{:S(2)}, u32[]{:S(2)}) collective-permute-start(bf16[256,1792]{1,0:T(8,128)(2,1)S(1)} %convolution_convert_fusion), channel_id=1, source_target_pairs={{0,1},{1,0},{2,3},{3,2},{4,5},{5,4},{6,7},{7,6},{8,9},{9,8},{10,11... | collective-permute-start | bytes 2752520 | tf_op jit(solution)/shard_map/ppermute | solution.py:21
  67.0 2.1 %collective-permute-done.2 = bf16[256,1792]{1,0:T(8,128)(2,1)S(1)} collective-permute-done((bf16[256,1792]{1,0:T(8,128)(2,1)S(1)}, bf16[256,1792]{1,0:T(8,128)(2,1)S(1)}, u32[]{:S(2)}, u32[]{:S(2)}) %collective-permute-start.2) | collective-permute-done | bytes 917536 | tf_op jit(solution)/shard_map/ppermute | solution.py:21
  69.1 2.2 %add_convert_fusion = bf16[256,1792]{1,0:T(8,128)(2,1)} fusion(bf16[256,1792]{1,0:T(8,128)(2,1)S(1)} %collective-permute-done.2, bf16[1792,896]{1,0:T(8,128)(2,1)S(1)} %copy-done.4, bf16[2,256,896]{2,1,0:T(8,128)(2,1)S(1)} %copy-done), kind=kOutput, calls=%fused_computation.8 | convolution fusion | flops 823459840 | bytes 5505024 | tf_op jit(solution)/shard_map/dot_general | solution.py:67
  71.3 6.4 %all-to-all-start.1 = ((bf16[4,64,1792]{2,1,0:T(8,128)(2,1)}), bf16[4,64,1792]{2,1,0:T(8,128)(2,1)S(1)}, u32[]{:S(2)}, u32[]{:S(2)}) async-start(bf16[4,64,1792]{2,1,0:T(8,128)(2,1)} %bitcast.9), calls=%async_computation.1 | async-start | bytes 1835008 | tf_op jit(solution)/shard_map/all_to_all | solution.py:91
  77.8 2.3 %collective-permute-start.3 = (bf16[64,448]{1,0:T(8,128)(2,1)S(1)}, bf16[64,448]{1,0:T(8,128)(2,1)S(1)}, u32[]{:S(2)}, u32[]{:S(2)}) collective-permute-start(bf16[64,448]{1,0:T(8,128)(2,1)S(1)} %get-tuple-element.60), channel_id=1, source_target_pairs={{0,128},{128,256},{256,384},{384,0},{1,129},{129,257},{257,385},{3... | collective-permute-start | bytes 172040 | tf_op jit(solution)/shard_map/ppermute | solution.py:17
  80.1 3.6 %collective-permute-start.4 = (bf16[64,448]{1,0:T(8,128)(2,1)S(1)}, bf16[64,448]{1,0:T(8,128)(2,1)S(1)}, u32[]{:S(2)}, u32[]{:S(2)}) collective-permute-start(bf16[64,448]{1,0:T(8,128)(2,1)S(1)} %get-tuple-element.59), channel_id=1, source_target_pairs={{0,256},{128,384},{256,0},{384,128},{1,257},{129,385},{257,1},{385... | collective-permute-start | bytes 172040 | tf_op jit(solution)/shard_map/ppermute | solution.py:17
  83.8 3.5 %collective-permute-start.5 = (bf16[64,448]{1,0:T(8,128)(2,1)S(1)}, bf16[64,448]{1,0:T(8,128)(2,1)S(1)}, u32[]{:S(2)}, u32[]{:S(2)}) collective-permute-start(bf16[64,448]{1,0:T(8,128)(2,1)S(1)} %get-tuple-element.58), channel_id=1, source_target_pairs={{0,384},{128,0},{256,128},{384,256},{1,385},{129,1},{257,129},{385... | collective-permute-start | bytes 172040 | tf_op jit(solution)/shard_map/ppermute | solution.py:17
  87.3 1.3 collective-permute-done.4
  88.5 2.8 %collective-permute-done.5 = bf16[64,448]{1,0:T(8,128)(2,1)S(1)} collective-permute-done((bf16[64,448]{1,0:T(8,128)(2,1)S(1)}, bf16[64,448]{1,0:T(8,128)(2,1)S(1)}, u32[]{:S(2)}, u32[]{:S(2)}) %collective-permute-start.5) | collective-permute-done | bytes 57376 | tf_op jit(solution)/shard_map/ppermute | solution.py:17
  92.2 9.0 %all-to-all-done.1 = bf16[4,64,1792]{2,1,0:T(8,128)(2,1)S(1)} async-done(((bf16[4,64,1792]{2,1,0:T(8,128)(2,1)}), bf16[4,64,1792]{2,1,0:T(8,128)(2,1)S(1)}, u32[]{:S(2)}, u32[]{:S(2)}) %all-to-all-start.1) | async-done | bytes 917536 | tf_op jit(solution)/shard_map/all_to_all | solution.py:91
  101.7 7.7 %collective-permute-start.6 = (bf16[64,1792]{1,0:T(8,128)(2,1)S(1)}, bf16[64,1792]{1,0:T(8,128)(2,1)S(1)}, u32[]{:S(2)}, u32[]{:S(2)}) collective-permute-start(bf16[64,1792]{1,0:T(8,128)(2,1)S(1)} %get-tuple-element.56), channel_id=1, source_target_pairs={{0,0},{1,33},{2,10},{3,43},{4,20},{5,53},{6,30},{7,63},{8,8},{9,41... | collective-permute-start | bytes 688136 | tf_op jit(solution)/shard_map/ppermute | solution.py:33
  109.4 18.6 %all_gather.17 = bf16[256,1792]{1,0:T(8,128)(2,1)S(1)} all-gather(bf16[64,1792]{1,0:T(8,128)(2,1)S(1)} %get-tuple-element.57), channel_id=1, replica_groups=mesh['x'=4,'yl'=2,'z'=8,'yh'=4,'c'=2] {'yh'}, dimensions={0}, use_global_device_ids=true | all-gather | bytes 1146880 | tf_op jit(solution)/shard_map/all_gather | solution.py:101
  128.0 2.4 %collective-permute-start.7 = (bf16[256,1792]{1,0:T(8,128)(2,1)S(1)}, bf16[256,1792]{1,0:T(8,128)(2,1)S(1)}, u32[]{:S(2)}, u32[]{:S(2)}) collective-permute-start(bf16[256,1792]{1,0:T(8,128)(2,1)S(1)} %all_gather.17), channel_id=1, source_target_pairs={{0,1},{1,0},{2,3},{3,2},{4,5},{5,4},{6,7},{7,6},{8,9},{9,8},{10,11... | collective-permute-start | bytes 2752520 | tf_op jit(solution)/shard_map/ppermute | solution.py:21
  130.4 5.3 %collective-permute-start.8 = (bf16[64,1792]{1,0:T(8,128)(2,1)S(1)}, bf16[64,1792]{1,0:T(8,128)(2,1)S(1)}, u32[]{:S(2)}, u32[]{:S(2)}) collective-permute-start(bf16[64,1792]{1,0:T(8,128)(2,1)S(1)} %collective-permute-done.6), channel_id=1, source_target_pairs={{0,0},{1,4},{2,7},{3,3},{4,6},{5,2},{6,5},{7,1},{8,9},{9,13},{10,8... | collective-permute-start | bytes 688136 | tf_op jit(solution)/shard_map/ppermute | solution.py:42
  135.7 3.0 %convolution_convert_fusion.2 = bf16[256,896]{1,0:T(8,128)(2,1)S(1)} fusion(bf16[256,1792]{1,0:T(8,128)(2,1)S(1)} %all_gather.17, bf16[1792,896]{1,0:T(8,128)(2,1)} %all-gather.5.cloned.1.call-done), kind=kOutput, calls=%fused_computation.11 | convolution fusion | flops 822312960 | bytes 4587520 | tf_op jit(solution)/shard_map/dot_general | solution.py:67
  138.8 1.1 fusion.6
  141.2 4.1 %all-to-all-start.2 = ((bf16[16,32,896]{2,1,0:T(8,128)(2,1)}), bf16[16,32,896]{2,1,0:T(8,128)(2,1)S(1)}, u32[]{:S(2)}, u32[]{:S(2)}) async-start(bf16[16,32,896]{2,1,0:T(8,128)(2,1)} %bitcast.22), calls=%async_computation.2 | async-start | bytes 1835008 | tf_op jit(solution)/shard_map/all_to_all | solution.py:111
  147.3 2.5 %collective-permute-start.9 = (bf16[320,448]{0,1:T(8,128)(2,1)}, bf16[320,448]{0,1:T(8,128)(2,1)S(1)}, u32[]{:S(2)}, u32[]{:S(2)}) collective-permute-start(bf16[320,448]{0,1:T(8,128)(2,1)} %get-tuple-element.54), channel_id=1, source_target_pairs={{0,128},{128,256},{256,384},{384,0},{1,129},{129,257},{257,385},{3... | collective-permute-start | bytes 860168 | tf_op jit(solution)/shard_map/ppermute | solution.py:17
  149.9 3.7 %collective-permute-start.10 = (bf16[320,448]{0,1:T(8,128)(2,1)S(1)}, bf16[320,448]{0,1:T(8,128)(2,1)S(1)}, u32[]{:S(2)}, u32[]{:S(2)}) collective-permute-start(bf16[320,448]{0,1:T(8,128)(2,1)S(1)} %get-tuple-element.53), channel_id=1, source_target_pairs={{0,256},{128,384},{256,0},{384,128},{1,257},{129,385},{257,1},{385... | collective-permute-start | bytes 860168 | tf_op jit(solution)/shard_map/ppermute | solution.py:17
  153.6 2.8 %collective-permute-start.11 = (bf16[320,448]{0,1:T(8,128)(2,1)S(1)}, bf16[320,448]{0,1:T(8,128)(2,1)S(1)}, u32[]{:S(2)}, u32[]{:S(2)}) collective-permute-start(bf16[320,448]{0,1:T(8,128)(2,1)S(1)} %get-tuple-element.52), channel_id=1, source_target_pairs={{0,384},{128,0},{256,128},{384,256},{1,385},{129,1},{257,129},{385... | collective-permute-start | bytes 860168 | tf_op jit(solution)/shard_map/ppermute | solution.py:17
  156.5 5.3 %collective-permute-done.9 = bf16[320,448]{0,1:T(8,128)(2,1)S(1)} collective-permute-done((bf16[320,448]{0,1:T(8,128)(2,1)}, bf16[320,448]{0,1:T(8,128)(2,1)S(1)}, u32[]{:S(2)}, u32[]{:S(2)}) %collective-permute-start.9) | collective-permute-done | bytes 286752 | tf_op jit(solution)/shard_map/ppermute | solution.py:17
  161.8 3.2 %collective-permute-done.10 = bf16[320,448]{0,1:T(8,128)(2,1)S(1)} collective-permute-done((bf16[320,448]{0,1:T(8,128)(2,1)S(1)}, bf16[320,448]{0,1:T(8,128)(2,1)S(1)}, u32[]{:S(2)}, u32[]{:S(2)}) %collective-permute-start.10) | collective-permute-done | bytes 286752 | tf_op jit(solution)/shard_map/ppermute | solution.py:17
  165.1 4.2 %collective-permute-done.11 = bf16[320,448]{0,1:T(8,128)(2,1)S(1)} collective-permute-done((bf16[320,448]{0,1:T(8,128)(2,1)S(1)}, bf16[320,448]{0,1:T(8,128)(2,1)S(1)}, u32[]{:S(2)}, u32[]{:S(2)}) %collective-permute-start.11) | collective-permute-done | bytes 286752 | tf_op jit(solution)/shard_map/ppermute | solution.py:17
  169.3 3.5 %collective-permute-start.12 = (bf16[4,256,448]{1,2,0:T(8,128)(2,1)S(1)}, bf16[4,256,448]{1,2,0:T(8,128)(2,1)S(1)}, u32[]{:S(2)}, u32[]{:S(2)}) collective-permute-start(bf16[4,256,448]{1,2,0:T(8,128)(2,1)S(1)} %fusion.21), channel_id=1, source_target_pairs={{0,1},{1,0},{2,3},{3,2},{4,5},{5,4},{6,7},{7,6},{8,9},{9,8},{10,11... | collective-permute-start | bytes 2752520 | tf_op jit(solution)/shard_map/ppermute | solution.py:21
  175.0 5.0 %bitcast_convert_fusion = bf16[896,448]{0,1:T(8,128)(2,1)} fusion(bf16[4,2,256,896]{3,2,1,0:T(8,128)(2,1)} %bitcast.93, bf16[4,1,256,448]{2,3,1,0:T(8,128)(2,1)S(1)} %bitcast.94, bf16[4,1,256,448]{2,3,1,0:T(8,128)(2,1)S(1)} %bitcast.89), kind=kOutput, calls=%fused_computation.9 | convolution fusion | flops 1645486080 | bytes 6307840 | tf_op jit(solution)/shard_map/dot_general | solution.py:67
  (65 shorter events, 11.2 us)
Async XLA Ops:
  7.2 14.6 %copy-start.3 = (bf16[256,448]{0,1:T(8,128)(2,1)S(1)}, bf16[256,448]{0,1:T(8,128)(2,1)}, u32[]{:S(2)}) copy-start(bf16[256,448]{0,1:T(8,128)(2,1)} %param.5) | copy-start | bytes 688132
  7.2 53.9 %all-gather.5.cloned.1.call-start = ((), (), s32[]{:S(2)}) async-start(), calls=%async_computation.3 | async-start | bytes 4014080 | tf_op jit(solution)/shard_map/all_gather | solution.py:77
  9.7 49.6 %all-to-all-start = ((bf16[16,32,896]{2,1,0:T(8,128)(2,1)}), bf16[16,32,896]{2,1,0:T(8,128)(2,1)S(1)}, u32[]{:S(2)}, u32[]{:S(2)}) async-start(bf16[16,32,896]{2,1,0:T(8,128)(2,1)} %broadcast_in_dim.41), calls=%async_computation | async-start | bytes 1835008 | tf_op jit(solution)/shard_map/all_to_all | solution.py:80
  21.7 123.7 %all-gather.7.cloned.1.call-start = ((), (), s32[]{:S(2)}) async-start(), calls=%async_computation.4 | async-start | bytes 4587520 | tf_op jit(solution)/shard_map/all_gather | solution.py:113
  21.9 26.4 %collective-permute-start = (bf16[256,448]{1,0:T(8,128)(2,1)S(1)}, bf16[256,448]{1,0:T(8,128)(2,1)S(1)}, u32[]{:S(2)}, u32[]{:S(2)}) collective-permute-start(bf16[256,448]{1,0:T(8,128)(2,1)S(1)} %copy.29), channel_id=1, source_target_pairs={{0,0},{4,1},{7,2},{3,3},{6,4},{2,5},{5,6},{1,7},{9,8},{13,9},{8,10... | collective-permute-start | bytes 688136 | tf_op jit(solution)/shard_map/ppermute | solution.py:42
  48.3 11.0 %collective-permute-start.1 = (bf16[256,448]{1,0:T(8,128)(2,1)S(1)}, bf16[256,448]{1,0:T(8,128)(2,1)S(1)}, u32[]{:S(2)}, u32[]{:S(2)}) collective-permute-start(bf16[256,448]{1,0:T(8,128)(2,1)S(1)} %collective-permute-done), channel_id=1, source_target_pairs={{0,0},{1,33},{2,58},{3,27},{4,52},{5,21},{6,46},{7,15},{8,8},{9,41... | collective-permute-start | bytes 688136 | tf_op jit(solution)/shard_map/ppermute | solution.py:33
  61.1 8.0 %copy-start = (bf16[2,256,896]{2,1,0:T(8,128)(2,1)S(1)}, bf16[2,256,896]{2,1,0:T(8,128)(2,1)}, u32[]{:S(2)}) copy-start(bf16[2,256,896]{2,1,0:T(8,128)(2,1)} %pad_maximum_fusion.3) | copy-start | bytes 2752516
  61.1 8.0 %copy-start.4 = (bf16[1792,896]{1,0:T(8,128)(2,1)S(1)}, bf16[1792,896]{1,0:T(8,128)(2,1)}, u32[]{:S(2)}) copy-start(bf16[1792,896]{1,0:T(8,128)(2,1)} %all-gather.5.cloned.1.call-done) | copy-start | bytes 9633796
  64.4 4.7 %collective-permute-start.2 = (bf16[256,1792]{1,0:T(8,128)(2,1)S(1)}, bf16[256,1792]{1,0:T(8,128)(2,1)S(1)}, u32[]{:S(2)}, u32[]{:S(2)}) collective-permute-start(bf16[256,1792]{1,0:T(8,128)(2,1)S(1)} %convolution_convert_fusion), channel_id=1, source_target_pairs={{0,1},{1,0},{2,3},{3,2},{4,5},{5,4},{6,7},{7,6},{8,9},{9,8},{10,11... | collective-permute-start | bytes 2752520 | tf_op jit(solution)/shard_map/ppermute | solution.py:21
  71.3 29.9 %all-to-all-start.1 = ((bf16[4,64,1792]{2,1,0:T(8,128)(2,1)}), bf16[4,64,1792]{2,1,0:T(8,128)(2,1)S(1)}, u32[]{:S(2)}, u32[]{:S(2)}) async-start(bf16[4,64,1792]{2,1,0:T(8,128)(2,1)} %bitcast.9), calls=%async_computation.1 | async-start | bytes 1835008 | tf_op jit(solution)/shard_map/all_to_all | solution.py:91
  77.8 9.5 %collective-permute-start.3 = (bf16[64,448]{1,0:T(8,128)(2,1)S(1)}, bf16[64,448]{1,0:T(8,128)(2,1)S(1)}, u32[]{:S(2)}, u32[]{:S(2)}) collective-permute-start(bf16[64,448]{1,0:T(8,128)(2,1)S(1)} %get-tuple-element.60), channel_id=1, source_target_pairs={{0,128},{128,256},{256,384},{384,0},{1,129},{129,257},{257,385},{3... | collective-permute-start | bytes 172040 | tf_op jit(solution)/shard_map/ppermute | solution.py:17
  80.1 8.4 %collective-permute-start.4 = (bf16[64,448]{1,0:T(8,128)(2,1)S(1)}, bf16[64,448]{1,0:T(8,128)(2,1)S(1)}, u32[]{:S(2)}, u32[]{:S(2)}) collective-permute-start(bf16[64,448]{1,0:T(8,128)(2,1)S(1)} %get-tuple-element.59), channel_id=1, source_target_pairs={{0,256},{128,384},{256,0},{384,128},{1,257},{129,385},{257,1},{385... | collective-permute-start | bytes 172040 | tf_op jit(solution)/shard_map/ppermute | solution.py:17
  83.8 7.6 %collective-permute-start.5 = (bf16[64,448]{1,0:T(8,128)(2,1)S(1)}, bf16[64,448]{1,0:T(8,128)(2,1)S(1)}, u32[]{:S(2)}, u32[]{:S(2)}) collective-permute-start(bf16[64,448]{1,0:T(8,128)(2,1)S(1)} %get-tuple-element.58), channel_id=1, source_target_pairs={{0,384},{128,0},{256,128},{384,256},{1,385},{129,1},{257,129},{385... | collective-permute-start | bytes 172040 | tf_op jit(solution)/shard_map/ppermute | solution.py:17
  101.7 26.4 %collective-permute-start.6 = (bf16[64,1792]{1,0:T(8,128)(2,1)S(1)}, bf16[64,1792]{1,0:T(8,128)(2,1)S(1)}, u32[]{:S(2)}, u32[]{:S(2)}) collective-permute-start(bf16[64,1792]{1,0:T(8,128)(2,1)S(1)} %get-tuple-element.56), channel_id=1, source_target_pairs={{0,0},{1,33},{2,10},{3,43},{4,20},{5,53},{6,30},{7,63},{8,8},{9,41... | collective-permute-start | bytes 688136 | tf_op jit(solution)/shard_map/ppermute | solution.py:33
  128.0 10.7 %collective-permute-start.7 = (bf16[256,1792]{1,0:T(8,128)(2,1)S(1)}, bf16[256,1792]{1,0:T(8,128)(2,1)S(1)}, u32[]{:S(2)}, u32[]{:S(2)}) collective-permute-start(bf16[256,1792]{1,0:T(8,128)(2,1)S(1)} %all_gather.17), channel_id=1, source_target_pairs={{0,1},{1,0},{2,3},{3,2},{4,5},{5,4},{6,7},{7,6},{8,9},{9,8},{10,11... | collective-permute-start | bytes 2752520 | tf_op jit(solution)/shard_map/ppermute | solution.py:21
  130.4 8.3 %copy-start.5 = (bf16[1792,896]{1,0:T(8,128)(2,1)S(1)}, bf16[1792,896]{1,0:T(8,128)(2,1)}, u32[]{:S(2)}) copy-start(bf16[1792,896]{1,0:T(8,128)(2,1)} %all-gather.5.cloned.1.call-done) | copy-start | bytes 9633796
  130.4 14.9 %collective-permute-start.8 = (bf16[64,1792]{1,0:T(8,128)(2,1)S(1)}, bf16[64,1792]{1,0:T(8,128)(2,1)S(1)}, u32[]{:S(2)}, u32[]{:S(2)}) collective-permute-start(bf16[64,1792]{1,0:T(8,128)(2,1)S(1)} %collective-permute-done.6), channel_id=1, source_target_pairs={{0,0},{1,4},{2,7},{3,3},{4,6},{5,2},{6,5},{7,1},{8,9},{9,13},{10,8... | collective-permute-start | bytes 688136 | tf_op jit(solution)/shard_map/ppermute | solution.py:42
  141.2 38.8 %all-to-all-start.2 = ((bf16[16,32,896]{2,1,0:T(8,128)(2,1)}), bf16[16,32,896]{2,1,0:T(8,128)(2,1)S(1)}, u32[]{:S(2)}, u32[]{:S(2)}) async-start(bf16[16,32,896]{2,1,0:T(8,128)(2,1)} %bitcast.22), calls=%async_computation.2 | async-start | bytes 1835008 | tf_op jit(solution)/shard_map/all_to_all | solution.py:111
  147.3 14.5 %collective-permute-start.9 = (bf16[320,448]{0,1:T(8,128)(2,1)}, bf16[320,448]{0,1:T(8,128)(2,1)S(1)}, u32[]{:S(2)}, u32[]{:S(2)}) collective-permute-start(bf16[320,448]{0,1:T(8,128)(2,1)} %get-tuple-element.54), channel_id=1, source_target_pairs={{0,128},{128,256},{256,384},{384,0},{1,129},{129,257},{257,385},{3... | collective-permute-start | bytes 860168 | tf_op jit(solution)/shard_map/ppermute | solution.py:17
  149.9 15.2 %collective-permute-start.10 = (bf16[320,448]{0,1:T(8,128)(2,1)S(1)}, bf16[320,448]{0,1:T(8,128)(2,1)S(1)}, u32[]{:S(2)}, u32[]{:S(2)}) collective-permute-start(bf16[320,448]{0,1:T(8,128)(2,1)S(1)} %get-tuple-element.53), channel_id=1, source_target_pairs={{0,256},{128,384},{256,0},{384,128},{1,257},{129,385},{257,1},{385... | collective-permute-start | bytes 860168 | tf_op jit(solution)/shard_map/ppermute | solution.py:17
  153.6 15.7 %collective-permute-start.11 = (bf16[320,448]{0,1:T(8,128)(2,1)S(1)}, bf16[320,448]{0,1:T(8,128)(2,1)S(1)}, u32[]{:S(2)}, u32[]{:S(2)}) collective-permute-start(bf16[320,448]{0,1:T(8,128)(2,1)S(1)} %get-tuple-element.52), channel_id=1, source_target_pairs={{0,384},{128,0},{256,128},{384,256},{1,385},{129,1},{257,129},{385... | collective-permute-start | bytes 860168 | tf_op jit(solution)/shard_map/ppermute | solution.py:17
  165.1 4.2 %copy-start.1 = (bf16[320,448]{0,1:T(8,128)(2,1)}, bf16[320,448]{0,1:T(8,128)(2,1)S(1)}, u32[]{:S(2)}) copy-start(bf16[320,448]{0,1:T(8,128)(2,1)S(1)} %collective-permute-done.10) | copy-start | bytes 860164
  169.3 3.5 %copy-start.2 = (bf16[320,448]{0,1:T(8,128)(2,1)}, bf16[320,448]{0,1:T(8,128)(2,1)S(1)}, u32[]{:S(2)}) copy-start(bf16[320,448]{0,1:T(8,128)(2,1)S(1)} %collective-permute-done.11) | copy-start | bytes 860164
  169.3 5.7 %collective-permute-start.12 = (bf16[4,256,448]{1,2,0:T(8,128)(2,1)S(1)}, bf16[4,256,448]{1,2,0:T(8,128)(2,1)S(1)}, u32[]{:S(2)}, u32[]{:S(2)}) collective-permute-start(bf16[4,256,448]{1,2,0:T(8,128)(2,1)S(1)} %fusion.21), channel_id=1, source_target_pairs={{0,1},{1,0},{2,3},{3,2},{4,5},{5,4},{6,7},{7,6},{8,9},{9,8},{10,11... | collective-permute-start | bytes 2752520 | tf_op jit(solution)/shard_map/ppermute | solution.py:21
Sparse Core Ops, SparseCore 0:
  10.1 50.8 all-gather.4
  63.1 52.2 all-gather.6

commit v17 on v16

--- a/solution.py
+++ b/solution.py
@@ -112,13 +112,14 @@
 
     far = lax.all_gather(near, "x", axis=0, tiled=False)
     far, grad_own, activated = lax.optimization_barrier((far, grad_own, activated))
-    both = jnp.concatenate([grad_own, activated], axis=0)
-    both = shift_blocks(both.reshape(5 * pair, NX, cols).transpose(1, 0, 2), here)
-    far_own = in_order([part[: 4 * pair] for part in both], here)
+    blocks = shift_blocks(grad_own.reshape(4 * pair, NX, cols).transpose(1, 0, 2), here)
+    moved = shift_blocks(activated.reshape(pair, NX, cols).transpose(1, 0, 2), here)
+    far_own = in_order(blocks, here)
+    far_own, moved[1] = lax.optimization_barrier((far_own, moved[1]))
     far_other = swap_cores(far_own)
     far_grad = jnp.stack([far_own, far_other], axis=1)
     weight_grad = dot(far.reshape(-1, feats), far_grad.reshape(-1, cols), ((0,), (0,))).astype(BF)
-    out = in_order([part[4 * pair :] for part in both], here).reshape(NX * pair, cols)
+    out = in_order(moved, here).reshape(NX * pair, cols)
     ig, weight_grad, out = lax.optimization_barrier((ig, weight_grad, out))
     input_grad = jnp.sum(ig.astype(jnp.float32), axis=0).astype(BF)
     return out, input_grad, weight_grad

time: 189 us -> 189 us (level)
  starting transfers between devices: 69.4 us -> 79.4 us
  waiting for transfers between devices: 59.5 us -> 52.7 us
  matrix products: 14.6 us -> 12.6 us
    ppermute x6 -> x9, starting transfers between devices: 18.4 us -> 26.9 us  [along_x(): return lax.ppermute(value, 'x', [(i, (i + shift) % NX) for i in range(NX)])]
    ppermute x6 -> x9, waiting for transfers between devices: 16.8 us -> 10 us  [along_x(): return lax.ppermute(value, 'x', [(i, (i + shift) % NX) for i in range(NX)])]
    broadcast_in_dim x6 -> x0, local copies, waits for them, and re-layouts: 2.12 us -> none  [in_order(): lax.dynamic_update_index_in_dim(out, parts[r], here + (NX - r) & NX - 1, 0)]
    dot_general x5, matrix products: 14.6 us -> 12.6 us  [dot(): lax.dot_general(a, b, (contract, ((), ())), preferred_element_type=jnp.fl...]
  transfers between devices with their start and end apart: 18 -> 21, of which waited for: 10 -> 11; matrix products, arithmetic and copies ran while one was open for 13% -> 11% of each run, Pallas kernels for 0% -> 0%
where the time goes in v17:
time: 189 us; the launch traced here: 188 us
  starting transfers between devices  79.4 us (42%)
  waiting for transfers between devices  52.7 us (28%)
  blocking collectives  18.9 us (10%)
  between operations  14.5 us (8%)
  matrix products  12.6 us (7%)
  local copies, waits for them, and re-layouts  7.2 us (4%)
  other arithmetic  2.77 us (1%)
    ppermute x9, starting transfers between devices, along_x(): return lax.ppermute(value, 'x', [(i, (i + shift) % NX) for i in range(NX)])  26.9 us
    ppermute x2, waiting for transfers between devices, within_z(): return lax.ppermute(value, ('z', 'yh', 'c'), pairs)  21.4 us
    all_gather x1, blocking collectives, body(): grad_own = lax.all_gather(hidden_grad, 'yh', axis=0, tiled=True)  18.9 us
    dot_general x5, matrix products, dot(): lax.dot_general(a, b, (contract, ((), ())), preferred_element_type=jnp.fl...  12.6 us
    all_to_all x1, starting transfers between devices, body(): lax.all_to_all(near, ('z', 'yl'), split_axis=0, concat_axis=0)  12 us
    ppermute x3, starting transfers between devices, swap_cores(): return lax.ppermute(value, 'c', [(0, 1), (1, 0)])  10.1 us
    ppermute x9, waiting for transfers between devices, along_x(): return lax.ppermute(value, 'x', [(i, (i + shift) % NX) for i in range(NX)])  10 us
    ppermute x2, starting transfers between devices, within_z(): return lax.ppermute(value, ('z', 'yh', 'c'), pairs)  9.66 us
  transfers between devices with their start and end apart: 21, of which 11 were waited for; matrix products, arithmetic and copies ran while one was open for 11% of the time, Pallas kernels for 0%

profile of v17, /device:TPU:1, one launch (start us, length us, event | category | flops | bytes accessed | tf_op | source)
XLA Modules:
  0.0 188.1 jit_solution(8852572881097887633)
XLA Ops:
  7.9 1.8 broadcast_in_dim.41
  9.7 12.0 %all-to-all-start = ((bf16[16,32,896]{2,1,0:T(8,128)(2,1)}), bf16[16,32,896]{2,1,0:T(8,128)(2,1)S(1)}, u32[]{:S(2)}, u32[]{:S(2)}) async-start(bf16[16,32,896]{2,1,0:T(8,128)(2,1)} %broadcast_in_dim.41), calls=%async_computation | async-start | bytes 1835008 | tf_op jit(solution)/shard_map/all_to_all | solution.py:80
  21.9 5.0 %collective-permute-start = (bf16[256,448]{1,0:T(8,128)(2,1)S(1)}, bf16[256,448]{1,0:T(8,128)(2,1)S(1)}, u32[]{:S(2)}, u32[]{:S(2)}) collective-permute-start(bf16[256,448]{1,0:T(8,128)(2,1)S(1)} %copy.25), channel_id=1, source_target_pairs={{0,0},{4,1},{7,2},{3,3},{6,4},{2,5},{5,6},{1,7},{9,8},{13,9},{8,10... | collective-permute-start | bytes 688136 | tf_op jit(solution)/shard_map/ppermute | solution.py:42
  26.9 21.4 %collective-permute-done = bf16[256,448]{1,0:T(8,128)(2,1)S(1)} collective-permute-done((bf16[256,448]{1,0:T(8,128)(2,1)S(1)}, bf16[256,448]{1,0:T(8,128)(2,1)S(1)}, u32[]{:S(2)}, u32[]{:S(2)}) %collective-permute-start) | collective-permute-done | bytes 229408 | tf_op jit(solution)/shard_map/ppermute | solution.py:42
  48.3 1.9 %collective-permute-start.1 = (bf16[256,448]{1,0:T(8,128)(2,1)S(1)}, bf16[256,448]{1,0:T(8,128)(2,1)S(1)}, u32[]{:S(2)}, u32[]{:S(2)}) collective-permute-start(bf16[256,448]{1,0:T(8,128)(2,1)S(1)} %collective-permute-done), channel_id=1, source_target_pairs={{0,0},{1,33},{2,58},{3,27},{4,52},{5,21},{6,46},{7,15},{8,8},{9,41... | collective-permute-start | bytes 688136 | tf_op jit(solution)/shard_map/ppermute | solution.py:33
  50.2 9.1 %collective-permute-done.1 = bf16[256,448]{1,0:T(8,128)(2,1)S(1)} collective-permute-done((bf16[256,448]{1,0:T(8,128)(2,1)S(1)}, bf16[256,448]{1,0:T(8,128)(2,1)S(1)}, u32[]{:S(2)}, u32[]{:S(2)}) %collective-permute-start.1) | collective-permute-done | bytes 229408 | tf_op jit(solution)/shard_map/ppermute | solution.py:33
  61.1 3.3 %convolution_convert_fusion = bf16[256,1792]{1,0:T(8,128)(2,1)S(1)} fusion(bf16[1792,896]{1,0:T(8,128)(2,1)} %all-gather.5.cloned.1.call-done, bf16[2,256,896]{2,1,0:T(8,128)(2,1)} %pad_maximum_fusion.2), kind=kOutput, calls=%fused_computation | convolution fusion | flops 822542336 | bytes 4587520 | tf_op jit(solution)/shard_map/dot_general | solution.py:67
  64.4 2.6 %collective-permute-start.2 = (bf16[256,1792]{1,0:T(8,128)(2,1)S(1)}, bf16[256,1792]{1,0:T(8,128)(2,1)S(1)}, u32[]{:S(2)}, u32[]{:S(2)}) collective-permute-start(bf16[256,1792]{1,0:T(8,128)(2,1)S(1)} %convolution_convert_fusion), channel_id=1, source_target_pairs={{0,1},{1,0},{2,3},{3,2},{4,5},{5,4},{6,7},{7,6},{8,9},{9,8},{10,11... | collective-permute-start | bytes 2752520 | tf_op jit(solution)/shard_map/ppermute | solution.py:21
  67.0 2.1 %collective-permute-done.2 = bf16[256,1792]{1,0:T(8,128)(2,1)S(1)} collective-permute-done((bf16[256,1792]{1,0:T(8,128)(2,1)S(1)}, bf16[256,1792]{1,0:T(8,128)(2,1)S(1)}, u32[]{:S(2)}, u32[]{:S(2)}) %collective-permute-start.2) | collective-permute-done | bytes 917536 | tf_op jit(solution)/shard_map/ppermute | solution.py:21
  69.1 2.1 %add_convert_fusion = bf16[256,1792]{1,0:T(8,128)(2,1)} fusion(bf16[256,1792]{1,0:T(8,128)(2,1)S(1)} %collective-permute-done.2, bf16[1792,896]{1,0:T(8,128)(2,1)S(1)} %copy-done.3, bf16[2,256,896]{2,1,0:T(8,128)(2,1)S(1)} %copy-done), kind=kOutput, calls=%fused_computation.8 | convolution fusion | flops 823459840 | bytes 5505024 | tf_op jit(solution)/shard_map/dot_general | solution.py:67
  71.3 6.5 %all-to-all-start.1 = ((bf16[4,64,1792]{2,1,0:T(8,128)(2,1)}), bf16[4,64,1792]{2,1,0:T(8,128)(2,1)S(1)}, u32[]{:S(2)}, u32[]{:S(2)}) async-start(bf16[4,64,1792]{2,1,0:T(8,128)(2,1)} %bitcast.9), calls=%async_computation.1 | async-start | bytes 1835008 | tf_op jit(solution)/shard_map/all_to_all | solution.py:91
  77.8 2.3 %collective-permute-start.3 = (bf16[64,448]{1,0:T(8,128)(2,1)S(1)}, bf16[64,448]{1,0:T(8,128)(2,1)S(1)}, u32[]{:S(2)}, u32[]{:S(2)}) collective-permute-start(bf16[64,448]{1,0:T(8,128)(2,1)S(1)} %get-tuple-element.67), channel_id=1, source_target_pairs={{0,128},{128,256},{256,384},{384,0},{1,129},{129,257},{257,385},{3... | collective-permute-start | bytes 172040 | tf_op jit(solution)/shard_map/ppermute | solution.py:17
  80.1 3.6 %collective-permute-start.4 = (bf16[64,448]{1,0:T(8,128)(2,1)S(1)}, bf16[64,448]{1,0:T(8,128)(2,1)S(1)}, u32[]{:S(2)}, u32[]{:S(2)}) collective-permute-start(bf16[64,448]{1,0:T(8,128)(2,1)S(1)} %get-tuple-element.66), channel_id=1, source_target_pairs={{0,256},{128,384},{256,0},{384,128},{1,257},{129,385},{257,1},{385... | collective-permute-start | bytes 172040 | tf_op jit(solution)/shard_map/ppermute | solution.py:17
  83.8 3.5 %collective-permute-start.5 = (bf16[64,448]{1,0:T(8,128)(2,1)S(1)}, bf16[64,448]{1,0:T(8,128)(2,1)S(1)}, u32[]{:S(2)}, u32[]{:S(2)}) collective-permute-start(bf16[64,448]{1,0:T(8,128)(2,1)S(1)} %get-tuple-element.65), channel_id=1, source_target_pairs={{0,384},{128,0},{256,128},{384,256},{1,385},{129,1},{257,129},{385... | collective-permute-start | bytes 172040 | tf_op jit(solution)/shard_map/ppermute | solution.py:17
  87.3 1.3 collective-permute-done.4
  88.5 2.8 %collective-permute-done.5 = bf16[64,448]{1,0:T(8,128)(2,1)S(1)} collective-permute-done((bf16[64,448]{1,0:T(8,128)(2,1)S(1)}, bf16[64,448]{1,0:T(8,128)(2,1)S(1)}, u32[]{:S(2)}, u32[]{:S(2)}) %collective-permute-start.5) | collective-permute-done | bytes 57376 | tf_op jit(solution)/shard_map/ppermute | solution.py:17
  92.2 9.0 %all-to-all-done.1 = bf16[4,64,1792]{2,1,0:T(8,128)(2,1)S(1)} async-done(((bf16[4,64,1792]{2,1,0:T(8,128)(2,1)}), bf16[4,64,1792]{2,1,0:T(8,128)(2,1)S(1)}, u32[]{:S(2)}, u32[]{:S(2)}) %all-to-all-start.1) | async-done | bytes 917536 | tf_op jit(solution)/shard_map/all_to_all | solution.py:91
  101.6 7.7 %collective-permute-start.6 = (bf16[64,1792]{1,0:T(8,128)(2,1)S(1)}, bf16[64,1792]{1,0:T(8,128)(2,1)S(1)}, u32[]{:S(2)}, u32[]{:S(2)}) collective-permute-start(bf16[64,1792]{1,0:T(8,128)(2,1)S(1)} %get-tuple-element.59), channel_id=1, source_target_pairs={{0,0},{1,33},{2,10},{3,43},{4,20},{5,53},{6,30},{7,63},{8,8},{9,41... | collective-permute-start | bytes 688136 | tf_op jit(solution)/shard_map/ppermute | solution.py:33
  109.4 18.9 %all_gather.17 = bf16[256,1792]{1,0:T(8,128)(2,1)S(1)} all-gather(bf16[64,1792]{1,0:T(8,128)(2,1)S(1)} %get-tuple-element.60), channel_id=1, replica_groups=mesh['x'=4,'yl'=2,'z'=8,'yh'=4,'c'=2] {'yh'}, dimensions={0}, use_global_device_ids=true | all-gather | bytes 1146880 | tf_op jit(solution)/shard_map/all_gather | solution.py:101
  128.3 2.3 %collective-permute-start.7 = (bf16[256,1792]{1,0:T(8,128)(2,1)S(1)}, bf16[256,1792]{1,0:T(8,128)(2,1)S(1)}, u32[]{:S(2)}, u32[]{:S(2)}) collective-permute-start(bf16[256,1792]{1,0:T(8,128)(2,1)S(1)} %all_gather.17), channel_id=1, source_target_pairs={{0,1},{1,0},{2,3},{3,2},{4,5},{5,4},{6,7},{7,6},{8,9},{9,8},{10,11... | collective-permute-start | bytes 2752520 | tf_op jit(solution)/shard_map/ppermute | solution.py:21
  130.6 4.7 %collective-permute-start.8 = (bf16[64,1792]{1,0:T(8,128)(2,1)S(1)}, bf16[64,1792]{1,0:T(8,128)(2,1)S(1)}, u32[]{:S(2)}, u32[]{:S(2)}) collective-permute-start(bf16[64,1792]{1,0:T(8,128)(2,1)S(1)} %collective-permute-done.6), channel_id=1, source_target_pairs={{0,0},{1,4},{2,7},{3,3},{4,6},{5,2},{6,5},{7,1},{8,9},{9,13},{10,8... | collective-permute-start | bytes 688136 | tf_op jit(solution)/shard_map/ppermute | solution.py:42
  135.3 3.0 %convolution_convert_fusion.2 = bf16[256,896]{1,0:T(8,128)(2,1)S(1)} fusion(bf16[256,1792]{1,0:T(8,128)(2,1)S(1)} %all_gather.17, bf16[1792,896]{1,0:T(8,128)(2,1)} %all-gather.5.cloned.1.call-done), kind=kOutput, calls=%fused_computation.11 | convolution fusion | flops 822312960 | bytes 4587520 | tf_op jit(solution)/shard_map/dot_general | solution.py:67
  140.8 4.6 %all-to-all-start.2 = ((bf16[16,32,896]{2,1,0:T(8,128)(2,1)}), bf16[16,32,896]{2,1,0:T(8,128)(2,1)S(1)}, u32[]{:S(2)}, u32[]{:S(2)}) async-start(bf16[16,32,896]{2,1,0:T(8,128)(2,1)} %bitcast.22), calls=%async_computation.2 | async-start | bytes 1835008 | tf_op jit(solution)/shard_map/all_to_all | solution.py:111
  146.8 2.6 %collective-permute-start.9 = (bf16[256,448]{0,1:T(8,128)(2,1)}, bf16[256,448]{0,1:T(8,128)(2,1)S(1)}, u32[]{:S(2)}, u32[]{:S(2)}) collective-permute-start(bf16[256,448]{0,1:T(8,128)(2,1)} %get-tuple-element.58), channel_id=1, source_target_pairs={{0,128},{128,256},{256,384},{384,0},{1,129},{129,257},{257,385},{3... | collective-permute-start | bytes 688136 | tf_op jit(solution)/shard_map/ppermute | solution.py:17
  149.4 3.6 %collective-permute-start.10 = (bf16[256,448]{0,1:T(8,128)(2,1)}, bf16[256,448]{0,1:T(8,128)(2,1)S(1)}, u32[]{:S(2)}, u32[]{:S(2)}) collective-permute-start(bf16[256,448]{0,1:T(8,128)(2,1)} %get-tuple-element.57), channel_id=1, source_target_pairs={{0,256},{128,384},{256,0},{384,128},{1,257},{129,385},{257,1},{385... | collective-permute-start | bytes 688136 | tf_op jit(solution)/shard_map/ppermute | solution.py:17
  153.0 2.8 %collective-permute-start.11 = (bf16[256,448]{0,1:T(8,128)(2,1)S(1)}, bf16[256,448]{0,1:T(8,128)(2,1)S(1)}, u32[]{:S(2)}, u32[]{:S(2)}) collective-permute-start(bf16[256,448]{0,1:T(8,128)(2,1)S(1)} %get-tuple-element.56), channel_id=1, source_target_pairs={{0,384},{128,0},{256,128},{384,256},{1,385},{129,1},{257,129},{385... | collective-permute-start | bytes 688136 | tf_op jit(solution)/shard_map/ppermute | solution.py:17
  156.6 2.8 %collective-permute-start.12 = (bf16[64,448]{1,0:T(8,128)(2,1)S(1)}, bf16[64,448]{1,0:T(8,128)(2,1)S(1)}, u32[]{:S(2)}, u32[]{:S(2)}) collective-permute-start(bf16[64,448]{1,0:T(8,128)(2,1)S(1)} %bitcast.101), channel_id=1, source_target_pairs={{0,128},{128,256},{256,384},{384,0},{1,129},{129,257},{257,385},{3... | collective-permute-start | bytes 172040 | tf_op jit(solution)/shard_map/ppermute | solution.py:17
  160.6 3.3 %collective-permute-done.11 = bf16[256,448]{0,1:T(8,128)(2,1)S(1)} collective-permute-done((bf16[256,448]{0,1:T(8,128)(2,1)S(1)}, bf16[256,448]{0,1:T(8,128)(2,1)S(1)}, u32[]{:S(2)}, u32[]{:S(2)}) %collective-permute-start.11) | collective-permute-done | bytes 229408 | tf_op jit(solution)/shard_map/ppermute | solution.py:17
  163.9 5.2 %collective-permute-start.13 = (bf16[4,256,448]{1,2,0:T(8,128)(2,1)S(1)}, bf16[4,256,448]{1,2,0:T(8,128)(2,1)S(1)}, u32[]{:S(2)}, u32[]{:S(2)}) collective-permute-start(bf16[4,256,448]{1,2,0:T(8,128)(2,1)S(1)} %bitcast_dynamic-update-slice_fusion), channel_id=1, source_target_pairs={{0,1},{1,0},{2,3},{3,2},{4,5},{5,4},{6,7},{7,6},{8,9},{9,8},{10,11... | collective-permute-start | bytes 2752520 | tf_op jit(solution)/shard_map/ppermute | solution.py:21
  169.1 1.9 %collective-permute-start.14 = (bf16[64,448]{1,0:T(8,128)(2,1)S(1)}, bf16[64,448]{1,0:T(8,128)(2,1)S(1)}, u32[]{:S(2)}, u32[]{:S(2)}) collective-permute-start(bf16[64,448]{1,0:T(8,128)(2,1)S(1)} %bitcast.103), channel_id=1, source_target_pairs={{0,256},{128,384},{256,0},{384,128},{1,257},{129,385},{257,1},{385... | collective-permute-start | bytes 172040 | tf_op jit(solution)/shard_map/ppermute | solution.py:17
  171.1 3.9 %collective-permute-start.15 = (bf16[64,448]{1,0:T(8,128)(2,1)S(1)}, bf16[64,448]{1,0:T(8,128)(2,1)S(1)}, u32[]{:S(2)}, u32[]{:S(2)}) collective-permute-start(bf16[64,448]{1,0:T(8,128)(2,1)S(1)} %bitcast.102), channel_id=1, source_target_pairs={{0,384},{128,0},{256,128},{384,256},{1,385},{129,1},{257,129},{385... | collective-permute-start | bytes 172040 | tf_op jit(solution)/shard_map/ppermute | solution.py:17
  176.7 2.9 %bitcast_convert_fusion = bf16[896,448]{0,1:T(8,128)(2,1)} fusion(bf16[4,2,256,896]{3,2,1,0:T(8,128)(2,1)S(1)} %bitcast.104, bf16[4,1,256,448]{2,3,1,0:T(8,128)(2,1)S(1)} %bitcast.105, bf16[4,1,256,448]{2,3,1,0:T(8,128)(2,1)S(1)} %bitcast.97), kind=kOutput, calls=%fused_computation.9 | convolution fusion | flops 1645486080 | bytes 6307840 | tf_op jit(solution)/shard_map/dot_general | solution.py:67
  (65 shorter events, 13.2 us)
Async XLA Ops:
  7.2 14.6 %copy-start.1 = (bf16[256,448]{0,1:T(8,128)(2,1)S(1)}, bf16[256,448]{0,1:T(8,128)(2,1)}, u32[]{:S(2)}) copy-start(bf16[256,448]{0,1:T(8,128)(2,1)} %param.5) | copy-start | bytes 688132
  7.2 53.9 %all-gather.5.cloned.1.call-start = ((), (), s32[]{:S(2)}) async-start(), calls=%async_computation.3 | async-start | bytes 4014080 | tf_op jit(solution)/shard_map/all_gather | solution.py:77
  9.7 49.6 %all-to-all-start = ((bf16[16,32,896]{2,1,0:T(8,128)(2,1)}), bf16[16,32,896]{2,1,0:T(8,128)(2,1)S(1)}, u32[]{:S(2)}, u32[]{:S(2)}) async-start(bf16[16,32,896]{2,1,0:T(8,128)(2,1)} %broadcast_in_dim.41), calls=%async_computation | async-start | bytes 1835008 | tf_op jit(solution)/shard_map/all_to_all | solution.py:80
  21.7 123.7 %all-gather.7.cloned.1.call-start = ((), (), s32[]{:S(2)}) async-start(), calls=%async_computation.4 | async-start | bytes 4587520 | tf_op jit(solution)/shard_map/all_gather | solution.py:113
  21.9 26.4 %collective-permute-start = (bf16[256,448]{1,0:T(8,128)(2,1)S(1)}, bf16[256,448]{1,0:T(8,128)(2,1)S(1)}, u32[]{:S(2)}, u32[]{:S(2)}) collective-permute-start(bf16[256,448]{1,0:T(8,128)(2,1)S(1)} %copy.25), channel_id=1, source_target_pairs={{0,0},{4,1},{7,2},{3,3},{6,4},{2,5},{5,6},{1,7},{9,8},{13,9},{8,10... | collective-permute-start | bytes 688136 | tf_op jit(solution)/shard_map/ppermute | solution.py:42
  48.3 11.0 %collective-permute-start.1 = (bf16[256,448]{1,0:T(8,128)(2,1)S(1)}, bf16[256,448]{1,0:T(8,128)(2,1)S(1)}, u32[]{:S(2)}, u32[]{:S(2)}) collective-permute-start(bf16[256,448]{1,0:T(8,128)(2,1)S(1)} %collective-permute-done), channel_id=1, source_target_pairs={{0,0},{1,33},{2,58},{3,27},{4,52},{5,21},{6,46},{7,15},{8,8},{9,41... | collective-permute-start | bytes 688136 | tf_op jit(solution)/shard_map/ppermute | solution.py:33
  61.1 8.0 %copy-start = (bf16[2,256,896]{2,1,0:T(8,128)(2,1)S(1)}, bf16[2,256,896]{2,1,0:T(8,128)(2,1)}, u32[]{:S(2)}) copy-start(bf16[2,256,896]{2,1,0:T(8,128)(2,1)} %pad_maximum_fusion.2) | copy-start | bytes 2752516
  61.1 8.0 %copy-start.3 = (bf16[1792,896]{1,0:T(8,128)(2,1)S(1)}, bf16[1792,896]{1,0:T(8,128)(2,1)}, u32[]{:S(2)}) copy-start(bf16[1792,896]{1,0:T(8,128)(2,1)} %all-gather.5.cloned.1.call-done) | copy-start | bytes 9633796
  64.4 4.7 %collective-permute-start.2 = (bf16[256,1792]{1,0:T(8,128)(2,1)S(1)}, bf16[256,1792]{1,0:T(8,128)(2,1)S(1)}, u32[]{:S(2)}, u32[]{:S(2)}) collective-permute-start(bf16[256,1792]{1,0:T(8,128)(2,1)S(1)} %convolution_convert_fusion), channel_id=1, source_target_pairs={{0,1},{1,0},{2,3},{3,2},{4,5},{5,4},{6,7},{7,6},{8,9},{9,8},{10,11... | collective-permute-start | bytes 2752520 | tf_op jit(solution)/shard_map/ppermute | solution.py:21
  71.3 29.9 %all-to-all-start.1 = ((bf16[4,64,1792]{2,1,0:T(8,128)(2,1)}), bf16[4,64,1792]{2,1,0:T(8,128)(2,1)S(1)}, u32[]{:S(2)}, u32[]{:S(2)}) async-start(bf16[4,64,1792]{2,1,0:T(8,128)(2,1)} %bitcast.9), calls=%async_computation.1 | async-start | bytes 1835008 | tf_op jit(solution)/shard_map/all_to_all | solution.py:91
  77.8 9.5 %collective-permute-start.3 = (bf16[64,448]{1,0:T(8,128)(2,1)S(1)}, bf16[64,448]{1,0:T(8,128)(2,1)S(1)}, u32[]{:S(2)}, u32[]{:S(2)}) collective-permute-start(bf16[64,448]{1,0:T(8,128)(2,1)S(1)} %get-tuple-element.67), channel_id=1, source_target_pairs={{0,128},{128,256},{256,384},{384,0},{1,129},{129,257},{257,385},{3... | collective-permute-start | bytes 172040 | tf_op jit(solution)/shard_map/ppermute | solution.py:17
  80.1 8.4 %collective-permute-start.4 = (bf16[64,448]{1,0:T(8,128)(2,1)S(1)}, bf16[64,448]{1,0:T(8,128)(2,1)S(1)}, u32[]{:S(2)}, u32[]{:S(2)}) collective-permute-start(bf16[64,448]{1,0:T(8,128)(2,1)S(1)} %get-tuple-element.66), channel_id=1, source_target_pairs={{0,256},{128,384},{256,0},{384,128},{1,257},{129,385},{257,1},{385... | collective-permute-start | bytes 172040 | tf_op jit(solution)/shard_map/ppermute | solution.py:17
  83.8 7.6 %collective-permute-start.5 = (bf16[64,448]{1,0:T(8,128)(2,1)S(1)}, bf16[64,448]{1,0:T(8,128)(2,1)S(1)}, u32[]{:S(2)}, u32[]{:S(2)}) collective-permute-start(bf16[64,448]{1,0:T(8,128)(2,1)S(1)} %get-tuple-element.65), channel_id=1, source_target_pairs={{0,384},{128,0},{256,128},{384,256},{1,385},{129,1},{257,129},{385... | collective-permute-start | bytes 172040 | tf_op jit(solution)/shard_map/ppermute | solution.py:17
  101.6 26.6 %collective-permute-start.6 = (bf16[64,1792]{1,0:T(8,128)(2,1)S(1)}, bf16[64,1792]{1,0:T(8,128)(2,1)S(1)}, u32[]{:S(2)}, u32[]{:S(2)}) collective-permute-start(bf16[64,1792]{1,0:T(8,128)(2,1)S(1)} %get-tuple-element.59), channel_id=1, source_target_pairs={{0,0},{1,33},{2,10},{3,43},{4,20},{5,53},{6,30},{7,63},{8,8},{9,41... | collective-permute-start | bytes 688136 | tf_op jit(solution)/shard_map/ppermute | solution.py:33
  128.3 10.0 %collective-permute-start.7 = (bf16[256,1792]{1,0:T(8,128)(2,1)S(1)}, bf16[256,1792]{1,0:T(8,128)(2,1)S(1)}, u32[]{:S(2)}, u32[]{:S(2)}) collective-permute-start(bf16[256,1792]{1,0:T(8,128)(2,1)S(1)} %all_gather.17), channel_id=1, source_target_pairs={{0,1},{1,0},{2,3},{3,2},{4,5},{5,4},{6,7},{7,6},{8,9},{9,8},{10,11... | collective-permute-start | bytes 2752520 | tf_op jit(solution)/shard_map/ppermute | solution.py:21
  130.6 7.7 %copy-start.4 = (bf16[1792,896]{1,0:T(8,128)(2,1)S(1)}, bf16[1792,896]{1,0:T(8,128)(2,1)}, u32[]{:S(2)}) copy-start(bf16[1792,896]{1,0:T(8,128)(2,1)} %all-gather.5.cloned.1.call-done) | copy-start | bytes 9633796
  130.6 14.8 %collective-permute-start.8 = (bf16[64,1792]{1,0:T(8,128)(2,1)S(1)}, bf16[64,1792]{1,0:T(8,128)(2,1)S(1)}, u32[]{:S(2)}, u32[]{:S(2)}) collective-permute-start(bf16[64,1792]{1,0:T(8,128)(2,1)S(1)} %collective-permute-done.6), channel_id=1, source_target_pairs={{0,0},{1,4},{2,7},{3,3},{4,6},{5,2},{6,5},{7,1},{8,9},{9,13},{10,8... | collective-permute-start | bytes 688136 | tf_op jit(solution)/shard_map/ppermute | solution.py:42
  140.8 38.9 %all-to-all-start.2 = ((bf16[16,32,896]{2,1,0:T(8,128)(2,1)}), bf16[16,32,896]{2,1,0:T(8,128)(2,1)S(1)}, u32[]{:S(2)}, u32[]{:S(2)}) async-start(bf16[16,32,896]{2,1,0:T(8,128)(2,1)} %bitcast.22), calls=%async_computation.2 | async-start | bytes 1835008 | tf_op jit(solution)/shard_map/all_to_all | solution.py:111
  146.8 12.7 %collective-permute-start.9 = (bf16[256,448]{0,1:T(8,128)(2,1)}, bf16[256,448]{0,1:T(8,128)(2,1)S(1)}, u32[]{:S(2)}, u32[]{:S(2)}) collective-permute-start(bf16[256,448]{0,1:T(8,128)(2,1)} %get-tuple-element.58), channel_id=1, source_target_pairs={{0,128},{128,256},{256,384},{384,0},{1,129},{129,257},{257,385},{3... | collective-permute-start | bytes 688136 | tf_op jit(solution)/shard_map/ppermute | solution.py:17
  149.4 11.2 %collective-permute-start.10 = (bf16[256,448]{0,1:T(8,128)(2,1)}, bf16[256,448]{0,1:T(8,128)(2,1)S(1)}, u32[]{:S(2)}, u32[]{:S(2)}) collective-permute-start(bf16[256,448]{0,1:T(8,128)(2,1)} %get-tuple-element.57), channel_id=1, source_target_pairs={{0,256},{128,384},{256,0},{384,128},{1,257},{129,385},{257,1},{385... | collective-permute-start | bytes 688136 | tf_op jit(solution)/shard_map/ppermute | solution.py:17
  153.0 10.9 %collective-permute-start.11 = (bf16[256,448]{0,1:T(8,128)(2,1)S(1)}, bf16[256,448]{0,1:T(8,128)(2,1)S(1)}, u32[]{:S(2)}, u32[]{:S(2)}) collective-permute-start(bf16[256,448]{0,1:T(8,128)(2,1)S(1)} %get-tuple-element.56), channel_id=1, source_target_pairs={{0,384},{128,0},{256,128},{384,256},{1,385},{129,1},{257,129},{385... | collective-permute-start | bytes 688136 | tf_op jit(solution)/shard_map/ppermute | solution.py:17
  156.6 20.1 %copy-start.2 = (bf16[8,256,896]{2,1,0:T(8,128)(2,1)S(1)}, bf16[8,256,896]{2,1,0:T(8,128)(2,1)}, u32[]{:S(2)}) copy-start(bf16[8,256,896]{2,1,0:T(8,128)(2,1)} %all-gather.7.cloned.1.call-done) | copy-start | bytes 11010052
  156.6 7.3 %collective-permute-start.12 = (bf16[64,448]{1,0:T(8,128)(2,1)S(1)}, bf16[64,448]{1,0:T(8,128)(2,1)S(1)}, u32[]{:S(2)}, u32[]{:S(2)}) collective-permute-start(bf16[64,448]{1,0:T(8,128)(2,1)S(1)} %bitcast.101), channel_id=1, source_target_pairs={{0,128},{128,256},{256,384},{384,0},{1,129},{129,257},{257,385},{3... | collective-permute-start | bytes 172040 | tf_op jit(solution)/shard_map/ppermute | solution.py:17
  163.9 12.8 %collective-permute-start.13 = (bf16[4,256,448]{1,2,0:T(8,128)(2,1)S(1)}, bf16[4,256,448]{1,2,0:T(8,128)(2,1)S(1)}, u32[]{:S(2)}, u32[]{:S(2)}) collective-permute-start(bf16[4,256,448]{1,2,0:T(8,128)(2,1)S(1)} %bitcast_dynamic-update-slice_fusion), channel_id=1, source_target_pairs={{0,1},{1,0},{2,3},{3,2},{4,5},{5,4},{6,7},{7,6},{8,9},{9,8},{10,11... | collective-permute-start | bytes 2752520 | tf_op jit(solution)/shard_map/ppermute | solution.py:21
  169.1 7.1 %collective-permute-start.14 = (bf16[64,448]{1,0:T(8,128)(2,1)S(1)}, bf16[64,448]{1,0:T(8,128)(2,1)S(1)}, u32[]{:S(2)}, u32[]{:S(2)}) collective-permute-start(bf16[64,448]{1,0:T(8,128)(2,1)S(1)} %bitcast.103), channel_id=1, source_target_pairs={{0,256},{128,384},{256,0},{384,128},{1,257},{129,385},{257,1},{385... | collective-permute-start | bytes 172040 | tf_op jit(solution)/shard_map/ppermute | solution.py:17
  171.1 5.6 %collective-permute-start.15 = (bf16[64,448]{1,0:T(8,128)(2,1)S(1)}, bf16[64,448]{1,0:T(8,128)(2,1)S(1)}, u32[]{:S(2)}, u32[]{:S(2)}) collective-permute-start(bf16[64,448]{1,0:T(8,128)(2,1)S(1)} %bitcast.102), channel_id=1, source_target_pairs={{0,384},{128,0},{256,128},{384,256},{1,385},{129,1},{257,129},{385... | collective-permute-start | bytes 172040 | tf_op jit(solution)/shard_map/ppermute | solution.py:17
Sparse Core Ops, SparseCore 0:
  10.1 50.8 all-gather.4
  63.1 52.2 all-gather.6

commit v18 on v17

--- a/solution.py
+++ b/solution.py
@@ -115,7 +115,7 @@
     blocks = shift_blocks(grad_own.reshape(4 * pair, NX, cols).transpose(1, 0, 2), here)
     moved = shift_blocks(activated.reshape(pair, NX, cols).transpose(1, 0, 2), here)
     far_own = in_order(blocks, here)
-    far_own, moved[1] = lax.optimization_barrier((far_own, moved[1]))
+    far_own, *moved = lax.optimization_barrier((far_own, *moved))
     far_other = swap_cores(far_own)
     far_grad = jnp.stack([far_own, far_other], axis=1)
     weight_grad = dot(far.reshape(-1, feats), far_grad.reshape(-1, cols), ((0,), (0,))).astype(BF)

time: 189 us -> 189 us (level)
  waiting for transfers between devices: 52.7 us -> 50 us
  starting transfers between devices: 79.4 us -> 81.7 us
    ppermute x9, waiting for transfers between devices: 10 us -> 5.35 us  [along_x(): return lax.ppermute(value, 'x', [(i, (i + shift) % NX) for i in range(NX)])]
    ppermute x3, waiting for transfers between devices: 2.08 us -> 4.06 us  [swap_cores(): return lax.ppermute(value, 'c', [(0, 1), (1, 0)])]
  transfers between devices with their start and end apart: 21 -> 21, of which waited for: 11 -> 9; matrix products, arithmetic and copies ran while one was open for 11% -> 11% of each run, Pallas kernels for 0% -> 0%
where the time goes in v18:
time: 189 us; the launch traced here: 188 us
  starting transfers between devices  81.7 us (43%)
  waiting for transfers between devices  50 us (26%)
  blocking collectives  18.9 us (10%)
  between operations  14.6 us (8%)
  matrix products  12.6 us (7%)
  local copies, waits for them, and re-layouts  7.22 us (4%)
  other arithmetic  2.77 us (1%)
    ppermute x9, starting transfers between devices, along_x(): return lax.ppermute(value, 'x', [(i, (i + shift) % NX) for i in range(NX)])  28.2 us
    ppermute x2, waiting for transfers between devices, within_z(): return lax.ppermute(value, ('z', 'yh', 'c'), pairs)  21.4 us
    all_gather x1, blocking collectives, body(): grad_own = lax.all_gather(hidden_grad, 'yh', axis=0, tiled=True)  18.9 us
    dot_general x5, matrix products, dot(): lax.dot_general(a, b, (contract, ((), ())), preferred_element_type=jnp.fl...  12.6 us
    all_to_all x1, starting transfers between devices, body(): lax.all_to_all(near, ('z', 'yl'), split_axis=0, concat_axis=0)  12 us
    ppermute x3, starting transfers between devices, swap_cores(): return lax.ppermute(value, 'c', [(0, 1), (1, 0)])  11 us
    ppermute x2, starting transfers between devices, within_z(): return lax.ppermute(value, ('z', 'yh', 'c'), pairs)  9.66 us
    ppermute x2, starting transfers between devices, along_z(): return lax.ppermute(value, ('z', 'yh', 'c'), pairs)  9.65 us
  transfers between devices with their start and end apart: 21, of which 9 were waited for; matrix products, arithmetic and copies ran while one was open for 11% of the time, Pallas kernels for 0%

profile of v18, /device:TPU:1, one launch (start us, length us, event | category | flops | bytes accessed | tf_op | source)
XLA Modules:
  0.0 187.7 jit_solution(11072619863184042873)
XLA Ops:
  7.9 1.8 broadcast_in_dim.43
  9.7 12.0 %all-to-all-start = ((bf16[16,32,896]{2,1,0:T(8,128)(2,1)}), bf16[16,32,896]{2,1,0:T(8,128)(2,1)S(1)}, u32[]{:S(2)}, u32[]{:S(2)}) async-start(bf16[16,32,896]{2,1,0:T(8,128)(2,1)} %broadcast_in_dim.43), calls=%async_computation | async-start | bytes 1835008 | tf_op jit(solution)/shard_map/all_to_all | solution.py:80
  21.9 5.0 %collective-permute-start = (bf16[256,448]{1,0:T(8,128)(2,1)S(1)}, bf16[256,448]{1,0:T(8,128)(2,1)S(1)}, u32[]{:S(2)}, u32[]{:S(2)}) collective-permute-start(bf16[256,448]{1,0:T(8,128)(2,1)S(1)} %copy.24), channel_id=1, source_target_pairs={{0,0},{4,1},{7,2},{3,3},{6,4},{2,5},{5,6},{1,7},{9,8},{13,9},{8,10... | collective-permute-start | bytes 688136 | tf_op jit(solution)/shard_map/ppermute | solution.py:42
  26.9 21.4 %collective-permute-done = bf16[256,448]{1,0:T(8,128)(2,1)S(1)} collective-permute-done((bf16[256,448]{1,0:T(8,128)(2,1)S(1)}, bf16[256,448]{1,0:T(8,128)(2,1)S(1)}, u32[]{:S(2)}, u32[]{:S(2)}) %collective-permute-start) | collective-permute-done | bytes 229408 | tf_op jit(solution)/shard_map/ppermute | solution.py:42
  48.3 1.9 %collective-permute-start.1 = (bf16[256,448]{1,0:T(8,128)(2,1)S(1)}, bf16[256,448]{1,0:T(8,128)(2,1)S(1)}, u32[]{:S(2)}, u32[]{:S(2)}) collective-permute-start(bf16[256,448]{1,0:T(8,128)(2,1)S(1)} %collective-permute-done), channel_id=1, source_target_pairs={{0,0},{1,33},{2,58},{3,27},{4,52},{5,21},{6,46},{7,15},{8,8},{9,41... | collective-permute-start | bytes 688136 | tf_op jit(solution)/shard_map/ppermute | solution.py:33
  50.2 9.1 %collective-permute-done.1 = bf16[256,448]{1,0:T(8,128)(2,1)S(1)} collective-permute-done((bf16[256,448]{1,0:T(8,128)(2,1)S(1)}, bf16[256,448]{1,0:T(8,128)(2,1)S(1)}, u32[]{:S(2)}, u32[]{:S(2)}) %collective-permute-start.1) | collective-permute-done | bytes 229408 | tf_op jit(solution)/shard_map/ppermute | solution.py:33
  61.1 3.3 %convolution_convert_fusion = bf16[256,1792]{1,0:T(8,128)(2,1)S(1)} fusion(bf16[1792,896]{1,0:T(8,128)(2,1)} %all-gather.5.cloned.1.call-done, bf16[2,256,896]{2,1,0:T(8,128)(2,1)} %pad_maximum_fusion.2), kind=kOutput, calls=%fused_computation | convolution fusion | flops 822542336 | bytes 4587520 | tf_op jit(solution)/shard_map/dot_general | solution.py:67
  64.4 2.6 %collective-permute-start.2 = (bf16[256,1792]{1,0:T(8,128)(2,1)S(1)}, bf16[256,1792]{1,0:T(8,128)(2,1)S(1)}, u32[]{:S(2)}, u32[]{:S(2)}) collective-permute-start(bf16[256,1792]{1,0:T(8,128)(2,1)S(1)} %convolution_convert_fusion), channel_id=1, source_target_pairs={{0,1},{1,0},{2,3},{3,2},{4,5},{5,4},{6,7},{7,6},{8,9},{9,8},{10,11... | collective-permute-start | bytes 2752520 | tf_op jit(solution)/shard_map/ppermute | solution.py:21
  67.0 2.1 %collective-permute-done.2 = bf16[256,1792]{1,0:T(8,128)(2,1)S(1)} collective-permute-done((bf16[256,1792]{1,0:T(8,128)(2,1)S(1)}, bf16[256,1792]{1,0:T(8,128)(2,1)S(1)}, u32[]{:S(2)}, u32[]{:S(2)}) %collective-permute-start.2) | collective-permute-done | bytes 917536 | tf_op jit(solution)/shard_map/ppermute | solution.py:21
  69.1 2.1 %add_convert_fusion = bf16[256,1792]{1,0:T(8,128)(2,1)} fusion(bf16[256,1792]{1,0:T(8,128)(2,1)S(1)} %collective-permute-done.2, bf16[1792,896]{1,0:T(8,128)(2,1)S(1)} %copy-done.3, bf16[2,256,896]{2,1,0:T(8,128)(2,1)S(1)} %copy-done), kind=kOutput, calls=%fused_computation.8 | convolution fusion | flops 823459840 | bytes 5505024 | tf_op jit(solution)/shard_map/dot_general | solution.py:67
  71.3 6.5 %all-to-all-start.1 = ((bf16[4,64,1792]{2,1,0:T(8,128)(2,1)}), bf16[4,64,1792]{2,1,0:T(8,128)(2,1)S(1)}, u32[]{:S(2)}, u32[]{:S(2)}) async-start(bf16[4,64,1792]{2,1,0:T(8,128)(2,1)} %bitcast.9), calls=%async_computation.1 | async-start | bytes 1835008 | tf_op jit(solution)/shard_map/all_to_all | solution.py:91
  77.8 2.3 %collective-permute-start.3 = (bf16[64,448]{1,0:T(8,128)(2,1)S(1)}, bf16[64,448]{1,0:T(8,128)(2,1)S(1)}, u32[]{:S(2)}, u32[]{:S(2)}) collective-permute-start(bf16[64,448]{1,0:T(8,128)(2,1)S(1)} %get-tuple-element.73), channel_id=1, source_target_pairs={{0,128},{128,256},{256,384},{384,0},{1,129},{129,257},{257,385},{3... | collective-permute-start | bytes 172040 | tf_op jit(solution)/shard_map/ppermute | solution.py:17
  80.1 3.6 %collective-permute-start.4 = (bf16[64,448]{1,0:T(8,128)(2,1)S(1)}, bf16[64,448]{1,0:T(8,128)(2,1)S(1)}, u32[]{:S(2)}, u32[]{:S(2)}) collective-permute-start(bf16[64,448]{1,0:T(8,128)(2,1)S(1)} %get-tuple-element.72), channel_id=1, source_target_pairs={{0,256},{128,384},{256,0},{384,128},{1,257},{129,385},{257,1},{385... | collective-permute-start | bytes 172040 | tf_op jit(solution)/shard_map/ppermute | solution.py:17
  83.8 3.5 %collective-permute-start.5 = (bf16[64,448]{1,0:T(8,128)(2,1)S(1)}, bf16[64,448]{1,0:T(8,128)(2,1)S(1)}, u32[]{:S(2)}, u32[]{:S(2)}) collective-permute-start(bf16[64,448]{1,0:T(8,128)(2,1)S(1)} %get-tuple-element.71), channel_id=1, source_target_pairs={{0,384},{128,0},{256,128},{384,256},{1,385},{129,1},{257,129},{385... | collective-permute-start | bytes 172040 | tf_op jit(solution)/shard_map/ppermute | solution.py:17
  88.5 2.8 %collective-permute-done.5 = bf16[64,448]{1,0:T(8,128)(2,1)S(1)} collective-permute-done((bf16[64,448]{1,0:T(8,128)(2,1)S(1)}, bf16[64,448]{1,0:T(8,128)(2,1)S(1)}, u32[]{:S(2)}, u32[]{:S(2)}) %collective-permute-start.5) | collective-permute-done | bytes 57376 | tf_op jit(solution)/shard_map/ppermute | solution.py:17
  92.2 9.0 %all-to-all-done.1 = bf16[4,64,1792]{2,1,0:T(8,128)(2,1)S(1)} async-done(((bf16[4,64,1792]{2,1,0:T(8,128)(2,1)}), bf16[4,64,1792]{2,1,0:T(8,128)(2,1)S(1)}, u32[]{:S(2)}, u32[]{:S(2)}) %all-to-all-start.1) | async-done | bytes 917536 | tf_op jit(solution)/shard_map/all_to_all | solution.py:91
  101.6 7.7 %collective-permute-start.6 = (bf16[64,1792]{1,0:T(8,128)(2,1)S(1)}, bf16[64,1792]{1,0:T(8,128)(2,1)S(1)}, u32[]{:S(2)}, u32[]{:S(2)}) collective-permute-start(bf16[64,1792]{1,0:T(8,128)(2,1)S(1)} %get-tuple-element.65), channel_id=1, source_target_pairs={{0,0},{1,33},{2,10},{3,43},{4,20},{5,53},{6,30},{7,63},{8,8},{9,41... | collective-permute-start | bytes 688136 | tf_op jit(solution)/shard_map/ppermute | solution.py:33
  109.4 18.9 %all_gather.17 = bf16[256,1792]{1,0:T(8,128)(2,1)S(1)} all-gather(bf16[64,1792]{1,0:T(8,128)(2,1)S(1)} %get-tuple-element.66), channel_id=1, replica_groups=mesh['x'=4,'yl'=2,'z'=8,'yh'=4,'c'=2] {'yh'}, dimensions={0}, use_global_device_ids=true | all-gather | bytes 1146880 | tf_op jit(solution)/shard_map/all_gather | solution.py:101
  128.3 2.3 %collective-permute-start.7 = (bf16[256,1792]{1,0:T(8,128)(2,1)S(1)}, bf16[256,1792]{1,0:T(8,128)(2,1)S(1)}, u32[]{:S(2)}, u32[]{:S(2)}) collective-permute-start(bf16[256,1792]{1,0:T(8,128)(2,1)S(1)} %all_gather.17), channel_id=1, source_target_pairs={{0,1},{1,0},{2,3},{3,2},{4,5},{5,4},{6,7},{7,6},{8,9},{9,8},{10,11... | collective-permute-start | bytes 2752520 | tf_op jit(solution)/shard_map/ppermute | solution.py:21
  130.6 4.7 %collective-permute-start.8 = (bf16[64,1792]{1,0:T(8,128)(2,1)S(1)}, bf16[64,1792]{1,0:T(8,128)(2,1)S(1)}, u32[]{:S(2)}, u32[]{:S(2)}) collective-permute-start(bf16[64,1792]{1,0:T(8,128)(2,1)S(1)} %collective-permute-done.6), channel_id=1, source_target_pairs={{0,0},{1,4},{2,7},{3,3},{4,6},{5,2},{6,5},{7,1},{8,9},{9,13},{10,8... | collective-permute-start | bytes 688136 | tf_op jit(solution)/shard_map/ppermute | solution.py:42
  135.3 3.0 %convolution_convert_fusion.2 = bf16[256,896]{1,0:T(8,128)(2,1)S(1)} fusion(bf16[256,1792]{1,0:T(8,128)(2,1)S(1)} %all_gather.17, bf16[1792,896]{1,0:T(8,128)(2,1)} %all-gather.5.cloned.1.call-done), kind=kOutput, calls=%fused_computation.11 | convolution fusion | flops 822312960 | bytes 4587520 | tf_op jit(solution)/shard_map/dot_general | solution.py:67
  140.8 4.6 %all-to-all-start.2 = ((bf16[16,32,896]{2,1,0:T(8,128)(2,1)}), bf16[16,32,896]{2,1,0:T(8,128)(2,1)S(1)}, u32[]{:S(2)}, u32[]{:S(2)}) async-start(bf16[16,32,896]{2,1,0:T(8,128)(2,1)} %bitcast.22), calls=%async_computation.2 | async-start | bytes 1835008 | tf_op jit(solution)/shard_map/all_to_all | solution.py:111
  146.8 2.6 %collective-permute-start.9 = (bf16[256,448]{0,1:T(8,128)(2,1)}, bf16[256,448]{0,1:T(8,128)(2,1)S(1)}, u32[]{:S(2)}, u32[]{:S(2)}) collective-permute-start(bf16[256,448]{0,1:T(8,128)(2,1)} %get-tuple-element.64), channel_id=1, source_target_pairs={{0,128},{128,256},{256,384},{384,0},{1,129},{129,257},{257,385},{3... | collective-permute-start | bytes 688136 | tf_op jit(solution)/shard_map/ppermute | solution.py:17
  149.4 3.6 %collective-permute-start.10 = (bf16[256,448]{0,1:T(8,128)(2,1)}, bf16[256,448]{0,1:T(8,128)(2,1)S(1)}, u32[]{:S(2)}, u32[]{:S(2)}) collective-permute-start(bf16[256,448]{0,1:T(8,128)(2,1)} %get-tuple-element.63), channel_id=1, source_target_pairs={{0,256},{128,384},{256,0},{384,128},{1,257},{129,385},{257,1},{385... | collective-permute-start | bytes 688136 | tf_op jit(solution)/shard_map/ppermute | solution.py:17
  153.0 2.8 %collective-permute-start.11 = (bf16[256,448]{0,1:T(8,128)(2,1)S(1)}, bf16[256,448]{0,1:T(8,128)(2,1)S(1)}, u32[]{:S(2)}, u32[]{:S(2)}) collective-permute-start(bf16[256,448]{0,1:T(8,128)(2,1)S(1)} %get-tuple-element.62), channel_id=1, source_target_pairs={{0,384},{128,0},{256,128},{384,256},{1,385},{129,1},{257,129},{385... | collective-permute-start | bytes 688136 | tf_op jit(solution)/shard_map/ppermute | solution.py:17
  156.7 2.5 %collective-permute-start.12 = (bf16[64,448]{1,0:T(8,128)(2,1)S(1)}, bf16[64,448]{1,0:T(8,128)(2,1)S(1)}, u32[]{:S(2)}, u32[]{:S(2)}) collective-permute-start(bf16[64,448]{1,0:T(8,128)(2,1)S(1)} %bitcast.103), channel_id=1, source_target_pairs={{0,128},{128,256},{256,384},{384,0},{1,129},{129,257},{257,385},{3... | collective-permute-start | bytes 172040 | tf_op jit(solution)/shard_map/ppermute | solution.py:17
  159.2 3.2 %collective-permute-start.13 = (bf16[64,448]{1,0:T(8,128)(2,1)S(1)}, bf16[64,448]{1,0:T(8,128)(2,1)S(1)}, u32[]{:S(2)}, u32[]{:S(2)}) collective-permute-start(bf16[64,448]{1,0:T(8,128)(2,1)S(1)} %bitcast.104), channel_id=1, source_target_pairs={{0,256},{128,384},{256,0},{384,128},{1,257},{129,385},{257,1},{385... | collective-permute-start | bytes 172040 | tf_op jit(solution)/shard_map/ppermute | solution.py:17
  162.6 4.1 %collective-permute-start.14 = (bf16[64,448]{1,0:T(8,128)(2,1)S(1)}, bf16[64,448]{1,0:T(8,128)(2,1)S(1)}, u32[]{:S(2)}, u32[]{:S(2)}) collective-permute-start(bf16[64,448]{1,0:T(8,128)(2,1)S(1)} %bitcast.105), channel_id=1, source_target_pairs={{0,384},{128,0},{256,128},{384,256},{1,385},{129,1},{257,129},{385... | collective-permute-start | bytes 172040 | tf_op jit(solution)/shard_map/ppermute | solution.py:17
  166.8 1.3 collective-permute-done.14
  168.1 6.2 %collective-permute-start.15 = (bf16[4,256,448]{1,2,0:T(8,128)(2,1)S(1)}, bf16[4,256,448]{1,2,0:T(8,128)(2,1)S(1)}, u32[]{:S(2)}, u32[]{:S(2)}) collective-permute-start(bf16[4,256,448]{1,2,0:T(8,128)(2,1)S(1)} %bitcast_dynamic-update-slice_fusion), channel_id=1, source_target_pairs={{0,1},{1,0},{2,3},{3,2},{4,5},{5,4},{6,7},{7,6},{8,9},{9,8},{10,11... | collective-permute-start | bytes 2752520 | tf_op jit(solution)/shard_map/ppermute | solution.py:21
  174.4 2.0 %collective-permute-done.15 = bf16[4,256,448]{1,2,0:T(8,128)(2,1)S(1)} collective-permute-done((bf16[4,256,448]{1,2,0:T(8,128)(2,1)S(1)}, bf16[4,256,448]{1,2,0:T(8,128)(2,1)S(1)}, u32[]{:S(2)}, u32[]{:S(2)}) %collective-permute-start.15) | collective-permute-done | bytes 917536 | tf_op jit(solution)/shard_map/ppermute | solution.py:21
  176.4 2.9 %bitcast_convert_fusion = bf16[896,448]{0,1:T(8,128)(2,1)} fusion(bf16[4,2,256,896]{3,2,1,0:T(8,128)(2,1)S(1)} %bitcast.106, bf16[4,1,256,448]{2,3,1,0:T(8,128)(2,1)S(1)} %bitcast.107, bf16[4,1,256,448]{2,3,1,0:T(8,128)(2,1)S(1)} %bitcast.98), kind=kOutput, calls=%fused_computation.9 | convolution fusion | flops 1645486080 | bytes 6307840 | tf_op jit(solution)/shard_map/dot_general | solution.py:67
  (66 shorter events, 11.8 us)
Async XLA Ops:
  7.2 14.6 %copy-start.1 = (bf16[256,448]{0,1:T(8,128)(2,1)S(1)}, bf16[256,448]{0,1:T(8,128)(2,1)}, u32[]{:S(2)}) copy-start(bf16[256,448]{0,1:T(8,128)(2,1)} %param.5) | copy-start | bytes 688132
  7.2 53.9 %all-gather.5.cloned.1.call-start = ((), (), s32[]{:S(2)}) async-start(), calls=%async_computation.3 | async-start | bytes 4014080 | tf_op jit(solution)/shard_map/all_gather | solution.py:77
  9.7 49.6 %all-to-all-start = ((bf16[16,32,896]{2,1,0:T(8,128)(2,1)}), bf16[16,32,896]{2,1,0:T(8,128)(2,1)S(1)}, u32[]{:S(2)}, u32[]{:S(2)}) async-start(bf16[16,32,896]{2,1,0:T(8,128)(2,1)} %broadcast_in_dim.43), calls=%async_computation | async-start | bytes 1835008 | tf_op jit(solution)/shard_map/all_to_all | solution.py:80
  21.7 123.7 %all-gather.7.cloned.1.call-start = ((), (), s32[]{:S(2)}) async-start(), calls=%async_computation.4 | async-start | bytes 4587520 | tf_op jit(solution)/shard_map/all_gather | solution.py:113
  21.9 26.4 %collective-permute-start = (bf16[256,448]{1,0:T(8,128)(2,1)S(1)}, bf16[256,448]{1,0:T(8,128)(2,1)S(1)}, u32[]{:S(2)}, u32[]{:S(2)}) collective-permute-start(bf16[256,448]{1,0:T(8,128)(2,1)S(1)} %copy.24), channel_id=1, source_target_pairs={{0,0},{4,1},{7,2},{3,3},{6,4},{2,5},{5,6},{1,7},{9,8},{13,9},{8,10... | collective-permute-start | bytes 688136 | tf_op jit(solution)/shard_map/ppermute | solution.py:42
  48.3 11.0 %collective-permute-start.1 = (bf16[256,448]{1,0:T(8,128)(2,1)S(1)}, bf16[256,448]{1,0:T(8,128)(2,1)S(1)}, u32[]{:S(2)}, u32[]{:S(2)}) collective-permute-start(bf16[256,448]{1,0:T(8,128)(2,1)S(1)} %collective-permute-done), channel_id=1, source_target_pairs={{0,0},{1,33},{2,58},{3,27},{4,52},{5,21},{6,46},{7,15},{8,8},{9,41... | collective-permute-start | bytes 688136 | tf_op jit(solution)/shard_map/ppermute | solution.py:33
  61.1 8.0 %copy-start = (bf16[2,256,896]{2,1,0:T(8,128)(2,1)S(1)}, bf16[2,256,896]{2,1,0:T(8,128)(2,1)}, u32[]{:S(2)}) copy-start(bf16[2,256,896]{2,1,0:T(8,128)(2,1)} %pad_maximum_fusion.2) | copy-start | bytes 2752516
  61.1 8.0 %copy-start.3 = (bf16[1792,896]{1,0:T(8,128)(2,1)S(1)}, bf16[1792,896]{1,0:T(8,128)(2,1)}, u32[]{:S(2)}) copy-start(bf16[1792,896]{1,0:T(8,128)(2,1)} %all-gather.5.cloned.1.call-done) | copy-start | bytes 9633796
  64.4 4.7 %collective-permute-start.2 = (bf16[256,1792]{1,0:T(8,128)(2,1)S(1)}, bf16[256,1792]{1,0:T(8,128)(2,1)S(1)}, u32[]{:S(2)}, u32[]{:S(2)}) collective-permute-start(bf16[256,1792]{1,0:T(8,128)(2,1)S(1)} %convolution_convert_fusion), channel_id=1, source_target_pairs={{0,1},{1,0},{2,3},{3,2},{4,5},{5,4},{6,7},{7,6},{8,9},{9,8},{10,11... | collective-permute-start | bytes 2752520 | tf_op jit(solution)/shard_map/ppermute | solution.py:21
  71.3 29.9 %all-to-all-start.1 = ((bf16[4,64,1792]{2,1,0:T(8,128)(2,1)}), bf16[4,64,1792]{2,1,0:T(8,128)(2,1)S(1)}, u32[]{:S(2)}, u32[]{:S(2)}) async-start(bf16[4,64,1792]{2,1,0:T(8,128)(2,1)} %bitcast.9), calls=%async_computation.1 | async-start | bytes 1835008 | tf_op jit(solution)/shard_map/all_to_all | solution.py:91
  77.8 9.5 %collective-permute-start.3 = (bf16[64,448]{1,0:T(8,128)(2,1)S(1)}, bf16[64,448]{1,0:T(8,128)(2,1)S(1)}, u32[]{:S(2)}, u32[]{:S(2)}) collective-permute-start(bf16[64,448]{1,0:T(8,128)(2,1)S(1)} %get-tuple-element.73), channel_id=1, source_target_pairs={{0,128},{128,256},{256,384},{384,0},{1,129},{129,257},{257,385},{3... | collective-permute-start | bytes 172040 | tf_op jit(solution)/shard_map/ppermute | solution.py:17
  80.1 8.4 %collective-permute-start.4 = (bf16[64,448]{1,0:T(8,128)(2,1)S(1)}, bf16[64,448]{1,0:T(8,128)(2,1)S(1)}, u32[]{:S(2)}, u32[]{:S(2)}) collective-permute-start(bf16[64,448]{1,0:T(8,128)(2,1)S(1)} %get-tuple-element.72), channel_id=1, source_target_pairs={{0,256},{128,384},{256,0},{384,128},{1,257},{129,385},{257,1},{385... | collective-permute-start | bytes 172040 | tf_op jit(solution)/shard_map/ppermute | solution.py:17
  83.8 7.6 %collective-permute-start.5 = (bf16[64,448]{1,0:T(8,128)(2,1)S(1)}, bf16[64,448]{1,0:T(8,128)(2,1)S(1)}, u32[]{:S(2)}, u32[]{:S(2)}) collective-permute-start(bf16[64,448]{1,0:T(8,128)(2,1)S(1)} %get-tuple-element.71), channel_id=1, source_target_pairs={{0,384},{128,0},{256,128},{384,256},{1,385},{129,1},{257,129},{385... | collective-permute-start | bytes 172040 | tf_op jit(solution)/shard_map/ppermute | solution.py:17
  101.6 26.6 %collective-permute-start.6 = (bf16[64,1792]{1,0:T(8,128)(2,1)S(1)}, bf16[64,1792]{1,0:T(8,128)(2,1)S(1)}, u32[]{:S(2)}, u32[]{:S(2)}) collective-permute-start(bf16[64,1792]{1,0:T(8,128)(2,1)S(1)} %get-tuple-element.65), channel_id=1, source_target_pairs={{0,0},{1,33},{2,10},{3,43},{4,20},{5,53},{6,30},{7,63},{8,8},{9,41... | collective-permute-start | bytes 688136 | tf_op jit(solution)/shard_map/ppermute | solution.py:33
  128.3 10.0 %collective-permute-start.7 = (bf16[256,1792]{1,0:T(8,128)(2,1)S(1)}, bf16[256,1792]{1,0:T(8,128)(2,1)S(1)}, u32[]{:S(2)}, u32[]{:S(2)}) collective-permute-start(bf16[256,1792]{1,0:T(8,128)(2,1)S(1)} %all_gather.17), channel_id=1, source_target_pairs={{0,1},{1,0},{2,3},{3,2},{4,5},{5,4},{6,7},{7,6},{8,9},{9,8},{10,11... | collective-permute-start | bytes 2752520 | tf_op jit(solution)/shard_map/ppermute | solution.py:21
  130.6 7.7 %copy-start.4 = (bf16[1792,896]{1,0:T(8,128)(2,1)S(1)}, bf16[1792,896]{1,0:T(8,128)(2,1)}, u32[]{:S(2)}) copy-start(bf16[1792,896]{1,0:T(8,128)(2,1)} %all-gather.5.cloned.1.call-done) | copy-start | bytes 9633796
  130.6 14.8 %collective-permute-start.8 = (bf16[64,1792]{1,0:T(8,128)(2,1)S(1)}, bf16[64,1792]{1,0:T(8,128)(2,1)S(1)}, u32[]{:S(2)}, u32[]{:S(2)}) collective-permute-start(bf16[64,1792]{1,0:T(8,128)(2,1)S(1)} %collective-permute-done.6), channel_id=1, source_target_pairs={{0,0},{1,4},{2,7},{3,3},{4,6},{5,2},{6,5},{7,1},{8,9},{9,13},{10,8... | collective-permute-start | bytes 688136 | tf_op jit(solution)/shard_map/ppermute | solution.py:42
  140.8 38.6 %all-to-all-start.2 = ((bf16[16,32,896]{2,1,0:T(8,128)(2,1)}), bf16[16,32,896]{2,1,0:T(8,128)(2,1)S(1)}, u32[]{:S(2)}, u32[]{:S(2)}) async-start(bf16[16,32,896]{2,1,0:T(8,128)(2,1)} %bitcast.22), calls=%async_computation.2 | async-start | bytes 1835008 | tf_op jit(solution)/shard_map/all_to_all | solution.py:111
  146.8 15.8 %collective-permute-start.9 = (bf16[256,448]{0,1:T(8,128)(2,1)}, bf16[256,448]{0,1:T(8,128)(2,1)S(1)}, u32[]{:S(2)}, u32[]{:S(2)}) collective-permute-start(bf16[256,448]{0,1:T(8,128)(2,1)} %get-tuple-element.64), channel_id=1, source_target_pairs={{0,128},{128,256},{256,384},{384,0},{1,129},{129,257},{257,385},{3... | collective-permute-start | bytes 688136 | tf_op jit(solution)/shard_map/ppermute | solution.py:17
  149.4 17.3 %collective-permute-start.10 = (bf16[256,448]{0,1:T(8,128)(2,1)}, bf16[256,448]{0,1:T(8,128)(2,1)S(1)}, u32[]{:S(2)}, u32[]{:S(2)}) collective-permute-start(bf16[256,448]{0,1:T(8,128)(2,1)} %get-tuple-element.63), channel_id=1, source_target_pairs={{0,256},{128,384},{256,0},{384,128},{1,257},{129,385},{257,1},{385... | collective-permute-start | bytes 688136 | tf_op jit(solution)/shard_map/ppermute | solution.py:17
  153.0 13.8 %collective-permute-start.11 = (bf16[256,448]{0,1:T(8,128)(2,1)S(1)}, bf16[256,448]{0,1:T(8,128)(2,1)S(1)}, u32[]{:S(2)}, u32[]{:S(2)}) collective-permute-start(bf16[256,448]{0,1:T(8,128)(2,1)S(1)} %get-tuple-element.62), channel_id=1, source_target_pairs={{0,384},{128,0},{256,128},{384,256},{1,385},{129,1},{257,129},{385... | collective-permute-start | bytes 688136 | tf_op jit(solution)/shard_map/ppermute | solution.py:17
  156.7 10.2 %collective-permute-start.12 = (bf16[64,448]{1,0:T(8,128)(2,1)S(1)}, bf16[64,448]{1,0:T(8,128)(2,1)S(1)}, u32[]{:S(2)}, u32[]{:S(2)}) collective-permute-start(bf16[64,448]{1,0:T(8,128)(2,1)S(1)} %bitcast.103), channel_id=1, source_target_pairs={{0,128},{128,256},{256,384},{384,0},{1,129},{129,257},{257,385},{3... | collective-permute-start | bytes 172040 | tf_op jit(solution)/shard_map/ppermute | solution.py:17
  159.2 7.7 %collective-permute-start.13 = (bf16[64,448]{1,0:T(8,128)(2,1)S(1)}, bf16[64,448]{1,0:T(8,128)(2,1)S(1)}, u32[]{:S(2)}, u32[]{:S(2)}) collective-permute-start(bf16[64,448]{1,0:T(8,128)(2,1)S(1)} %bitcast.104), channel_id=1, source_target_pairs={{0,256},{128,384},{256,0},{384,128},{1,257},{129,385},{257,1},{385... | collective-permute-start | bytes 172040 | tf_op jit(solution)/shard_map/ppermute | solution.py:17
  162.4 13.9 %copy-start.2 = (bf16[8,256,896]{2,1,0:T(8,128)(2,1)S(1)}, bf16[8,256,896]{2,1,0:T(8,128)(2,1)}, u32[]{:S(2)}) copy-start(bf16[8,256,896]{2,1,0:T(8,128)(2,1)} %all-gather.7.cloned.1.call-done) | copy-start | bytes 11010052
  162.6 5.6 %collective-permute-start.14 = (bf16[64,448]{1,0:T(8,128)(2,1)S(1)}, bf16[64,448]{1,0:T(8,128)(2,1)S(1)}, u32[]{:S(2)}, u32[]{:S(2)}) collective-permute-start(bf16[64,448]{1,0:T(8,128)(2,1)S(1)} %bitcast.105), channel_id=1, source_target_pairs={{0,384},{128,0},{256,128},{384,256},{1,385},{129,1},{257,129},{385... | collective-permute-start | bytes 172040 | tf_op jit(solution)/shard_map/ppermute | solution.py:17
  168.1 8.2 %collective-permute-start.15 = (bf16[4,256,448]{1,2,0:T(8,128)(2,1)S(1)}, bf16[4,256,448]{1,2,0:T(8,128)(2,1)S(1)}, u32[]{:S(2)}, u32[]{:S(2)}) collective-permute-start(bf16[4,256,448]{1,2,0:T(8,128)(2,1)S(1)} %bitcast_dynamic-update-slice_fusion), channel_id=1, source_target_pairs={{0,1},{1,0},{2,3},{3,2},{4,5},{5,4},{6,7},{7,6},{8,9},{9,8},{10,11... | collective-permute-start | bytes 2752520 | tf_op jit(solution)/shard_map/ppermute | solution.py:21
Sparse Core Ops, SparseCore 0:
  10.1 50.8 all-gather.4
  63.1 52.2 all-gather.6
